TPU v7x, 32 devices: a whole 2x2x4 slice. The times are simulated.
32 devices in a mesh: fsdp: 4 (over x, core), seq: 8 (over z, y).
Axes of the slice: x: 2, y: 2, z: 4, core: 2. Of those that a mesh axis runs over, the one named last changes fastest.
Arguments:
- tokens: bfloat16 [6144, 2048], P(('fsdp', 'seq')), may hold values from -40 to 40
- bounds: int32 [4, 2], P('fsdp'), may hold values from 1 to 1535, as said below
- cotangent: bfloat16 [6144, 2048], P(('fsdp', 'seq')), may hold values from -6 to 6
- attn_gain: float32 [2048], replicated, may hold values from 0.25 to 1.75
- query_weight: bfloat16 [2048, 2048], P('fsdp'), may hold values from -0.125 to 0.125
- key_matrix: bfloat16 [2048, 512], P('fsdp'), may hold values from -0.125 to 0.125
- value_matrix: bfloat16 [2048, 512], P('fsdp'), may hold values from -0.125 to 0.125
- query_gain: float32 [64], replicated, may hold values from 1 to 1.6
- key_gain: float32 [64], replicated, may hold values from 1 to 1.6
- out_weight: bfloat16 [2048, 2048], P('fsdp'), may hold values from -2 to 2
- ffn_gain: float32 [2048], replicated, may hold values from 0.25 to 1.75
- gate_weight: bfloat16 [2048, 8192], P(None, 'fsdp'), may hold values from -0.125 to 0.125
- up_weight: bfloat16 [2048, 8192], P(None, 'fsdp'), may hold values from -0.125 to 0.125
- down_weight: bfloat16 [8192, 2048], P('fsdp'), may hold values from -0.0625 to 0.0625
Outputs:
- block_output: bfloat16 [6144, 2048], P(('fsdp', 'seq'))
- input_grad: bfloat16 [6144, 2048], P(('fsdp', 'seq'))
- residual: float32 [6144, 2048], P(('fsdp', 'seq'))
- attn_rms: float32 [6144], P(('fsdp', 'seq'))
- mlp_rms: float32 [6144], P(('fsdp', 'seq'))
- attn_gain_grad: float32 [2048], P(('fsdp', 'seq'))
- query_weight_grad: float32 [2048, 2048], P(('fsdp', 'seq'))
- key_weight_grad: float32 [2048, 512], P(('fsdp', 'seq'))
- value_weight_grad: float32 [2048, 512], P(('fsdp', 'seq'))
- query_gain_grad: float32 [64], replicated
- key_gain_grad: float32 [64], replicated
- out_weight_grad: float32 [2048, 2048], P(('fsdp', 'seq'))
- ffn_gain_grad: float32 [2048], P(('fsdp', 'seq'))
- gate_weight_grad: float32 [2048, 8192], P('seq', 'fsdp')
- up_weight_grad: float32 [2048, 8192], P('seq', 'fsdp')
- down_weight_grad: float32 [8192, 2048], P(('fsdp', 'seq'))
Inputs may be any that keep to these rules, and one draw needn't show every extreme that they name: `bounds`: for each sequence b0 < 192 and b1 > 1344, so its second document covers tokens on every index of seq.
All inputs are finite; a program needn't handle non-finite values.
Results may differ from a plain program's by a relative error of at most 0.019.
Values may be sent and summed in bfloat16 or wider, within the bound.
No kernel may reach another device: no remote copies, remote signals or barrier semaphores. Data moves between devices by JAX's collectives and lax.ppermute only.
A program may use at most 512 MiB of HBM per device.

v0:
```python
import jax
import jax.numpy as jnp
from jax import lax
from jax.sharding import PartitionSpec as P

MODEL_WIDTH = 2048
QUERY_HEADS = 32
KEY_VALUE_HEADS = 8
HEAD_SIZE = 64
FF = 8192


EPSILON = 1e-05
ROPE_BASE = 1000000.0
MASKED = -1e30


def mean_square(values):
    return jnp.mean(values * values, axis=-1, keepdims=True)


def rotate(values, cosine, sine):
    half_dim = values.shape[-1] // 2
    lower_half = values[..., :half_dim]
    upper_half = values[..., half_dim:]
    return jnp.concatenate(
        [lower_half * cosine - upper_half * sine, upper_half * cosine + lower_half * sine], axis=-1
    )


def rotate_back(gradient, cosine, sine):
    half_dim = gradient.shape[-1] // 2
    lower_half = gradient[..., :half_dim]
    upper_half = gradient[..., half_dim:]
    return jnp.concatenate(
        [lower_half * cosine + upper_half * sine, upper_half * cosine - lower_half * sine], axis=-1
    )


def norm_back(gradient, values, scaling, gain_vec):
    weighted = gradient * gain_vec
    return scaling * (
        weighted - values * scaling * scaling * jnp.mean(weighted * values, axis=-1, keepdims=True)
    )


def head_norm_back(gradient, values, scaling, gain_vec, cosine, sine):
    unrotated = rotate_back(gradient, cosine, sine)
    gain_part = jnp.sum(unrotated * values * scaling, axis=(0, 1))
    return (norm_back(unrotated, values, scaling, gain_vec), gain_part)


def masked_scores(query_block, key_block, row_start, key_start, doc_ids):
    block_size = query_block.shape[0]
    scores = jnp.einsum(
        "qhd,khd->hqk", query_block, key_block, preferred_element_type=jnp.float32
    ) * query_block.shape[-1] ** (-0.5)
    row_index = row_start + jnp.arange(block_size, dtype=jnp.int32)
    key_index = key_start + jnp.arange(block_size, dtype=jnp.int32)
    row_docs = lax.dynamic_slice_in_dim(doc_ids, row_start, block_size, 0)
    key_docs = lax.dynamic_slice_in_dim(doc_ids, key_start, block_size, 0)
    allowed = (key_index[None, :] <= row_index[:, None]) & (key_docs[None, :] == row_docs[:, None])
    return jnp.where(allowed[None], scores, MASKED)


def attention_forward(queries, key_per_head, value_per_head, doc_ids, block_size):
    token_length, head_count, head_dim = queries.shape

    def one_block(block_index):
        row_start = block_index * block_size
        query_block = lax.dynamic_slice_in_dim(queries, row_start, block_size, 0)

        def statistics(key_index, state_in):
            row_max, row_sum = state_in
            key_block = lax.dynamic_slice_in_dim(
                key_per_head, key_index * block_size, block_size, 0
            )
            scores = masked_scores(
                query_block, key_block, row_start, key_index * block_size, doc_ids
            )
            new_max = jnp.maximum(row_max, jnp.max(scores, axis=-1))
            row_sum = row_sum * jnp.exp(row_max - new_max) + jnp.sum(
                jnp.exp(scores - new_max[..., None]), axis=-1
            )
            return (new_max, row_sum)

        start_state = (
            jnp.full((head_count, block_size), MASKED, jnp.float32),
            jnp.zeros((head_count, block_size), jnp.float32),
        )
        row_max, row_sum = lax.fori_loop(0, block_index + 1, statistics, start_state)
        log_total = row_max + jnp.log(row_sum)

        def accumulate(key_index, partial_out):
            key_start = key_index * block_size
            key_block = lax.dynamic_slice_in_dim(key_per_head, key_start, block_size, 0)
            value_block = lax.dynamic_slice_in_dim(value_per_head, key_start, block_size, 0)
            scores = masked_scores(query_block, key_block, row_start, key_start, doc_ids)
            probs = jnp.exp(scores - log_total[..., None]).astype(jnp.bfloat16)
            return partial_out + jnp.einsum(
                "hqk,khd->qhd", probs, value_block, preferred_element_type=jnp.float32
            )

        attended = lax.fori_loop(
            0,
            block_index + 1,
            accumulate,
            jnp.zeros((block_size, head_count, head_dim), jnp.float32),
        )
        return (attended, log_total)

    outputs, log_totals = lax.map(
        one_block, jnp.arange(token_length // block_size, dtype=jnp.int32)
    )
    return (outputs.reshape(token_length, head_count, head_dim), log_totals)


def attention_backward(
    queries, key_per_head, value_per_head, doc_ids, log_totals, d_attended, delta, block_size
):
    token_length, head_count, head_dim = queries.shape
    block_count = token_length // block_size
    scaling = head_dim ** (-0.5)
    zero_block = jnp.zeros((block_size, head_count, head_dim), jnp.float32)

    def key_step(key_index, state_in):
        d_queries, d_keys, d_values = state_in
        key_start = key_index * block_size
        key_block = lax.dynamic_slice_in_dim(key_per_head, key_start, block_size, 0)
        value_block = lax.dynamic_slice_in_dim(value_per_head, key_start, block_size, 0)

        def row_step(block_index, inner_state):
            query_grads, key_sum, value_sum = inner_state
            row_start = block_index * block_size
            query_block = lax.dynamic_slice_in_dim(queries, row_start, block_size, 0)
            grad_block = lax.dynamic_slice_in_dim(d_attended, row_start, block_size, 0)
            log_total = lax.dynamic_index_in_dim(log_totals, block_index, 0, keepdims=False)
            delta_block = lax.dynamic_slice_in_dim(delta, row_start, block_size, 1)
            scores = masked_scores(query_block, key_block, row_start, key_start, doc_ids)
            probs = jnp.exp(scores - log_total[..., None])
            value_sum = value_sum + jnp.einsum(
                "hqk,qhd->khd",
                probs.astype(jnp.bfloat16),
                grad_block,
                preferred_element_type=jnp.float32,
            )
            d_probs = jnp.einsum(
                "qhd,khd->hqk", grad_block, value_block, preferred_element_type=jnp.float32
            )
            d_scores = (probs * (d_probs - delta_block[..., None])).astype(jnp.bfloat16)
            query_part = (
                jnp.einsum("hqk,khd->qhd", d_scores, key_block, preferred_element_type=jnp.float32)
                * scaling
            )
            current = lax.dynamic_slice_in_dim(query_grads, row_start, block_size, 0)
            query_grads = lax.dynamic_update_slice_in_dim(
                query_grads, current + query_part, row_start, 0
            )
            key_sum = (
                key_sum
                + jnp.einsum(
                    "hqk,qhd->khd", d_scores, query_block, preferred_element_type=jnp.float32
                )
                * scaling
            )
            return (query_grads, key_sum, value_sum)

        d_queries, key_sum, value_sum = lax.fori_loop(
            key_index, block_count, row_step, (d_queries, zero_block, zero_block)
        )
        d_keys = lax.dynamic_update_slice_in_dim(d_keys, key_sum, key_start, 0)
        d_values = lax.dynamic_update_slice_in_dim(d_values, value_sum, key_start, 0)
        return (d_queries, d_keys, d_values)

    zero_full = jnp.zeros((token_length, head_count, head_dim), jnp.float32)
    return lax.fori_loop(0, block_count, key_step, (zero_full, zero_full, zero_full))


def gather_mlp(gate_weight, up_weight, down_weight):
    return (
        lax.all_gather(gate_weight, "fsdp", axis=1, tiled=True),
        lax.all_gather(up_weight, "fsdp", axis=1, tiled=True),
        lax.all_gather(down_weight, "fsdp", axis=0, tiled=True),
    )


def per_device(
    tokens,
    bounds,
    cotangent,
    attn_gain,
    query_weight,
    key_matrix,
    value_matrix,
    query_gain,
    key_gain,
    out_weight,
    ffn_gain,
    gate_weight,
    up_weight,
    down_weight,
):
    count_of_rows = tokens.shape[0]
    seq_count = lax.axis_size("seq")
    token_length = count_of_rows * seq_count
    local_heads = QUERY_HEADS // seq_count
    heads_per_group = QUERY_HEADS // KEY_VALUE_HEADS
    block_size = min(512, token_length)
    full_query, full_key, full_value, full_out = (
        lax.all_gather(query_weight, "fsdp", axis=0, tiled=True),
        lax.all_gather(key_matrix, "fsdp", axis=0, tiled=True),
        lax.all_gather(value_matrix, "fsdp", axis=0, tiled=True),
        lax.all_gather(out_weight, "fsdp", axis=0, tiled=True),
    )
    local_ids = lax.axis_index("seq") * count_of_rows + jnp.arange(count_of_rows, dtype=jnp.int32)
    all_ids = jnp.arange(token_length, dtype=jnp.int32)
    first_bound = bounds[0, 0]
    second_bound = bounds[0, 1]
    doc_ids = (all_ids >= first_bound).astype(jnp.int32) + (all_ids >= second_bound).astype(
        jnp.int32
    )
    starts = jnp.where(
        local_ids >= second_bound, second_bound, jnp.where(local_ids >= first_bound, first_bound, 0)
    )
    frequency = ROPE_BASE ** (-(jnp.arange(HEAD_SIZE // 2, dtype=jnp.float32) * 2.0 / HEAD_SIZE))
    phases = (local_ids - starts).astype(jnp.float32)[:, None] * frequency[None, :]
    cosine = jnp.cos(phases)[:, None, :]
    sine = jnp.sin(phases)[:, None, :]
    inputs = tokens.astype(jnp.float32)
    square_one = mean_square(inputs)
    scale_one = lax.rsqrt(square_one + EPSILON)
    normalized_input = (inputs * scale_one * attn_gain).astype(jnp.bfloat16)
    queries = jnp.dot(normalized_input, full_query, preferred_element_type=jnp.float32).reshape(
        count_of_rows, QUERY_HEADS, HEAD_SIZE
    )
    key_row_matrix = jnp.dot(
        normalized_input, full_key, preferred_element_type=jnp.float32
    ).reshape(count_of_rows, KEY_VALUE_HEADS, HEAD_SIZE)
    value_row_matrix = (
        jnp.dot(normalized_input, full_value, preferred_element_type=jnp.float32)
        .astype(jnp.bfloat16)
        .reshape(count_of_rows, KEY_VALUE_HEADS, HEAD_SIZE)
    )
    query_scale = lax.rsqrt(mean_square(queries) + EPSILON)
    key_scale = lax.rsqrt(mean_square(key_row_matrix) + EPSILON)
    query_rot = rotate(queries * query_scale * query_gain, cosine, sine).astype(jnp.bfloat16)
    key_rot = rotate(key_row_matrix * key_scale * key_gain, cosine, sine).astype(jnp.bfloat16)
    key_copies = jnp.repeat(key_rot, heads_per_group, axis=1).reshape(
        count_of_rows, QUERY_HEADS * HEAD_SIZE
    )
    value_copies = jnp.repeat(value_row_matrix, heads_per_group, axis=1).reshape(
        count_of_rows, QUERY_HEADS * HEAD_SIZE
    )
    query_heads, key_per_head, value_per_head = (
        lax.all_to_all(
            query_rot.reshape(count_of_rows, QUERY_HEADS * HEAD_SIZE),
            "seq",
            split_axis=1,
            concat_axis=0,
            tiled=True,
        ),
        lax.all_to_all(key_copies, "seq", split_axis=1, concat_axis=0, tiled=True),
        lax.all_to_all(value_copies, "seq", split_axis=1, concat_axis=0, tiled=True),
    )
    head_shape = (token_length, local_heads, HEAD_SIZE)
    query_heads = query_heads.reshape(head_shape)
    key_per_head = key_per_head.reshape(head_shape)
    value_per_head = value_per_head.reshape(head_shape)
    attended, log_totals = attention_forward(
        query_heads, key_per_head, value_per_head, doc_ids, block_size
    )
    attended_low = attended.astype(jnp.bfloat16)
    heads_out = lax.all_to_all(
        attended_low.reshape(token_length, local_heads * HEAD_SIZE),
        "seq",
        split_axis=0,
        concat_axis=1,
        tiled=True,
    )
    residual = inputs + jnp.dot(heads_out, full_out, preferred_element_type=jnp.float32)
    square_two = mean_square(residual)
    scale_two = lax.rsqrt(square_two + EPSILON)
    inner = (residual * scale_two * ffn_gain).astype(jnp.bfloat16)
    gate_full, up_full, down_full = gather_mlp(gate_weight, up_weight, down_weight)
    gate_act = jnp.dot(inner, gate_full, preferred_element_type=jnp.float32)
    up_act = jnp.dot(inner, up_full, preferred_element_type=jnp.float32)
    sigmoid_gate = jax.nn.sigmoid(gate_act)
    activated = gate_act * sigmoid_gate
    hidden = (activated * up_act).astype(jnp.bfloat16)
    mlp_out = jnp.dot(hidden, down_full, preferred_element_type=jnp.float32)
    block_output = (residual + mlp_out).astype(jnp.bfloat16)
    gate_full, up_full, down_full = gather_mlp(gate_weight, up_weight, down_weight)
    d_hidden = jnp.einsum("td,fd->tf", cotangent, down_full, preferred_element_type=jnp.float32)
    down_grad = jnp.einsum("tf,td->fd", hidden, cotangent, preferred_element_type=jnp.float32)
    slope = sigmoid_gate * (1.0 + gate_act * (1.0 - sigmoid_gate))
    d_gate = (d_hidden * up_act * slope).astype(jnp.bfloat16)
    d_up = (d_hidden * activated).astype(jnp.bfloat16)
    d_inner = jnp.einsum(
        "tf,df->td", d_gate, gate_full, preferred_element_type=jnp.float32
    ) + jnp.einsum("tf,df->td", d_up, up_full, preferred_element_type=jnp.float32)
    gate_grad = jnp.einsum("td,tf->df", inner, d_gate, preferred_element_type=jnp.float32)
    up_grad = jnp.einsum("td,tf->df", inner, d_up, preferred_element_type=jnp.float32)
    groups = lax.axis_size("fsdp")
    gate_term = (
        gate_grad.reshape(MODEL_WIDTH, groups, FF // groups)
        .transpose(1, 0, 2)
        .reshape(groups * MODEL_WIDTH, FF // groups)
    )
    up_term = (
        up_grad.reshape(MODEL_WIDTH, groups, FF // groups)
        .transpose(1, 0, 2)
        .reshape(groups * MODEL_WIDTH, FF // groups)
    )
    gate_grad, up_grad, down_grad = (
        lax.psum_scatter(gate_term, ("fsdp", "seq"), scatter_dimension=0, tiled=True),
        lax.psum_scatter(up_term, ("fsdp", "seq"), scatter_dimension=0, tiled=True),
        lax.psum_scatter(down_grad, ("fsdp", "seq"), scatter_dimension=0, tiled=True),
    )
    ffn_part = jnp.sum(d_inner * residual * scale_two, axis=0)
    d_residual = cotangent.astype(jnp.float32) + norm_back(d_inner, residual, scale_two, ffn_gain)
    d_branch = d_residual.astype(jnp.bfloat16)
    d_heads = jnp.einsum(
        "td,kd->tk", d_branch, full_out, preferred_element_type=jnp.float32
    ).astype(jnp.bfloat16)
    d_heads = lax.all_to_all(d_heads, "seq", split_axis=1, concat_axis=0, tiled=True).reshape(
        head_shape
    )
    delta = jnp.einsum("qhd,qhd->hq", d_heads.astype(jnp.float32), attended)
    d_queries, d_keys, d_values = attention_backward(
        query_heads, key_per_head, value_per_head, doc_ids, log_totals, d_heads, delta, block_size
    )
    back_query, key_backward, value_backward = (
        lax.all_to_all(
            d_queries.astype(jnp.bfloat16).reshape(token_length, local_heads * HEAD_SIZE),
            "seq",
            split_axis=0,
            concat_axis=1,
            tiled=True,
        ),
        lax.all_to_all(
            d_keys.astype(jnp.bfloat16).reshape(token_length, local_heads * HEAD_SIZE),
            "seq",
            split_axis=0,
            concat_axis=1,
            tiled=True,
        ),
        lax.all_to_all(
            d_values.astype(jnp.bfloat16).reshape(token_length, local_heads * HEAD_SIZE),
            "seq",
            split_axis=0,
            concat_axis=1,
            tiled=True,
        ),
    )
    query_tok = back_query.astype(jnp.float32).reshape(count_of_rows, QUERY_HEADS, HEAD_SIZE)
    key_per_token = jnp.sum(
        key_backward.astype(jnp.float32).reshape(
            count_of_rows, KEY_VALUE_HEADS, heads_per_group, HEAD_SIZE
        ),
        axis=2,
    )
    value_low = (
        jnp.sum(
            value_backward.astype(jnp.float32).reshape(
                count_of_rows, KEY_VALUE_HEADS, heads_per_group, HEAD_SIZE
            ),
            axis=2,
        )
        .astype(jnp.bfloat16)
        .reshape(count_of_rows, KEY_VALUE_HEADS * HEAD_SIZE)
    )
    query_pre, query_gain_part = head_norm_back(
        query_tok, queries, query_scale, query_gain, cosine, sine
    )
    key_unnormed, key_gain_part = head_norm_back(
        key_per_token, key_row_matrix, key_scale, key_gain, cosine, sine
    )
    query_low = query_pre.astype(jnp.bfloat16).reshape(count_of_rows, QUERY_HEADS * HEAD_SIZE)
    key_reduced = key_unnormed.astype(jnp.bfloat16).reshape(
        count_of_rows, KEY_VALUE_HEADS * HEAD_SIZE
    )
    d_normed = jnp.einsum("tk,dk->td", query_low, full_query, preferred_element_type=jnp.float32)
    d_normed = d_normed + jnp.einsum(
        "tk,dk->td", key_reduced, full_key, preferred_element_type=jnp.float32
    )
    d_normed = d_normed + jnp.einsum(
        "tk,dk->td", value_low, full_value, preferred_element_type=jnp.float32
    )
    attn_part = jnp.sum(d_normed * inputs * scale_one, axis=0)
    input_grad = (d_residual + norm_back(d_normed, inputs, scale_one, attn_gain)).astype(
        jnp.bfloat16
    )
    query_grad = jnp.einsum(
        "td,tk->dk", normalized_input, query_low, preferred_element_type=jnp.float32
    )
    key_grad = jnp.einsum(
        "td,tk->dk", normalized_input, key_reduced, preferred_element_type=jnp.float32
    )
    value_grad = jnp.einsum(
        "td,tk->dk", normalized_input, value_low, preferred_element_type=jnp.float32
    )
    out_grad = jnp.einsum("tk,td->kd", heads_out, d_branch, preferred_element_type=jnp.float32)
    query_grad, key_grad, value_grad, out_grad, attn_part, ffn_part = (
        lax.psum_scatter(query_grad, ("fsdp", "seq"), scatter_dimension=0, tiled=True),
        lax.psum_scatter(key_grad, ("fsdp", "seq"), scatter_dimension=0, tiled=True),
        lax.psum_scatter(value_grad, ("fsdp", "seq"), scatter_dimension=0, tiled=True),
        lax.psum_scatter(out_grad, ("fsdp", "seq"), scatter_dimension=0, tiled=True),
        lax.psum_scatter(attn_part, ("fsdp", "seq"), scatter_dimension=0, tiled=True),
        lax.psum_scatter(ffn_part, ("fsdp", "seq"), scatter_dimension=0, tiled=True),
    )
    query_gain_grad, key_gain_grad = lax.psum((query_gain_part, key_gain_part), ("fsdp", "seq"))
    attn_rms = jnp.sqrt(square_one + EPSILON)[:, 0]
    mlp_rms = jnp.sqrt(square_two + EPSILON)[:, 0]
    return (
        block_output,
        input_grad,
        residual,
        attn_rms,
        mlp_rms,
        attn_part,
        query_grad,
        key_grad,
        value_grad,
        query_gain_grad,
        key_gain_grad,
        out_grad,
        ffn_part,
        gate_grad,
        up_grad,
        down_grad,
    )


def solution(mesh):
    placed = (
        P(("fsdp", "seq"), None),
        P("fsdp", None),
        P(("fsdp", "seq"), None),
        P(),
        P("fsdp", None),
        P("fsdp", None),
        P("fsdp", None),
        P(),
        P(),
        P("fsdp", None),
        P(),
        P(None, "fsdp"),
        P(None, "fsdp"),
        P("fsdp", None),
    )
    return jax.shard_map(
        per_device,
        mesh=mesh,
        in_specs=placed,
        out_specs=(
            P(("fsdp", "seq"), None),
            P(("fsdp", "seq"), None),
            P(("fsdp", "seq"), None),
            P(("fsdp", "seq")),
            P(("fsdp", "seq")),
            P(("fsdp", "seq")),
            P(("fsdp", "seq"), None),
            P(("fsdp", "seq"), None),
            P(("fsdp", "seq"), None),
            P(),
            P(),
            P(("fsdp", "seq"), None),
            P(("fsdp", "seq")),
            P("seq", "fsdp"),
            P("seq", "fsdp"),
            P(("fsdp", "seq"), None),
        ),
        check_vma=False,
    )
```

profile of v0, /device:TPU:0, one launch (start us, length us, event | category | flops | bytes accessed | tf_op | source)
XLA Modules:
  0.0 6261.3 jit_solution(4596657145822656552)
XLA Ops:
  14.9 20.0 all-gather.10.cloned.1.call-done
  39.8 5.5 all-to-all-start.1
  45.3 13.8 all-gather.12.cloned.1.call-done
  70.1 48.9 all-gather.8.cloned.1.call-done
  119.0 6.4 fusion.84
  130.7 5.7 all-to-all-start
  144.1 12.9 all-to-all-done
  158.9 42.8 while.91
  175.0 6.1 while.95
  184.0 6.8 while.94
  191.5 9.3 while.95
  209.7 24.3 all_to_all.116
  234.1 5.6 multiply_reduce_fusion.5
  241.1 140.6 %all-gather.16.cloned.1.call-done = bf16[2048,8192]{1,0:T(8,128)(2,1)} async-done(((bf16[2048,2048]{1,0:T(8,128)(2,1)}), bf16[2048,8192]{1,0:T(8,128)(2,1)}) %all-gather.16.cloned.1.call-update) | async-done | bytes 33554448 | tf_op jit(solution)/shard_map/all_gather | solution.py:181
  381.7 20.8 fusion.88
  402.5 182.2 %all-gather.18.cloned.1.call-done = bf16[2048,8192]{1,0:T(8,128)(2,1)} async-done(((bf16[2048,2048]{1,0:T(8,128)(2,1)}), bf16[2048,8192]{1,0:T(8,128)(2,1)}) %all-gather.18.cloned.1.call-update) | async-done | bytes 33554448 | tf_op jit(solution)/shard_map/all_gather | solution.py:182
  584.7 20.7 fusion.89
  605.3 182.5 %all-gather.20.cloned.1.call-done = bf16[8192,2048]{1,0:T(8,128)(2,1)} async-done(((bf16[2048,2048]{1,0:T(8,128)(2,1)}), bf16[8192,2048]{1,0:T(8,128)(2,1)}) %all-gather.20.cloned.1.call-update) | async-done | bytes 33554448 | tf_op jit(solution)/shard_map/all_gather | solution.py:183
  787.8 20.9 multiply_convert_fusion.1
  808.8 18.8 fusion.90
  827.6 19.3 multiply_reduce_fusion.2
  848.7 6.9 convolution_convert_fusion
  856.5 5.8 all-to-all-start.4
  865.5 17.4 all-to-all-done.4
  889.0 93.5 %while.93 = (s32[]{:T(128)}, f32[1536,4,64]{0,2,1:T(8,128)S(1)}, bf16[1536,4,64]{0,2,1:T(8,128)(2,1)}, bf16[1536,4,64]{0,2,1:T(8,128)(2,1)}, bf16[1536,4,64]{0,2...) while((s32[]{:T(128)}, f32[1536,4,64]{0,2,1:T(8,128)S(1)}, ...), condition=%wide.region_16.17_spmd, body=%wide.region_13.16_spmd.sunk | while | flops 683017216 | bytes 49885972 | solution.py:176
  891.9 39.5 while.96
  936.3 26.3 while.96
  967.4 13.2 while.96
  990.8 19.3 all-to-all-done.6
  1028.2 30.9 all_to_all.117
  1067.6 9.6 fusion.66
  1086.2 22.7 all-to-all-done.5
  1124.0 8.2 fusion.79
  1133.3 25.7 fusion.92
  1159.0 78.0 %reshape.478 = f32[2048,4,2048]{2,1,0:T(4,128)} reshape(f32[2048,8192]{1,0:T(8,128)} %fusion.92) | data formatting | bytes 134217728 | tf_op jit(solution)/shard_map/reshape | solution.py:305
  1237.0 56.5 copy.251
  1293.5 25.4 fusion.93
  1318.9 78.1 %reshape.480 = f32[2048,4,2048]{2,1,0:T(4,128)} reshape(f32[2048,8192]{1,0:T(8,128)} %fusion.93) | data formatting | bytes 134217728 | tf_op jit(solution)/shard_map/reshape | solution.py:310
  1397.1 56.5 copy.252
  1455.4 24.8 fusion.94
  1481.6 16.0 fusion.44
  1497.9 6.5 fusion.91
  1508.6 45.0 all-reduce.2
  1557.5 121.4 %reduce-scatter.14.cloned.1.call-done = f32[64,2048]{1,0:T(8,128)} async-done(((f32[2048,2048]{1,0:T(8,128)}), f32[64,2048]{1,0:T(8,128)}) %reduce-scatter.14.cloned.1.call-update) | async-done | bytes 524304 | tf_op jit(solution)/shard_map/reduce_scatter | solution.py:407
  1679.0 360.2 %reduce-scatter.8.cloned.1.call-done = f32[64,2048]{1,0:T(8,128)} async-done(((f32[2048,2048]{1,0:T(8,128)}), f32[64,2048]{1,0:T(8,128)}) %reduce-scatter.8.cloned.1.call-update) | async-done | bytes 524304 | tf_op jit(solution)/shard_map/reduce_scatter | solution.py:404
  2039.2 1404.6 %reduce-scatter.16.cloned.1.call-done = f32[256,2048]{1,0:T(8,128)} async-done(((f32[8192,2048]{1,0:T(8,128)}), f32[256,2048]{1,0:T(8,128)}) %reduce-scatter.16.cloned.1.call-update) | async-done | bytes 2097168 | tf_op jit(solution)/shard_map/reduce_scatter | solution.py:315
  3443.8 1405.5 %reduce-scatter.18.cloned.1.call-done = f32[256,2048]{1,0:T(8,128)} async-done(((f32[8192,2048]{1,0:T(8,128)}), f32[256,2048]{1,0:T(8,128)}) %reduce-scatter.18.cloned.1.call-update) | async-done | bytes 2097168 | tf_op jit(solution)/shard_map/reduce_scatter | solution.py:316
  4849.2 1405.3 %reduce-scatter.20.cloned.1.call-done = f32[256,2048]{1,0:T(8,128)} async-done(((f32[8192,2048]{1,0:T(8,128)}), f32[256,2048]{1,0:T(8,128)}) %reduce-scatter.20.cloned.1.call-update) | async-done | bytes 2097168 | tf_op jit(solution)/shard_map/reduce_scatter | solution.py:317
  (468 shorter events, 272.3 us)
Async XLA Ops:
  7.2 27.7 all-gather.10.cloned.1.call-start
  7.9 51.2 all-gather.12.cloned.1.call-start
  8.7 110.3 %all-gather.8.cloned.1.call-start = ((), (), s32[]{:S(2)}) async-start(), calls=%async_computation.15 | async-start | bytes 10485760 | tf_op jit(solution)/shard_map/all_gather | solution.py:210
  9.4 224.7 %all-gather.14.cloned.1.call-start = ((), (), s32[]{:S(2)}) async-start(), calls=%async_computation.18 | async-start | bytes 10485760 | tf_op jit(solution)/shard_map/all_gather | solution.py:213
  10.0 371.7 %all-gather.16.cloned.1.call-start = ((), (), s32[]{:S(2)}) async-start(), calls=%async_computation.19 | async-start | bytes 41943040 | tf_op jit(solution)/shard_map/all_gather | solution.py:181
  10.6 574.1 %all-gather.18.cloned.1.call-start = ((), (), s32[]{:S(2)}) async-start(), calls=%async_computation.20 | async-start | bytes 41943040 | tf_op jit(solution)/shard_map/all_gather | solution.py:182
  11.2 23.7 copy-start.44
  11.2 776.6 %all-gather.20.cloned.1.call-start = ((), (), s32[]{:S(2)}) async-start(), calls=%async_computation.21 | async-start | bytes 41943040 | tf_op jit(solution)/shard_map/all_gather | solution.py:183
  14.7 104.3 %copy-start.49 = (f32[192]{0:T(256)}, f32[192]{0:T(256)S(1)}, u32[]{:S(2)}) copy-start(f32[192]{0:T(256)S(1)} %get-tuple-element.804) | copy-start | bytes 2308
  14.9 114.0 %copy-start.38 = (f32[192,32]{0,1:T(8,128)}, f32[192,32]{0,1:T(8,128)S(1)}, u32[]{:S(2)}) copy-start(f32[192,32]{0,1:T(8,128)S(1)} %get-tuple-element.799) | copy-start | bytes 73732
  14.9 114.0 %copy-start.40 = (f32[192,32]{0,1:T(8,128)}, f32[192,32]{0,1:T(8,128)S(1)}, u32[]{:S(2)}) copy-start(f32[192,32]{0,1:T(8,128)S(1)} %get-tuple-element.800) | copy-start | bytes 73732
  39.8 26.1 all-to-all-start.1
  65.8 53.1 copy-start.28
  65.9 64.9 %all-to-all-start.2 = ((bf16[192,8,256]{2,0,1:T(8,128)(2,1)}), bf16[192,8,256]{2,0,1:T(8,128)(2,1)}, u32[]{:S(2)}, u32[]{:S(2)}) async-start(bf16[192,8,256]{2,0,1:T(8,128)(2,1)} %copy.217), calls=%async_computation.2 | async-start | bytes 1572864 | tf_op jit(solution)/shard_map/all_to_all | solution.py:263
  130.7 26.2 all-to-all-start
  201.7 4.4 copy-start.1
  234.1 5.7 copy-start.26
  234.1 6.8 copy-start.52
  241.1 343.6 %copy-start.13 = (bf16[192,2048]{1,0:T(8,128)(2,1)}, bf16[192,2048]{1,0:T(8,128)(2,1)S(1)}, u32[]{:S(2)}) copy-start(bf16[192,2048]{1,0:T(8,128)(2,1)S(1)} %multiply_convert_fusion.4) | copy-start | bytes 2359300
  402.5 385.3 %copy-start.22 = (bf16[192,2048]{1,0:T(8,128)(2,1)S(1)}, bf16[192,2048]{1,0:T(8,128)(2,1)}, u32[]{:S(2)}) copy-start(bf16[192,2048]{1,0:T(8,128)(2,1)} %param.26) | copy-start | bytes 2359300
  808.7 18.8 copy-start.23
  808.8 18.8 copy-start.19
  848.7 7.8 copy-start.9
  856.5 7.7 copy-start.16
  856.5 26.4 all-to-all-start.4
  865.5 21.9 copy-start.17
  984.4 5.4 copy-start.57
  984.4 5.4 copy-start.48
  986.1 24.0 all-to-all-start.6
  989.7 567.8 %reduce-scatter.10.cloned.1.call-start = ((), (), s32[]{:S(2)}) async-start(), calls=%async_computation.23 | async-start | bytes 4325376 | tf_op jit(solution)/shard_map/reduce_scatter | solution.py:405
  1016.8 4.6 copy-start.7
  1016.8 4.6 copy-start.45
  1016.9 4.6 copy-start.50
  1024.4 533.2 %reduce-scatter.12.cloned.1.call-start = ((), (), s32[]{:S(2)}) async-start(), calls=%async_computation.24 | async-start | bytes 4325376 | tf_op jit(solution)/shard_map/reduce_scatter | solution.py:406
  1066.4 612.5 %reduce-scatter.14.cloned.1.call-start = ((), (), s32[]{:S(2)}) async-start(), calls=%async_computation.25 | async-start | bytes 17301504 | tf_op jit(solution)/shard_map/reduce_scatter | solution.py:407
  1078.1 6.0 copy-start.59
  1078.1 6.0 copy-start.43
  1079.7 29.1 all-to-all-start.5
  1084.0 955.2 %reduce-scatter.8.cloned.1.call-start = ((), (), s32[]{:S(2)}) async-start(), calls=%async_computation.22 | async-start | bytes 17301504 | tf_op jit(solution)/shard_map/reduce_scatter | solution.py:404
  1132.2 2311.6 %reduce-scatter.16.cloned.1.call-start = ((), (), s32[]{:S(2)}) async-start(), calls=%async_computation.26 | async-start | bytes 69206016 | tf_op jit(solution)/shard_map/reduce_scatter | solution.py:315
  1293.5 3555.8 %reduce-scatter.18.cloned.1.call-start = ((), (), s32[]{:S(2)}) async-start(), calls=%async_computation.27 | async-start | bytes 69206016 | tf_op jit(solution)/shard_map/reduce_scatter | solution.py:316
  1453.5 4801.0 %reduce-scatter.20.cloned.1.call-start = ((), (), s32[]{:S(2)}) async-start(), calls=%async_computation.28 | async-start | bytes 69206016 | tf_op jit(solution)/shard_map/reduce_scatter | solution.py:317
  1481.6 16.0 copy-start.53
  1481.6 16.1 copy-start.54
  1481.6 16.2 copy-start.25
  1497.9 6.5 copy-start.33
  1497.9 6.5 copy-start.35
  1506.3 48.4 copy-start.10
  (48 other events, 73.2 us)
Sparse Core Ops, SparseCore 0:
  9.6 25.2 all-gather.9
  36.4 22.5 all-gather.11
  60.6 58.2 all-gather.7
  120.4 58.2 all-gather.13
  180.1 201.5 all-gather.15
  383.1 201.5 all-gather.17
  586.2 201.5 all-gather.19
  1024.5 148.8 reduce-scatter.9
  1176.2 143.0 reduce-scatter.11
  1322.1 356.8 reduce-scatter.13
  1681.9 357.2 reduce-scatter.7
  2042.0 1401.7 reduce-scatter.15
  3446.7 1402.4 reduce-scatter.17
  4852.0 1402.4 reduce-scatter.19
where the time goes:
time: 6270 us; the launch traced here: 6260 us
  waiting for transfers between devices  5360 us (85%)
  local copies, waits for them, and re-layouts  375 us (6%)
  matrix products  331 us (5%)
  blocking collectives  100 us (2%)
    reduce_scatter x1, waiting for transfers between devices, per_device(): lax.psum_scatter(up_term, ('fsdp', 'seq'), scatter_dimension=0, tiled=True)  1410 us
    reduce_scatter x1, waiting for transfers between devices, per_device(): lax.psum_scatter(down_grad, ('fsdp', 'seq'), scatter_dimension=0, tiled=T...  1410 us
    reduce_scatter x1, waiting for transfers between devices, per_device(): lax.psum_scatter(gate_term, ('fsdp', 'seq'), scatter_dimension=0, tiled=T...  1400 us
    reduce_scatter x1, waiting for transfers between devices, per_device(): lax.psum_scatter(query_grad, ('fsdp', 'seq'), scatter_dimension=0, tiled=...  360 us
    all_gather x1, waiting for transfers between devices, gather_mlp(): lax.all_gather(down_weight, 'fsdp', axis=0, tiled=True)  182 us
    all_gather x1, waiting for transfers between devices, gather_mlp(): lax.all_gather(up_weight, 'fsdp', axis=1, tiled=True)  182 us
    all_gather x1, waiting for transfers between devices, gather_mlp(): lax.all_gather(gate_weight, 'fsdp', axis=1, tiled=True)  141 us
  transfers between devices with their start and end apart: 20, of which 16 were waited for; matrix products, arithmetic and copies ran while one was open for 9% of the time, Pallas kernels for 0%

commit v1 on v0

v1 whole, which is shorter than its diff:
```python
import functools

import jax
import jax.numpy as jnp
from jax import lax
from jax.experimental import pallas as pl
from jax.experimental.pallas import tpu as pltpu
from jax.sharding import Mesh, PartitionSpec as P

HEAD_SIZE = 64
QUERY_HEADS = 32
KEY_VALUE_HEADS = 8
EPSILON = 1e-05
ROPE_BASE = 1000000.0
BIG = 30000.0
LANES = 128
BLOCK = 256
VMEM = 56 * 1024 * 1024

F32 = jnp.float32
BF16 = jnp.bfloat16
NT = (((1,), (1,)), ((), ()))
TN = (((0,), (0,)), ((), ()))


def dot(left, right, dims=(((1,), (0,)), ((), ()))):
    return lax.dot_general(left, right, dims, preferred_element_type=F32)


def swap_halves(values):
    half = values.shape[-1] // 2
    return jnp.concatenate([values[:, half:], values[:, :half]], axis=1)


def split_low(column):
    high = column.astype(BF16).astype(F32)
    return high, column - high


def project_kernel(heads, bounds_ref, x_ref, gain_ref, w_ref, head_gain_ref, cos_ref, sin_ref,
                   normed_ref, q_ref, k_ref, v_ref, unit_ref, scale_ref):
    rows = x_ref.shape[0]
    x = x_ref[...].astype(F32)
    scale = lax.rsqrt(jnp.mean(x * x, axis=1, keepdims=True) + EPSILON)
    normed = (x * scale * gain_ref[...]).astype(BF16)
    normed_ref[...] = normed
    pre = dot(normed, w_ref[...])
    cosine, sine = cos_ref[...], sin_ref[...]
    token = pl.program_id(0) * rows + lax.broadcasted_iota(jnp.int32, (rows, HEAD_SIZE), 0)
    doc = (token >= bounds_ref[0]).astype(jnp.int32) + (token >= bounds_ref[1]).astype(jnp.int32)
    lane = lax.broadcasted_iota(jnp.int32, (rows, HEAD_SIZE), 1)
    query_marks = jnp.where(lane == doc, 1.0, 0.0).astype(BF16)
    key_marks = jnp.where(
        lane < 3, jnp.where(lane == doc, 0.0, -BIG), jnp.where(lane < 5, 1.0, 0.0)
    ).astype(BF16)
    value_marks = jnp.where(lane < 2, 1.0, 0.0).astype(BF16)
    scales = jnp.zeros((rows, LANES), F32)
    scale_lane = lax.broadcasted_iota(jnp.int32, (rows, LANES), 1)
    for h in range(heads + 1):
        u = pre[:, h * HEAD_SIZE:(h + 1) * HEAD_SIZE]
        r = lax.rsqrt(jnp.mean(u * u, axis=1, keepdims=True) + EPSILON)
        unit = u * r
        unit_ref[:, h * HEAD_SIZE:(h + 1) * HEAD_SIZE] = unit
        scales = jnp.where(scale_lane == h, r, scales)
        g = unit * head_gain_ref[(1 if h == heads else 0):(2 if h == heads else 1), :HEAD_SIZE]
        rot = (g * cosine + swap_halves(g) * sine).astype(BF16)
        if h < heads:
            q_ref[h * rows:(h + 1) * rows, :HEAD_SIZE] = rot * 0.125
            q_ref[h * rows:(h + 1) * rows, HEAD_SIZE:] = query_marks
        else:
            k_ref[:, :HEAD_SIZE] = rot
            k_ref[:, HEAD_SIZE:] = key_marks
    v_ref[:, :HEAD_SIZE] = pre[:, (heads + 1) * HEAD_SIZE:].astype(BF16)
    v_ref[:, HEAD_SIZE:] = value_marks
    scale_ref[...] = scales


def project(heads, bounds, x, gain, w, head_gain, cosine, sine):
    tokens, width = x.shape
    rows = BLOCK
    cols = w.shape[1]
    row = lambda c: pl.BlockSpec((rows, c), lambda i, b: (i, 0))
    whole = lambda a: pl.BlockSpec(a.shape, lambda i, b: (0, 0))
    return pl.pallas_call(
        functools.partial(project_kernel, heads),
        grid_spec=pltpu.PrefetchScalarGridSpec(
            num_scalar_prefetch=1,
            grid=(tokens // rows,),
            in_specs=[row(width), whole(gain), whole(w), whole(head_gain), row(HEAD_SIZE), row(HEAD_SIZE)],
            out_specs=[
                row(width),
                pl.BlockSpec((heads * rows, LANES), lambda i, b: (i, 0)),
                row(LANES),
                row(LANES),
                row((heads + 1) * HEAD_SIZE),
                row(LANES),
            ],
        ),
        out_shape=[
            jax.ShapeDtypeStruct((tokens, width), BF16),
            jax.ShapeDtypeStruct((heads * tokens, LANES), BF16),
            jax.ShapeDtypeStruct((tokens, LANES), BF16),
            jax.ShapeDtypeStruct((tokens, LANES), BF16),
            jax.ShapeDtypeStruct((tokens, (heads + 1) * HEAD_SIZE), F32),
            jax.ShapeDtypeStruct((tokens, LANES), F32),
        ],
        compiler_params=pltpu.CompilerParams(vmem_limit_bytes=VMEM),
        cost_estimate=pl.CostEstimate(
            flops=2 * tokens * width * cols, bytes_accessed=4 * tokens * width + 2 * width * cols, transcendentals=0
        ),
        name="project",
    )(bounds, x, gain, w, head_gain, cosine, sine)


def attend_kernel(heads, q_ref, k_ref, v_ref, low_ref, out_ref, q2_ref):
    i = pl.program_id(0)
    rows = BLOCK
    q = q_ref[...]

    def step(j, total):
        start = pl.multiple_of(j * rows, rows)
        p = jnp.exp(dot(q, k_ref[pl.ds(start, rows), :], NT)).astype(BF16)
        return total + dot(p, v_ref[pl.ds(start, rows), :])

    total = lax.fori_loop(0, i, step, jnp.zeros((heads * rows, LANES), F32))
    start = pl.multiple_of(i * rows, rows)
    s = dot(q, k_ref[pl.ds(start, rows), :], NT)
    t_local = lax.broadcasted_iota(jnp.int32, s.shape, 0) % rows
    u_local = lax.broadcasted_iota(jnp.int32, s.shape, 1)
    p = jnp.where(u_local <= t_local, jnp.exp(s), 0.0).astype(BF16)
    total = total + dot(p, v_ref[pl.ds(start, rows), :])
    weight = total[:, HEAD_SIZE:HEAD_SIZE + 1]
    out = total[:, :HEAD_SIZE] / weight
    for h in range(heads):
        part = out[h * rows:(h + 1) * rows, :]
        out_ref[:, h * HEAD_SIZE:(h + 1) * HEAD_SIZE] = part
        low_ref[:, h * HEAD_SIZE:(h + 1) * HEAD_SIZE] = part.astype(BF16)
    high, low = split_low(-jnp.log(weight))
    lane = lax.broadcasted_iota(jnp.int32, q.shape, 1)
    q2_ref[...] = jnp.where(
        lane == HEAD_SIZE + 3, high.astype(BF16), jnp.where(lane == HEAD_SIZE + 4, low.astype(BF16), q)
    )


def attend(heads, q, k, v):
    tokens = k.shape[0]
    rows = BLOCK
    return pl.pallas_call(
        functools.partial(attend_kernel, heads),
        grid=(tokens // rows,),
        in_specs=[
            pl.BlockSpec((heads * rows, LANES), lambda i: (i, 0)),
            pl.BlockSpec((tokens, LANES), lambda i: (0, 0)),
            pl.BlockSpec((tokens, LANES), lambda i: (0, 0)),
        ],
        out_specs=[
            pl.BlockSpec((rows, heads * HEAD_SIZE), lambda i: (i, 0)),
            pl.BlockSpec((rows, heads * HEAD_SIZE), lambda i: (i, 0)),
            pl.BlockSpec((heads * rows, LANES), lambda i: (i, 0)),
        ],
        out_shape=[
            jax.ShapeDtypeStruct((tokens, heads * HEAD_SIZE), BF16),
            jax.ShapeDtypeStruct((tokens, heads * HEAD_SIZE), F32),
            jax.ShapeDtypeStruct((heads * tokens, LANES), BF16),
        ],
        compiler_params=pltpu.CompilerParams(vmem_limit_bytes=VMEM),
        cost_estimate=pl.CostEstimate(
            flops=16 * heads * tokens * tokens * LANES // 4, bytes_accessed=8 * tokens * LANES, transcendentals=0
        ),
        name="attend",
    )(q, k, v)


def attend_back_kernel(heads, q_ref, k_ref, v_ref, grad_ref, out_ref, unit_ref, scale_ref, head_gain_ref,
                       cos_ref, sin_ref, dqkv_ref, gains_ref, g_scr, dq_scr, dk_scr, dv_scr):
    rows = BLOCK
    tokens = k_ref.shape[0]
    blocks = tokens // rows
    wide = heads * rows

    def prepare(i, carry):
        start = pl.multiple_of(i * rows, rows)
        lane = lax.broadcasted_iota(jnp.int32, (rows, HEAD_SIZE), 1)
        for h in range(heads):
            cols = slice(h * HEAD_SIZE, (h + 1) * HEAD_SIZE)
            grad = grad_ref[pl.ds(start, rows), cols]
            delta = jnp.sum(grad.astype(F32) * out_ref[pl.ds(start, rows), cols], axis=1, keepdims=True)
            high, low = split_low(-delta)
            marks = jnp.where(lane == 0, high, jnp.where(lane == 1, low, 0.0)).astype(BF16)
            at = pl.ds(pl.multiple_of(i * wide + h * rows, rows), rows)
            g_scr[at, :HEAD_SIZE] = grad
            g_scr[at, HEAD_SIZE:] = marks
        at = pl.ds(pl.multiple_of(i * wide, wide), wide)
        dq_scr[at, :] = jnp.zeros((wide, LANES), F32)
        return carry

    lax.fori_loop(0, blocks, prepare, 0)

    def key_step(j, carry):
        start = pl.multiple_of(j * rows, rows)
        k = k_ref[pl.ds(start, rows), :]
        v = v_ref[pl.ds(start, rows), :]

        def pair(i, diagonal):
            at = pl.ds(pl.multiple_of(i * wide, wide), wide)
            q = q_ref[at, :]
            g = g_scr[at, :]
            p = jnp.exp(dot(k, q, NT))
            if diagonal:
                u_local = lax.broadcasted_iota(jnp.int32, p.shape, 0)
                t_local = lax.broadcasted_iota(jnp.int32, p.shape, 1) % rows
                p = jnp.where(u_local <= t_local, p, 0.0)
            dv = dot(p.astype(BF16), g)
            ds = (p * dot(v, g, NT)).astype(BF16)
            dk = dot(ds, q)
            dq_scr[at, :] += dot(ds, k, TN)
            return dk, dv

        def query_step(i, state):
            dk, dv = pair(i, False)
            return state[0] + dk, state[1] + dv

        dk, dv = lax.fori_loop(j + 1, blocks, query_step, pair(j, True))
        dk_scr[pl.ds(start, rows), :] = dk
        dv_scr[pl.ds(start, rows), :] = dv
        return carry

    lax.fori_loop(0, blocks, key_step, 0)

    def finish(i, carry):
        start = pl.multiple_of(i * rows, rows)
        at = pl.ds(start, rows)
        cosine, sine = cos_ref[at, :], sin_ref[at, :]
        scales = scale_ref[at, :]
        sums = list(carry)
        for h in range(heads + 1):
            cols = slice(h * HEAD_SIZE, (h + 1) * HEAD_SIZE)
            if h < heads:
                d = dq_scr[pl.ds(pl.multiple_of(i * wide + h * rows, rows), rows), :HEAD_SIZE] * 0.125
            else:
                d = dk_scr[at, :HEAD_SIZE]
            which = 0 if h < heads else 1
            e = d * cosine - swap_halves(d) * sine
            unit = unit_ref[at, cols]
            sums[which] = sums[which] + jnp.sum(e * unit, axis=0, keepdims=True)
            w = e * head_gain_ref[which:which + 1, :HEAD_SIZE]
            r = scales[:, h:h + 1]
            dqkv_ref[at, cols] = (r * (w - unit * jnp.mean(w * unit, axis=1, keepdims=True))).astype(BF16)
        dqkv_ref[at, (heads + 1) * HEAD_SIZE:] = dv_scr[at, :HEAD_SIZE].astype(BF16)
        return tuple(sums)

    zero = jnp.zeros((1, HEAD_SIZE), F32)
    q_sum, k_sum = lax.fori_loop(0, blocks, finish, (zero, zero))
    gains_ref[...] = jnp.zeros(gains_ref.shape, F32)
    gains_ref[0:1, :HEAD_SIZE] = q_sum
    gains_ref[0:1, HEAD_SIZE:] = k_sum


def attend_back(heads, q, k, v, grad, out, unit, scale, head_gain, cosine, sine):
    tokens = k.shape[0]
    return pl.pallas_call(
        functools.partial(attend_back_kernel, heads),
        out_shape=[
            jax.ShapeDtypeStruct((tokens, (heads + 2) * HEAD_SIZE), BF16),
            jax.ShapeDtypeStruct((8, LANES), F32),
        ],
        scratch_shapes=[
            pltpu.VMEM((heads * tokens, LANES), BF16),
            pltpu.VMEM((heads * tokens, LANES), F32),
            pltpu.VMEM((tokens, LANES), F32),
            pltpu.VMEM((tokens, LANES), F32),
        ],
        compiler_params=pltpu.CompilerParams(vmem_limit_bytes=VMEM),
        cost_estimate=pl.CostEstimate(
            flops=40 * heads * tokens * tokens * LANES // 4, bytes_accessed=16 * tokens * LANES, transcendentals=0
        ),
        name="attend_back",
    )(q, k, v, grad, out, unit, scale, head_gain, cosine, sine)


def per_device(
    tokens, bounds, cotangent, attn_gain, query_weight, key_matrix, value_matrix,
    query_gain, key_gain, out_weight, ffn_gain, gate_weight, up_weight, down_weight,
):
    fsdp = ("fo", "fi")
    seq = ("so", "si")
    every = fsdp + seq
    group = ("fo", "fi", "si")
    rows, width = tokens.shape
    f_count = lax.axis_size(fsdp)
    s_count = lax.axis_size(seq)
    z_count = lax.axis_size("so")
    f_index = lax.axis_index(fsdp)
    s_index = lax.axis_index(seq)
    z_index = lax.axis_index("so")
    y_index = lax.axis_index("si")
    length = rows * s_count
    heads = QUERY_HEADS // s_count
    copies = max(1, s_count // KEY_VALUE_HEADS)
    kv_cols = HEAD_SIZE
    assert KEY_VALUE_HEADS * copies == s_count
    q_cols = heads * HEAD_SIZE
    cols = q_cols + 2 * kv_cols

    all_cols = jnp.concatenate(
        [
            query_weight.reshape(-1, s_count, q_cols),
            jnp.repeat(key_matrix.reshape(-1, KEY_VALUE_HEADS, kv_cols), copies, axis=1),
            jnp.repeat(value_matrix.reshape(-1, KEY_VALUE_HEADS, kv_cols), copies, axis=1),
        ],
        axis=2,
    )
    own_cols = lax.dynamic_index_in_dim(all_cols, s_index, 1, keepdims=False)
    w_own = lax.all_gather(own_cols, fsdp, axis=0, tiled=True)
    x_full = lax.all_gather(tokens, seq, axis=0, tiled=True)
    c_group = lax.all_gather(cotangent, group, axis=0, tiled=True)
    w_all = lax.all_gather(all_cols.reshape(-1, s_count * cols), fsdp, axis=0, tiled=True)
    out_full = lax.all_gather(out_weight, fsdp, axis=0, tiled=True)

    ids = jnp.arange(length, dtype=jnp.int32)
    b0, b1 = bounds[0, 0], bounds[0, 1]
    starts = jnp.where(ids >= b1, b1, jnp.where(ids >= b0, b0, 0))
    frequency = ROPE_BASE ** (-(jnp.arange(HEAD_SIZE // 2, dtype=F32) * 2.0 / HEAD_SIZE))
    phases = (ids - starts).astype(F32)[:, None] * frequency[None, :]
    cosine, sine = jnp.cos(phases), jnp.sin(phases)
    cos2 = jnp.concatenate([cosine, cosine], axis=1)
    sin2 = jnp.concatenate([-sine, sine], axis=1)
    head_gain = jnp.zeros((8, LANES), F32).at[0, :HEAD_SIZE].set(query_gain).at[1, :HEAD_SIZE].set(key_gain)

    normed, q, k, v, unit, scale = project(
        heads, bounds[0], x_full, attn_gain[None, :], w_own, head_gain, cos2, sin2
    )
    attended_low, attended, q2 = attend(heads, q, k, v)
    heads_out = lax.all_to_all(attended_low, seq, split_axis=0, concat_axis=1, tiled=True)

    inputs = tokens.astype(F32)
    square_one = jnp.mean(inputs * inputs, axis=1, keepdims=True)
    scale_one = lax.rsqrt(square_one + EPSILON)
    residual = inputs + dot(heads_out, out_full)
    square_two = jnp.mean(residual * residual, axis=1, keepdims=True)
    scale_two = lax.rsqrt(square_two + EPSILON)
    inner = (residual * scale_two * ffn_gain).astype(BF16)

    units = gate_weight.shape[1]
    part = units // s_count
    mine = z_count * part
    gate_own = lax.dynamic_index_in_dim(
        gate_weight.reshape(width, z_count, 2, part), y_index, 2, keepdims=False
    ).reshape(width, mine)
    up_own = lax.dynamic_index_in_dim(
        up_weight.reshape(width, z_count, 2, part), y_index, 2, keepdims=False
    ).reshape(width, mine)
    down_own = lax.dynamic_index_in_dim(
        down_weight.reshape(z_count, 2, part, width), y_index, 1, keepdims=False
    ).reshape(mine, width)
    d_hidden = dot(c_group, down_own, NT)
    inner_group = lax.all_gather(inner, group, axis=0, tiled=True)
    gate = dot(inner_group, gate_own)
    up = dot(inner_group, up_own)
    sigma = jax.nn.sigmoid(gate)
    active = gate * sigma
    hidden = (active * up).astype(BF16)
    d_gate = (d_hidden * up * (sigma * (1.0 + gate * (1.0 - sigma)))).astype(BF16)
    d_up = (d_hidden * active).astype(BF16)
    d_inner_part = (dot(d_gate, gate_own, NT) + dot(d_up, up_own, NT)).astype(BF16)
    d_inner = lax.psum_scatter(d_inner_part, group, scatter_dimension=0, tiled=True).astype(F32)
    mlp_part = dot(hidden, down_own).astype(BF16)
    mlp_out = lax.psum_scatter(mlp_part, group, scatter_dimension=0, tiled=True).astype(F32)
    block_output = (residual + mlp_out).astype(BF16)

    down_part = dot(hidden, c_group, TN).astype(BF16)
    gate_part = dot(inner_group, d_gate, TN).astype(BF16)
    up_part = dot(inner_group, d_up, TN).astype(BF16)
    down_grad = lax.psum_scatter(down_part, "so", scatter_dimension=0, tiled=True).astype(F32)

    def owner_rows(partial):
        rows_here = lax.psum_scatter(partial, "so", scatter_dimension=0, tiled=True)
        spread = lax.all_to_all(
            rows_here.reshape(2, width // s_count, mine), "si", split_axis=0, concat_axis=0, tiled=True
        )
        return (
            spread.reshape(2, width // s_count, z_count, part)
            .transpose(1, 2, 0, 3)
            .reshape(width // s_count, units)
            .astype(F32)
        )

    gate_grad = owner_rows(gate_part)
    up_grad = owner_rows(up_part)

    ffn_part = jnp.sum(d_inner * residual * scale_two, axis=0)
    ffn_gain_grad = lax.psum_scatter(ffn_part, every, scatter_dimension=0, tiled=True)
    weighted = d_inner * ffn_gain
    d_residual = cotangent.astype(F32) + scale_two * (
        weighted - residual * scale_two * scale_two * jnp.mean(weighted * residual, axis=1, keepdims=True)
    )
    d_branch = d_residual.astype(BF16)
    d_heads = dot(d_branch, out_full, NT).astype(BF16)
    d_attended = lax.all_to_all(d_heads, seq, split_axis=1, concat_axis=0, tiled=True)

    attended_cols = lax.all_to_all(heads_out, fsdp, split_axis=1, concat_axis=0, tiled=True)
    branch_group = lax.all_gather(d_branch, fsdp, axis=0, tiled=True)
    out_part = dot(attended_cols, branch_group, TN).astype(BF16)
    out_grad = lax.psum_scatter(out_part, seq, scatter_dimension=0, tiled=True).astype(F32)

    d_qkv, gain_parts = attend_back(
        heads, q2, k, v, d_attended, attended, unit, scale, head_gain, cos2, sin2
    )
    gain_sums = lax.psum(gain_parts[0], every)

    proj_part = dot(normed, d_qkv, TN).astype(BF16)
    proj_rows = lax.psum_scatter(proj_part, fsdp, scatter_dimension=0, tiled=True)
    proj_grad = lax.all_to_all(proj_rows, seq, split_axis=0, concat_axis=1, tiled=True).astype(F32)
    own_rows = proj_grad.shape[0]
    by_device = proj_grad.reshape(own_rows, s_count, cols)
    query_grad = by_device[:, :, :q_cols].reshape(own_rows, s_count * q_cols)

    def fold(values):
        return values.reshape(own_rows, KEY_VALUE_HEADS, copies, kv_cols).sum(axis=2).reshape(own_rows, -1)

    key_grad = fold(by_device[:, :, q_cols:q_cols + kv_cols])
    value_grad = fold(by_device[:, :, q_cols + kv_cols:])

    d_tok = lax.all_to_all(d_qkv, seq, split_axis=0, concat_axis=1, tiled=True)
    d_normed = dot(d_tok, w_all, NT)
    attn_part = jnp.sum(d_normed * inputs * scale_one, axis=0)
    attn_gain_grad = lax.psum_scatter(attn_part, every, scatter_dimension=0, tiled=True)
    weighted = d_normed * attn_gain
    input_grad = (
        d_residual
        + scale_one
        * (weighted - inputs * scale_one * scale_one * jnp.mean(weighted * inputs, axis=1, keepdims=True))
    ).astype(BF16)
    attn_rms = jnp.sqrt(square_one + EPSILON)[:, 0]
    mlp_rms = jnp.sqrt(square_two + EPSILON)[:, 0]
    return (
        block_output, input_grad, residual, attn_rms, mlp_rms, attn_gain_grad,
        query_grad, key_grad, value_grad, gain_sums[:HEAD_SIZE], gain_sums[HEAD_SIZE:],
        out_grad, ffn_gain_grad, gate_grad, up_grad, down_grad,
    )


def solution(mesh):
    f_count, s_count = mesh.shape["fsdp"], mesh.shape["seq"]
    fine = Mesh(mesh.devices.reshape(f_count // 2, 2, s_count // 2, 2), ("fo", "fi", "so", "si"))
    f, s = ("fo", "fi"), ("so", "si")
    every = P(f + s, None)
    vector = P(f + s)
    placed = (
        every, P(f, None), every, P(), P(f, None), P(f, None), P(f, None), P(), P(),
        P(f, None), P(), P(None, f), P(None, f), P(f, None),
    )
    return jax.shard_map(
        per_device,
        mesh=fine,
        in_specs=placed,
        out_specs=(
            every, every, every, vector, vector, vector, every, every, every, P(), P(),
            every, vector, P(s, f), P(s, f), every,
        ),
        check_vma=False,
    )
```

time: 6270 us -> 969 us (0.15)
  waiting for transfers between devices: 5360 us -> 454 us
  local copies, waits for them, and re-layouts: 375 us -> 95.1 us
  matrix products: 331 us -> 138 us
  Pallas kernels: 0 us -> 74.7 us
    reduce_scatter x7, waiting for transfers between devices: 4700 us -> 240 us  [the longest x1 78.2 us: per_device(): lax.psum_scatter(down_part, 'so', scatter_dimension=0, tiled=True)]
    all_gather x7, waiting for transfers between devices: 588 us -> 213 us  [the longest x1 101 us: per_device(): x_full = lax.all_gather(tokens, seq, axis=0, tiled=True)]
    dot_general x63 -> x14, matrix products: 331 us -> 138 us  [dot(): return lax.dot_general(left, right, dims, preferred_element_type=F32)]
    reshape x7 -> x4, local copies, waits for them, and re-layouts: 163 us -> 6.38 us  [the longest x1 4 us: per_device(): query_weight.reshape(-1, s_count, q_cols)]
    transpose x2 -> x0, local copies, waits for them, and re-layouts: 113 us -> none  [the longest x1 56.5 us: per_device(): up_term = up_grad.reshape(MODEL_WIDTH, groups, FF // groups).transpose(1,...]
    all_to_all x6 -> x3, waiting for transfers between devices: 75.2 us -> 0.01 us  [the longest x1 0.01 us: owner_rows(): lax.all_to_all(rows_here.reshape(2, width // s_count, mine), 'si', split_...]
    pallas_call x0 -> x3, Pallas kernels: none -> 74.7 us  [the longest x1 36.6 us: attend_back(): pl.pallas_call(functools.partial(attend_back_kernel, heads), out_shape=[j...]
  transfers between devices with their start and end apart: 20 -> 17, of which waited for: 16 -> 11; matrix products, arithmetic and copies ran while one was open for 9% -> 20% of each run, Pallas kernels for 0% -> 8%
where the time goes in v1:
time: 969 us; the launch traced here: 958 us
  waiting for transfers between devices  454 us (47%)
  blocking collectives  143 us (15%)
  matrix products  138 us (14%)
  local copies, waits for them, and re-layouts  95.1 us (10%)
  Pallas kernels  74.7 us (8%)
  other arithmetic  24 us (2%)
  between operations  14.7 us (2%)
  starting transfers between devices  14.5 us (1%)
    dot_general x14, matrix products, dot(): return lax.dot_general(left, right, dims, preferred_element_type=F32)  138 us
    all_gather x1, waiting for transfers between devices, per_device(): x_full = lax.all_gather(tokens, seq, axis=0, tiled=True)  101 us
    reduce_scatter x1, waiting for transfers between devices, per_device(): lax.psum_scatter(down_part, 'so', scatter_dimension=0, tiled=True)  78.2 us
    reduce_scatter x1, waiting for transfers between devices, per_device(): lax.psum_scatter(out_part, seq, scatter_dimension=0, tiled=True).astype(F32)  64.1 us
    all_gather x1, waiting for transfers between devices, per_device(): lax.all_gather(all_cols.reshape(-1, s_count * cols), fsdp, axis=0, tiled=...  56.4 us
    all_to_all x1, blocking collectives, per_device(): lax.all_to_all(d_heads, seq, split_axis=1, concat_axis=0, tiled=True)  46.8 us
    unnamed x1, blocking collectives  39.9 us
    reduce_scatter x1, waiting for transfers between devices, per_device(): lax.psum_scatter(d_inner_part, group, scatter_dimension=0, tiled=True)  38.3 us
  transfers between devices with their start and end apart: 17, of which 11 were waited for; matrix products, arithmetic and copies ran while one was open for 20% of the time, Pallas kernels for 8%

profile of v1, /device:TPU:0, one launch (start us, length us, event | category | flops | bytes accessed | tf_op | source)
XLA Modules:
  0.0 958.3 jit_solution(3693205536340812579)
XLA Ops:
  7.2 3.9 copy.93
  11.2 4.0 copy.96
  29.6 14.4 %all-gather.21.cloned.1.call-done = bf16[2048,1,384]{2,0,1:T(8,128)(2,1)} async-done(((bf16[512,1,384]{2,0,1:T(8,128)(2,1)}), bf16[2048,1,384]{2,0,1:T(8,128)(2,1)}) %all-gather.21.cloned.1.call-update) | async-done | bytes 1572880 | tf_op jit(solution)/shard_map/all_gather | solution.py:314
  44.0 101.2 %all-gather.9.cloned.1.call-done.x_ref = bf16[1536,2048]{1,0:T(8,128)(2,1)} async-done(((bf16[192,2048]{1,0:T(8,128)(2,1)}), bf16[1536,2048]{1,0:T(8,128)(2,1)}) %all-gather.9.cloned.1.call-update) | async-done | bytes 6291472 | tf_op jit(solution)/shard_map/all_gather | solution.py:315
  145.2 22.1 %project.1 = (bf16[1536,2048]{1,0:T(8,128)(2,1)}, bf16[6144,128]{1,0:T(8,128)(2,1)}, bf16[1536,128]{1,0:T(8,128)(2,1)}, bf16[1536,128]{1,0:T(8,128)(2,1)}, f32[1536,320]{1,0:T(8,128)}, /*index=5*/f32[1536,128]{1,0:T(8,128)}) custom-call(s32[2]{0:T(128)} %bitcast.119, bf16[1536,2048]{1,0:T(8,128)(2,1)} %all-gather.9.cloned.1.call-done.x_ref, ...), custom_call_target="tpu_custom_call" | custom-call | flops 2415919104 | bytes 14155776 | tf_op jit(solution)/shard_map/project/pallas_call | solution.py:84
  167.3 16.0 %attend.1 = (bf16[1536,256]{1,0:T(8,128)(2,1)}, f32[1536,256]{1,0:T(8,128)}, bf16[6144,128]{1,0:T(8,128)(2,1)}) custom-call(bf16[6144,128]{1,0:T(8,128)(2,1)} %get-tuple-element.51.q_ref, bf16[1536,128]{1,0:T(8,128)(2,1)} %get-tuple-element.52.k_ref, bf16[1536,128]{1,0:T(8,128)(2,1)} %get-tuple-element.53.v_ref), custom_call_target="tpu_custom_call" | custom-call | flops 4831838208 | bytes 1572864 | tf_op jit(solution)/shard_map/attend/pallas_call | solution.py:148
  183.3 23.5 %all_to_all.99 = bf16[8,192,256]{2,1,0:T(8,128)(2,1)S(1)} all-to-all(bf16[8,192,256]{2,1,0:T(8,128)(2,1)} %bitcast.114), channel_id=1, replica_groups=mesh['fo'=2,'fi'=2,'so'=4,'si'=2] {'so','si'}, dimensions={0} | all-to-all | bytes 1572864 | tf_op jit(solution)/shard_map/all_to_all | solution.py:334
  207.7 5.3 multiply_reduce_fusion
  215.5 12.5 %copy.101 = bf16[2048,2048]{0,1:T(8,128)(2,1)} copy(bf16[2048,2048]{1,0:T(8,128)(2,1)} %param.29) | data formatting | bytes 16777216 | tf_op args[11]
  227.9 12.4 %copy.102 = bf16[2048,2048]{0,1:T(8,128)(2,1)} copy(bf16[2048,2048]{1,0:T(8,128)(2,1)} %param.30) | data formatting | bytes 16777216 | tf_op args[12]
  240.3 5.1 constant_dynamic-slice_fusion
  246.5 6.8 constant_dynamic-slice_fusion.1
  253.3 6.2 all-gather.13.cloned.1.call-done
  259.5 11.8 %fusion.31 = f32[1536,1024]{1,0:T(8,128)} fusion(bf16[1536,2048]{1,0:T(8,128)(2,1)} %all-gather.13.cloned.1.call-done, bf16[2048,1024]{0,1:T(8,128)(2,1)} %bitcast.96), kind=kOutput, calls=%fused_computation.76 | convolution fusion | flops 6442450944 | bytes 16777216 | tf_op jit(solution)/shard_map/dot_general | solution.py:27
  271.3 8.9 fusion.30
  280.2 26.6 %all-gather.15.cloned.1.call-done = bf16[1536,2048]{1,0:T(8,128)(2,1)} async-done(((bf16[192,2048]{1,0:T(8,128)(2,1)}), bf16[1536,2048]{1,0:T(8,128)(2,1)}) %all-gather.15.cloned.1.call-update) | async-done | bytes 6291472 | tf_op jit(solution)/shard_map/all_gather | solution.py:316
  306.8 16.2 %fusion.2 = (bf16[1536,1024]{1,0:T(8,128)(2,1)S(1)}, bf16[1536,1024]{1,0:T(8,128)(2,1)S(1)}, bf16[1536,1024]{1,0:T(8,128)(2,1)}) fusion(f32[1536,1024]{1,0:T(8,128)} %fusion.30, f32[1536,1024]{1,0:T(8,128)} %fusion.31, bf16[1024,2048]{1,0:T(8,128)(2,1)} %bitcast.100, bf16[1536,2048]{1,0:T(8,128)(2,1)} %all-gather.15.cloned.1.call-done), kind=kOutput, calls=%fused_computation.6 | convolution fusion | flops 6466043904 | bytes 32505856 | tf_op jit(solution)/shard_map/dot_general | solution.py:27
  323.0 9.6 %fusion.32 = f32[1536,2048]{1,0:T(8,128)} fusion(bf16[1536,1024]{1,0:T(8,128)(2,1)S(1)} %get-tuple-element.70, bf16[2048,1024]{0,1:T(8,128)(2,1)S(1)} %bitcast.99), kind=kOutput, calls=%fused_computation.77 | convolution fusion | flops 6442450944 | bytes 19922944 | tf_op jit(solution)/shard_map/dot_general | solution.py:27
  332.6 11.5 %add_convert_fusion = bf16[1536,2048]{1,0:T(8,128)(2,1)} fusion(f32[1536,2048]{1,0:T(8,128)} %fusion.32, bf16[1536,1024]{1,0:T(8,128)(2,1)S(1)} %get-tuple-element.69, bf16[2048,1024]{0,1:T(8,128)(2,1)S(1)} %bitcast.97), kind=kOutput, calls=%fused_computation | convolution fusion | flops 6448742400 | bytes 26214400 | tf_op jit(solution)/shard_map/dot_general | solution.py:27
  344.2 11.2 %convolution_convert_fusion.3 = bf16[2048,1024]{1,0:T(8,128)(2,1)} fusion(bf16[1536,2048]{1,0:T(8,128)(2,1)} %all-gather.13.cloned.1.call-done, bf16[1536,1024]{1,0:T(8,128)(2,1)} %copy-done.25), kind=kOutput, calls=%fused_computation.12 | convolution fusion | flops 6444548096 | bytes 13631488 | tf_op jit(solution)/shard_map/dot_general | solution.py:27
  355.5 12.0 %convolution_convert_fusion.2 = bf16[2048,1024]{1,0:T(8,128)(2,1)} fusion(bf16[1536,2048]{1,0:T(8,128)(2,1)} %all-gather.13.cloned.1.call-done, bf16[1536,1024]{1,0:T(8,128)(2,1)} %copy-done.26), kind=kOutput, calls=%fused_computation.11 | convolution fusion | flops 6444548096 | bytes 13631488 | tf_op jit(solution)/shard_map/dot_general | solution.py:27
  367.7 38.3 %reduce-scatter.10.cloned.1.call-done = bf16[192,2048]{1,0:T(8,128)(2,1)} async-done(((bf16[1536,2048]{1,0:T(8,128)(2,1)}), bf16[192,2048]{1,0:T(8,128)(2,1)}) %reduce-scatter.10.cloned.1.call-update) | async-done | bytes 786448 | tf_op jit(solution)/shard_map/reduce_scatter | solution.py:366
  410.4 11.3 %convolution_convert_fusion.1 = bf16[1024,2048]{1,0:T(8,128)(2,1)} fusion(bf16[1536,1024]{1,0:T(8,128)(2,1)} %get-tuple-element.71, bf16[1536,2048]{1,0:T(8,128)(2,1)} %all-gather.15.cloned.1.call-done), kind=kOutput, calls=%fused_computation.10 | convolution fusion | flops 6444548096 | bytes 13631488 | tf_op jit(solution)/shard_map/dot_general | solution.py:27
  421.7 4.6 copy.106
  427.5 6.4 convolution_convert_fusion.6
  433.9 46.8 %all_to_all.100 = bf16[192,8,256]{2,0,1:T(8,128)(2,1)} all-to-all(bf16[192,8,256]{2,0,1:T(8,128)(2,1)S(1)} %bitcast.102), channel_id=1, replica_groups=mesh['fo'=2,'fi'=2,'so'=4,'si'=2] {'so','si'}, dimensions={1} | all-to-all | bytes 1572864 | tf_op jit(solution)/shard_map/all_to_all | solution.py:399
  480.7 36.6 %attend_back.1 = (bf16[1536,384]{1,0:T(8,128)(2,1)}, f32[8,128]{1,0:T(8,128)}) custom-call(bf16[6144,128]{1,0:T(8,128)(2,1)} %get-tuple-element.55.q_ref, bf16[1536,128]{1,0:T(8,128)(2,1)} %get-tuple-element.52.k_ref, bf16[1536,128]{1,0:T(8,128)(2,1)} %get-tuple-element.53.v_ref, bf16[1536,256]{1,0:T(8,128)(2,1)} %bitcast.112, ...), custom_call_target="tpu_custom_call" | custom-call | flops 12079595520 | bytes 3145728 | tf_op jit(solution)/shard_map/attend_back/pallas_call | solution.py:261
  517.3 7.8 convolution_convert_fusion.5
  525.2 11.2 %convolution_convert_fusion = bf16[1536,2048]{1,0:T(8,128)(2,1)} fusion(bf16[1536,1024]{1,0:T(8,128)(2,1)} %get-tuple-element.71, bf16[1024,2048]{1,0:T(8,128)(2,1)} %bitcast.101), kind=kOutput, calls=%fused_computation.1 | convolution fusion | flops 6445596672 | bytes 13631488 | tf_op jit(solution)/shard_map/dot_general | solution.py:27
  540.9 14.8 %all_to_all.101 = bf16[192,4,512]{2,0,1:T(8,128)(2,1)} all-to-all(bf16[192,4,512]{2,0,1:T(8,128)(2,1)S(1)} %copy.111), channel_id=1, replica_groups=mesh['fo'=2,'fi'=2,'so'=4,'si'=2] {'fo','fi'}, dimensions={1} | all-to-all | bytes 1572864 | tf_op jit(solution)/shard_map/all_to_all | solution.py:401
  555.7 3.6 all-to-all-start.5
  559.3 20.9 %reduce-scatter.18.cloned.1.call-done = bf16[512,1024]{1,0:T(8,128)(2,1)} async-done(((bf16[2048,1024]{1,0:T(8,128)(2,1)}), bf16[512,1024]{1,0:T(8,128)(2,1)}) %reduce-scatter.18.cloned.1.call-update) | async-done | bytes 1048592 | tf_op jit(solution)/shard_map/reduce_scatter | solution.py:377
  580.2 18.4 %all_to_all.102 = bf16[2,256,1024]{2,1,0:T(8,128)(2,1)} all-to-all(bf16[2,256,1024]{2,1,0:T(8,128)(2,1)} %bitcast.111), channel_id=1, replica_groups=mesh['fo'=2,'fi'=2,'so'=4,'si'=2] {'si'}, dimensions={0} | all-to-all | bytes 2097152 | tf_op jit(solution)/shard_map/all_to_all | solution.py:378
  598.7 4.3 all-to-all-start.2
  603.2 7.7 all-gather.19.cloned.1.call-done
  611.0 5.4 convolution_convert_fusion.4
  617.2 78.2 %reduce-scatter.20.cloned.1.call-done = bf16[256,2048]{1,0:T(8,128)(2,1)} async-done(((bf16[1024,2048]{1,0:T(8,128)(2,1)}), bf16[256,2048]{1,0:T(8,128)(2,1)}) %reduce-scatter.20.cloned.1.call-update) | async-done | bytes 1048592 | tf_op jit(solution)/shard_map/reduce_scatter | solution.py:374
  701.1 4.6 copy.123
  705.7 4.0 reshape.232
  712.8 5.0 copy.122
  717.8 3.9 reshape.233
  725.0 56.4 %all-gather.17.cloned.1.call-done = bf16[2048,3072]{0,1:T(8,128)(2,1)} async-done(((bf16[512,3072]{0,1:T(8,128)(2,1)}), bf16[2048,3072]{0,1:T(8,128)(2,1)}) %all-gather.17.cloned.1.call-update) | async-done | bytes 12582928 | tf_op jit(solution)/shard_map/all_gather | solution.py:317
  781.4 9.0 fusion.20
  790.3 39.9 %all-reduce.3 = (f32[2048]{0:T(1024)}, f32[128]{0:T(128)}, f32[2048]{0:T(1024)}) all-reduce(f32[2048]{0:T(1024)S(1)} %get-tuple-element.64, f32[128]{0:T(128)S(1)} %slice_bitcast_fusion.1, f32[2048]{0:T(1024)S(1)} %get-tuple-element.62), channel_id=5, replica_groups=mesh['fo'=2,'fi'=2,'so'=4,'si'=2] {'fo','fi','so','si'}, use_global_device_ids=true, to_apply=%region_7.8.clone | all-reduce | flops 4224 | bytes 33792
  830.8 5.7 all-to-all-start.3
  840.4 38.2 %reduce-scatter.8.cloned.1.call-done = bf16[192,2048]{1,0:T(8,128)(2,1)} async-done(((bf16[1536,2048]{1,0:T(8,128)(2,1)}), bf16[192,2048]{1,0:T(8,128)(2,1)}) %reduce-scatter.8.cloned.1.call-update) | async-done | bytes 786448 | tf_op jit(solution)/shard_map/reduce_scatter | solution.py:368
  878.6 4.0 fusion.17
  885.5 64.1 %reduce-scatter.14.cloned.1.call-done = bf16[64,2048]{1,0:T(8,128)(2,1)} async-done(((bf16[512,2048]{1,0:T(8,128)(2,1)}), bf16[64,2048]{1,0:T(8,128)(2,1)}) %reduce-scatter.14.cloned.1.call-update) | async-done | bytes 262160 | tf_op jit(solution)/shard_map/reduce_scatter | solution.py:404
  (131 shorter events, 51.4 us)
Async XLA Ops:
  7.2 36.8 %all-gather.21.cloned.1.call-start = ((), (), s32[]{:S(2)}) async-start(), calls=%async_computation.27 | async-start | bytes 1966080 | tf_op jit(solution)/shard_map/all_gather | solution.py:314
  11.2 4.0 copy-start.13
  11.2 4.7 copy-start.14
  18.9 1.8 copy-start.2
  20.7 2.4 copy-start.22
  20.7 2.4 copy-start.23
  20.7 2.6 copy-start.20
  21.5 123.8 %all-gather.9.cloned.1.call-start = ((), (), s32[]{:S(2)}) async-start(), calls=%async_computation.14 | async-start | bytes 7077888 | tf_op jit(solution)/shard_map/all_gather | solution.py:315
  22.2 184.7 %all-gather.11.cloned.1.call-start = ((), (), s32[]{:S(2)}) async-start(), calls=%async_computation.15 | async-start | bytes 10485760 | tf_op jit(solution)/shard_map/all_gather | solution.py:318
  23.0 236.5 %all-gather.13.cloned.1.call-start = ((), (), s32[]{:S(2)}) async-start(), calls=%async_computation.16 | async-start | bytes 7077888 | tf_op jit(solution)/shard_map/all_gather | solution.py:357
  23.2 6.4 copy-start.18
  183.3 24.4 %copy-start.4 = (bf16[192,2048]{1,0:T(8,128)(2,1)S(1)}, bf16[192,2048]{1,0:T(8,128)(2,1)}, u32[]{:S(2)}) copy-start(bf16[192,2048]{1,0:T(8,128)(2,1)} %param.18) | copy-start | bytes 2359300
  206.8 0.9 copy-start.6
  207.7 6.0 copy-start.15
  213.1 665.5 %copy-start = (f32[192,2048]{1,0:T(8,128)}, f32[192,2048]{1,0:T(8,128)S(1)}, u32[]{:S(2)}) copy-start(f32[192,2048]{1,0:T(8,128)S(1)} %get-tuple-element.88) | copy-start | bytes 4718596
  213.7 194.0 %copy-start.17 = (f32[192]{0:T(256)}, f32[192]{0:T(256)S(1)}, u32[]{:S(2)}) copy-start(f32[192]{0:T(256)S(1)} %get-tuple-element.80) | copy-start | bytes 2308
  214.8 91.9 %all-gather.15.cloned.1.call-start = ((), (), s32[]{:S(2)}) async-start(), calls=%async_computation.18 | async-start | bytes 7077888 | tf_op jit(solution)/shard_map/all_gather | solution.py:316
  215.4 190.6 %reduce-scatter.10.cloned.1.call-start = ((), (), s32[]{:S(2)}) async-start(), calls=%async_computation.19 | async-start | bytes 7077888 | tf_op jit(solution)/shard_map/reduce_scatter | solution.py:366
  240.3 6.2 copy-start.1
  259.5 11.9 %copy-start.9 = (bf16[2048,4,1,256]{0,3,2,1:T(8,128)(2,1)S(1)}, bf16[2048,4,1,256]{0,3,2,1:T(8,128)(2,1)}, u32[]{:S(2)}) copy-start(bf16[2048,4,1,256]{0,3,2,1:T(8,128)(2,1)} %get-tuple-element.93) | copy-start | bytes 12582916
  259.5 11.9 %copy-start.24 = (bf16[1536,2048]{1,0:T(8,128)(2,1)S(1)}, bf16[1536,2048]{1,0:T(8,128)(2,1)}, u32[]{:S(2)}) copy-start(bf16[1536,2048]{1,0:T(8,128)(2,1)} %all-gather.13.cloned.1.call-done) | copy-start | bytes 18874372
  306.8 16.3 %copy-start.10 = (bf16[2048,4,1,256]{0,3,2,1:T(8,128)(2,1)S(1)}, bf16[2048,4,1,256]{0,3,2,1:T(8,128)(2,1)}, u32[]{:S(2)}) copy-start(bf16[2048,4,1,256]{0,3,2,1:T(8,128)(2,1)} %get-tuple-element.93) | copy-start | bytes 12582916
  323.0 9.6 %copy-start.25 = (bf16[1536,1024]{1,0:T(8,128)(2,1)}, bf16[1536,1024]{1,0:T(8,128)(2,1)S(1)}, u32[]{:S(2)}) copy-start(bf16[1536,1024]{1,0:T(8,128)(2,1)S(1)} %get-tuple-element.70) | copy-start | bytes 9437188
  323.0 9.6 %copy-start.26 = (bf16[1536,1024]{1,0:T(8,128)(2,1)}, bf16[1536,1024]{1,0:T(8,128)(2,1)S(1)}, u32[]{:S(2)}) copy-start(bf16[1536,1024]{1,0:T(8,128)(2,1)S(1)} %get-tuple-element.69) | copy-start | bytes 9437188
  323.0 9.6 %copy-start.8 = (bf16[2048,4,1,256]{0,3,2,1:T(8,128)(2,1)S(1)}, bf16[2048,4,1,256]{0,3,2,1:T(8,128)(2,1)}, u32[]{:S(2)}) copy-start(bf16[2048,4,1,256]{0,3,2,1:T(8,128)(2,1)} %get-tuple-element.92) | copy-start | bytes 12582916
  344.2 211.6 %reduce-scatter.16.cloned.1.call-start = ((), (), s32[]{:S(2)}) async-start(), calls=%async_computation.24 | async-start | bytes 5242880 | tf_op jit(solution)/shard_map/reduce_scatter | solution.py:377
  355.4 224.8 %reduce-scatter.18.cloned.1.call-start = ((), (), s32[]{:S(2)}) async-start(), calls=%async_computation.25 | async-start | bytes 5242880 | tf_op jit(solution)/shard_map/reduce_scatter | solution.py:377
  367.5 40.2 %copy-start.3 = (bf16[192,2048]{1,0:T(8,128)(2,1)S(1)}, bf16[192,2048]{1,0:T(8,128)(2,1)}, u32[]{:S(2)}) copy-start(bf16[192,2048]{1,0:T(8,128)(2,1)} %param.20) | copy-start | bytes 2359300
  367.5 243.5 %all-gather.19.cloned.1.call-start = ((), (), s32[]{:S(2)}) async-start(), calls=%async_computation.22 | async-start | bytes 3932160 | tf_op jit(solution)/shard_map/all_gather | solution.py:402
  407.7 13.9 %copy-start.19 = (f32[192]{0:T(256)}, f32[192]{0:T(256)S(1)}, u32[]{:S(2)}) copy-start(f32[192]{0:T(256)S(1)} %broadcast_multiply_fusion.1) | copy-start | bytes 2308
  410.3 285.1 %reduce-scatter.20.cloned.1.call-start = ((), (), s32[]{:S(2)}) async-start(), calls=%async_computation.26 | async-start | bytes 5242880 | tf_op jit(solution)/shard_map/reduce_scatter | solution.py:374
  421.7 359.7 %all-gather.17.cloned.1.call-start = ((), (), s32[]{:S(2)}) async-start(), calls=%async_computation.20 | async-start | bytes 15728640 | tf_op jit(solution)/shard_map/all_gather | solution.py:317
  426.4 1.1 copy-start.12
  426.4 404.4 %reduce-scatter.12.cloned.1.call-start = ((), (), s32[]{:S(2)}) async-start(), calls=%async_computation.21 | async-start | bytes 1966080 | tf_op jit(solution)/shard_map/reduce_scatter | solution.py:412
  525.1 353.4 %reduce-scatter.8.cloned.1.call-start = ((), (), s32[]{:S(2)}) async-start(), calls=%async_computation.17 | async-start | bytes 7077888 | tf_op jit(solution)/shard_map/reduce_scatter | solution.py:368
  536.4 1.1 copy-start.7
  555.7 24.5 %all-to-all-start.5 = ((bf16[2,256,1024]{2,1,0:T(8,128)(2,1)}), bf16[2,256,1024]{2,1,0:T(8,128)(2,1)S(1)}, u32[]{:S(2)}, u32[]{:S(2)}) async-start(bf16[2,256,1024]{2,1,0:T(8,128)(2,1)} %bitcast.110), calls=%async_computation.10 | async-start | bytes 2097152 | tf_op jit(solution)/shard_map/all_to_all | solution.py:378
  580.2 30.7 %copy-start.11 = (bf16[2,256,1024]{2,1,0:T(8,128)(2,1)}, bf16[2,256,1024]{2,1,0:T(8,128)(2,1)S(1)}, u32[]{:S(2)}) copy-start(bf16[2,256,1024]{2,1,0:T(8,128)(2,1)S(1)} %all-to-all-done.5) | copy-start | bytes 3145732
  598.7 123.8 %all-to-all-start.2 = ((bf16[8,192,384]{2,1,0:T(8,128)(2,1)}), bf16[8,192,384]{2,1,0:T(8,128)(2,1)}, u32[]{:S(2)}, u32[]{:S(2)}) async-start(bf16[8,192,384]{2,1,0:T(8,128)(2,1)} %bitcast.108), calls=%async_computation.4 | async-start | bytes 2359296 | tf_op jit(solution)/shard_map/all_to_all | solution.py:424
  602.9 346.7 %reduce-scatter.14.cloned.1.call-start = ((), (), s32[]{:S(2)}) async-start(), calls=%async_computation.23 | async-start | bytes 2359296 | tf_op jit(solution)/shard_map/reduce_scatter | solution.py:404
  611.0 5.4 copy-start.5
  617.2 164.2 %copy-start.21 = (f32[192]{0:T(256)}, f32[192]{0:T(256)S(1)}, u32[]{:S(2)}) copy-start(f32[192]{0:T(256)S(1)} %get-tuple-element.82) | copy-start | bytes 2308
  717.8 63.5 %copy-start.16 = (f32[2048]{0:T(1024)S(1)}, f32[2048]{0:T(1024)}, u32[]{:S(2)}) copy-start(f32[2048]{0:T(1024)} %param.21) | copy-start | bytes 24580
  830.8 51.8 %all-to-all-start.3 = ((bf16[8,64,384]{2,1,0:T(8,128)(2,1)}), bf16[8,64,384]{2,1,0:T(8,128)(2,1)S(1)}, u32[]{:S(2)}, u32[]{:S(2)}) async-start(bf16[8,64,384]{2,1,0:T(8,128)(2,1)} %bitcast.117), calls=%async_computation.6 | async-start | bytes 786432 | tf_op jit(solution)/shard_map/all_to_all | solution.py:413
Sparse Core Ops, SparseCore 0:
  21.6 22.3 all-gather.20
  46.2 99.0 all-gather.8
  146.8 56.4 all-gather.10
  215.0 44.4 all-gather.12
  261.2 45.5 all-gather.14
  344.3 61.7 reduce-scatter.9
  408.5 89.3 reduce-scatter.15
  500.2 80.0 reduce-scatter.17
  581.9 29.0 all-gather.18
  613.2 82.1 reduce-scatter.19
  697.0 84.3 all-gather.16
  783.8 28.3 reduce-scatter.11
  815.9 62.6 reduce-scatter.7
  881.9 67.6 reduce-scatter.13

commit v2 on v1

v2 whole, which is shorter than its diff:
```python
import functools

import jax
import jax.numpy as jnp
from jax import lax
from jax.experimental import pallas as pl
from jax.experimental.pallas import tpu as pltpu
from jax.sharding import Mesh, PartitionSpec as P

HEAD_SIZE = 64
QUERY_HEADS = 32
KEY_VALUE_HEADS = 8
EPSILON = 1e-05
ROPE_BASE = 1000000.0
BIG = 30000.0
LANES = 128
BLOCK = 256
VMEM = 60 * 1024 * 1024
COST = pl.CostEstimate(flops=1000, bytes_accessed=1000, transcendentals=0)

F32 = jnp.float32
BF16 = jnp.bfloat16
NT = (((1,), (1,)), ((), ()))
TN = (((0,), (0,)), ((), ()))


def dot(left, right, dims=(((1,), (0,)), ((), ()))):
    return lax.dot_general(left, right, dims, preferred_element_type=F32)


def split_low(values):
    high = values.astype(BF16)
    return high, (values - high.astype(F32)).astype(BF16)


def head_means(values, ones):
    high, low = split_low(values)
    return (dot(high, ones) + dot(low, ones)) * (1.0 / HEAD_SIZE)


def head_ones():
    row = lax.broadcasted_iota(jnp.int32, (LANES, LANES), 0) // HEAD_SIZE
    col = lax.broadcasted_iota(jnp.int32, (LANES, LANES), 1) // HEAD_SIZE
    return jnp.where(row == col, 1.0, 0.0).astype(BF16)


def swap_halves(values):
    lane = lax.broadcasted_iota(jnp.int32, values.shape, 1) % HEAD_SIZE
    half = HEAD_SIZE // 2
    return jnp.where(
        lane < half, pltpu.roll(values, LANES - half, 1), pltpu.roll(values, half, 1)
    )


def project_kernel(heads, count, fresh, index_ref, bounds_ref, *refs):
    x_refs = refs[:count]
    gain_ref, w_ref, head_gain_ref, cos_ref, sin_ref = refs[count:count + 5]
    refs = refs[count + 5 + (0 if fresh else 6):]
    normed_ref, q_ref, k_ref, v_ref, unit_ref, scale_ref, x_scr = refs
    i = pl.program_id(0)
    rows = x_scr.shape[0]
    for r in range(count):
        @pl.when(i == r)
        def _(r=r):
            x_scr[...] = x_refs[r][...]

    x = x_scr[...].astype(F32)
    scale = lax.rsqrt(jnp.mean(x * x, axis=1, keepdims=True) + EPSILON)
    normed = (x * scale * gain_ref[...]).astype(BF16)
    normed_ref[...] = normed
    pre = dot(normed, w_ref[...])
    cosine, sine = cos_ref[...], sin_ref[...]
    shape = (rows, LANES)
    token = index_ref[i] * rows + lax.broadcasted_iota(jnp.int32, shape, 0)
    doc = (token >= bounds_ref[0]).astype(jnp.int32) + (token >= bounds_ref[1]).astype(jnp.int32)
    lane = lax.broadcasted_iota(jnp.int32, shape, 1)
    mark = lane - HEAD_SIZE
    query_marks = jnp.where(mark == doc, 1.0, 0.0)
    key_marks = jnp.where(mark < 3, jnp.where(mark == doc, 0.0, -BIG), jnp.where(mark < 5, 1.0, 0.0))
    value_marks = jnp.where(mark < 2, 1.0, 0.0)
    ones = head_ones()

    def place(values, segment, marks):
        group = values if segment % 2 == 0 else pltpu.roll(values, HEAD_SIZE, 1)
        return jnp.where(lane < HEAD_SIZE, group, marks).astype(BF16)

    for g in range(pre.shape[1] // LANES):
        cols = slice(g * LANES, (g + 1) * LANES)
        u = pre[:, cols]
        r = lax.rsqrt(head_means(u * u, ones) + EPSILON)
        unit = u * r
        unit_ref[:, cols] = unit
        scale_ref[:, cols] = r
        gained = unit * head_gain_ref[0:1, cols]
        rot = (gained * cosine + swap_halves(gained) * sine).astype(BF16).astype(F32)
        for segment in (2 * g, 2 * g + 1):
            if segment < heads:
                q_ref[segment] = place(rot * 0.125, segment, query_marks)
            elif segment == heads:
                k_ref[...] = place(rot, segment, key_marks)
            elif segment == heads + 1:
                v_ref[...] = place(u, segment, value_marks)


def project(heads, blocks, index, bounds, gain, w, head_gain, cosine, sine, length, held=None):
    rows, width = blocks[0].shape
    count = len(blocks)
    cols = w.shape[1]
    row = lambda c: pl.BlockSpec((rows, c), lambda i, n, b: (n[i], 0))
    whole = lambda a: pl.BlockSpec(a.shape, lambda i, n, b: (0, 0))
    fresh = held is None
    held = () if fresh else held
    outs = [
        jax.ShapeDtypeStruct((length, width), BF16),
        jax.ShapeDtypeStruct((heads, length, LANES), BF16),
        jax.ShapeDtypeStruct((length, LANES), BF16),
        jax.ShapeDtypeStruct((length, LANES), BF16),
        jax.ShapeDtypeStruct((length, cols), F32),
        jax.ShapeDtypeStruct((length, cols), F32),
    ]
    tokens = rows * count
    return pl.pallas_call(
        functools.partial(project_kernel, heads, count, fresh),
        grid_spec=pltpu.PrefetchScalarGridSpec(
            num_scalar_prefetch=2,
            grid=(count,),
            in_specs=[whole(b) for b in blocks]
            + [whole(gain), whole(w), whole(head_gain), row(LANES), row(LANES)]
            + [pl.BlockSpec(memory_space=pl.ANY)] * len(held),
            out_specs=[
                row(width),
                pl.BlockSpec((heads, rows, LANES), lambda i, n, b: (0, n[i], 0)),
                row(LANES),
                row(LANES),
                row(cols),
                row(cols),
            ],
            scratch_shapes=[pltpu.VMEM((rows, width), BF16)],
        ),
        out_shape=outs,
        input_output_aliases={2 + count + 5 + n: n for n in range(len(held))},
        compiler_params=pltpu.CompilerParams(vmem_limit_bytes=VMEM),
        cost_estimate=COST,
        name="project",
    )(index, bounds, *blocks, gain, w, head_gain, cosine, sine, *held)


def attend_kernel(heads, q_ref, k_ref, v_ref, low_ref, out_ref, q2_ref):
    i = pl.program_id(0)
    rows = BLOCK
    q = q_ref[...].reshape(heads * rows, LANES)

    def step(j, total):
        start = pl.multiple_of(j * rows, rows)
        p = jnp.exp(dot(q, k_ref[pl.ds(start, rows), :], NT)).astype(BF16)
        return total + dot(p, v_ref[pl.ds(start, rows), :])

    total = lax.fori_loop(0, i, step, jnp.zeros((heads * rows, LANES), F32))
    start = pl.multiple_of(i * rows, rows)
    s = dot(q, k_ref[pl.ds(start, rows), :], NT)
    t_local = lax.broadcasted_iota(jnp.int32, s.shape, 0) % rows
    u_local = lax.broadcasted_iota(jnp.int32, s.shape, 1)
    p = jnp.where(u_local <= t_local, jnp.exp(s), 0.0).astype(BF16)
    total = total + dot(p, v_ref[pl.ds(start, rows), :])
    weight = total[:, HEAD_SIZE:HEAD_SIZE + 1]
    out = total[:, :HEAD_SIZE] / weight
    for h in range(heads):
        part = out[h * rows:(h + 1) * rows, :]
        out_ref[:, h * HEAD_SIZE:(h + 1) * HEAD_SIZE] = part
        low_ref[:, h * HEAD_SIZE:(h + 1) * HEAD_SIZE] = part.astype(BF16)
    high, low = split_low(-jnp.log(weight))
    lane = lax.broadcasted_iota(jnp.int32, q.shape, 1)
    q2 = jnp.where(lane == HEAD_SIZE + 3, high, jnp.where(lane == HEAD_SIZE + 4, low, q))
    q2_ref[...] = q2.reshape(heads, rows, LANES)


def attend(heads, q, k, v):
    tokens = k.shape[0]
    rows = BLOCK
    return pl.pallas_call(
        functools.partial(attend_kernel, heads),
        grid=(tokens // rows,),
        in_specs=[
            pl.BlockSpec((heads, rows, LANES), lambda i: (0, i, 0)),
            pl.BlockSpec((tokens, LANES), lambda i: (0, 0)),
            pl.BlockSpec((tokens, LANES), lambda i: (0, 0)),
        ],
        out_specs=[
            pl.BlockSpec((rows, heads * HEAD_SIZE), lambda i: (i, 0)),
            pl.BlockSpec((rows, heads * HEAD_SIZE), lambda i: (i, 0)),
            pl.BlockSpec((heads, rows, LANES), lambda i: (0, i, 0)),
        ],
        out_shape=[
            jax.ShapeDtypeStruct((tokens, heads * HEAD_SIZE), BF16),
            jax.ShapeDtypeStruct((tokens, heads * HEAD_SIZE), F32),
            jax.ShapeDtypeStruct((heads, tokens, LANES), BF16),
        ],
        compiler_params=pltpu.CompilerParams(vmem_limit_bytes=VMEM),
        cost_estimate=COST,
        name="attend",
    )(q, k, v)


def attend_back_kernel(heads, q_ref, k_ref, v_ref, grad_ref, out_ref, unit_ref, scale_ref, head_gain_ref,
                       cos_ref, sin_ref, dqkv_ref, gains_ref, g_scr, dq_scr, dk_scr, dv_scr):
    rows = BLOCK
    tokens = k_ref.shape[0]
    blocks = tokens // rows
    wide = heads * rows

    def prepare(i, carry):
        at = pl.ds(pl.multiple_of(i * rows, rows), rows)
        lane = lax.broadcasted_iota(jnp.int32, (rows, HEAD_SIZE), 1)
        for h in range(heads):
            cols = slice(h * HEAD_SIZE, (h + 1) * HEAD_SIZE)
            grad = grad_ref[at, cols]
            delta = jnp.sum(grad.astype(F32) * out_ref[at, cols], axis=1, keepdims=True)
            high, low = split_low(-delta)
            g_scr[h, at, :HEAD_SIZE] = grad
            g_scr[h, at, HEAD_SIZE:] = jnp.where(lane == 0, high, jnp.where(lane == 1, low, jnp.zeros_like(low)))
        dq_scr[:, at, :] = jnp.zeros((heads, rows, LANES), F32)
        return carry

    lax.fori_loop(0, blocks, prepare, 0)

    def key_step(j, carry):
        start = pl.multiple_of(j * rows, rows)
        k = k_ref[pl.ds(start, rows), :]
        v = v_ref[pl.ds(start, rows), :]

        def pair(i, diagonal):
            at = pl.ds(pl.multiple_of(i * rows, rows), rows)
            q = q_ref[:, at, :].reshape(wide, LANES)
            g = g_scr[:, at, :].reshape(wide, LANES)
            p = jnp.exp(dot(k, q, NT))
            if diagonal:
                u_local = lax.broadcasted_iota(jnp.int32, p.shape, 0)
                t_local = lax.broadcasted_iota(jnp.int32, p.shape, 1) % rows
                p = jnp.where(u_local <= t_local, p, 0.0)
            dv = dot(p.astype(BF16), g)
            ds = (p * dot(v, g, NT)).astype(BF16)
            dk = dot(ds, q)
            dq_scr[:, at, :] += dot(ds, k, TN).reshape(heads, rows, LANES)
            return dk, dv

        def query_step(i, state):
            dk, dv = pair(i, False)
            return state[0] + dk, state[1] + dv

        dk, dv = lax.fori_loop(j + 1, blocks, query_step, pair(j, True))
        dk_scr[pl.ds(start, rows), :] = dk
        dv_scr[pl.ds(start, rows), :] = dv
        return carry

    lax.fori_loop(0, blocks, key_step, 0)
    groups = unit_ref.shape[1] // LANES
    ones = head_ones()

    def finish(i, carry):
        at = pl.ds(pl.multiple_of(i * rows, rows), rows)
        cosine, sine = cos_ref[at, :], sin_ref[at, :]
        lane = lax.broadcasted_iota(jnp.int32, (rows, LANES), 1)

        def segment_of(s):
            if s < heads:
                return dq_scr[s, at, :] * 0.125
            return (dk_scr if s == heads else dv_scr)[at, :]

        sums = list(carry)
        for g in range(groups):
            cols = slice(g * LANES, (g + 1) * LANES)
            first = segment_of(2 * g)
            last = segment_of(2 * g + 1) if 2 * g + 1 < heads + 2 else first
            d = jnp.where(lane < HEAD_SIZE, first, pltpu.roll(last, HEAD_SIZE, 1))
            e = d * cosine - swap_halves(d) * sine
            unit = unit_ref[at, cols]
            sums[g] = sums[g] + jnp.sum(e * unit, axis=0, keepdims=True)
            w = e * head_gain_ref[0:1, cols]
            normal = scale_ref[at, cols] * (w - unit * head_means(w * unit, ones))
            is_value = lane + g * LANES >= (heads + 1) * HEAD_SIZE
            dqkv_ref[at, cols] = jnp.where(is_value, d, normal).astype(BF16)
        return tuple(sums)

    zero = jnp.zeros((1, LANES), F32)
    sums = lax.fori_loop(0, blocks, finish, (zero,) * groups)
    gains_ref[...] = jnp.zeros(gains_ref.shape, F32)
    for g in range(groups):
        gains_ref[0:1, g * LANES:(g + 1) * LANES] = sums[g]


def attend_back(heads, q, k, v, grad, out, unit, scale, head_gain, cosine, sine):
    tokens = k.shape[0]
    cols = unit.shape[1]
    return pl.pallas_call(
        functools.partial(attend_back_kernel, heads),
        out_shape=[
            jax.ShapeDtypeStruct((tokens, cols), BF16),
            jax.ShapeDtypeStruct((8, cols), F32),
        ],
        scratch_shapes=[
            pltpu.VMEM((heads, tokens, LANES), BF16),
            pltpu.VMEM((heads, tokens, LANES), F32),
            pltpu.VMEM((tokens, LANES), F32),
            pltpu.VMEM((tokens, LANES), F32),
        ],
        compiler_params=pltpu.CompilerParams(vmem_limit_bytes=VMEM),
        cost_estimate=COST,
        name="attend_back",
    )(q, k, v, grad, out, unit, scale, head_gain, cosine, sine)


def feed_kernel(layouts, weight_count, index_ref, *refs):
    tiles = sum(layouts[0])
    sides = []
    for layout in layouts:
        others = refs[tiles:tiles + len(layout)]
        sides.append((refs[:tiles], [(o, t) for o, count in zip(others, layout) for t in range(count)]))
        refs = refs[tiles + len(layout):]
    gate_ref, up_ref, down_ref = refs[:3]
    da_ref, db_ref, ma_ref, mb_ref, hidden_ref, dgu_ref, x_scr, c_scr, gu_scr, down_scr, sem, w_sem = refs[3:]
    i = pl.program_id(0)
    half = x_scr.shape[1] // 2

    def copies(t):
        slot = t % 2
        found = []
        for (own, others), scratch, which in ((sides[0], x_scr, 0), (sides[1], c_scr, 1)):
            other, place = others[t]
            found.append(
                pltpu.make_async_copy(own[t], scratch.at[slot, pl.ds(0, half)], sem.at[slot, which, 0])
            )
            found.append(
                pltpu.make_async_copy(
                    other.at[pl.ds(place * half, half)],
                    scratch.at[slot, pl.ds(half, half)],
                    sem.at[slot, which, 1],
                )
            )
        return found

    mine = hidden_ref.shape[1]
    part = mine // weight_count

    def weight_copies(n):
        at = pl.ds(pl.multiple_of(index_ref[n] * part, part), part)
        return [
            pltpu.make_async_copy(gate_ref.at[:, at], gu_scr.at[:, pl.ds(n * part, part)], w_sem.at[n, 0]),
            pltpu.make_async_copy(up_ref.at[:, at], gu_scr.at[:, pl.ds(mine + n * part, part)], w_sem.at[n, 1]),
            pltpu.make_async_copy(down_ref.at[at], down_scr.at[pl.ds(n * part, part)], w_sem.at[n, 2]),
        ]

    for t in range(tiles):
        @pl.when(i == t)
        def _(t=t):
            if t == 0:
                needed = copies(0) + [copy for n in range(weight_count) for copy in weight_copies(n)]
                for copy in needed:
                    copy.start()
            else:
                needed = copies(t)
            if t + 1 < tiles:
                for copy in copies(t + 1):
                    copy.start()
            for copy in needed:
                copy.wait()

    slot = lax.rem(i, 2)
    both = dot(x_scr[slot], gu_scr[...])
    gate, up = both[:, :mine], both[:, mine:]
    d_hidden = dot(c_scr[slot], down_scr[...], NT)
    sigma = 1.0 / (1.0 + jnp.exp(-gate))
    active = gate * sigma
    hidden = (active * up).astype(BF16)
    hidden_ref[...] = hidden
    dgu_ref[:, :mine] = (d_hidden * up * (sigma * (1.0 + gate * (1.0 - sigma)))).astype(BF16)
    dgu_ref[:, mine:] = (d_hidden * active).astype(BF16)
    d_inner = dot(dgu_ref[...], gu_scr[...], NT)
    mlp = dot(hidden, down_scr[...])
    da_ref[0] = d_inner[:half].astype(BF16)
    db_ref[0] = d_inner[half:].astype(BF16)
    ma_ref[0] = mlp[:half].astype(BF16)
    mb_ref[0] = mlp[half:].astype(BF16)


def feed(x_stage, c_stage, index, weights, part):
    (x_own, x_others), (c_own, c_others) = x_stage, c_stage
    tiles = len(x_own)
    half = x_own[0].shape[0]
    rows = 2 * half
    gate, up, down = weights
    width = gate.shape[0]
    blocks = index.shape[0]
    mine = blocks * part
    halves = pl.BlockSpec((1, half, width), lambda i, n: (i, 0, 0))
    return pl.pallas_call(
        functools.partial(
            feed_kernel, tuple(tuple(o.shape[0] // half for o in others) for others in (x_others, c_others)), blocks
        ),
        grid_spec=pltpu.PrefetchScalarGridSpec(
            num_scalar_prefetch=1,
            grid=(tiles,),
            in_specs=[pl.BlockSpec(memory_space=pl.ANY)] * (2 * tiles + len(x_others) + len(c_others) + 3),
            out_specs=[halves] * 4
            + [
                pl.BlockSpec((rows, mine), lambda i, n: (i, 0)),
                pl.BlockSpec((rows, 2 * mine), lambda i, n: (i, 0)),
            ],
            scratch_shapes=[
                pltpu.VMEM((2, rows, width), BF16),
                pltpu.VMEM((2, rows, width), BF16),
                pltpu.VMEM((width, 2 * mine), BF16),
                pltpu.VMEM((mine, width), BF16),
                pltpu.SemaphoreType.DMA((2, 2, 2)),
                pltpu.SemaphoreType.DMA((blocks, 3)),
            ],
        ),
        out_shape=[jax.ShapeDtypeStruct((tiles, half, width), BF16)] * 4
        + [
            jax.ShapeDtypeStruct((tiles * rows, mine), BF16),
            jax.ShapeDtypeStruct((tiles * rows, 2 * mine), BF16),
        ],
        compiler_params=pltpu.CompilerParams(vmem_limit_bytes=VMEM),
        cost_estimate=COST,
        name="feed",
    )(index, *x_own, *x_others, *c_own, *c_others, gate, up, down)


def stage_arrays(stages):
    arrays, layout = [], []
    for own, others in stages:
        half = own[0].shape[0]
        arrays += list(own) + list(others)
        layout.append((half, len(own), tuple(o.shape[0] // half for o in others)))
    return arrays, tuple(layout)


def stack_rows(refs, layout, scratch):
    at = row = 0
    for half, tiles, others in layout:
        places = [(at + tiles + n, t) for n, count in enumerate(others) for t in range(count)]
        for t, (other, place) in enumerate(places):
            scratch[row:row + half, :] = refs[at + t][...]
            scratch[row + half:row + 2 * half, :] = refs[other][place * half:(place + 1) * half, :]
            row += 2 * half
        at += tiles + len(others)


def gate_grad_kernel(array_count, layout, far, index_ref, *refs):
    arrays, refs = refs[:array_count], refs[array_count:]
    rights, outs, scratch = refs[:len(layout)], refs[len(layout):-1], refs[-1]
    stack_rows(arrays, layout, scratch)
    row = 0
    total = None
    for right in rights:
        size = right.shape[0]
        term = dot(scratch[row:row + size, :], right[...], TN)
        total = term if total is None else total + term
        row += size
    total = total.astype(BF16)
    mine = total.shape[1] // 2
    steps = pl.num_programs(0) // far
    for k in range(far):
        @pl.when(pl.program_id(0) // steps == far - 1 - k)
        def _(k=k):
            outs[k][...] = total[:, :mine]
            outs[far + k][...] = total[:, mine:]


def gate_grad(stages, rights, za, far):
    arrays, layout = stage_arrays(stages)
    width = arrays[0].shape[1]
    units = rights[0].shape[1]
    rows = sum(r.shape[0] for r in rights)
    step = min(256, width // far)
    steps = width // far // step
    block = lambda i, n: (n[0] ^ (far - 1 - i // steps)) * steps + i % steps
    out = lambda k: pl.BlockSpec(
        (step, units // 2), lambda i, n: (jnp.clip(i - (far - 1 - k) * steps, 0, steps - 1), 0)
    )
    return pl.pallas_call(
        functools.partial(gate_grad_kernel, len(arrays), layout, far),
        grid_spec=pltpu.PrefetchScalarGridSpec(
            num_scalar_prefetch=1,
            grid=(width // step,),
            in_specs=[pl.BlockSpec((p.shape[0], step), lambda i, n: (0, block(i, n))) for p in arrays]
            + [pl.BlockSpec(r.shape, lambda i, n: (0, 0)) for r in rights],
            out_specs=[out(k) for k in range(far)] * 2,
            scratch_shapes=[pltpu.VMEM((rows, step), BF16)],
        ),
        out_shape=[jax.ShapeDtypeStruct((width // far, units // 2), BF16)] * (2 * far),
        compiler_params=pltpu.CompilerParams(vmem_limit_bytes=VMEM),
        cost_estimate=COST,
        name="gate_grad",
    )(za.astype(jnp.int32).reshape(1), *arrays, *rights)


def down_grad_kernel(array_count, layout, *refs):
    arrays, refs = refs[:array_count], refs[array_count:]
    lefts, (out_ref, left_scr, scratch) = refs[:len(layout)], refs[len(layout):]

    @pl.when(pl.program_id(0) == 0)
    def _():
        col = 0
        for left in lefts:
            size = left.shape[0]
            left_scr[:, col:col + size] = left[...].T
            col += size

    stack_rows(arrays, layout, scratch)
    out_ref[...] = dot(left_scr[...], scratch[...]).astype(BF16)


def down_grad(lefts, stages):
    arrays, layout = stage_arrays(stages)
    width = arrays[0].shape[1]
    units = lefts[0].shape[1]
    rows = sum(r.shape[0] for r in lefts)
    step = min(256, width)
    return pl.pallas_call(
        functools.partial(down_grad_kernel, len(arrays), layout),
        grid=(width // step,),
        in_specs=[pl.BlockSpec((p.shape[0], step), lambda i: (0, i)) for p in arrays]
        + [pl.BlockSpec(r.shape, lambda i: (0, 0)) for r in lefts],
        out_specs=pl.BlockSpec((units, step), lambda i: (0, i)),
        out_shape=jax.ShapeDtypeStruct((units, width), BF16),
        scratch_shapes=[pltpu.VMEM((units, rows), BF16), pltpu.VMEM((rows, step), BF16)],
        compiler_params=pltpu.CompilerParams(vmem_limit_bytes=VMEM),
        cost_estimate=COST,
        name="down_grad",
    )(*arrays, *lefts)


def place_kernel(index_ref, *refs):
    parts, outs = refs[:-2], refs[-2:]
    for d, ref in enumerate(parts):
        @pl.when(pl.program_id(1) == d)
        def _(ref=ref):
            rows = outs[0].shape[0]
            for n, out_ref in enumerate(outs):
                out_ref[...] = ref[n * rows:(n + 1) * rows, :].astype(F32)


def place(parts, own, part):
    devices = len(parts)
    rows, mine = parts[0].shape[0] // 2, parts[0].shape[1]
    blocks = mine // part
    if part % LANES:
        stack = jnp.stack(parts).reshape(devices, 2, rows, blocks, part)
        stack = jnp.stack([take(stack, own ^ d) for d in range(devices)])
        both = stack.transpose(1, 2, 3, 0, 4).reshape(2, rows, -1).astype(F32)
        return both[0], both[1]
    return pl.pallas_call(
        place_kernel,
        grid_spec=pltpu.PrefetchScalarGridSpec(
            num_scalar_prefetch=1,
            grid=(blocks, devices),
            in_specs=[pl.BlockSpec((2 * rows, part), lambda b, d, n: (0, b))] * devices,
            out_specs=[pl.BlockSpec((rows, part), lambda b, d, n: (0, b * devices + (n[0] ^ d)))] * 2,
        ),
        out_shape=[jax.ShapeDtypeStruct((rows, devices * mine), F32)] * 2,
        compiler_params=pltpu.CompilerParams(vmem_limit_bytes=VMEM),
        cost_estimate=COST,
        name="place",
    )(own.astype(jnp.int32).reshape(1), *parts)


X, Y, Z, C = "fo", "si", "zb", "fi"


def swap(values, axis, offset=1):
    size = lax.axis_size(axis)
    return lax.ppermute(values, axis, [(i, i ^ offset) for i in range(size)])


def swap_cube(values, offset):
    if len(offset) == 1:
        return swap(values, offset[0])
    sizes = [lax.axis_size(a) for a in offset]
    total = 1
    for size in sizes:
        total *= size
    pairs = []
    for i in range(total):
        rest, place = i, []
        for size in reversed(sizes):
            place.append(rest % size ^ 1)
            rest //= size
        j = 0
        for size, p in zip(sizes, reversed(place)):
            j = j * size + p
        pairs.append((i, j))
    return lax.ppermute(values, offset, pairs)


def sync(*values):
    leaves, tree = jax.tree.flatten(values)
    return jax.tree.unflatten(tree, lax.optimization_barrier(leaves))


STAGES = (((),), ((X,), (Y,), (Z,)), ((X, Z), (X, Y), (Z, Y)))


def other_core(arrays):
    return swap(arrays[0] if len(arrays) == 1 else jnp.concatenate(arrays, axis=0), C)


def add_low(left, right):
    return (left.astype(F32) + right.astype(F32)).astype(BF16)


def send_home(stage, here, other):
    total = add_low(here, other)
    return [total[n] if not offset else swap_cube(total[n], offset) for n, offset in enumerate(STAGES[stage])]


def take(partial, block):
    return lax.dynamic_index_in_dim(partial, block, 0, keepdims=False)


def send_far(partial, za):
    return [swap(take(partial, za ^ k), "za", k) for k in range(1, lax.axis_size("za"))]


def add_far(partial, got, za):
    total = take(partial, za).astype(F32)
    for g in got:
        total = total + g.astype(F32)
    return total


def per_device(
    tokens, bounds, cotangent, attn_gain, query_weight, key_matrix, value_matrix,
    query_gain, key_gain, out_weight, ffn_gain, gate_weight, up_weight, down_weight,
):
    fsdp = ("fo", "fi")
    seq = ("za", "zb", "si")
    rows, width = tokens.shape
    f_count = lax.axis_size(fsdp)
    s_count = lax.axis_size(seq)
    far = lax.axis_size("za")
    f_index = lax.axis_index(fsdp)
    s_index = lax.axis_index(seq)
    za, zb, si = lax.axis_index("za"), lax.axis_index("zb"), lax.axis_index("si")
    length = rows * s_count
    heads = QUERY_HEADS // s_count
    copies = max(1, s_count // KEY_VALUE_HEADS)
    assert KEY_VALUE_HEADS * copies == s_count
    q_cols = heads * HEAD_SIZE
    cols = q_cols + 2 * HEAD_SIZE
    padded = -(-cols // LANES) * LANES
    all_q, all_kv = QUERY_HEADS * HEAD_SIZE, KEY_VALUE_HEADS * HEAD_SIZE

    pieces = [
        query_weight.reshape(-1, s_count, q_cols),
        jnp.repeat(key_matrix.reshape(-1, KEY_VALUE_HEADS, HEAD_SIZE), copies, axis=1),
        jnp.repeat(value_matrix.reshape(-1, KEY_VALUE_HEADS, HEAD_SIZE), copies, axis=1),
    ]
    kv_start = (s_index // copies) * HEAD_SIZE
    own_cols = [
        lax.dynamic_slice_in_dim(query_weight, s_index * q_cols, q_cols, 1),
        lax.dynamic_slice_in_dim(key_matrix, kv_start, HEAD_SIZE, 1),
        lax.dynamic_slice_in_dim(value_matrix, kv_start, HEAD_SIZE, 1),
    ]
    if padded > cols:
        pieces.append(jnp.zeros(pieces[0].shape[:2] + (padded - cols,), BF16))
        own_cols.append(jnp.zeros((query_weight.shape[0], padded - cols), BF16))
    w_own = lax.all_gather(jnp.concatenate(own_cols, axis=1), fsdp, axis=0, tiled=True)
    out_full = lax.all_gather(out_weight, fsdp, axis=0, tiled=True)
    w_rows = jnp.concatenate(pieces, axis=2).reshape(-1, s_count * padded)
    w_quarters = lambda n: w_rows[n * (w_rows.shape[0] // 4):(n + 1) * (w_rows.shape[0] // 4)]

    far_list = [(k, swap(tokens, "za", k)) for k in range(1, far)]
    x_y, x_z, c_x = swap(tokens, Y), swap(tokens, Z), swap(cotangent, X)
    ids = jnp.arange(length, dtype=jnp.int32)
    b0, b1 = bounds[0, 0], bounds[0, 1]
    starts = jnp.where(ids >= b1, b1, jnp.where(ids >= b0, b0, 0))
    frequency = ROPE_BASE ** (-(jnp.arange(HEAD_SIZE // 2, dtype=F32) * 2.0 / HEAD_SIZE))
    phases = (ids - starts).astype(F32)[:, None] * frequency[None, :]
    cosine, sine = jnp.cos(phases), jnp.sin(phases)
    cos2 = jnp.concatenate([cosine] * 4, axis=1)
    sin2 = jnp.concatenate([-sine, sine] * 2, axis=1)
    head_gain = jnp.concatenate(
        [query_gain] * heads + [key_gain] + [jnp.ones((padded - cols + HEAD_SIZE,), F32)]
    )[None, :]
    far_list, x_y, x_z, c_x, w_rows, cos2, sin2 = sync([b for _, b in far_list], x_y, x_z, c_x, w_rows, cos2, sin2)

    def some_project(blocks, held):
        index = jnp.stack([((za ^ k) * 2 + (zb ^ dz)) * 2 + (si ^ dy) for (k, dz, dy), _ in blocks])
        return project(
            heads, [b for _, b in blocks], index.astype(jnp.int32), bounds[0], attn_gain[None, :], w_own, head_gain,
            cos2, sin2, length, held,
        )

    far_y = [swap(b, Y) for b in far_list]
    far_z = [swap(b, Z) for b in far_list]
    held = some_project([((0, 0, 0), tokens), ((0, 0, 1), x_y), ((0, 1, 0), x_z)], None)
    far_y, far_z, held, x_y = sync(far_y, far_z, held, x_y)
    x_yz = swap(x_y, Z)
    far_yz = [swap(b, Y) for b in far_z]
    for n, k in enumerate(range(1, far)):
        held = some_project([((k, 0, 0), far_list[n]), ((k, 0, 1), far_y[n]), ((k, 1, 0), far_z[n])], held)
    x_yz, far_yz, held, cot, w_rows = sync(x_yz, far_yz, held, cotangent, w_rows)
    c_y, c_z = swap(cot, Y), swap(cot, Z)
    w_x = [swap(w_quarters(0), X)]
    w_c = swap(w_rows, C)
    held = some_project([((0, 1, 1), x_yz)] + [((k, 1, 1), far_yz[n]) for n, k in enumerate(range(1, far))], held)
    normed, q, k, v, unit, scale = held
    attended_low, attended, q2 = attend(heads, q, k, v)
    c_y, c_z, attended_low, c_x, w_c, w_x = sync(c_y, c_z, attended_low, c_x, w_c, w_x)
    heads_out = lax.all_to_all(attended_low, seq, split_axis=0, concat_axis=1, tiled=True)
    c_xz = swap(c_z, X)
    w_xc = [swap(w_x[0], C)]
    c_one = [c_x, c_y, c_z]
    c_own_other, c_one_other = other_core([cot]), other_core(c_one)
    heads_out, c_xz, c_own_other, c_one_other, w_xc = sync(heads_out, c_xz, c_own_other, c_one_other, w_xc)

    c_two_other = other_core([c_xz])
    own_rows = out_weight.shape[0]
    left = []
    for offset in range(f_count):
        block = lax.dynamic_slice_in_dim(heads_out, (f_index ^ offset) * own_rows, own_rows, 1)
        left.append(swap(block, fsdp, offset) if offset else block)
    inputs = tokens.astype(F32)
    square_one = jnp.mean(inputs * inputs, axis=1, keepdims=True)
    scale_one = lax.rsqrt(square_one + EPSILON)
    residual = inputs + dot(heads_out, out_full)
    square_two = jnp.mean(residual * residual, axis=1, keepdims=True)
    scale_two = lax.rsqrt(square_two + EPSILON)
    inner = (residual * scale_two * ffn_gain).astype(BF16)
    inner, c_two_other, c_y, left = sync(inner, c_two_other, c_y, left)

    units = gate_weight.shape[1]
    part = units // s_count
    mine = far * part
    own_block = zb * 2 + si
    if part % LANES == 0:
        weights = (gate_weight, up_weight, down_weight)
        unit_index = (jnp.arange(far, dtype=jnp.int32) * 4 + own_block).astype(jnp.int32)
        width_of_part = part
    else:
        pick = lambda w: lax.dynamic_index_in_dim(
            w.reshape(width, far, 4, part), own_block, 2, keepdims=False
        ).reshape(width, mine)
        weights = (
            pick(gate_weight),
            pick(up_weight),
            lax.dynamic_index_in_dim(
                down_weight.reshape(far, 4, part, width), own_block, 1, keepdims=False
            ).reshape(mine, width),
        )
        unit_index = jnp.zeros((1,), jnp.int32)
        width_of_part = mine
    run = lambda x_stage, c_stage: feed(x_stage, c_stage, unit_index, weights, width_of_part)
    x, y, z = swap(inner, X), swap(inner, Y), swap(inner, Z)
    x_stages = [([inner], [other_core([inner])])]
    c_stages = [([cot], [c_own_other])]
    fed = [run(x_stages[0], c_stages[0])]
    x, y, z, fed = sync(x, y, z, fed)
    xy, xz, yz = swap(x, Y), swap(z, X), swap(y, Z)
    c_xy, c_yz = swap(c_y, X), swap(c_y, Z)
    x_stages.append(([x, y, z], [other_core([x, y, z])]))
    c_stages.append((c_one, [c_one_other]))
    fed.append(run(x_stages[1], c_stages[1]))
    xy, xz, yz, c_xy, c_yz, fed, x_stages = sync(xy, xz, yz, c_xy, c_yz, fed, x_stages)
    xyz, c_xyz = swap(xz, Y), swap(c_yz, X)
    x_stages.append(([xz, xy, yz], [other_core([xz, xy, yz])]))
    c_stages.append(([c_xz, c_xy, c_yz], [c_two_other, other_core([c_xy, c_yz])]))
    d_home = send_home(0, fed[0][0], swap(fed[0][1], C)) + send_home(1, fed[1][0], swap(fed[1][1], C))
    fed.append(run(x_stages[2], c_stages[2]))
    xyz, c_xyz, d_home, fed, x_stages, c_stages = sync(xyz, c_xyz, d_home, fed, x_stages, c_stages)
    two = add_low(fed[2][0], swap(fed[2][1], C))
    mid = rows // 2
    home = [swap_cube(two[n, :mid], offset) for n, offset in enumerate(STAGES[2])]
    x_stages.append(([xyz], [other_core([xyz])]))
    c_stages.append(([c_xyz], [other_core([c_xyz])]))
    fed.append(run(x_stages[3], c_stages[3]))
    two, home, fed, x_stages, c_stages = sync(two, home, fed, x_stages, c_stages)
    three = add_low(fed[3][0][0], swap(fed[3][1], C)[0])
    last = [swap_cube(two[n, mid:], offset) for n, offset in enumerate(STAGES[2])]
    d_home.append(swap_cube(three, (X, Z, Y)))
    m_other = swap(fed[2][3], C)
    gu = gate_grad(x_stages, [f[5] for f in fed], za, far)
    down_part = down_grad([f[4] for f in fed], c_stages).reshape(far, part, width)
    d_home, last, down_part, gu, fed, w_rows, m_other = sync(d_home, last, down_part, gu, fed, w_rows, m_other)
    d_home += [jnp.concatenate([low, high], axis=0) for low, high in zip(home, last)]
    quarter = width // far // 4

    def owner_block(values, offset):
        return lax.dynamic_slice_in_dim(values, (own_block ^ offset) * quarter, quarter, 0)

    def send_rows(parts, *offsets):
        return [
            swap(jnp.concatenate([owner_block(parts[k], o) for o in offsets], axis=0), "za", k) for k in range(1, far)
        ]

    def to_owners(gates, ups, gate_got, up_got):
        spread = []
        for offset, axes in enumerate(((), (Y,), (Z,), (Z, Y))):
            both = []
            for parts, got in ((gates, gate_got), (ups, up_got)):
                rows_here = owner_block(parts[0], offset).astype(F32)
                for k in range(far - 1):
                    pieces = [t for piece in got for t in jnp.split(piece[k], piece[k].shape[0] // quarter)]
                    rows_here = rows_here + pieces[offset].astype(F32)
                both.append(rows_here.astype(BF16))
            both = jnp.concatenate(both, axis=0)
            spread.append(swap_cube(both, axes) if axes else both)
        return spread

    gate_got = [send_rows(gu[:far], 0)]
    w_x.append(swap(w_quarters(1), X))
    m_other = [swap(fed[0][3], C), swap(fed[1][3], C), m_other, swap(fed[3][3], C)]
    d_inner = sum(a.astype(F32) for a in d_home)
    ffn_part = jnp.sum(d_inner * residual * scale_two, axis=0)
    weighted = d_inner * ffn_gain
    d_residual = cotangent.astype(F32) + scale_two * (
        weighted - residual * scale_two * scale_two * jnp.mean(weighted * residual, axis=1, keepdims=True)
    )
    d_branch = d_residual.astype(BF16)
    d_heads = dot(d_branch, out_full, NT).astype(BF16)
    d_heads, d_branch, gate_got, gu, w_x, m_other, fed = sync(d_heads, d_branch, gate_got, gu, w_x, m_other, fed)
    d_attended = lax.all_to_all(d_heads, seq, split_axis=1, concat_axis=0, tiled=True)
    gate_got.append(send_rows(gu[:far], 1))
    over = swap(d_branch, X)
    right = [d_branch, swap(d_branch, C), over, swap(over, C)]
    m = [add_low(f[2], other) for f, other in zip(fed, m_other)]
    d_attended, right, m, gate_got, gu, w_rows, fed = sync(d_attended, right, m, gate_got, gu, w_rows, fed)
    mixed = [
        jnp.concatenate([owner_block(gu[n + k], o) for n, o in ((0, 2), (0, 3), (far, 0), (far, 1))], axis=0)
        for k in range(1, far)
    ]
    mixed = [swap(t, "za", k + 1) for k, t in enumerate(mixed)]
    w_x.append(swap(w_rows[w_rows.shape[0] // 2:], X))
    m_far = swap(m[3][0], Y)
    out_part = dot(jnp.concatenate(left, axis=0), jnp.concatenate(right, axis=0), TN).astype(BF16)
    out_part = out_part.reshape(far, 2, 2, -1, width)
    pick = lambda values, index, axis: lax.dynamic_index_in_dim(values, index, axis, keepdims=False)
    out_y = swap(pick(out_part, 1 - si, 2), Y)
    d_qkv, gain_parts = attend_back(
        heads, q2, k, v, sync(d_attended, out_part)[0], attended, unit, scale, head_gain, cos2, sin2
    )
    d_qkv, gain_parts, gate_got, mixed, gu, m, m_far, w_x, out_part, out_y = sync(
        d_qkv, gain_parts, gate_got, mixed, gu, m, m_far, w_x, out_part, out_y
    )
    gate_got.append([t[:2 * quarter] for t in mixed])
    up_got = [[t[2 * quarter:] for t in mixed]]
    d_tok = lax.all_to_all(d_qkv, seq, split_axis=0, concat_axis=1, tiled=True)
    proj_part = dot(normed, d_qkv, TN).astype(BF16).reshape(2, 2, width // 4, padded)
    fi, fo = lax.axis_index(C), lax.axis_index(X)
    proj_core = add_low(pick(proj_part, fi, 1), swap(pick(proj_part, 1 - fi, 1), C))
    proj_x = swap(take(proj_core, 1 - fo), X)
    w_xc.append(swap(jnp.concatenate(w_x[1:], axis=0), C))
    m_x = swap(m[2][1], X)
    out_part = add_low(pick(out_part, si, 2), out_y)
    m_xz = add_low(m[2][0], m_far)
    d_tok, up_got, gate_got, gu, proj_core, proj_x, w_xc, out_part, m, m_x, m_xz, gain_parts, down_part = sync(
        d_tok, up_got, gate_got, gu, proj_core, proj_x, w_xc, out_part, m, m_x, m_xz, gain_parts, down_part
    )
    up_got.append(send_rows(gu[far:], 2, 3))
    m_z = [swap(m_xz, X), swap(m[2][2], Y)]
    out_z = swap(pick(out_part, 1 - zb, 1), Z)
    blocks = [w_rows, w_c, jnp.concatenate(w_x, axis=0), jnp.concatenate(w_xc, axis=0)]
    by_offset = jnp.stack([dot(d_tok, w, NT) for w in blocks])
    d_normed = jnp.concatenate([take(by_offset, f_index ^ n) for n in range(f_count)], axis=1)
    weighted = d_normed * attn_gain
    input_grad = (
        d_residual
        + scale_one
        * (weighted - inputs * scale_one * scale_one * jnp.mean(weighted * inputs, axis=1, keepdims=True))
    ).astype(BF16)
    proj_rows = add_low(take(proj_core, fo), proj_x)
    m_one = [m[1][0], add_low(m[1][1], m_x)]
    m_z, up_got, gate_got, input_grad, gu, proj_rows, m, m_one, out_z, out_part, gain_parts, down_part = sync(
        m_z, up_got, gate_got, input_grad, gu, proj_rows, m, m_one, out_z, out_part, gain_parts, down_part
    )
    proj = lax.all_to_all(proj_rows, seq, split_axis=0, concat_axis=1, tiled=True)
    down_half = part // 2
    down_got = [send_far(down_part[:, :down_half], za)]
    spread = to_owners(gu[:far], gu[far:], gate_got, up_got)
    m_one.append((m[1][2].astype(F32) + m_z[0].astype(F32) + m_z[1].astype(F32)).astype(BF16))
    out_part = add_low(pick(out_part, zb, 1), out_z)
    gain_row = gain_parts[0]
    pack = jnp.concatenate(
        [
            ffn_part,
            gain_row[:q_cols].reshape(heads, HEAD_SIZE).sum(axis=0),
            gain_row[q_cols:q_cols + HEAD_SIZE],
        ]
    ).reshape(-1, LANES)
    for axis in ("fi", "fo", "si", "zb", "za"):
        offset = 1
        while offset < lax.axis_size(axis):
            pack = pack + swap(pack, axis, offset)
            offset *= 2
    pack = pack.reshape(-1)
    proj, spread, m, m_one, out_part, down_part, down_got, pack = sync(
        proj, spread, m, m_one, out_part, down_part, down_got, pack
    )
    out_got = send_far(out_part, za)
    down_got.append(send_far(down_part[:, down_half:], za))
    m_last = [swap(m_one[0], X), swap(m_one[1], Y), swap(m_one[2], Z)]
    gate_up = place(spread, own_block, part)
    gate_mine, up_mine = gate_up
    down_mine = jnp.concatenate(
        [add_far(down_part[:, :down_half], down_got[0], za), add_far(down_part[:, down_half:], down_got[1], za)], axis=0
    )
    mlp_out = m[0][0].astype(F32) + sum(a.astype(F32) for a in m_last)
    block_output = (residual + mlp_out).astype(BF16)
    out_mine = add_far(out_part, out_got, za)
    proj = proj.astype(F32)
    count = proj.shape[0]
    by_device = proj.reshape(count, s_count, padded)

    def fold(values):
        return values.reshape(count, KEY_VALUE_HEADS, copies, HEAD_SIZE).sum(axis=2).reshape(count, -1)

    query_mine = by_device[:, :, :q_cols].reshape(count, QUERY_HEADS * HEAD_SIZE)
    key_mine = fold(by_device[:, :, q_cols:q_cols + HEAD_SIZE])
    value_mine = fold(by_device[:, :, q_cols + HEAD_SIZE:cols])

    my_w = lax.dynamic_slice_in_dim(w_rows, s_index * count, count, 0).astype(F32)
    my_gain = lax.dynamic_slice_in_dim(attn_gain, (f_index * s_count + s_index) * count, count, 0)
    attn_gain_mine = jnp.sum(my_w * proj, axis=1) / my_gain
    ffn_gain_mine = lax.dynamic_slice_in_dim(pack, (f_index * s_count + s_index) * count, count, 0)
    attn_rms = jnp.sqrt(square_one + EPSILON)[:, 0]
    mlp_rms = jnp.sqrt(square_two + EPSILON)[:, 0]
    return (
        block_output, input_grad, residual, attn_rms, mlp_rms, attn_gain_mine,
        query_mine, key_mine, value_mine, pack[width:width + HEAD_SIZE], pack[width + HEAD_SIZE:],
        out_mine, ffn_gain_mine, gate_mine, up_mine, down_mine,
    )


def solution(mesh):
    f_count, s_count = mesh.shape["fsdp"], mesh.shape["seq"]
    fine = Mesh(
        mesh.devices.reshape(f_count // 2, 2, s_count // 4, 2, 2), ("fo", "fi", "za", "zb", "si")
    )
    f, s = ("fo", "fi"), ("za", "zb", "si")
    every = P(f + s, None)
    vector = P(f + s)
    placed = (
        every, P(f, None), every, P(), P(f, None), P(f, None), P(f, None), P(), P(),
        P(f, None), P(), P(None, f), P(None, f), P(f, None),
    )
    return jax.shard_map(
        per_device,
        mesh=fine,
        in_specs=placed,
        out_specs=(
            every, every, every, vector, vector, vector, every, every, every, P(), P(),
            every, vector, P(s, f), P(s, f), every,
        ),
        check_vma=False,
    )
```

time: 969 us -> 680 us (0.70)
  waiting for transfers between devices: 454 us -> 203 us
  blocking collectives: 143 us -> 0 us
  Pallas kernels: 74.7 us -> 180 us
  matrix products: 138 us -> 33.1 us
  starting transfers between devices: 14.5 us -> 97.6 us
  other arithmetic: 24 us -> 78.6 us
  local copies, waits for them, and re-layouts: 95.1 us -> 63.3 us
    reduce_scatter x7 -> x0, waiting for transfers between devices: 240 us -> none  [the longest x1 78.2 us: per_device(): lax.psum_scatter(down_part, 'so', scatter_dimension=0, tiled=True)]
    all_gather x6 -> x1, waiting for transfers between devices: 213 us -> 0.01 us  [per_device(): lax.all_gather(jnp.concatenate(own_cols, axis=1), fsdp, axis=0, tiled=True)]
    ppermute x0 -> x86, waiting for transfers between devices: none -> 177 us  [the longest x78 162 us: swap(): return lax.ppermute(values, axis, [(i, i ^ offset) for i in range(size)])]
    pallas_call x1 -> x10, Pallas kernels: 22.1 us -> 133 us  [the longest x4 66.9 us: feed(): pl.pallas_call(functools.partial(feed_kernel, tuple((tuple((o.shape[0] //...]
    dot_general x14 -> x8, matrix products: 138 us -> 33.1 us  [dot(): return lax.dot_general(left, right, dims, preferred_element_type=F32)]
    all_to_all x4 -> x0, blocking collectives: 103 us -> none  [the longest x1 46.8 us: per_device(): lax.all_to_all(d_heads, seq, split_axis=1, concat_axis=0, tiled=True)]
    ppermute x0 -> x86, starting transfers between devices: none -> 75.3 us  [the longest x78 64.8 us: swap(): return lax.ppermute(values, axis, [(i, i ^ offset) for i in range(size)])]
    unnamed x1 -> x0, blocking collectives: 39.9 us -> none
  transfers between devices with their start and end apart: 17 -> 92, of which waited for: 11 -> 34; matrix products, arithmetic and copies ran while one was open for 20% -> 23% of each run, Pallas kernels for 8% -> 27%
where the time goes in v2:
time: 680 us; the launch traced here: 672 us
  waiting for transfers between devices  203 us (30%)
  Pallas kernels  180 us (26%)
  starting transfers between devices  97.6 us (14%)
  other arithmetic  78.6 us (12%)
  local copies, waits for them, and re-layouts  63.3 us (9%)
  matrix products  33.1 us (5%)
  between operations  15.7 us (2%)
    ppermute x78, waiting for transfers between devices, swap(): return lax.ppermute(values, axis, [(i, i ^ offset) for i in range(size)])  162 us
    pallas_call x4, Pallas kernels, feed(): pl.pallas_call(functools.partial(feed_kernel, tuple((tuple((o.shape[0] //...  66.9 us
    ppermute x78, starting transfers between devices, swap(): return lax.ppermute(values, axis, [(i, i ^ offset) for i in range(size)])  64.8 us
    dot_general x8, matrix products, dot(): return lax.dot_general(left, right, dims, preferred_element_type=F32)  33.1 us
    pallas_call x1, Pallas kernels, attend_back(): pl.pallas_call(functools.partial(attend_back_kernel, heads), out_shape=[j...  31.8 us
    convert_element_type x13, other arithmetic, add_low(): return (left.astype(F32) + right.astype(F32)).astype(BF16)  25.9 us
    pallas_call x1, Pallas kernels, gate_grad(): pl.pallas_call(functools.partial(gate_grad_kernel, len(arrays), layout, f...  23.5 us
    pallas_call x3, Pallas kernels, project(): pl.pallas_call(functools.partial(project_kernel, heads, count, fresh), gr...  23 us
  transfers between devices with their start and end apart: 92, of which 34 were waited for; matrix products, arithmetic and copies ran while one was open for 23% of the time, Pallas kernels for 27%

profile of v2, /device:TPU:0, one launch (start us, length us, event | category | flops | bytes accessed | tf_op | source)
XLA Modules:
  0.0 671.8 jit_solution(776091716767534339)
XLA Ops:
  11.2 4.1 collective-permute-start
  39.3 10.5 %collective-permute-done.refs_0_ = bf16[192,2048]{1,0:T(8,128)(2,1)} collective-permute-done((bf16[192,2048]{1,0:T(8,128)(2,1)S(1)}, bf16[192,2048]{1,0:T(8,128)(2,1)}, u32[]{:S(2)}, u32[]{:S(2)}) %collective-permute-start) | collective-permute-done | bytes 786464 | tf_op jit(solution)/shard_map/ppermute | solution.py:572
  54.3 8.6 %project.3 = (bf16[1536,2048]{1,0:T(8,128)(2,1)}, bf16[4,1536,128]{2,1,0:T(8,128)(2,1)}, bf16[1536,128]{1,0:T(8,128)(2,1)}, bf16[1536,128]{1,0:T(8,128)(2,1)}, f32[1536,384]{1,0:T(8,128)}, /*index=5*/f32[1536,384]{1,0:T(8,128)}) custom-call(s32[3]{0:T(128)} %get-tuple-element.758.index_ref, s32[2]{0:T(128)} %bitcast.198, bf16[192,2048]{1,0:T(8,128)(2,1)} %refs_0_.1, ...), custom_call_target="tpu_custom_call" | custom-call | flops 1000 | bytes 1000 | tf_op jit(solution)/shard_map/project/pallas_call | solution.py:122
  62.9 5.9 collective-permute-done.4.refs_1_
  72.8 8.0 %project.4 = (bf16[1536,2048]{1,0:T(8,128)(2,1)}, bf16[4,1536,128]{2,1,0:T(8,128)(2,1)}, bf16[1536,128]{1,0:T(8,128)(2,1)}, bf16[1536,128]{1,0:T(8,128)(2,1)}, f32[1536,384]{1,0:T(8,128)}, /*index=5*/f32[1536,384]{1,0:T(8,128)}) custom-call(s32[3]{0:T(128)} %get-tuple-element.759.index_ref, ...), custom_call_target="tpu_custom_call", output_to_operand_aliasing={{0}: (10, {}), {1}: (11, {}), {2}: (12, {}), {3}: (13, {}),... | custom-call | flops 1000 | bytes 1000 | tf_op jit(solution)/shard_map/project/pallas_call | solution.py:122
  80.9 7.2 %collective-permute-done.6.refs_0_ = bf16[192,2048]{1,0:T(8,128)(2,1)S(1)} collective-permute-done((bf16[192,2048]{1,0:T(8,128)(2,1)}, bf16[192,2048]{1,0:T(8,128)(2,1)S(1)}, u32[]{:S(2)}, u32[]{:S(2)}) %collective-permute-start.6) | collective-permute-done | bytes 786464 | tf_op jit(solution)/shard_map/ppermute | solution.py:572
  95.7 6.4 project.5
  102.0 16.1 %attend.1 = (bf16[1536,256]{1,0:T(8,128)(2,1)}, f32[1536,256]{1,0:T(8,128)}, bf16[4,1536,128]{2,1,0:T(8,128)(2,1)}) custom-call(bf16[4,1536,128]{2,1,0:T(8,128)(2,1)} %get-tuple-element.394.q_ref, bf16[1536,128]{1,0:T(8,128)(2,1)} %get-tuple-element.395.k_ref, bf16[1536,128]{1,0:T(8,128)(2,1)} %get-tuple-element.396.v_ref), custom_call_target="tpu_custom_call" | custom-call | flops 1000 | bytes 1000 | tf_op jit(solution)/shard_map/attend/pallas_call | solution.py:180
  121.2 8.0 %all-to-all-start = ((bf16[8,192,256]{2,1,0:T(8,128)(2,1)}), bf16[8,192,256]{2,1,0:T(8,128)(2,1)}, u32[]{:S(2)}, u32[]{:S(2)}) async-start(bf16[8,192,256]{2,1,0:T(8,128)(2,1)} %bitcast.191), calls=%async_computation | async-start | bytes 1572864 | tf_op jit(solution)/shard_map/all_to_all | solution.py:710
  130.0 20.1 %all-to-all-done = bf16[8,192,256]{2,1,0:T(8,128)(2,1)} async-done(((bf16[8,192,256]{2,1,0:T(8,128)(2,1)}), bf16[8,192,256]{2,1,0:T(8,128)(2,1)}, u32[]{:S(2)}, u32[]{:S(2)}) %all-to-all-start) | async-done | bytes 786464 | tf_op jit(solution)/shard_map/all_to_all | solution.py:710
  154.9 5.6 multiply_reduce_fusion.2
  167.8 11.0 %feed.4 = (bf16[1,192,2048]{2,1,0:T(8,128)(2,1)}, bf16[1,192,2048]{2,1,0:T(8,128)(2,1)}, bf16[1,192,2048]{2,1,0:T(8,128)(2,1)}, bf16[1,192,2048]{2,1,0:T(8,128)(...) custom-call(s32[2]{0:T(128)} %multiply_add_fusion.3.index_ref, ...), custom_call_target="tpu_custom_call" | custom-call | flops 1000 | bytes 1000 | tf_op jit(solution)/shard_map/feed/pallas_call | solution.py:395
  178.8 6.5 collective-permute-done.20.refs_0_.refs_2_
  193.9 22.3 %feed.5 = (bf16[3,192,2048]{2,1,0:T(8,128)(2,1)}, bf16[3,192,2048]{2,1,0:T(8,128)(2,1)}, bf16[3,192,2048]{2,1,0:T(8,128)(2,1)}, bf16[3,192,2048]{2,1,0:T(8,128)(...) custom-call(s32[2]{0:T(128)} %multiply_add_fusion.3.index_ref, bf16[192,2048]{1,0:T(8,128)(2,1)} %copy-done.13, ...), custom_call_target="tpu_custom_call" | custom-call | flops 1000 | bytes 1000 | tf_op jit(solution)/shard_map/feed/pallas_call | solution.py:395
  216.3 8.8 %collective-permute-done.25.refs_0_.refs_6_ = bf16[192,2048]{1,0:T(8,128)(2,1)} collective-permute-done((bf16[192,2048]{1,0:T(8,128)(2,1)}, bf16[192,2048]{1,0:T(8,128)(2,1)}, u32[]{:S(2)}, u32[]{:S(2)}) %collective-permute-start.25) | collective-permute-done | bytes 786464 | tf_op jit(solution)/shard_map/ppermute | solution.py:572
  234.5 3.1 collective-permute-done.32
  240.9 22.5 %feed.6 = (bf16[3,192,2048]{2,1,0:T(8,128)(2,1)}, bf16[3,192,2048]{2,1,0:T(8,128)(2,1)}, bf16[3,192,2048]{2,1,0:T(8,128)(2,1)}, bf16[3,192,2048]{2,1,0:T(8,128)(...) custom-call(s32[2]{0:T(128)} %multiply_add_fusion.3.index_ref, ...), custom_call_target="tpu_custom_call" | custom-call | flops 1000 | bytes 1000 | tf_op jit(solution)/shard_map/feed/pallas_call | solution.py:395
  263.4 4.8 collective-permute-done.34
  268.8 6.4 collective-permute-done.39
  283.4 11.0 %feed.7 = (bf16[1,192,2048]{2,1,0:T(8,128)(2,1)}, bf16[1,192,2048]{2,1,0:T(8,128)(2,1)}, bf16[1,192,2048]{2,1,0:T(8,128)(2,1)}, bf16[1,192,2048]{2,1,0:T(8,128)(...) custom-call(s32[2]{0:T(128)} %multiply_add_fusion.3.index_ref, ...), custom_call_target="tpu_custom_call" | custom-call | flops 1000 | bytes 1000 | tf_op jit(solution)/shard_map/feed/pallas_call | solution.py:395
  294.4 12.5 %collective-permute-done.41 = bf16[96,2048]{1,0:T(8,128)(2,1)} collective-permute-done((bf16[96,2048]{1,0:T(8,128)(2,1)}, bf16[96,2048]{1,0:T(8,128)(2,1)}, u32[]{:S(2)}, u32[]{:S(2)}) %collective-permute-start.41) | collective-permute-done | bytes 393248 | tf_op jit(solution)/shard_map/ppermute | solution.py:592
  307.4 5.0 collective-permute-done.45
  321.9 13.7 %down_grad.1 = bf16[512,2048]{1,0:T(8,128)(2,1)} custom-call(bf16[192,2048]{1,0:T(8,128)(2,1)} %refs_0_.2, bf16[192,2048]{1,0:T(8,128)(2,1)} %copy-done.25, bf16[192,2048]{1,0:T(8,128)(2,1)} %copy-done.11, bf16[192,2048]{1,0:T(8,128)(2,1)} %collective-permute-done.8.refs_5_.refs_3_, bf16[192,2048]{1,0:T(8,128)(2,1)} %copy-done.12, ...), custom_call_target="tpu_custom_call" | custom-call | flops 1000 | bytes 1000 | tf_op jit(solution)/shard_map/down_grad/pallas_call | solution.py:519
  335.7 23.5 %gate_grad.1 = (bf16[1024,512]{1,0:T(8,128)(2,1)}, bf16[1024,512]{1,0:T(8,128)(2,1)}, bf16[1024,512]{1,0:T(8,128)(2,1)}, bf16[1024,512]{1,0:T(8,128)(2,1)}) custom-call(s32[1]{0:T(128)} %bitcast.28.index_ref, bf16[192,2048]{1,0:T(8,128)(2,1)} %multiply_convert_fusion.refs_0_, bf16[192,2048]{1,0:T(8,128)(2,1)} %collective-permute-done.23.refs_1_, ...), custom_call_target="tpu_custom_call" | custom-call | flops 1000 | bytes 1000 | tf_op jit(solution)/shard_map/gate_grad/pallas_call | solution.py:480
  366.3 4.6 multiply_reduce_fusion
  372.4 6.5 convolution_convert_fusion.1
  378.9 5.6 collective-permute-done.52
  386.7 4.2 all-to-all-start.1
  394.8 4.9 add_convert_fusion.1
  399.7 4.2 add_convert_fusion
  407.3 15.5 %collective-permute-done.59 = bf16[256,512]{1,0:T(8,128)(2,1)S(1)} collective-permute-done((bf16[256,512]{1,0:T(8,128)(2,1)S(1)}, bf16[256,512]{1,0:T(8,128)(2,1)S(1)}, u32[]{:S(2)}, u32[]{:S(2)}) %collective-permute-start.59) | collective-permute-done | bytes 262176 | tf_op jit(solution)/shard_map/ppermute | solution.py:572
  429.2 4.0 fusion.18
  437.6 31.8 %attend_back.1 = (bf16[1536,384]{1,0:T(8,128)(2,1)}, f32[8,384]{1,0:T(8,128)}) custom-call(bf16[4,1536,128]{2,1,0:T(8,128)(2,1)} %get-tuple-element.406.q_ref, bf16[1536,128]{1,0:T(8,128)(2,1)} %get-tuple-element.395.k_ref, bf16[1536,128]{1,0:T(8,128)(2,1)} %get-tuple-element.396.v_ref, bf16[1536,256]{1,0:T(8,128)(2,1)} %bitcast.30.grad_ref, ...), custom_call_target="tpu_custom_call" | custom-call | flops 1000 | bytes 1000 | tf_op jit(solution)/shard_map/attend_back/pallas_call | solution.py:294
  469.4 7.5 %collective-permute-done.61 = bf16[192,2048]{1,0:T(8,128)(2,1)} collective-permute-done((bf16[192,2048]{1,0:T(8,128)(2,1)}, bf16[192,2048]{1,0:T(8,128)(2,1)}, u32[]{:S(2)}, u32[]{:S(2)}) %collective-permute-start.61) | collective-permute-done | bytes 786464 | tf_op jit(solution)/shard_map/ppermute | solution.py:572
  476.9 5.1 all-to-all-start.2
  481.9 3.3 pad_maximum_fusion.4
  485.2 6.4 convolution_convert_fusion
  504.3 5.1 all-to-all-done.2
  514.0 7.4 %collective-permute-done.65 = bf16[512,384]{1,0:T(8,128)(2,1)S(1)} collective-permute-done((bf16[512,384]{1,0:T(8,128)(2,1)}, bf16[512,384]{1,0:T(8,128)(2,1)S(1)}, u32[]{:S(2)}, u32[]{:S(2)}) %collective-permute-start.65) | collective-permute-done | bytes 393248 | tf_op jit(solution)/shard_map/ppermute | solution.py:572
  529.4 3.1 fusion.40
  532.5 3.1 convolution_bitcast_fusion
  535.6 3.1 fusion.37
  550.5 11.1 %collective-permute-done.71 = bf16[2,64,2048]{2,1,0:T(8,128)(2,1)S(1)} collective-permute-done((bf16[2,64,2048]{2,1,0:T(8,128)(2,1)S(1)}, bf16[2,64,2048]{2,1,0:T(8,128)(2,1)S(1)}, u32[]{:S(2)}, u32[]{:S(2)}) %collective-permute-start.71) | collective-permute-done | bytes 524320 | tf_op jit(solution)/shard_map/ppermute | solution.py:572
  564.2 4.8 all-to-all-start.3
  591.1 22.0 %collective-permute-done.79 = f32[17,128]{1,0:T(8,128)S(1)} collective-permute-done((f32[17,128]{1,0:T(8,128)S(1)}, f32[17,128]{1,0:T(8,128)S(1)}, u32[]{:S(2)}, u32[]{:S(2)}) %collective-permute-start.79) | collective-permute-done | bytes 8736 | tf_op jit(solution)/shard_map/ppermute | solution.py:572
  630.6 5.5 place.1
  645.3 13.3 %collective-permute-done.85 = bf16[128,2048]{1,0:T(8,128)(2,1)} collective-permute-done((bf16[128,2048]{1,0:T(8,128)(2,1)}, bf16[128,2048]{1,0:T(8,128)(2,1)}, u32[]{:S(2)}, u32[]{:S(2)}) %collective-permute-start.85) | collective-permute-done | bytes 524320 | tf_op jit(solution)/shard_map/ppermute | solution.py:572
  661.4 3.1 fusion.31
  (427 shorter events, 219.3 us)
Async XLA Ops:
  7.2 47.2 %all-gather.3.cloned.1.call-start = ((), (), s32[]{:S(2)}) async-start(), calls=%async_computation.4 | async-start | bytes 1966080 | tf_op jit(solution)/shard_map/all_gather | solution.py:667
  10.4 144.5 %all-gather.5.cloned.1.call-start = ((), (), s32[]{:S(2)}) async-start(), calls=%async_computation.5 | async-start | bytes 10485760 | tf_op jit(solution)/shard_map/all_gather | solution.py:668
  11.2 38.7 %collective-permute-start = (bf16[192,2048]{1,0:T(8,128)(2,1)S(1)}, bf16[192,2048]{1,0:T(8,128)(2,1)}, u32[]{:S(2)}, u32[]{:S(2)}) collective-permute-start(bf16[192,2048]{1,0:T(8,128)(2,1)S(1)} %copy-done.16), channel_id=1, source_target_pairs={{0,4},{4,0},{1,5},{5,1},{2,6},{6,2},{3,7},{7,3},{8,12},{12,8},{9,1... | collective-permute-start | bytes 2359304 | tf_op jit(solution)/shard_map/ppermute | solution.py:572
  15.3 34.6 %collective-permute-start.1 = (bf16[192,2048]{1,0:T(8,128)(2,1)S(1)}, bf16[192,2048]{1,0:T(8,128)(2,1)}, u32[]{:S(2)}, u32[]{:S(2)}) collective-permute-start(bf16[192,2048]{1,0:T(8,128)(2,1)S(1)} %copy-done.16), channel_id=1, source_target_pairs={{0,1},{1,0},{2,3},{3,2},{4,5},{5,4},{6,7},{7,6},{8,9},{9,8},{10,11... | collective-permute-start | bytes 2359304 | tf_op jit(solution)/shard_map/ppermute | solution.py:572
  16.8 34.5 %collective-permute-start.2 = (bf16[192,2048]{1,0:T(8,128)(2,1)S(1)}, bf16[192,2048]{1,0:T(8,128)(2,1)}, u32[]{:S(2)}, u32[]{:S(2)}) collective-permute-start(bf16[192,2048]{1,0:T(8,128)(2,1)S(1)} %copy-done.16), channel_id=1, source_target_pairs={{0,2},{2,0},{1,3},{3,1},{4,6},{6,4},{5,7},{7,5},{8,10},{10,8},{9,1... | collective-permute-start | bytes 2359304 | tf_op jit(solution)/shard_map/ppermute | solution.py:572
  18.4 32.9 %collective-permute-start.3 = (bf16[192,2048]{1,0:T(8,128)(2,1)S(1)}, bf16[192,2048]{1,0:T(8,128)(2,1)S(1)}, u32[]{:S(2)}, u32[]{:S(2)}) collective-permute-start(bf16[192,2048]{1,0:T(8,128)(2,1)S(1)} %copy-done.4), channel_id=1, source_target_pairs={{0,16},{16,0},{1,17},{17,1},{2,18},{18,2},{3,19},{19,3},{4,20},{20... | collective-permute-start | bytes 2359304 | tf_op jit(solution)/shard_map/ppermute | solution.py:572
  89.5 28.6 %collective-permute-start.10 = (bf16[512,3072]{1,0:T(8,128)(2,1)}, bf16[512,3072]{1,0:T(8,128)(2,1)}, u32[]{:S(2)}, u32[]{:S(2)}) collective-permute-start(bf16[512,3072]{1,0:T(8,128)(2,1)} %bitcast.161), channel_id=1, source_target_pairs={{0,8},{8,0},{1,9},{9,1},{2,10},{10,2},{3,11},{11,3},{4,12},{12,4},... | collective-permute-start | bytes 9437192 | tf_op jit(solution)/shard_map/ppermute | solution.py:572
  90.4 27.7 %collective-permute-start.8 = (bf16[192,2048]{1,0:T(8,128)(2,1)S(1)}, bf16[192,2048]{1,0:T(8,128)(2,1)}, u32[]{:S(2)}, u32[]{:S(2)}) collective-permute-start(bf16[192,2048]{1,0:T(8,128)(2,1)S(1)} %copy-done.4), channel_id=1, source_target_pairs={{0,1},{1,0},{2,3},{3,2},{4,5},{5,4},{6,7},{7,6},{8,9},{9,8},{10,11... | collective-permute-start | bytes 2359304 | tf_op jit(solution)/shard_map/ppermute | solution.py:572
  91.2 26.9 %collective-permute-start.9 = (bf16[192,2048]{1,0:T(8,128)(2,1)S(1)}, bf16[192,2048]{1,0:T(8,128)(2,1)S(1)}, u32[]{:S(2)}, u32[]{:S(2)}) collective-permute-start(bf16[192,2048]{1,0:T(8,128)(2,1)S(1)} %copy-done.4), channel_id=1, source_target_pairs={{0,2},{2,0},{1,3},{3,1},{4,6},{6,4},{5,7},{7,5},{8,10},{10,8},{9,1... | collective-permute-start | bytes 2359304 | tf_op jit(solution)/shard_map/ppermute | solution.py:572
  121.2 30.2 %collective-permute-start.14 = (bf16[576,2048]{1,0:T(8,128)(2,1)}, bf16[576,2048]{1,0:T(8,128)(2,1)}, u32[]{:S(2)}, u32[]{:S(2)}) collective-permute-start(bf16[576,2048]{1,0:T(8,128)(2,1)} %pad_maximum_fusion.1), channel_id=1, source_target_pairs={{0,8},{8,0},{1,9},{9,1},{2,10},{10,2},{3,11},{11,3},{4,12},{12,4},... | collective-permute-start | bytes 7077896 | tf_op jit(solution)/shard_map/ppermute | solution.py:572
  121.2 28.9 %all-to-all-start = ((bf16[8,192,256]{2,1,0:T(8,128)(2,1)}), bf16[8,192,256]{2,1,0:T(8,128)(2,1)}, u32[]{:S(2)}, u32[]{:S(2)}) async-start(bf16[8,192,256]{2,1,0:T(8,128)(2,1)} %bitcast.191), calls=%async_computation | async-start | bytes 1572864 | tf_op jit(solution)/shard_map/all_to_all | solution.py:710
  187.9 28.3 %collective-permute-start.27 = (bf16[192,2048]{1,0:T(8,128)(2,1)}, bf16[192,2048]{1,0:T(8,128)(2,1)}, u32[]{:S(2)}, u32[]{:S(2)}) collective-permute-start(bf16[192,2048]{1,0:T(8,128)(2,1)} %collective-permute-done.8.refs_5_.refs_3_), channel_id=1, source_target_pairs={{0,16},{16,0},{1,17},{17,1},{2,18},{18,2},{3,19},{19,3},{4,20},{20... | collective-permute-start | bytes 2359304 | tf_op jit(solution)/shard_map/ppermute | solution.py:572
  189.6 26.7 %collective-permute-start.28 = (bf16[192,2048]{1,0:T(8,128)(2,1)}, bf16[192,2048]{1,0:T(8,128)(2,1)}, u32[]{:S(2)}, u32[]{:S(2)}) collective-permute-start(bf16[192,2048]{1,0:T(8,128)(2,1)} %collective-permute-done.8.refs_5_.refs_3_), channel_id=1, source_target_pairs={{0,2},{2,0},{1,3},{3,1},{4,6},{6,4},{5,7},{7,5},{8,10},{10,8},{9,1... | collective-permute-start | bytes 2359304 | tf_op jit(solution)/shard_map/ppermute | solution.py:572
  189.9 26.4 %collective-permute-start.24 = (bf16[192,2048]{1,0:T(8,128)(2,1)}, bf16[192,2048]{1,0:T(8,128)(2,1)}, u32[]{:S(2)}, u32[]{:S(2)}) collective-permute-start(bf16[192,2048]{1,0:T(8,128)(2,1)} %copy-done.13), channel_id=1, source_target_pairs={{0,1},{1,0},{2,3},{3,2},{4,5},{5,4},{6,7},{7,6},{8,9},{9,8},{10,11... | collective-permute-start | bytes 2359304 | tf_op jit(solution)/shard_map/ppermute | solution.py:572
  190.5 34.6 %collective-permute-start.25 = (bf16[192,2048]{1,0:T(8,128)(2,1)}, bf16[192,2048]{1,0:T(8,128)(2,1)}, u32[]{:S(2)}, u32[]{:S(2)}) collective-permute-start(bf16[192,2048]{1,0:T(8,128)(2,1)} %copy-done.15), channel_id=1, source_target_pairs={{0,16},{16,0},{1,17},{17,1},{2,18},{18,2},{3,19},{19,3},{4,20},{20... | collective-permute-start | bytes 2359304 | tf_op jit(solution)/shard_map/ppermute | solution.py:572
  192.4 33.9 %collective-permute-start.26 = (bf16[192,2048]{1,0:T(8,128)(2,1)}, bf16[192,2048]{1,0:T(8,128)(2,1)}, u32[]{:S(2)}, u32[]{:S(2)}) collective-permute-start(bf16[192,2048]{1,0:T(8,128)(2,1)} %copy-done.14), channel_id=1, source_target_pairs={{0,2},{2,0},{1,3},{3,1},{4,6},{6,4},{5,7},{7,5},{8,10},{10,8},{9,1... | collective-permute-start | bytes 2359304 | tf_op jit(solution)/shard_map/ppermute | solution.py:572
  230.7 32.6 %collective-permute-start.30 = (bf16[192,2048]{1,0:T(8,128)(2,1)}, bf16[192,2048]{1,0:T(8,128)(2,1)}, u32[]{:S(2)}, u32[]{:S(2)}) collective-permute-start(bf16[192,2048]{1,0:T(8,128)(2,1)} %collective-permute-done.25.refs_0_.refs_6_), channel_id=1, source_target_pairs={{0,1},{1,0},{2,3},{3,2},{4,5},{5,4},{6,7},{7,6},{8,9},{9,8},{10,11... | collective-permute-start | bytes 2359304 | tf_op jit(solution)/shard_map/ppermute | solution.py:572
  231.4 32.0 %collective-permute-start.31 = (bf16[192,2048]{1,0:T(8,128)(2,1)}, bf16[192,2048]{1,0:T(8,128)(2,1)}, u32[]{:S(2)}, u32[]{:S(2)}) collective-permute-start(bf16[192,2048]{1,0:T(8,128)(2,1)} %collective-permute-done.28.refs_6_.refs_8_), channel_id=1, source_target_pairs={{0,16},{16,0},{1,17},{17,1},{2,18},{18,2},{3,19},{19,3},{4,20},{20... | collective-permute-start | bytes 2359304 | tf_op jit(solution)/shard_map/ppermute | solution.py:572
  237.6 30.6 %collective-permute-start.34 = (bf16[192,2048]{1,0:T(8,128)(2,1)}, bf16[192,2048]{1,0:T(8,128)(2,1)}, u32[]{:S(2)}, u32[]{:S(2)}) collective-permute-start(bf16[192,2048]{1,0:T(8,128)(2,1)} %get-tuple-element.713), channel_id=1, source_target_pairs={{0,16},{16,0},{1,17},{17,1},{2,18},{18,2},{3,19},{19,3},{4,20},{20... | collective-permute-start | bytes 2359304 | tf_op jit(solution)/shard_map/ppermute | solution.py:572
  238.1 30.1 %collective-permute-start.35 = (bf16[192,2048]{1,0:T(8,128)(2,1)}, bf16[192,2048]{1,0:T(8,128)(2,1)}, u32[]{:S(2)}, u32[]{:S(2)}) collective-permute-start(bf16[192,2048]{1,0:T(8,128)(2,1)} %get-tuple-element.712), channel_id=1, source_target_pairs={{0,1},{1,0},{2,3},{3,2},{4,5},{5,4},{6,7},{7,6},{8,9},{9,8},{10,11... | collective-permute-start | bytes 2359304 | tf_op jit(solution)/shard_map/ppermute | solution.py:572
  239.2 29.0 %collective-permute-start.36 = (bf16[192,2048]{1,0:T(8,128)(2,1)}, bf16[192,2048]{1,0:T(8,128)(2,1)}, u32[]{:S(2)}, u32[]{:S(2)}) collective-permute-start(bf16[192,2048]{1,0:T(8,128)(2,1)} %get-tuple-element.711), channel_id=1, source_target_pairs={{0,2},{2,0},{1,3},{3,1},{4,6},{6,4},{5,7},{7,5},{8,10},{10,8},{9,1... | collective-permute-start | bytes 2359304 | tf_op jit(solution)/shard_map/ppermute | solution.py:572
  279.2 27.7 %collective-permute-start.41 = (bf16[96,2048]{1,0:T(8,128)(2,1)}, bf16[96,2048]{1,0:T(8,128)(2,1)}, u32[]{:S(2)}, u32[]{:S(2)}) collective-permute-start(bf16[96,2048]{1,0:T(8,128)(2,1)} %get-tuple-element.709), channel_id=1, source_target_pairs={{0,17},{1,16},{16,1},{17,0},{2,19},{3,18},{18,3},{19,2},{4,21},{5,... | collective-permute-start | bytes 1179656 | tf_op jit(solution)/shard_map/ppermute | solution.py:592
  281.6 25.3 %collective-permute-start.42 = (bf16[96,2048]{1,0:T(8,128)(2,1)}, bf16[96,2048]{1,0:T(8,128)(2,1)}, u32[]{:S(2)}, u32[]{:S(2)}) collective-permute-start(bf16[96,2048]{1,0:T(8,128)(2,1)} %get-tuple-element.708), channel_id=1, source_target_pairs={{0,3},{1,2},{2,1},{3,0},{4,7},{5,6},{6,5},{7,4},{8,11},{9,10},{10,... | collective-permute-start | bytes 1179656 | tf_op jit(solution)/shard_map/ppermute | solution.py:592
  306.9 54.7 %collective-permute-start.50 = (bf16[3,192,2048]{2,1,0:T(8,128)(2,1)}, bf16[3,192,2048]{2,1,0:T(8,128)(2,1)}, u32[]{:S(2)}, u32[]{:S(2)}) collective-permute-start(bf16[3,192,2048]{2,1,0:T(8,128)(2,1)} %get-tuple-element.555), channel_id=1, source_target_pairs={{0,8},{8,0},{1,9},{9,1},{2,10},{10,2},{3,11},{11,3},{4,12},{12,4},... | collective-permute-start | bytes 7077896 | tf_op jit(solution)/shard_map/ppermute | solution.py:572
  314.7 46.9 %collective-permute-start.46 = (bf16[192,2048]{1,0:T(8,128)(2,1)}, bf16[192,2048]{1,0:T(8,128)(2,1)}, u32[]{:S(2)}, u32[]{:S(2)}) collective-permute-start(bf16[192,2048]{1,0:T(8,128)(2,1)} %fusion.45), channel_id=1, source_target_pairs={{0,19},{1,18},{2,17},{3,16},{16,3},{17,2},{18,1},{19,0},{4,23},{5,... | collective-permute-start | bytes 2359304 | tf_op jit(solution)/shard_map/ppermute | solution.py:592
  317.5 41.7 %collective-permute-start.47 = (bf16[96,2048]{1,0:T(8,128)(2,1)}, bf16[96,2048]{1,0:T(8,128)(2,1)S(1)}, u32[]{:S(2)}, u32[]{:S(2)}) collective-permute-start(bf16[96,2048]{1,0:T(8,128)(2,1)} %get-tuple-element.707), channel_id=1, source_target_pairs={{0,18},{2,16},{16,2},{18,0},{1,19},{3,17},{17,3},{19,1},{4,22},{6,... | collective-permute-start | bytes 1179656 | tf_op jit(solution)/shard_map/ppermute | solution.py:592
  319.6 41.5 %collective-permute-start.48 = (bf16[96,2048]{1,0:T(8,128)(2,1)}, bf16[96,2048]{1,0:T(8,128)(2,1)}, u32[]{:S(2)}, u32[]{:S(2)}) collective-permute-start(bf16[96,2048]{1,0:T(8,128)(2,1)} %get-tuple-element.706), channel_id=1, source_target_pairs={{0,17},{1,16},{16,1},{17,0},{2,19},{3,18},{18,3},{19,2},{4,21},{5,... | collective-permute-start | bytes 1179656 | tf_op jit(solution)/shard_map/ppermute | solution.py:592
  321.5 40.1 %collective-permute-start.49 = (bf16[96,2048]{1,0:T(8,128)(2,1)}, bf16[96,2048]{1,0:T(8,128)(2,1)}, u32[]{:S(2)}, u32[]{:S(2)}) collective-permute-start(bf16[96,2048]{1,0:T(8,128)(2,1)} %get-tuple-element.705), channel_id=1, source_target_pairs={{0,3},{1,2},{2,1},{3,0},{4,7},{5,6},{6,5},{7,4},{8,11},{9,10},{10,... | collective-permute-start | bytes 1179656 | tf_op jit(solution)/shard_map/ppermute | solution.py:592
  384.6 38.9 %collective-permute-start.56 = (bf16[192,2048]{1,0:T(8,128)(2,1)}, bf16[192,2048]{1,0:T(8,128)(2,1)}, u32[]{:S(2)}, u32[]{:S(2)}) collective-permute-start(bf16[192,2048]{1,0:T(8,128)(2,1)} %fusion.62), channel_id=1, source_target_pairs={{0,8},{8,0},{1,9},{9,1},{2,10},{10,2},{3,11},{11,3},{4,12},{12,4},... | collective-permute-start | bytes 2359304 | tf_op jit(solution)/shard_map/ppermute | solution.py:572
  386.7 36.8 %all-to-all-start.1 = ((bf16[192,8,256]{2,0,1:T(8,128)(2,1)}), bf16[192,8,256]{2,0,1:T(8,128)(2,1)}, u32[]{:S(2)}, u32[]{:S(2)}) async-start(bf16[192,8,256]{2,0,1:T(8,128)(2,1)} %bitcast.181), calls=%async_computation.1 | async-start | bytes 1572864 | tf_op jit(solution)/shard_map/all_to_all | solution.py:822
  391.9 30.9 %collective-permute-start.59 = (bf16[256,512]{1,0:T(8,128)(2,1)S(1)}, bf16[256,512]{1,0:T(8,128)(2,1)S(1)}, u32[]{:S(2)}, u32[]{:S(2)}) collective-permute-start(bf16[256,512]{1,0:T(8,128)(2,1)S(1)} %constant_dynamic-slice_fusion.7), channel_id=1, source_target_pairs={{0,4},{4,0},{1,5},{5,1},{2,6},{6,2},{3,7},{7,3},{8,12},{12,8},{9,1... | collective-permute-start | bytes 786440 | tf_op jit(solution)/shard_map/ppermute | solution.py:572
  427.0 49.9 %collective-permute-start.60 = (bf16[1024,512]{1,0:T(8,128)(2,1)}, bf16[1024,512]{1,0:T(8,128)(2,1)}, u32[]{:S(2)}, u32[]{:S(2)}) collective-permute-start(bf16[1024,512]{1,0:T(8,128)(2,1)} %pad_maximum_fusion.8), channel_id=1, source_target_pairs={{0,4},{4,0},{1,5},{5,1},{2,6},{6,2},{3,7},{7,3},{8,12},{12,8},{9,1... | collective-permute-start | bytes 3145736 | tf_op jit(solution)/shard_map/ppermute | solution.py:572
  428.2 48.7 %collective-permute-start.62 = (bf16[256,3072]{1,0:T(8,128)(2,1)}, bf16[256,3072]{1,0:T(8,128)(2,1)}, u32[]{:S(2)}, u32[]{:S(2)}) collective-permute-start(bf16[256,3072]{1,0:T(8,128)(2,1)} %slice.117), channel_id=1, source_target_pairs={{0,16},{16,0},{1,17},{17,1},{2,18},{18,2},{3,19},{19,3},{4,20},{20... | collective-permute-start | bytes 4718600 | tf_op jit(solution)/shard_map/ppermute | solution.py:572
  435.6 41.3 %collective-permute-start.63 = (bf16[2,2,64,2048]{3,2,0,1:T(8,128)(2,1)}, bf16[2,2,64,2048]{3,2,0,1:T(8,128)(2,1)}, u32[]{:S(2)}, u32[]{:S(2)}) collective-permute-start(bf16[2,2,64,2048]{3,2,0,1:T(8,128)(2,1)} %copy_bitcast_fusion), channel_id=1, source_target_pairs={{0,1},{1,0},{2,3},{3,2},{4,5},{5,4},{6,7},{7,6},{8,9},{9,8},{10,11... | collective-permute-start | bytes 3145736 | tf_op jit(solution)/shard_map/ppermute | solution.py:572
  437.0 39.9 %collective-permute-start.61 = (bf16[192,2048]{1,0:T(8,128)(2,1)}, bf16[192,2048]{1,0:T(8,128)(2,1)}, u32[]{:S(2)}, u32[]{:S(2)}) collective-permute-start(bf16[192,2048]{1,0:T(8,128)(2,1)} %bitcast.32), channel_id=1, source_target_pairs={{0,1},{1,0},{2,3},{3,2},{4,5},{5,4},{6,7},{7,6},{8,9},{9,8},{10,11... | collective-permute-start | bytes 2359304 | tf_op jit(solution)/shard_map/ppermute | solution.py:572
  476.9 32.5 %all-to-all-start.2 = ((bf16[8,192,384]{2,1,0:T(8,128)(2,1)}), bf16[8,192,384]{2,1,0:T(8,128)(2,1)}, u32[]{:S(2)}, u32[]{:S(2)}) async-start(bf16[8,192,384]{2,1,0:T(8,128)(2,1)} %bitcast.190), calls=%async_computation.2 | async-start | bytes 2359296 | tf_op jit(solution)/shard_map/all_to_all | solution.py:847
  485.2 36.2 %collective-permute-start.66 = (bf16[384,3072]{1,0:T(8,128)(2,1)}, bf16[384,3072]{1,0:T(8,128)(2,1)}, u32[]{:S(2)}, u32[]{:S(2)}) collective-permute-start(bf16[384,3072]{1,0:T(8,128)(2,1)} %pad_maximum_fusion.4), channel_id=1, source_target_pairs={{0,8},{8,0},{1,9},{9,1},{2,10},{10,2},{3,11},{11,3},{4,12},{12,4},... | collective-permute-start | bytes 7077896 | tf_op jit(solution)/shard_map/ppermute | solution.py:572
  521.4 40.3 %collective-permute-start.68 = (bf16[192,2048]{1,0:T(8,128)(2,1)S(1)}, bf16[192,2048]{1,0:T(8,128)(2,1)S(1)}, u32[]{:S(2)}, u32[]{:S(2)}) collective-permute-start(bf16[192,2048]{1,0:T(8,128)(2,1)S(1)} %copy-done.51), channel_id=1, source_target_pairs={{0,16},{16,0},{1,17},{17,1},{2,18},{18,2},{3,19},{19,3},{4,20},{20... | collective-permute-start | bytes 2359304 | tf_op jit(solution)/shard_map/ppermute | solution.py:572
  523.6 38.1 %collective-permute-start.69 = (bf16[192,2048]{1,0:T(8,128)(2,1)S(1)}, bf16[192,2048]{1,0:T(8,128)(2,1)S(1)}, u32[]{:S(2)}, u32[]{:S(2)}) collective-permute-start(bf16[192,2048]{1,0:T(8,128)(2,1)S(1)} %slice_bitcast_fusion.4), channel_id=1, source_target_pairs={{0,1},{1,0},{2,3},{3,2},{4,5},{5,4},{6,7},{7,6},{8,9},{9,8},{10,11... | collective-permute-start | bytes 2359304 | tf_op jit(solution)/shard_map/ppermute | solution.py:572
  564.2 53.6 %all-to-all-start.3 = ((bf16[8,64,384]{2,1,0:T(8,128)(2,1)}), bf16[8,64,384]{2,1,0:T(8,128)(2,1)}, u32[]{:S(2)}, u32[]{:S(2)}) async-start(bf16[8,64,384]{2,1,0:T(8,128)(2,1)} %bitcast.56), calls=%async_computation.3 | async-start | bytes 786432 | tf_op jit(solution)/shard_map/all_to_all | solution.py:876
  572.7 46.3 %collective-permute-start.72 = (bf16[512,512]{1,0:T(8,128)(2,1)}, bf16[512,512]{1,0:T(8,128)(2,1)S(1)}, u32[]{:S(2)}, u32[]{:S(2)}) collective-permute-start(bf16[512,512]{1,0:T(8,128)(2,1)} %pad_maximum_fusion.13), channel_id=1, source_target_pairs={{0,1},{1,0},{2,3},{3,2},{4,5},{5,4},{6,7},{7,6},{8,9},{9,8},{10,11... | collective-permute-start | bytes 1572872 | tf_op jit(solution)/shard_map/ppermute | solution.py:572
  575.5 43.4 %collective-permute-start.73 = (bf16[512,512]{1,0:T(8,128)(2,1)}, bf16[512,512]{1,0:T(8,128)(2,1)}, u32[]{:S(2)}, u32[]{:S(2)}) collective-permute-start(bf16[512,512]{1,0:T(8,128)(2,1)} %pad_maximum_fusion.14), channel_id=1, source_target_pairs={{0,2},{2,0},{1,3},{3,1},{4,6},{6,4},{5,7},{7,5},{8,10},{10,8},{9,1... | collective-permute-start | bytes 1572872 | tf_op jit(solution)/shard_map/ppermute | solution.py:572
  578.1 40.9 %collective-permute-start.74 = (bf16[512,512]{1,0:T(8,128)(2,1)}, bf16[512,512]{1,0:T(8,128)(2,1)}, u32[]{:S(2)}, u32[]{:S(2)}) collective-permute-start(bf16[512,512]{1,0:T(8,128)(2,1)} %pad_maximum_fusion.15), channel_id=1, source_target_pairs={{0,3},{1,2},{2,1},{3,0},{4,7},{5,6},{6,5},{7,4},{8,11},{9,10},{10,... | collective-permute-start | bytes 1572872 | tf_op jit(solution)/shard_map/ppermute | solution.py:592
  581.4 37.7 %collective-permute-start.75 = (bf16[128,2048]{1,0:T(8,128)(2,1)}, bf16[128,2048]{1,0:T(8,128)(2,1)}, u32[]{:S(2)}, u32[]{:S(2)}) collective-permute-start(bf16[128,2048]{1,0:T(8,128)(2,1)} %dynamic-slice_bitcast_fusion.2), channel_id=1, source_target_pairs={{0,4},{4,0},{1,5},{5,1},{2,6},{6,2},{3,7},{7,3},{8,12},{12,8},{9,1... | collective-permute-start | bytes 1572872 | tf_op jit(solution)/shard_map/ppermute | solution.py:572
  619.0 42.4 %collective-permute-start.83 = (bf16[192,2048]{1,0:T(8,128)(2,1)}, bf16[192,2048]{1,0:T(8,128)(2,1)}, u32[]{:S(2)}, u32[]{:S(2)}) collective-permute-start(bf16[192,2048]{1,0:T(8,128)(2,1)} %fusion.33), channel_id=1, source_target_pairs={{0,2},{2,0},{1,3},{3,1},{4,6},{6,4},{5,7},{7,5},{8,10},{10,8},{9,1... | collective-permute-start | bytes 2359304 | tf_op jit(solution)/shard_map/ppermute | solution.py:572
  619.5 41.9 %collective-permute-start.82 = (bf16[192,2048]{1,0:T(8,128)(2,1)}, bf16[192,2048]{1,0:T(8,128)(2,1)}, u32[]{:S(2)}, u32[]{:S(2)}) collective-permute-start(bf16[192,2048]{1,0:T(8,128)(2,1)} %fusion.34), channel_id=1, source_target_pairs={{0,1},{1,0},{2,3},{3,2},{4,5},{5,4},{6,7},{7,6},{8,9},{9,8},{10,11... | collective-permute-start | bytes 2359304 | tf_op jit(solution)/shard_map/ppermute | solution.py:572
  620.3 41.2 %collective-permute-start.81 = (bf16[192,2048]{1,0:T(8,128)(2,1)}, bf16[192,2048]{1,0:T(8,128)(2,1)}, u32[]{:S(2)}, u32[]{:S(2)}) collective-permute-start(bf16[192,2048]{1,0:T(8,128)(2,1)} %slice_bitcast_fusion.3), channel_id=1, source_target_pairs={{0,16},{16,0},{1,17},{17,1},{2,18},{18,2},{3,19},{19,3},{4,20},{20... | collective-permute-start | bytes 2359304 | tf_op jit(solution)/shard_map/ppermute | solution.py:572
  626.7 31.8 %collective-permute-start.85 = (bf16[128,2048]{1,0:T(8,128)(2,1)}, bf16[128,2048]{1,0:T(8,128)(2,1)}, u32[]{:S(2)}, u32[]{:S(2)}) collective-permute-start(bf16[128,2048]{1,0:T(8,128)(2,1)} %dynamic-slice_bitcast_fusion.1), channel_id=1, source_target_pairs={{0,4},{4,0},{1,5},{5,1},{2,6},{6,2},{3,7},{7,3},{8,12},{12,8},{9,1... | collective-permute-start | bytes 1572872 | tf_op jit(solution)/shard_map/ppermute | solution.py:572
  (122 other events, 1910.3 us)
Sparse Core Ops, SparseCore 0:
  10.5 30.7 all-gather.2
  42.9 62.0 all-gather.4

commit v3 on v2

--- a/solution.py
+++ b/solution.py
@@ -15,6 +15,7 @@
 BIG = 30000.0
 LANES = 128
 BLOCK = 256
+UNROLLED = 2048
 VMEM = 60 * 1024 * 1024
 COST = pl.CostEstimate(flops=1000, bytes_accessed=1000, transcendentals=0)
 
@@ -174,11 +175,45 @@
     q2_ref[...] = q2.reshape(heads, rows, LANES)
 
 
+def attend_unrolled_kernel(heads, rows, q_ref, k_ref, v_ref, low_ref, out_ref, q2_ref):
+    stretch = q_ref.shape[1]
+
+    def block(first, at):
+        q = q_ref[:, at:at + rows, :].reshape(heads * rows, LANES)
+        s = dot(q, k_ref[first:first + rows, :], NT)
+        t_local = lax.broadcasted_iota(jnp.int32, s.shape, 0) % rows
+        u_local = lax.broadcasted_iota(jnp.int32, s.shape, 1)
+        p = jnp.where(u_local <= t_local, jnp.exp(s), 0.0).astype(BF16)
+        total = dot(p, v_ref[first:first + rows, :])
+        if first:
+            p = jnp.exp(dot(q, k_ref[:first, :], NT)).astype(BF16)
+            total = total + dot(p, v_ref[:first, :])
+        weight = total[:, HEAD_SIZE:HEAD_SIZE + 1]
+        out = total[:, :HEAD_SIZE] / weight
+        for h in range(heads):
+            part = out[h * rows:(h + 1) * rows, :]
+            out_ref[at:at + rows, h * HEAD_SIZE:(h + 1) * HEAD_SIZE] = part
+            low_ref[at:at + rows, h * HEAD_SIZE:(h + 1) * HEAD_SIZE] = part.astype(BF16)
+        high, low = split_low(-jnp.log(weight))
+        lane = lax.broadcasted_iota(jnp.int32, q.shape, 1)
+        q2 = jnp.where(lane == HEAD_SIZE + 3, high, jnp.where(lane == HEAD_SIZE + 4, low, q))
+        q2_ref[:, at:at + rows, :] = q2.reshape(heads, rows, LANES)
+
+    for step in range(k_ref.shape[0] // stretch):
+        @pl.when(pl.program_id(0) == step)
+        def _(step=step):
+            for at in range(0, stretch, rows):
+                block(step * stretch + at, at)
+
+
 def attend(heads, q, k, v):
     tokens = k.shape[0]
-    rows = BLOCK
+    if tokens <= UNROLLED and tokens % (2 * BLOCK) == 0:
+        kernel, rows = functools.partial(attend_unrolled_kernel, heads, BLOCK // 2), 2 * BLOCK
+    else:
+        kernel, rows = functools.partial(attend_kernel, heads), BLOCK
     return pl.pallas_call(
-        functools.partial(attend_kernel, heads),
+        kernel,
         grid=(tokens // rows,),
         in_specs=[
             pl.BlockSpec((heads, rows, LANES), lambda i: (0, i, 0)),
@@ -201,12 +236,21 @@
     )(q, k, v)
 
 
-def attend_back_kernel(heads, q_ref, k_ref, v_ref, grad_ref, out_ref, unit_ref, scale_ref, head_gain_ref,
-                       cos_ref, sin_ref, dqkv_ref, gains_ref, g_scr, dq_scr, dk_scr, dv_scr):
+def attend_back_kernel(heads, q_ref, k_ref, v_ref, grad_ref, out_ref, unit_hbm, scale_hbm, head_gain_ref,
+                       cos_hbm, sin_hbm, dqkv_ref, gains_ref, g_scr, dq_scr, dk_scr, dv_scr,
+                       unit_ref, scale_ref, cos_ref, sin_ref, sems):
     rows = BLOCK
     tokens = k_ref.shape[0]
     blocks = tokens // rows
     wide = heads * rows
+    late = [
+        pltpu.make_async_copy(source, target, sems.at[n])
+        for n, (source, target) in enumerate(
+            ((unit_hbm, unit_ref), (scale_hbm, scale_ref), (cos_hbm, cos_ref), (sin_hbm, sin_ref))
+        )
+    ]
+    for copy in late:
+        copy.start()
 
     def prepare(i, carry):
         at = pl.ds(pl.multiple_of(i * rows, rows), rows)
@@ -223,36 +267,44 @@
 
     lax.fori_loop(0, blocks, prepare, 0)
 
+    def pair(j, i, diagonal):
+        at = pl.ds(i * rows, rows)
+        k = k_ref[pl.ds(j * rows, rows), :]
+        q = q_ref[:, at, :].reshape(wide, LANES)
+        g = g_scr[:, at, :].reshape(wide, LANES)
+        p = jnp.exp(dot(k, q, NT))
+        if diagonal:
+            u_local = lax.broadcasted_iota(jnp.int32, p.shape, 0)
+            t_local = lax.broadcasted_iota(jnp.int32, p.shape, 1) % rows
+            p = jnp.where(u_local <= t_local, p, 0.0)
+        dv = dot(p.astype(BF16), g)
+        ds = (p * dot(v_ref[pl.ds(j * rows, rows), :], g, NT)).astype(BF16)
+        dk = dot(ds, q)
+        dq_scr[:, at, :] += dot(ds, k, TN).reshape(heads, rows, LANES)
+        return dk, dv
+
     def key_step(j, carry):
-        start = pl.multiple_of(j * rows, rows)
-        k = k_ref[pl.ds(start, rows), :]
-        v = v_ref[pl.ds(start, rows), :]
-
-        def pair(i, diagonal):
-            at = pl.ds(pl.multiple_of(i * rows, rows), rows)
-            q = q_ref[:, at, :].reshape(wide, LANES)
-            g = g_scr[:, at, :].reshape(wide, LANES)
-            p = jnp.exp(dot(k, q, NT))
-            if diagonal:
-                u_local = lax.broadcasted_iota(jnp.int32, p.shape, 0)
-                t_local = lax.broadcasted_iota(jnp.int32, p.shape, 1) % rows
-                p = jnp.where(u_local <= t_local, p, 0.0)
-            dv = dot(p.astype(BF16), g)
-            ds = (p * dot(v, g, NT)).astype(BF16)
-            dk = dot(ds, q)
-            dq_scr[:, at, :] += dot(ds, k, TN).reshape(heads, rows, LANES)
-            return dk, dv
-
         def query_step(i, state):
-            dk, dv = pair(i, False)
+            dk, dv = pair(j, i, False)
             return state[0] + dk, state[1] + dv
 
-        dk, dv = lax.fori_loop(j + 1, blocks, query_step, pair(j, True))
-        dk_scr[pl.ds(start, rows), :] = dk
-        dv_scr[pl.ds(start, rows), :] = dv
+        state = pair(j, j, True)
+        if tokens <= UNROLLED:
+            for i in range(j + 1, blocks):
+                state = query_step(i, state)
+        else:
+            state = lax.fori_loop(j + 1, blocks, query_step, state)
+        dk_scr[pl.ds(j * rows, rows), :] = state[0]
+        dv_scr[pl.ds(j * rows, rows), :] = state[1]
         return carry
 
-    lax.fori_loop(0, blocks, key_step, 0)
+    if tokens <= UNROLLED:
+        for j in range(blocks):
+            key_step(j, 0)
+    else:
+        lax.fori_loop(0, blocks, key_step, 0)
+    for copy in late:
+        copy.wait()
     groups = unit_ref.shape[1] // LANES
     ones = head_ones()
 
@@ -291,8 +343,11 @@
 def attend_back(heads, q, k, v, grad, out, unit, scale, head_gain, cosine, sine):
     tokens = k.shape[0]
     cols = unit.shape[1]
+    vmem, late = pl.BlockSpec(memory_space=pltpu.VMEM), pl.BlockSpec(memory_space=pl.ANY)
     return pl.pallas_call(
         functools.partial(attend_back_kernel, heads),
+        in_specs=[vmem] * 5 + [late] * 2 + [vmem] + [late] * 2,
+        out_specs=[vmem] * 2,
         out_shape=[
             jax.ShapeDtypeStruct((tokens, cols), BF16),
             jax.ShapeDtypeStruct((8, cols), F32),
@@ -302,6 +357,11 @@
             pltpu.VMEM((heads, tokens, LANES), F32),
             pltpu.VMEM((tokens, LANES), F32),
             pltpu.VMEM((tokens, LANES), F32),
+            pltpu.VMEM((tokens, cols), F32),
+            pltpu.VMEM((tokens, cols), F32),
+            pltpu.VMEM((tokens, LANES), F32),
+            pltpu.VMEM((tokens, LANES), F32),
+            pltpu.SemaphoreType.DMA((4,)),
         ],
         compiler_params=pltpu.CompilerParams(vmem_limit_bytes=VMEM),
         cost_estimate=COST,
@@ -310,12 +370,16 @@
 
 
 def feed_kernel(layouts, weight_count, index_ref, *refs):
-    tiles = sum(layouts[0])
+    tiles = sum(layouts[0][1])
     sides = []
-    for layout in layouts:
-        others = refs[tiles:tiles + len(layout)]
-        sides.append((refs[:tiles], [(o, t) for o, count in zip(others, layout) for t in range(count)]))
-        refs = refs[tiles + len(layout):]
+    for pieces, layout in layouts:
+        own = []
+        for count in pieces:
+            own.append(refs[:count])
+            refs = refs[count:]
+        others = refs[:len(layout)]
+        sides.append((own, [(o, t) for o, count in zip(others, layout) for t in range(count)]))
+        refs = refs[len(layout):]
     gate_ref, up_ref, down_ref = refs[:3]
     da_ref, db_ref, ma_ref, mb_ref, hidden_ref, dgu_ref, x_scr, c_scr, gu_scr, down_scr, sem, w_sem = refs[3:]
     i = pl.program_id(0)
@@ -326,14 +390,16 @@
         found = []
         for (own, others), scratch, which in ((sides[0], x_scr, 0), (sides[1], c_scr, 1)):
             other, place = others[t]
-            found.append(
-                pltpu.make_async_copy(own[t], scratch.at[slot, pl.ds(0, half)], sem.at[slot, which, 0])
-            )
+            size = half // len(own[t])
+            for n, piece in enumerate(own[t]):
+                found.append(
+                    pltpu.make_async_copy(piece, scratch.at[slot, pl.ds(n * size, size)], sem.at[slot, which, n + 1])
+                )
             found.append(
                 pltpu.make_async_copy(
                     other.at[pl.ds(place * half, half)],
                     scratch.at[slot, pl.ds(half, half)],
-                    sem.at[slot, which, 1],
+                    sem.at[slot, which, 0],
                 )
             )
         return found
@@ -385,7 +451,12 @@
 def feed(x_stage, c_stage, index, weights, part):
     (x_own, x_others), (c_own, c_others) = x_stage, c_stage
     tiles = len(x_own)
-    half = x_own[0].shape[0]
+    half = x_own[0][0].shape[0] * len(x_own[0])
+    layouts = tuple(
+        (tuple(len(t) for t in own), tuple(o.shape[0] // half for o in others))
+        for own, others in ((x_own, x_others), (c_own, c_others))
+    )
+    arrays = [a for own, others in ((x_own, x_others), (c_own, c_others)) for a in sum(own, []) + list(others)]
     rows = 2 * half
     gate, up, down = weights
     width = gate.shape[0]
@@ -393,13 +464,11 @@
     mine = blocks * part
     halves = pl.BlockSpec((1, half, width), lambda i, n: (i, 0, 0))
     return pl.pallas_call(
-        functools.partial(
-            feed_kernel, tuple(tuple(o.shape[0] // half for o in others) for others in (x_others, c_others)), blocks
-        ),
+        functools.partial(feed_kernel, layouts, blocks),
         grid_spec=pltpu.PrefetchScalarGridSpec(
             num_scalar_prefetch=1,
             grid=(tiles,),
-            in_specs=[pl.BlockSpec(memory_space=pl.ANY)] * (2 * tiles + len(x_others) + len(c_others) + 3),
+            in_specs=[pl.BlockSpec(memory_space=pl.ANY)] * (len(arrays) + 3),
             out_specs=[halves] * 4
             + [
                 pl.BlockSpec((rows, mine), lambda i, n: (i, 0)),
@@ -410,7 +479,7 @@
                 pltpu.VMEM((2, rows, width), BF16),
                 pltpu.VMEM((width, 2 * mine), BF16),
                 pltpu.VMEM((mine, width), BF16),
-                pltpu.SemaphoreType.DMA((2, 2, 2)),
+                pltpu.SemaphoreType.DMA((2, 2, 3)),
                 pltpu.SemaphoreType.DMA((blocks, 3)),
             ],
         ),
@@ -422,32 +491,35 @@
         compiler_params=pltpu.CompilerParams(vmem_limit_bytes=VMEM),
         cost_estimate=COST,
         name="feed",
-    )(index, *x_own, *x_others, *c_own, *c_others, gate, up, down)
+    )(index, *arrays, gate, up, down)
 
 
 def stage_arrays(stages):
     arrays, layout = [], []
     for own, others in stages:
-        half = own[0].shape[0]
-        arrays += list(own) + list(others)
-        layout.append((half, len(own), tuple(o.shape[0] // half for o in others)))
+        half = own[0][0].shape[0] * len(own[0])
+        arrays += sum(own, []) + list(others)
+        layout.append((half, tuple(len(t) for t in own), tuple(o.shape[0] // half for o in others)))
     return arrays, tuple(layout)
 
 
 def stack_rows(refs, layout, scratch):
     at = row = 0
     for half, tiles, others in layout:
-        places = [(at + tiles + n, t) for n, count in enumerate(others) for t in range(count)]
-        for t, (other, place) in enumerate(places):
-            scratch[row:row + half, :] = refs[at + t][...]
+        places = [(at + sum(tiles) + n, t) for n, count in enumerate(others) for t in range(count)]
+        for pieces, (other, place) in zip(tiles, places):
+            size = half // pieces
+            for n in range(pieces):
+                scratch[row + n * size:row + (n + 1) * size, :] = refs[at + n][...]
+            at += pieces
             scratch[row + half:row + 2 * half, :] = refs[other][place * half:(place + 1) * half, :]
             row += 2 * half
-        at += tiles + len(others)
-
-
-def gate_grad_kernel(array_count, layout, far, index_ref, *refs):
+        at += len(others)
+
+
+def gate_grad_kernel(array_count, layout, *refs):
     arrays, refs = refs[:array_count], refs[array_count:]
-    rights, outs, scratch = refs[:len(layout)], refs[len(layout):-1], refs[-1]
+    rights, (gate_ref, up_ref, scratch) = refs[:len(layout)], refs[len(layout):]
     stack_rows(arrays, layout, scratch)
     row = 0
     total = None
@@ -458,40 +530,28 @@
         row += size
     total = total.astype(BF16)
     mine = total.shape[1] // 2
-    steps = pl.num_programs(0) // far
-    for k in range(far):
-        @pl.when(pl.program_id(0) // steps == far - 1 - k)
-        def _(k=k):
-            outs[k][...] = total[:, :mine]
-            outs[far + k][...] = total[:, mine:]
-
-
-def gate_grad(stages, rights, za, far):
+    gate_ref[...] = total[:, :mine]
+    up_ref[...] = total[:, mine:]
+
+
+def gate_grad(stages, rights):
     arrays, layout = stage_arrays(stages)
     width = arrays[0].shape[1]
     units = rights[0].shape[1]
     rows = sum(r.shape[0] for r in rights)
-    step = min(256, width // far)
-    steps = width // far // step
-    block = lambda i, n: (n[0] ^ (far - 1 - i // steps)) * steps + i % steps
-    out = lambda k: pl.BlockSpec(
-        (step, units // 2), lambda i, n: (jnp.clip(i - (far - 1 - k) * steps, 0, steps - 1), 0)
-    )
+    step = min(256, width)
     return pl.pallas_call(
-        functools.partial(gate_grad_kernel, len(arrays), layout, far),
-        grid_spec=pltpu.PrefetchScalarGridSpec(
-            num_scalar_prefetch=1,
-            grid=(width // step,),
-            in_specs=[pl.BlockSpec((p.shape[0], step), lambda i, n: (0, block(i, n))) for p in arrays]
-            + [pl.BlockSpec(r.shape, lambda i, n: (0, 0)) for r in rights],
-            out_specs=[out(k) for k in range(far)] * 2,
-            scratch_shapes=[pltpu.VMEM((rows, step), BF16)],
-        ),
-        out_shape=[jax.ShapeDtypeStruct((width // far, units // 2), BF16)] * (2 * far),
+        functools.partial(gate_grad_kernel, len(arrays), layout),
+        grid=(width // step,),
+        in_specs=[pl.BlockSpec((p.shape[0], step), lambda i: (0, i)) for p in arrays]
+        + [pl.BlockSpec(r.shape, lambda i: (0, 0)) for r in rights],
+        out_specs=[pl.BlockSpec((step, units // 2), lambda i: (i, 0))] * 2,
+        out_shape=[jax.ShapeDtypeStruct((width, units // 2), BF16)] * 2,
+        scratch_shapes=[pltpu.VMEM((rows, step), BF16)],
         compiler_params=pltpu.CompilerParams(vmem_limit_bytes=VMEM),
         cost_estimate=COST,
         name="gate_grad",
-    )(za.astype(jnp.int32).reshape(1), *arrays, *rights)
+    )(*arrays, *rights)
 
 
 def down_grad_kernel(array_count, layout, *refs):
@@ -597,7 +657,7 @@
     return jax.tree.unflatten(tree, lax.optimization_barrier(leaves))
 
 
-STAGES = (((),), ((X,), (Y,), (Z,)), ((X, Z), (X, Y), (Z, Y)))
+STAGES = (((),), ((X,), (Y,), (Z,)), ((X, Z), (X, Y), (Z, Y), (X, Z, Y)))
 
 
 def other_core(arrays):
@@ -667,7 +727,8 @@
     w_own = lax.all_gather(jnp.concatenate(own_cols, axis=1), fsdp, axis=0, tiled=True)
     out_full = lax.all_gather(out_weight, fsdp, axis=0, tiled=True)
     w_rows = jnp.concatenate(pieces, axis=2).reshape(-1, s_count * padded)
-    w_quarters = lambda n: w_rows[n * (w_rows.shape[0] // 4):(n + 1) * (w_rows.shape[0] // 4)]
+    w_quarter = w_rows.shape[0] // 4
+    w_parts = [w_rows[:w_quarter], w_rows[w_quarter:2 * w_quarter], w_rows[2 * w_quarter:]]
 
     far_list = [(k, swap(tokens, "za", k)) for k in range(1, far)]
     x_y, x_z, c_x = swap(tokens, Y), swap(tokens, Z), swap(cotangent, X)
@@ -682,7 +743,9 @@
     head_gain = jnp.concatenate(
         [query_gain] * heads + [key_gain] + [jnp.ones((padded - cols + HEAD_SIZE,), F32)]
     )[None, :]
-    far_list, x_y, x_z, c_x, w_rows, cos2, sin2 = sync([b for _, b in far_list], x_y, x_z, c_x, w_rows, cos2, sin2)
+    far_list, x_y, x_z, c_x, w_rows, w_parts, cos2, sin2 = sync(
+        [b for _, b in far_list], x_y, x_z, c_x, w_rows, w_parts, cos2, sin2
+    )
 
     def some_project(blocks, held):
         index = jnp.stack([((za ^ k) * 2 + (zb ^ dz)) * 2 + (si ^ dy) for (k, dz, dy), _ in blocks])
@@ -699,27 +762,30 @@
     far_yz = [swap(b, Y) for b in far_z]
     for n, k in enumerate(range(1, far)):
         held = some_project([((k, 0, 0), far_list[n]), ((k, 0, 1), far_y[n]), ((k, 1, 0), far_z[n])], held)
-    x_yz, far_yz, held, cot, w_rows = sync(x_yz, far_yz, held, cotangent, w_rows)
+    w_c = swap(w_rows, C)
+    c_own_other = other_core([cotangent])
+    x_yz, far_yz, held, w_c, c_own_other, cot, c_x, w_parts = sync(
+        x_yz, far_yz, held, w_c, c_own_other, cotangent, c_x, w_parts
+    )
     c_y, c_z = swap(cot, Y), swap(cot, Z)
-    w_x = [swap(w_quarters(0), X)]
-    w_c = swap(w_rows, C)
+    w_x = [swap(w_parts[0], X)]
+    mid = rows // 2
+    c_xy, c_xz = [swap(c_x[:mid], Y)], [swap(c_x[:mid], Z)]
     held = some_project([((0, 1, 1), x_yz)] + [((k, 1, 1), far_yz[n]) for n, k in enumerate(range(1, far))], held)
     normed, q, k, v, unit, scale = held
     attended_low, attended, q2 = attend(heads, q, k, v)
-    c_y, c_z, attended_low, c_x, w_c, w_x = sync(c_y, c_z, attended_low, c_x, w_c, w_x)
+    c_y, c_z, attended_low, c_x, c_xy, c_xz, w_x = sync(c_y, c_z, attended_low, c_x, c_xy, c_xz, w_x)
     heads_out = lax.all_to_all(attended_low, seq, split_axis=0, concat_axis=1, tiled=True)
-    c_xz = swap(c_z, X)
-    w_xc = [swap(w_x[0], C)]
+    c_xyz = [swap(c_xy[0], Z)]
+    c_xy.append(swap(c_y[mid:], X))
+    c_xz.append(swap(c_z[mid:], X))
+    c_yz = swap(c_z, Y)
     c_one = [c_x, c_y, c_z]
-    c_own_other, c_one_other = other_core([cot]), other_core(c_one)
-    heads_out, c_xz, c_own_other, c_one_other, w_xc = sync(heads_out, c_xz, c_own_other, c_one_other, w_xc)
-
-    c_two_other = other_core([c_xz])
-    own_rows = out_weight.shape[0]
-    left = []
-    for offset in range(f_count):
-        block = lax.dynamic_slice_in_dim(heads_out, (f_index ^ offset) * own_rows, own_rows, 1)
-        left.append(swap(block, fsdp, offset) if offset else block)
+    c_one_other = other_core(c_one)
+    c_xyz.append(swap(c_xz[1], Y))
+    heads_out, c_xz, c_xy, c_yz, c_xyz, c_one_other = sync(heads_out, c_xz, c_xy, c_yz, c_xyz, c_one_other)
+    c_two = [c_xz, c_xy, [c_yz], c_xyz]
+
     inputs = tokens.astype(F32)
     square_one = jnp.mean(inputs * inputs, axis=1, keepdims=True)
     scale_one = lax.rsqrt(square_one + EPSILON)
@@ -727,7 +793,7 @@
     square_two = jnp.mean(residual * residual, axis=1, keepdims=True)
     scale_two = lax.rsqrt(square_two + EPSILON)
     inner = (residual * scale_two * ffn_gain).astype(BF16)
-    inner, c_two_other, c_y, left = sync(inner, c_two_other, c_y, left)
+    (inner,) = sync(inner)
 
     units = gate_weight.shape[1]
     part = units // s_count
@@ -752,64 +818,56 @@
         width_of_part = mine
     run = lambda x_stage, c_stage: feed(x_stage, c_stage, unit_index, weights, width_of_part)
     x, y, z = swap(inner, X), swap(inner, Y), swap(inner, Z)
-    x_stages = [([inner], [other_core([inner])])]
-    c_stages = [([cot], [c_own_other])]
+    x_stages = [([[inner]], [other_core([inner])])]
+    c_stages = [([[cot]], [c_own_other])]
     fed = [run(x_stages[0], c_stages[0])]
-    x, y, z, fed = sync(x, y, z, fed)
+    x, y, z, fed, inner, c_two = sync(x, y, z, fed, inner, c_two)
     xy, xz, yz = swap(x, Y), swap(z, X), swap(y, Z)
-    c_xy, c_yz = swap(c_y, X), swap(c_y, Z)
-    x_stages.append(([x, y, z], [other_core([x, y, z])]))
-    c_stages.append((c_one, [c_one_other]))
+    xyz = swap_cube(inner, (X, Z, Y))
+    x_stages.append(([[x], [y], [z]], [other_core([x, y, z])]))
+    c_stages.append(([[c] for c in c_one], [c_one_other]))
+    c_two_other = other_core(sum(c_two, []))
     fed.append(run(x_stages[1], c_stages[1]))
-    xy, xz, yz, c_xy, c_yz, fed, x_stages = sync(xy, xz, yz, c_xy, c_yz, fed, x_stages)
-    xyz, c_xyz = swap(xz, Y), swap(c_yz, X)
-    x_stages.append(([xz, xy, yz], [other_core([xz, xy, yz])]))
-    c_stages.append(([c_xz, c_xy, c_yz], [c_two_other, other_core([c_xy, c_yz])]))
+    xy, xz, yz, xyz, fed, x_stages, w_parts, c_two, c_two_other = sync(
+        xy, xz, yz, xyz, fed, x_stages, w_parts, c_two, c_two_other
+    )
+    x_stages.append(([[xz], [xy], [yz], [xyz]], [other_core([xz, xy, yz, xyz])]))
+    c_stages.append((c_two, [c_two_other]))
     d_home = send_home(0, fed[0][0], swap(fed[0][1], C)) + send_home(1, fed[1][0], swap(fed[1][1], C))
+    w_x.append(swap(w_parts[1], X))
     fed.append(run(x_stages[2], c_stages[2]))
-    xyz, c_xyz, d_home, fed, x_stages, c_stages = sync(xyz, c_xyz, d_home, fed, x_stages, c_stages)
-    two = add_low(fed[2][0], swap(fed[2][1], C))
-    mid = rows // 2
-    home = [swap_cube(two[n, :mid], offset) for n, offset in enumerate(STAGES[2])]
-    x_stages.append(([xyz], [other_core([xyz])]))
-    c_stages.append(([c_xyz], [other_core([c_xyz])]))
-    fed.append(run(x_stages[3], c_stages[3]))
-    two, home, fed, x_stages, c_stages = sync(two, home, fed, x_stages, c_stages)
-    three = add_low(fed[3][0][0], swap(fed[3][1], C)[0])
-    last = [swap_cube(two[n, mid:], offset) for n, offset in enumerate(STAGES[2])]
-    d_home.append(swap_cube(three, (X, Z, Y)))
-    m_other = swap(fed[2][3], C)
-    gu = gate_grad(x_stages, [f[5] for f in fed], za, far)
-    down_part = down_grad([f[4] for f in fed], c_stages).reshape(far, part, width)
-    d_home, last, down_part, gu, fed, w_rows, m_other = sync(d_home, last, down_part, gu, fed, w_rows, m_other)
-    d_home += [jnp.concatenate([low, high], axis=0) for low, high in zip(home, last)]
+    d_home, fed, x_stages, w_x = sync(d_home, fed, x_stages, w_x)
+    far_xz, far_xy, far_yz, far_xyz = add_low(fed[2][0], swap(fed[2][1], C))
+    hops = [swap(far_xyz, Y), swap(far_xy, X), swap(far_yz, Z)]
+    down_part = down_grad([f[4] for f in fed], c_stages)
+    far_xz, hops, d_home, down_part, fed = sync(far_xz, hops, d_home, down_part, fed)
+    d_home += [swap_cube(add_low(far_xz, hops[0]), (X, Z)), swap(add_low(hops[1], hops[2]), Y)]
+    m_other = [swap(f[3], C) for f in fed[:2]]
+    gate_part, up_part = gate_grad(x_stages, [f[5] for f in fed])
+    d_home, down_part, gate_part, up_part, fed, m_other, heads_out = sync(
+        d_home, down_part, gate_part, up_part, fed, m_other, heads_out
+    )
+    gate_far = lax.psum_scatter(gate_part, "za", scatter_dimension=0, tiled=True)
+    up_far = lax.psum_scatter(up_part, "za", scatter_dimension=0, tiled=True)
+    down_far = lax.psum_scatter(down_part, "za", scatter_dimension=0, tiled=True)
     quarter = width // far // 4
 
     def owner_block(values, offset):
         return lax.dynamic_slice_in_dim(values, (own_block ^ offset) * quarter, quarter, 0)
 
-    def send_rows(parts, *offsets):
-        return [
-            swap(jnp.concatenate([owner_block(parts[k], o) for o in offsets], axis=0), "za", k) for k in range(1, far)
-        ]
-
-    def to_owners(gates, ups, gate_got, up_got):
+    def to_owners(gates, ups):
         spread = []
         for offset, axes in enumerate(((), (Y,), (Z,), (Z, Y))):
-            both = []
-            for parts, got in ((gates, gate_got), (ups, up_got)):
-                rows_here = owner_block(parts[0], offset).astype(F32)
-                for k in range(far - 1):
-                    pieces = [t for piece in got for t in jnp.split(piece[k], piece[k].shape[0] // quarter)]
-                    rows_here = rows_here + pieces[offset].astype(F32)
-                both.append(rows_here.astype(BF16))
-            both = jnp.concatenate(both, axis=0)
+            both = jnp.concatenate([owner_block(gates, offset), owner_block(ups, offset)], axis=0)
             spread.append(swap_cube(both, axes) if axes else both)
         return spread
 
-    gate_got = [send_rows(gu[:far], 0)]
-    w_x.append(swap(w_quarters(1), X))
-    m_other = [swap(fed[0][3], C), swap(fed[1][3], C), m_other, swap(fed[3][3], C)]
+    m_other.append(swap(fed[2][3], C))
+    own_rows = out_weight.shape[0]
+    left = []
+    for offset in range(f_count):
+        block = lax.dynamic_slice_in_dim(heads_out, (f_index ^ offset) * own_rows, own_rows, 1)
+        left.append(swap(block, fsdp, offset) if offset else block)
     d_inner = sum(a.astype(F32) for a in d_home)
     ffn_part = jnp.sum(d_inner * residual * scale_two, axis=0)
     weighted = d_inner * ffn_gain
@@ -818,20 +876,16 @@
     )
     d_branch = d_residual.astype(BF16)
     d_heads = dot(d_branch, out_full, NT).astype(BF16)
-    d_heads, d_branch, gate_got, gu, w_x, m_other, fed = sync(d_heads, d_branch, gate_got, gu, w_x, m_other, fed)
+    d_heads, d_branch, m_other, fed, left = sync(d_heads, d_branch, m_other, fed, left)
     d_attended = lax.all_to_all(d_heads, seq, split_axis=1, concat_axis=0, tiled=True)
-    gate_got.append(send_rows(gu[:far], 1))
     over = swap(d_branch, X)
     right = [d_branch, swap(d_branch, C), over, swap(over, C)]
-    m = [add_low(f[2], other) for f, other in zip(fed, m_other)]
-    d_attended, right, m, gate_got, gu, w_rows, fed = sync(d_attended, right, m, gate_got, gu, w_rows, fed)
-    mixed = [
-        jnp.concatenate([owner_block(gu[n + k], o) for n, o in ((0, 2), (0, 3), (far, 0), (far, 1))], axis=0)
-        for k in range(1, far)
-    ]
-    mixed = [swap(t, "za", k + 1) for k, t in enumerate(mixed)]
-    w_x.append(swap(w_rows[w_rows.shape[0] // 2:], X))
-    m_far = swap(m[3][0], Y)
+    m = [add_low(f[2], other) for f, other in zip(fed[:2], m_other)]
+    m.append([add_low(fed[2][2][n], m_other[2][n]) for n in range(4)])
+    m_far = swap(m[2][3], Y)
+    d_attended, right, m, m_far, w_parts, w_x = sync(d_attended, right, m, m_far, w_parts, w_x)
+    w_x.append(swap(w_parts[2], X))
+    w_xc = [swap(jnp.concatenate(w_x[:2], axis=0), C)]
     out_part = dot(jnp.concatenate(left, axis=0), jnp.concatenate(right, axis=0), TN).astype(BF16)
     out_part = out_part.reshape(far, 2, 2, -1, width)
     pick = lambda values, index, axis: lax.dynamic_index_in_dim(values, index, axis, keepdims=False)
@@ -839,26 +893,23 @@
     d_qkv, gain_parts = attend_back(
         heads, q2, k, v, sync(d_attended, out_part)[0], attended, unit, scale, head_gain, cos2, sin2
     )
-    d_qkv, gain_parts, gate_got, mixed, gu, m, m_far, w_x, out_part, out_y = sync(
-        d_qkv, gain_parts, gate_got, mixed, gu, m, m_far, w_x, out_part, out_y
-    )
-    gate_got.append([t[:2 * quarter] for t in mixed])
-    up_got = [[t[2 * quarter:] for t in mixed]]
+    d_qkv, gain_parts, m, m_far, w_x, w_xc, out_part, out_y = sync(
+        d_qkv, gain_parts, m, m_far, w_x, w_xc, out_part, out_y
+    )
     d_tok = lax.all_to_all(d_qkv, seq, split_axis=0, concat_axis=1, tiled=True)
     proj_part = dot(normed, d_qkv, TN).astype(BF16).reshape(2, 2, width // 4, padded)
     fi, fo = lax.axis_index(C), lax.axis_index(X)
     proj_core = add_low(pick(proj_part, fi, 1), swap(pick(proj_part, 1 - fi, 1), C))
     proj_x = swap(take(proj_core, 1 - fo), X)
-    w_xc.append(swap(jnp.concatenate(w_x[1:], axis=0), C))
-    m_x = swap(m[2][1], X)
+    w_xc.append(swap(w_x[2], C))
+    m_x, m_yz = swap(m[2][1], X), swap(m[2][2], Y)
     out_part = add_low(pick(out_part, si, 2), out_y)
     m_xz = add_low(m[2][0], m_far)
-    d_tok, up_got, gate_got, gu, proj_core, proj_x, w_xc, out_part, m, m_x, m_xz, gain_parts, down_part = sync(
-        d_tok, up_got, gate_got, gu, proj_core, proj_x, w_xc, out_part, m, m_x, m_xz, gain_parts, down_part
-    )
-    up_got.append(send_rows(gu[far:], 2, 3))
-    m_z = [swap(m_xz, X), swap(m[2][2], Y)]
-    out_z = swap(pick(out_part, 1 - zb, 1), Z)
+    d_tok, proj_core, proj_x, w_xc, out_part, m, m_x, m_yz, m_xz, gain_parts, gate_far, up_far = sync(
+        d_tok, proj_core, proj_x, w_xc, out_part, m, m_x, m_yz, m_xz, gain_parts, gate_far, up_far
+    )
+    m_z = [swap(m_xz, X), m_yz]
+    spread = to_owners(gate_far, up_far)
     blocks = [w_rows, w_c, jnp.concatenate(w_x, axis=0), jnp.concatenate(w_xc, axis=0)]
     by_offset = jnp.stack([dot(d_tok, w, NT) for w in blocks])
     d_normed = jnp.concatenate([take(by_offset, f_index ^ n) for n in range(f_count)], axis=1)
@@ -870,15 +921,13 @@
     ).astype(BF16)
     proj_rows = add_low(take(proj_core, fo), proj_x)
     m_one = [m[1][0], add_low(m[1][1], m_x)]
-    m_z, up_got, gate_got, input_grad, gu, proj_rows, m, m_one, out_z, out_part, gain_parts, down_part = sync(
-        m_z, up_got, gate_got, input_grad, gu, proj_rows, m, m_one, out_z, out_part, gain_parts, down_part
+    m_z, spread, input_grad, proj_rows, m, m_one, out_part, gain_parts = sync(
+        m_z, spread, input_grad, proj_rows, m, m_one, out_part, gain_parts
     )
     proj = lax.all_to_all(proj_rows, seq, split_axis=0, concat_axis=1, tiled=True)
-    down_half = part // 2
-    down_got = [send_far(down_part[:, :down_half], za)]
-    spread = to_owners(gu[:far], gu[far:], gate_got, up_got)
+    m_last = [swap(m_one[0], X), swap(m_one[1], Y)]
     m_one.append((m[1][2].astype(F32) + m_z[0].astype(F32) + m_z[1].astype(F32)).astype(BF16))
-    out_part = add_low(pick(out_part, zb, 1), out_z)
+    out_z = swap(pick(out_part, 1 - zb, 1), Z)
     gain_row = gain_parts[0]
     pack = jnp.concatenate(
         [
@@ -893,17 +942,14 @@
             pack = pack + swap(pack, axis, offset)
             offset *= 2
     pack = pack.reshape(-1)
-    proj, spread, m, m_one, out_part, down_part, down_got, pack = sync(
-        proj, spread, m, m_one, out_part, down_part, down_got, pack
-    )
+    gate_mine, up_mine = place(spread, own_block, part)
+    proj, gate_mine, up_mine, m, m_one, m_last, out_part, out_z, down_far, pack = sync(
+        proj, gate_mine, up_mine, m, m_one, m_last, out_part, out_z, down_far, pack
+    )
+    out_part = add_low(pick(out_part, zb, 1), out_z)
     out_got = send_far(out_part, za)
-    down_got.append(send_far(down_part[:, down_half:], za))
-    m_last = [swap(m_one[0], X), swap(m_one[1], Y), swap(m_one[2], Z)]
-    gate_up = place(spread, own_block, part)
-    gate_mine, up_mine = gate_up
-    down_mine = jnp.concatenate(
-        [add_far(down_part[:, :down_half], down_got[0], za), add_far(down_part[:, down_half:], down_got[1], za)], axis=0
-    )
+    m_last.append(swap(m_one[2], Z))
+    down_mine = down_far.astype(F32)
     mlp_out = m[0][0].astype(F32) + sum(a.astype(F32) for a in m_last)
     block_output = (residual + mlp_out).astype(BF16)
     out_mine = add_far(out_part, out_got, za)

time: 680 us -> 622 us (0.915)
  waiting for transfers between devices: 203 us -> 177 us
  Pallas kernels: 180 us -> 161 us
    ppermute x78 -> x73, waiting for transfers between devices: 162 us -> 107 us  [swap(): return lax.ppermute(values, axis, [(i, i ^ offset) for i in range(size)])]
    pallas_call x7 -> x6, Pallas kernels: 138 us -> 119 us  [the longest x3 61.5 us: feed(): pl.pallas_call(functools.partial(feed_kernel, layouts, blocks), grid_spec...]
    all_to_all x1, waiting for transfers between devices: 5.05 us -> 22 us  [per_device(): d_tok = lax.all_to_all(d_qkv, seq, split_axis=0, concat_axis=1, tiled=True)]
    ppermute x8 -> x3, waiting for transfers between devices: 14.9 us -> 29.7 us  [swap_cube(): return lax.ppermute(values, offset, pairs)]
    all_to_all x1, waiting for transfers between devices: 20.1 us -> 6.9 us  [per_device(): lax.all_to_all(attended_low, seq, split_axis=0, concat_axis=1, tiled=True)]
    reduce_scatter x0 -> x3, waiting for transfers between devices: none -> 7.67 us  [the longest x1 7.65 us: per_device(): up_far = lax.psum_scatter(up_part, 'za', scatter_dimension=0, tiled=True)]
    unnamed x162 -> x151, local copies, waits for them, and re-layouts: 19.2 us -> 25.7 us
    ppermute x78 -> x73, starting transfers between devices: 64.8 us -> 68.6 us  [swap(): return lax.ppermute(values, axis, [(i, i ^ offset) for i in range(size)])]
  transfers between devices with their start and end apart: 92 -> 85, of which waited for: 34 -> 34; matrix products, arithmetic and copies ran while one was open for 23% -> 23% of each run, Pallas kernels for 27% -> 26%
where the time goes in v3:
time: 622 us; the launch traced here: 614 us
  waiting for transfers between devices  177 us (28%)
  Pallas kernels  161 us (26%)
  starting transfers between devices  91.5 us (15%)
  other arithmetic  73.7 us (12%)
  local copies, waits for them, and re-layouts  58.5 us (9%)
  matrix products  36.4 us (6%)
  between operations  15.3 us (2%)
    ppermute x73, waiting for transfers between devices, swap(): return lax.ppermute(values, axis, [(i, i ^ offset) for i in range(size)])  107 us
    ppermute x73, starting transfers between devices, swap(): return lax.ppermute(values, axis, [(i, i ^ offset) for i in range(size)])  68.6 us
    pallas_call x3, Pallas kernels, feed(): pl.pallas_call(functools.partial(feed_kernel, layouts, blocks), grid_spec...  61.5 us
    dot_general x8, matrix products, dot(): return lax.dot_general(left, right, dims, preferred_element_type=F32)  36.4 us
    convert_element_type x13, other arithmetic, add_low(): return (left.astype(F32) + right.astype(F32)).astype(BF16)  31.8 us
    ppermute x3, waiting for transfers between devices, swap_cube(): return lax.ppermute(values, offset, pairs)  29.7 us
    pallas_call x1, Pallas kernels, attend_back(): pl.pallas_call(functools.partial(attend_back_kernel, heads), in_specs=[vm...  26.8 us
    unnamed x151, local copies, waits for them, and re-layouts  25.7 us
  transfers between devices with their start and end apart: 85, of which 34 were waited for; matrix products, arithmetic and copies ran while one was open for 23% of the time, Pallas kernels for 26%

profile of v3, /device:TPU:0, one launch (start us, length us, event | category | flops | bytes accessed | tf_op | source)
XLA Modules:
  0.0 613.5 jit_solution(1720551568865656235)
XLA Ops:
  11.2 4.1 collective-permute-start
  42.9 7.0 %collective-permute-done.refs_0_ = bf16[192,2048]{1,0:T(8,128)(2,1)} collective-permute-done((bf16[192,2048]{1,0:T(8,128)(2,1)S(1)}, bf16[192,2048]{1,0:T(8,128)(2,1)}, u32[]{:S(2)}, u32[]{:S(2)}) %collective-permute-start) | collective-permute-done | bytes 786464 | tf_op jit(solution)/shard_map/ppermute | solution.py:632
  54.4 8.3 %project.3 = (bf16[1536,2048]{1,0:T(8,128)(2,1)}, bf16[4,1536,128]{2,1,0:T(8,128)(2,1)}, bf16[1536,128]{1,0:T(8,128)(2,1)}, bf16[1536,128]{1,0:T(8,128)(2,1)}, f32[1536,384]{1,0:T(8,128)}, /*index=5*/f32[1536,384]{1,0:T(8,128)}) custom-call(s32[3]{0:T(128)} %get-tuple-element.644.index_ref, s32[2]{0:T(128)} %bitcast.183, bf16[192,2048]{1,0:T(8,128)(2,1)} %refs_0_.1, ...), custom_call_target="tpu_custom_call" | custom-call | flops 1000 | bytes 1000 | tf_op jit(solution)/shard_map/project/pallas_call | solution.py:123
  62.8 8.8 %collective-permute-done.4.refs_1_ = bf16[192,2048]{1,0:T(8,128)(2,1)} collective-permute-done((bf16[192,2048]{1,0:T(8,128)(2,1)}, bf16[192,2048]{1,0:T(8,128)(2,1)}, u32[]{:S(2)}, u32[]{:S(2)}) %collective-permute-start.4) | collective-permute-done | bytes 786464 | tf_op jit(solution)/shard_map/ppermute | solution.py:632
  74.4 8.0 %project.4 = (bf16[1536,2048]{1,0:T(8,128)(2,1)}, bf16[4,1536,128]{2,1,0:T(8,128)(2,1)}, bf16[1536,128]{1,0:T(8,128)(2,1)}, bf16[1536,128]{1,0:T(8,128)(2,1)}, f32[1536,384]{1,0:T(8,128)}, /*index=5*/f32[1536,384]{1,0:T(8,128)}) custom-call(s32[3]{0:T(128)} %get-tuple-element.645.index_ref, ...), custom_call_target="tpu_custom_call", output_to_operand_aliasing={{0}: (10, {}), {1}: (11, {}), {2}: (12, {}), {3}: (13, {}),... | custom-call | flops 1000 | bytes 1000 | tf_op jit(solution)/shard_map/project/pallas_call | solution.py:123
  82.5 9.3 %collective-permute-done.6.refs_0_ = bf16[192,2048]{1,0:T(8,128)(2,1)S(1)} collective-permute-done((bf16[192,2048]{1,0:T(8,128)(2,1)}, bf16[192,2048]{1,0:T(8,128)(2,1)S(1)}, u32[]{:S(2)}, u32[]{:S(2)}) %collective-permute-start.6) | collective-permute-done | bytes 786464 | tf_op jit(solution)/shard_map/ppermute | solution.py:632
  99.8 6.3 %project.5 = (bf16[1536,2048]{1,0:T(8,128)(2,1)}, bf16[4,1536,128]{2,1,0:T(8,128)(2,1)}, bf16[1536,128]{1,0:T(8,128)(2,1)}, bf16[1536,128]{1,0:T(8,128)(2,1)}, f32[1536,384]{1,0:T(8,128)}, /*index=5*/f32[1536,384]{1,0:T(8,128)}) custom-call(s32[2]{0:T(128)} %pad_add_fusion.2.index_ref, ...), custom_call_target="tpu_custom_call", output_to_operand_aliasing={{0}: (9, {}), {1}: (10, {}), {2}: (11, {}), {3}: (12, {}), ... | custom-call | flops 1000 | bytes 1000 | tf_op jit(solution)/shard_map/project/pallas_call | solution.py:123
  106.1 10.0 %attend.1 = (bf16[1536,256]{1,0:T(8,128)(2,1)}, f32[1536,256]{1,0:T(8,128)}, bf16[4,1536,128]{2,1,0:T(8,128)(2,1)}) custom-call(bf16[4,1536,128]{2,1,0:T(8,128)(2,1)} %get-tuple-element.345.q_ref, bf16[1536,128]{1,0:T(8,128)(2,1)} %get-tuple-element.346.k_ref, bf16[1536,128]{1,0:T(8,128)(2,1)} %get-tuple-element.347.v_ref), custom_call_target="tpu_custom_call" | custom-call | flops 1000 | bytes 1000 | tf_op jit(solution)/shard_map/attend/pallas_call | solution.py:215
  116.1 3.1 collective-permute-done.12.refs_7_.refs_8_
  122.2 4.3 all-to-all-start
  132.9 7.8 %collective-permute-done.15.refs_6_.refs_7_ = bf16[96,2048]{1,0:T(8,128)(2,1)S(1)} collective-permute-done((bf16[96,2048]{1,0:T(8,128)(2,1)S(1)}, bf16[96,2048]{1,0:T(8,128)(2,1)S(1)}, u32[]{:S(2)}, u32[]{:S(2)}) %collective-permute-start.15) | collective-permute-done | bytes 393248 | tf_op jit(solution)/shard_map/ppermute | solution.py:632
  140.7 6.9 %all-to-all-done = bf16[8,192,256]{2,1,0:T(8,128)(2,1)} async-done(((bf16[8,192,256]{2,1,0:T(8,128)(2,1)}), bf16[8,192,256]{2,1,0:T(8,128)(2,1)}, u32[]{:S(2)}, u32[]{:S(2)}) %all-to-all-start) | async-done | bytes 786464 | tf_op jit(solution)/shard_map/all_to_all | solution.py:778
  150.7 4.8 collective-permute-done.17.refs_9_.refs_10_
  155.5 7.8 %collective-permute-done.19.refs_11_.refs_12_ = bf16[96,2048]{1,0:T(8,128)(2,1)S(1)} collective-permute-done((bf16[96,2048]{1,0:T(8,128)(2,1)S(1)}, bf16[96,2048]{1,0:T(8,128)(2,1)S(1)}, u32[]{:S(2)}, u32[]{:S(2)}) %collective-permute-start.19) | collective-permute-done | bytes 393248 | tf_op jit(solution)/shard_map/ppermute | solution.py:632
  163.4 5.8 multiply_reduce_fusion.2
  175.9 11.1 %feed.3 = (bf16[1,192,2048]{2,1,0:T(8,128)(2,1)}, bf16[1,192,2048]{2,1,0:T(8,128)(2,1)}, bf16[1,192,2048]{2,1,0:T(8,128)(2,1)}, bf16[1,192,2048]{2,1,0:T(8,128)(...) custom-call(s32[2]{0:T(128)} %multiply_add_fusion.3.index_ref, ...), custom_call_target="tpu_custom_call" | custom-call | flops 1000 | bytes 1000 | tf_op jit(solution)/shard_map/feed/pallas_call | solution.py:466
  186.9 4.2 collective-permute-done.21.refs_0_.refs_2_
  206.9 22.3 %feed.4 = (bf16[3,192,2048]{2,1,0:T(8,128)(2,1)}, bf16[3,192,2048]{2,1,0:T(8,128)(2,1)}, bf16[3,192,2048]{2,1,0:T(8,128)(2,1)}, bf16[3,192,2048]{2,1,0:T(8,128)(...) custom-call(s32[2]{0:T(128)} %multiply_add_fusion.3.index_ref, ...), custom_call_target="tpu_custom_call" | custom-call | flops 1000 | bytes 1000 | tf_op jit(solution)/shard_map/feed/pallas_call | solution.py:466
  229.3 11.6 %collective-permute-done.28.refs_3_.refs_9_ = bf16[192,2048]{1,0:T(8,128)(2,1)} collective-permute-done((bf16[192,2048]{1,0:T(8,128)(2,1)}, bf16[192,2048]{1,0:T(8,128)(2,1)}, u32[]{:S(2)}, u32[]{:S(2)}) %collective-permute-start.28) | collective-permute-done | bytes 786464 | tf_op jit(solution)/shard_map/ppermute | solution.py:652
  253.1 28.1 %feed.5 = (bf16[4,192,2048]{2,1,0:T(8,128)(2,1)}, bf16[4,192,2048]{2,1,0:T(8,128)(2,1)}, bf16[4,192,2048]{2,1,0:T(8,128)(2,1)}, bf16[4,192,2048]{2,1,0:T(8,128)(...) custom-call(s32[2]{0:T(128)} %multiply_add_fusion.3.index_ref, ...), custom_call_target="tpu_custom_call" | custom-call | flops 1000 | bytes 1000 | tf_op jit(solution)/shard_map/feed/pallas_call | solution.py:466
  281.4 5.9 collective-permute-done.38
  287.3 3.2 add_convert_fusion
  295.0 13.8 %down_grad.1 = bf16[512,2048]{1,0:T(8,128)(2,1)} custom-call(bf16[192,2048]{1,0:T(8,128)(2,1)} %refs_0_.2, bf16[192,2048]{1,0:T(8,128)(2,1)} %copy-done.26, bf16[192,2048]{1,0:T(8,128)(2,1)} %copy-done.5, bf16[192,2048]{1,0:T(8,128)(2,1)} %copy-done.6, bf16[192,2048]{1,0:T(8,128)(2,1)} %copy-done.7, ...), custom_call_target="tpu_custom_call" | custom-call | flops 1000 | bytes 1000 | tf_op jit(solution)/shard_map/down_grad/pallas_call | solution.py:579
  308.8 3.2 collective-permute-done.39
  320.8 20.5 %gate_grad.1 = (bf16[2048,512]{1,0:T(8,128)(2,1)}, bf16[2048,512]{1,0:T(8,128)(2,1)}) custom-call(bf16[192,2048]{1,0:T(8,128)(2,1)} %multiply_convert_fusion.refs_0_, bf16[192,2048]{1,0:T(8,128)(2,1)} %copy-done.27, bf16[192,2048]{1,0:T(8,128)(2,1)} %collective-permute-done.21.refs_0_.refs_2_, bf16[192,2048]{1,0:T(8,128)(2,1)} %collective-permute-done.22.refs_1_.refs_3_, ...), custom_call_target="tpu_custom_call" | custom-call | flops 1000 | bytes 1000 | tf_op jit(solution)/shard_map/gate_grad/pallas_call | solution.py:543
  344.8 4.1 multiply_reduce_fusion
  350.3 7.4 %convolution_convert_fusion.1 = bf16[192,2048]{1,0:T(8,128)(2,1)} fusion(bf16[192,2048]{1,0:T(8,128)(2,1)} %fusion.64, bf16[2048,2048]{1,0:T(8,128)(2,1)} %all-gather.5.cloned.1.call-done), kind=kOutput, calls=%fused_computation.29 | convolution fusion | flops 1611005952 | bytes 9961472 | tf_op jit(solution)/shard_map/dot_general | solution.py:29
  362.6 4.6 all-to-all-start.1
  367.2 5.3 fusion.47
  374.5 5.2 collective-permute-done.51
  382.2 4.1 add_convert_fusion.1
  386.4 9.7 %collective-permute-done.53 = bf16[192,2048]{1,0:T(8,128)(2,1)} collective-permute-done((bf16[192,2048]{1,0:T(8,128)(2,1)S(1)}, bf16[192,2048]{1,0:T(8,128)(2,1)}, u32[]{:S(2)}, u32[]{:S(2)}) %collective-permute-start.53) | collective-permute-done | bytes 786464 | tf_op jit(solution)/shard_map/ppermute | solution.py:632
  403.2 3.7 fusion.18
  410.8 26.8 %attend_back.1 = (bf16[1536,384]{1,0:T(8,128)(2,1)}, f32[8,384]{1,0:T(8,128)}) custom-call(bf16[4,1536,128]{2,1,0:T(8,128)(2,1)} %get-tuple-element.358.q_ref, bf16[1536,128]{1,0:T(8,128)(2,1)} %get-tuple-element.346.k_ref, bf16[1536,128]{1,0:T(8,128)(2,1)} %get-tuple-element.347.v_ref, bf16[1536,256]{1,0:T(8,128)(2,1)} %bitcast.25.grad_ref, ...), custom_call_target="tpu_custom_call" | custom-call | flops 1000 | bytes 1000 | tf_op jit(solution)/shard_map/attend_back/pallas_call | solution.py:347
  437.6 4.3 all-to-all-start.2
  441.9 6.6 %convolution_convert_fusion = bf16[2048,384]{1,0:T(8,128)(2,1)S(1)} fusion(bf16[1536,2048]{1,0:T(8,128)(2,1)} %get-tuple-element.535, bf16[1536,384]{1,0:T(8,128)(2,1)} %get-tuple-element.534), kind=kOutput, calls=%fused_computation.24 | convolution fusion | flops 2416705536 | bytes 9043968 | tf_op jit(solution)/shard_map/dot_general | solution.py:29
  463.4 22.0 %all-to-all-done.2 = bf16[8,192,384]{2,1,0:T(8,128)(2,1)} async-done(((bf16[8,192,384]{2,1,0:T(8,128)(2,1)}), bf16[8,192,384]{2,1,0:T(8,128)(2,1)}, u32[]{:S(2)}, u32[]{:S(2)}) %all-to-all-start.2) | async-done | bytes 1179680 | tf_op jit(solution)/shard_map/all_to_all | solution.py:899
  487.9 7.6 %reduce-scatter.6.cloned.1.call-done = bf16[1024,512]{1,0:T(8,128)(2,1)} async-done(((bf16[2048,512]{1,0:T(8,128)(2,1)}), bf16[1024,512]{1,0:T(8,128)(2,1)}) %reduce-scatter.6.cloned.1.call-update) | async-done | bytes 1048592 | tf_op jit(solution)/shard_map/reduce_scatter | solution.py:851
  502.3 3.5 convolution_bitcast_fusion.1
  505.8 3.1 convolution_bitcast_fusion
  509.0 3.1 fusion.36
  512.1 3.1 fusion.39
  525.6 18.0 %collective-permute-done.65.refs_3_ = bf16[512,512]{1,0:T(8,128)(2,1)} collective-permute-done((bf16[512,512]{1,0:T(8,128)(2,1)S(1)}, bf16[512,512]{1,0:T(8,128)(2,1)}, u32[]{:S(2)}, u32[]{:S(2)}) %collective-permute-start.65) | collective-permute-done | bytes 524320 | tf_op jit(solution)/shard_map/ppermute | solution.py:652
  546.4 3.7 collective-permute-done.70
  551.4 4.3 all-to-all-start.3
  560.7 4.8 collective-permute-done.72
  571.3 5.5 place.1
  592.1 9.5 %collective-permute-done.75 = bf16[64,2048]{1,0:T(8,128)(2,1)} collective-permute-done((bf16[64,2048]{1,0:T(8,128)(2,1)}, bf16[64,2048]{1,0:T(8,128)(2,1)}, u32[]{:S(2)}, u32[]{:S(2)}) %collective-permute-start.75) | collective-permute-done | bytes 262176 | tf_op jit(solution)/shard_map/ppermute | solution.py:632
  (389 shorter events, 201.6 us)
Async XLA Ops:
  7.2 47.2 %all-gather.3.cloned.1.call-start = ((), (), s32[]{:S(2)}) async-start(), calls=%async_computation.7 | async-start | bytes 1966080 | tf_op jit(solution)/shard_map/all_gather | solution.py:727
  10.4 152.9 %all-gather.5.cloned.1.call-start = ((), (), s32[]{:S(2)}) async-start(), calls=%async_computation.8 | async-start | bytes 10485760 | tf_op jit(solution)/shard_map/all_gather | solution.py:728
  11.2 38.7 %collective-permute-start = (bf16[192,2048]{1,0:T(8,128)(2,1)S(1)}, bf16[192,2048]{1,0:T(8,128)(2,1)}, u32[]{:S(2)}, u32[]{:S(2)}) collective-permute-start(bf16[192,2048]{1,0:T(8,128)(2,1)S(1)} %copy-done.12), channel_id=1, source_target_pairs={{0,4},{4,0},{1,5},{5,1},{2,6},{6,2},{3,7},{7,3},{8,12},{12,8},{9,1... | collective-permute-start | bytes 2359304 | tf_op jit(solution)/shard_map/ppermute | solution.py:632
  15.3 34.6 %collective-permute-start.1 = (bf16[192,2048]{1,0:T(8,128)(2,1)S(1)}, bf16[192,2048]{1,0:T(8,128)(2,1)}, u32[]{:S(2)}, u32[]{:S(2)}) collective-permute-start(bf16[192,2048]{1,0:T(8,128)(2,1)S(1)} %copy-done.12), channel_id=1, source_target_pairs={{0,1},{1,0},{2,3},{3,2},{4,5},{5,4},{6,7},{7,6},{8,9},{9,8},{10,11... | collective-permute-start | bytes 2359304 | tf_op jit(solution)/shard_map/ppermute | solution.py:632
  16.8 34.5 %collective-permute-start.2 = (bf16[192,2048]{1,0:T(8,128)(2,1)S(1)}, bf16[192,2048]{1,0:T(8,128)(2,1)}, u32[]{:S(2)}, u32[]{:S(2)}) collective-permute-start(bf16[192,2048]{1,0:T(8,128)(2,1)S(1)} %copy-done.12), channel_id=1, source_target_pairs={{0,2},{2,0},{1,3},{3,1},{4,6},{6,4},{5,7},{7,5},{8,10},{10,8},{9,1... | collective-permute-start | bytes 2359304 | tf_op jit(solution)/shard_map/ppermute | solution.py:632
  18.4 32.9 %collective-permute-start.3 = (bf16[192,2048]{1,0:T(8,128)(2,1)S(1)}, bf16[192,2048]{1,0:T(8,128)(2,1)S(1)}, u32[]{:S(2)}, u32[]{:S(2)}) collective-permute-start(bf16[192,2048]{1,0:T(8,128)(2,1)S(1)} %copy-done.1), channel_id=1, source_target_pairs={{0,16},{16,0},{1,17},{17,1},{2,18},{18,2},{3,19},{19,3},{4,20},{20... | collective-permute-start | bytes 2359304 | tf_op jit(solution)/shard_map/ppermute | solution.py:632
  51.3 41.5 %collective-permute-start.8 = (bf16[512,3072]{1,0:T(8,128)(2,1)}, bf16[512,3072]{1,0:T(8,128)(2,1)}, u32[]{:S(2)}, u32[]{:S(2)}) collective-permute-start(bf16[512,3072]{1,0:T(8,128)(2,1)} %bitcast.84), channel_id=1, source_target_pairs={{0,8},{8,0},{1,9},{9,1},{2,10},{10,2},{3,11},{11,3},{4,12},{12,4},... | collective-permute-start | bytes 9437192 | tf_op jit(solution)/shard_map/ppermute | solution.py:632
  53.2 29.3 %collective-permute-start.9 = (bf16[192,2048]{1,0:T(8,128)(2,1)S(1)}, bf16[192,2048]{1,0:T(8,128)(2,1)S(1)}, u32[]{:S(2)}, u32[]{:S(2)}) collective-permute-start(bf16[192,2048]{1,0:T(8,128)(2,1)S(1)} %copy-done.1), channel_id=1, source_target_pairs={{0,8},{8,0},{1,9},{9,1},{2,10},{10,2},{3,11},{11,3},{4,12},{12,4},... | collective-permute-start | bytes 2359304 | tf_op jit(solution)/shard_map/ppermute | solution.py:632
  92.8 27.6 %collective-permute-start.10 = (bf16[192,2048]{1,0:T(8,128)(2,1)S(1)}, bf16[192,2048]{1,0:T(8,128)(2,1)S(1)}, u32[]{:S(2)}, u32[]{:S(2)}) collective-permute-start(bf16[192,2048]{1,0:T(8,128)(2,1)S(1)} %copy-done.1), channel_id=1, source_target_pairs={{0,1},{1,0},{2,3},{3,2},{4,5},{5,4},{6,7},{7,6},{8,9},{9,8},{10,11... | collective-permute-start | bytes 2359304 | tf_op jit(solution)/shard_map/ppermute | solution.py:632
  94.1 26.3 %collective-permute-start.11 = (bf16[192,2048]{1,0:T(8,128)(2,1)S(1)}, bf16[192,2048]{1,0:T(8,128)(2,1)S(1)}, u32[]{:S(2)}, u32[]{:S(2)}) collective-permute-start(bf16[192,2048]{1,0:T(8,128)(2,1)S(1)} %copy-done.1), channel_id=1, source_target_pairs={{0,2},{2,0},{1,3},{3,1},{4,6},{6,4},{5,7},{7,5},{8,10},{10,8},{9,1... | collective-permute-start | bytes 2359304 | tf_op jit(solution)/shard_map/ppermute | solution.py:632
  95.1 25.3 %collective-permute-start.14 = (bf16[128,3072]{1,0:T(8,128)(2,1)}, bf16[128,3072]{1,0:T(8,128)(2,1)}, u32[]{:S(2)}, u32[]{:S(2)}) collective-permute-start(bf16[128,3072]{1,0:T(8,128)(2,1)} %bitcast.176), channel_id=1, source_target_pairs={{0,16},{16,0},{1,17},{17,1},{2,18},{18,2},{3,19},{19,3},{4,20},{20... | collective-permute-start | bytes 2359304 | tf_op jit(solution)/shard_map/ppermute | solution.py:632
  98.1 22.3 %collective-permute-start.13 = (bf16[96,2048]{1,0:T(8,128)(2,1)}, bf16[96,2048]{1,0:T(8,128)(2,1)}, u32[]{:S(2)}, u32[]{:S(2)}) collective-permute-start(bf16[96,2048]{1,0:T(8,128)(2,1)} %slice.112), channel_id=1, source_target_pairs={{0,2},{2,0},{1,3},{3,1},{4,6},{6,4},{5,7},{7,5},{8,10},{10,8},{9,1... | collective-permute-start | bytes 1179656 | tf_op jit(solution)/shard_map/ppermute | solution.py:632
  122.2 41.1 %collective-permute-start.20 = (bf16[576,2048]{1,0:T(8,128)(2,1)}, bf16[576,2048]{1,0:T(8,128)(2,1)}, u32[]{:S(2)}, u32[]{:S(2)}) collective-permute-start(bf16[576,2048]{1,0:T(8,128)(2,1)} %pad_maximum_fusion.2), channel_id=1, source_target_pairs={{0,8},{8,0},{1,9},{9,1},{2,10},{10,2},{3,11},{11,3},{4,12},{12,4},... | collective-permute-start | bytes 7077896 | tf_op jit(solution)/shard_map/ppermute | solution.py:632
  122.2 25.4 %all-to-all-start = ((bf16[8,192,256]{2,1,0:T(8,128)(2,1)}), bf16[8,192,256]{2,1,0:T(8,128)(2,1)}, u32[]{:S(2)}, u32[]{:S(2)}) async-start(bf16[8,192,256]{2,1,0:T(8,128)(2,1)} %bitcast.14), calls=%async_computation | async-start | bytes 1572864 | tf_op jit(solution)/shard_map/all_to_all | solution.py:778
  126.5 361.4 %reduce-scatter.4.cloned.1.call-start = ((), (), s32[]{:S(2)}) async-start(), calls=%async_computation.9 | async-start | bytes 3145728 | tf_op jit(solution)/shard_map/reduce_scatter | solution.py:850
  126.6 28.9 %collective-permute-start.17 = (bf16[192,2048]{1,0:T(8,128)(2,1)S(1)}, bf16[192,2048]{1,0:T(8,128)(2,1)S(1)}, u32[]{:S(2)}, u32[]{:S(2)}) collective-permute-start(bf16[192,2048]{1,0:T(8,128)(2,1)S(1)} %collective-permute-done.11.refs_6_.refs_4_), channel_id=1, source_target_pairs={{0,1},{1,0},{2,3},{3,2},{4,5},{5,4},{6,7},{7,6},{8,9},{9,8},{10,11... | collective-permute-start | bytes 2359304 | tf_op jit(solution)/shard_map/ppermute | solution.py:632
  140.7 22.6 %collective-permute-start.19 = (bf16[96,2048]{1,0:T(8,128)(2,1)S(1)}, bf16[96,2048]{1,0:T(8,128)(2,1)S(1)}, u32[]{:S(2)}, u32[]{:S(2)}) collective-permute-start(bf16[96,2048]{1,0:T(8,128)(2,1)S(1)} %collective-permute-done.15.refs_6_.refs_7_), channel_id=1, source_target_pairs={{0,1},{1,0},{2,3},{3,2},{4,5},{5,4},{6,7},{7,6},{8,9},{9,8},{10,11... | collective-permute-start | bytes 1179656 | tf_op jit(solution)/shard_map/ppermute | solution.py:632
  201.5 39.5 %collective-permute-start.30 = (bf16[768,2048]{1,0:T(8,128)(2,1)}, bf16[768,2048]{1,0:T(8,128)(2,1)}, u32[]{:S(2)}, u32[]{:S(2)}) collective-permute-start(bf16[768,2048]{1,0:T(8,128)(2,1)} %constant_dynamic-update-slice_fusion), channel_id=1, source_target_pairs={{0,8},{8,0},{1,9},{9,1},{2,10},{10,2},{3,11},{11,3},{4,12},{12,4},... | collective-permute-start | bytes 9437192 | tf_op jit(solution)/shard_map/ppermute | solution.py:632
  201.9 27.4 %collective-permute-start.25 = (bf16[192,2048]{1,0:T(8,128)(2,1)}, bf16[192,2048]{1,0:T(8,128)(2,1)}, u32[]{:S(2)}, u32[]{:S(2)}) collective-permute-start(bf16[192,2048]{1,0:T(8,128)(2,1)} %collective-permute-done.21.refs_0_.refs_2_), channel_id=1, source_target_pairs={{0,1},{1,0},{2,3},{3,2},{4,5},{5,4},{6,7},{7,6},{8,9},{9,8},{10,11... | collective-permute-start | bytes 2359304 | tf_op jit(solution)/shard_map/ppermute | solution.py:632
  203.5 25.8 %collective-permute-start.26 = (bf16[192,2048]{1,0:T(8,128)(2,1)}, bf16[192,2048]{1,0:T(8,128)(2,1)}, u32[]{:S(2)}, u32[]{:S(2)}) collective-permute-start(bf16[192,2048]{1,0:T(8,128)(2,1)} %collective-permute-done.23.refs_2_.refs_4_), channel_id=1, source_target_pairs={{0,16},{16,0},{1,17},{17,1},{2,18},{18,2},{3,19},{19,3},{4,20},{20... | collective-permute-start | bytes 2359304 | tf_op jit(solution)/shard_map/ppermute | solution.py:632
  204.0 25.3 %collective-permute-start.27 = (bf16[192,2048]{1,0:T(8,128)(2,1)}, bf16[192,2048]{1,0:T(8,128)(2,1)}, u32[]{:S(2)}, u32[]{:S(2)}) collective-permute-start(bf16[192,2048]{1,0:T(8,128)(2,1)} %collective-permute-done.22.refs_1_.refs_3_), channel_id=1, source_target_pairs={{0,2},{2,0},{1,3},{3,1},{4,6},{6,4},{5,7},{7,5},{8,10},{10,8},{9,1... | collective-permute-start | bytes 2359304 | tf_op jit(solution)/shard_map/ppermute | solution.py:632
  205.5 35.5 %collective-permute-start.28 = (bf16[192,2048]{1,0:T(8,128)(2,1)}, bf16[192,2048]{1,0:T(8,128)(2,1)}, u32[]{:S(2)}, u32[]{:S(2)}) collective-permute-start(bf16[192,2048]{1,0:T(8,128)(2,1)} %multiply_convert_fusion.refs_0_), channel_id=1, source_target_pairs={{0,19},{1,18},{2,17},{3,16},{16,3},{17,2},{18,1},{19,0},{4,23},{5,... | collective-permute-start | bytes 2359304 | tf_op jit(solution)/shard_map/ppermute | solution.py:652
  243.8 37.5 %collective-permute-start.37 = (bf16[128,3072]{1,0:T(8,128)(2,1)}, bf16[128,3072]{1,0:T(8,128)(2,1)}, u32[]{:S(2)}, u32[]{:S(2)}) collective-permute-start(bf16[128,3072]{1,0:T(8,128)(2,1)} %bitcast.88), channel_id=1, source_target_pairs={{0,16},{16,0},{1,17},{17,1},{2,18},{18,2},{3,19},{19,3},{4,20},{20... | collective-permute-start | bytes 2359304 | tf_op jit(solution)/shard_map/ppermute | solution.py:632
  248.4 32.9 %collective-permute-start.33 = (bf16[192,2048]{1,0:T(8,128)(2,1)}, bf16[192,2048]{1,0:T(8,128)(2,1)S(1)}, u32[]{:S(2)}, u32[]{:S(2)}) collective-permute-start(bf16[192,2048]{1,0:T(8,128)(2,1)} %get-tuple-element.611), channel_id=1, source_target_pairs={{0,16},{16,0},{1,17},{17,1},{2,18},{18,2},{3,19},{19,3},{4,20},{20... | collective-permute-start | bytes 2359304 | tf_op jit(solution)/shard_map/ppermute | solution.py:632
  248.9 32.5 %collective-permute-start.34 = (bf16[192,2048]{1,0:T(8,128)(2,1)}, bf16[192,2048]{1,0:T(8,128)(2,1)S(1)}, u32[]{:S(2)}, u32[]{:S(2)}) collective-permute-start(bf16[192,2048]{1,0:T(8,128)(2,1)} %get-tuple-element.610), channel_id=1, source_target_pairs={{0,1},{1,0},{2,3},{3,2},{4,5},{5,4},{6,7},{7,6},{8,9},{9,8},{10,11... | collective-permute-start | bytes 2359304 | tf_op jit(solution)/shard_map/ppermute | solution.py:632
  250.5 30.8 %collective-permute-start.35 = (bf16[192,2048]{1,0:T(8,128)(2,1)}, bf16[192,2048]{1,0:T(8,128)(2,1)S(1)}, u32[]{:S(2)}, u32[]{:S(2)}) collective-permute-start(bf16[192,2048]{1,0:T(8,128)(2,1)} %get-tuple-element.609), channel_id=1, source_target_pairs={{0,2},{2,0},{1,3},{3,1},{4,6},{6,4},{5,7},{7,5},{8,10},{10,8},{9,1... | collective-permute-start | bytes 2359304 | tf_op jit(solution)/shard_map/ppermute | solution.py:632
  313.5 27.9 %collective-permute-start.45 = (bf16[3,192,2048]{2,1,0:T(8,128)(2,1)}, bf16[3,192,2048]{2,1,0:T(8,128)(2,1)}, u32[]{:S(2)}, u32[]{:S(2)}) collective-permute-start(bf16[3,192,2048]{2,1,0:T(8,128)(2,1)} %get-tuple-element.483), channel_id=1, source_target_pairs={{0,8},{8,0},{1,9},{9,1},{2,10},{10,2},{3,11},{11,3},{4,12},{12,4},... | collective-permute-start | bytes 7077896 | tf_op jit(solution)/shard_map/ppermute | solution.py:632
  315.8 25.5 %collective-permute-start.42 = (bf16[192,2048]{1,0:T(8,128)(2,1)}, bf16[192,2048]{1,0:T(8,128)(2,1)S(1)}, u32[]{:S(2)}, u32[]{:S(2)}) collective-permute-start(bf16[192,2048]{1,0:T(8,128)(2,1)} %add_convert_fusion.10), channel_id=1, source_target_pairs={{0,18},{2,16},{16,2},{18,0},{1,19},{3,17},{17,3},{19,1},{4,22},{6,... | collective-permute-start | bytes 2359304 | tf_op jit(solution)/shard_map/ppermute | solution.py:652
  341.4 154.2 %reduce-scatter.6.cloned.1.call-start = ((), (), s32[]{:S(2)}) async-start(), calls=%async_computation.10 | async-start | bytes 3145728 | tf_op jit(solution)/shard_map/reduce_scatter | solution.py:851
  360.0 26.4 %collective-permute-start.50 = (bf16[192,2048]{1,0:T(8,128)(2,1)}, bf16[192,2048]{1,0:T(8,128)(2,1)}, u32[]{:S(2)}, u32[]{:S(2)}) collective-permute-start(bf16[192,2048]{1,0:T(8,128)(2,1)} %fusion.64), channel_id=1, source_target_pairs={{0,8},{8,0},{1,9},{9,1},{2,10},{10,2},{3,11},{11,3},{4,12},{12,4},... | collective-permute-start | bytes 2359304 | tf_op jit(solution)/shard_map/ppermute | solution.py:632
  362.6 36.4 %all-to-all-start.1 = ((bf16[192,8,256]{2,0,1:T(8,128)(2,1)}), bf16[192,8,256]{2,0,1:T(8,128)(2,1)}, u32[]{:S(2)}, u32[]{:S(2)}) async-start(bf16[192,8,256]{2,0,1:T(8,128)(2,1)} %bitcast.162), calls=%async_computation.1 | async-start | bytes 1572864 | tf_op jit(solution)/shard_map/all_to_all | solution.py:880
  372.5 23.6 %collective-permute-start.53 = (bf16[192,2048]{1,0:T(8,128)(2,1)S(1)}, bf16[192,2048]{1,0:T(8,128)(2,1)}, u32[]{:S(2)}, u32[]{:S(2)}) collective-permute-start(bf16[192,2048]{1,0:T(8,128)(2,1)S(1)} %get-tuple-element.599), channel_id=1, source_target_pairs={{0,1},{1,0},{2,3},{3,2},{4,5},{5,4},{6,7},{7,6},{8,9},{9,8},{10,11... | collective-permute-start | bytes 2359304 | tf_op jit(solution)/shard_map/ppermute | solution.py:632
  399.0 38.6 %collective-permute-start.54 = (bf16[256,3072]{1,0:T(8,128)(2,1)}, bf16[256,3072]{1,0:T(8,128)(2,1)}, u32[]{:S(2)}, u32[]{:S(2)}) collective-permute-start(bf16[256,3072]{1,0:T(8,128)(2,1)} %bitcast.171), channel_id=1, source_target_pairs={{0,16},{16,0},{1,17},{17,1},{2,18},{18,2},{3,19},{19,3},{4,20},{20... | collective-permute-start | bytes 4718600 | tf_op jit(solution)/shard_map/ppermute | solution.py:632
  403.2 34.4 %collective-permute-start.55 = (bf16[256,3072]{1,0:T(8,128)(2,1)}, bf16[256,3072]{1,0:T(8,128)(2,1)}, u32[]{:S(2)}, u32[]{:S(2)}) collective-permute-start(bf16[256,3072]{1,0:T(8,128)(2,1)} %pad_maximum_fusion.4), channel_id=1, source_target_pairs={{0,8},{8,0},{1,9},{9,1},{2,10},{10,2},{3,11},{11,3},{4,12},{12,4},... | collective-permute-start | bytes 4718600 | tf_op jit(solution)/shard_map/ppermute | solution.py:632
  409.3 28.2 %collective-permute-start.56 = (bf16[2,2,64,2048]{3,2,0,1:T(8,128)(2,1)}, bf16[2,2,64,2048]{3,2,0,1:T(8,128)(2,1)}, u32[]{:S(2)}, u32[]{:S(2)}) collective-permute-start(bf16[2,2,64,2048]{3,2,0,1:T(8,128)(2,1)} %copy_bitcast_fusion), channel_id=1, source_target_pairs={{0,1},{1,0},{2,3},{3,2},{4,5},{5,4},{6,7},{7,6},{8,9},{9,8},{10,11... | collective-permute-start | bytes 3145736 | tf_op jit(solution)/shard_map/ppermute | solution.py:632
  437.6 47.9 %all-to-all-start.2 = ((bf16[8,192,384]{2,1,0:T(8,128)(2,1)}), bf16[8,192,384]{2,1,0:T(8,128)(2,1)}, u32[]{:S(2)}, u32[]{:S(2)}) async-start(bf16[8,192,384]{2,1,0:T(8,128)(2,1)} %bitcast.175), calls=%async_computation.2 | async-start | bytes 2359296 | tf_op jit(solution)/shard_map/all_to_all | solution.py:899
  441.8 135.0 %reduce-scatter.8.cloned.1.call-start = ((), (), s32[]{:S(2)}) async-start(), calls=%async_computation.11 | async-start | bytes 3145728 | tf_op jit(solution)/shard_map/reduce_scatter | solution.py:852
  450.8 44.8 %collective-permute-start.59 = (bf16[256,3072]{1,0:T(8,128)(2,1)}, bf16[256,3072]{1,0:T(8,128)(2,1)}, u32[]{:S(2)}, u32[]{:S(2)}) collective-permute-start(bf16[256,3072]{1,0:T(8,128)(2,1)} %collective-permute-done.54), channel_id=1, source_target_pairs={{0,8},{8,0},{1,9},{9,1},{2,10},{10,2},{3,11},{11,3},{4,12},{12,4},... | collective-permute-start | bytes 4718600 | tf_op jit(solution)/shard_map/ppermute | solution.py:632
  451.1 44.5 %collective-permute-start.60 = (bf16[192,2048]{1,0:T(8,128)(2,1)}, bf16[192,2048]{1,0:T(8,128)(2,1)}, u32[]{:S(2)}, u32[]{:S(2)}) collective-permute-start(bf16[192,2048]{1,0:T(8,128)(2,1)} %get-tuple-element.543), channel_id=1, source_target_pairs={{0,16},{16,0},{1,17},{17,1},{2,18},{18,2},{3,19},{19,3},{4,20},{20... | collective-permute-start | bytes 2359304 | tf_op jit(solution)/shard_map/ppermute | solution.py:632
  451.7 43.8 %collective-permute-start.61 = (bf16[192,2048]{1,0:T(8,128)(2,1)}, bf16[192,2048]{1,0:T(8,128)(2,1)}, u32[]{:S(2)}, u32[]{:S(2)}) collective-permute-start(bf16[192,2048]{1,0:T(8,128)(2,1)} %get-tuple-element.544), channel_id=1, source_target_pairs={{0,1},{1,0},{2,3},{3,2},{4,5},{5,4},{6,7},{7,6},{8,9},{9,8},{10,11... | collective-permute-start | bytes 2359304 | tf_op jit(solution)/shard_map/ppermute | solution.py:632
  459.7 35.9 %collective-permute-start.58 = (bf16[512,384]{1,0:T(8,128)(2,1)}, bf16[512,384]{1,0:T(8,128)(2,1)S(1)}, u32[]{:S(2)}, u32[]{:S(2)}) collective-permute-start(bf16[512,384]{1,0:T(8,128)(2,1)} %dynamic-slice_bitcast_fusion.6), channel_id=1, source_target_pairs={{0,16},{16,0},{1,17},{17,1},{2,18},{18,2},{3,19},{19,3},{4,20},{20... | collective-permute-start | bytes 1179656 | tf_op jit(solution)/shard_map/ppermute | solution.py:632
  495.6 48.0 %collective-permute-start.62 = (bf16[192,2048]{1,0:T(8,128)(2,1)}, bf16[192,2048]{1,0:T(8,128)(2,1)}, u32[]{:S(2)}, u32[]{:S(2)}) collective-permute-start(bf16[192,2048]{1,0:T(8,128)(2,1)} %add_convert_fusion.3), channel_id=1, source_target_pairs={{0,16},{16,0},{1,17},{17,1},{2,18},{18,2},{3,19},{19,3},{4,20},{20... | collective-permute-start | bytes 2359304 | tf_op jit(solution)/shard_map/ppermute | solution.py:632
  498.5 25.9 %collective-permute-start.63 = (bf16[512,512]{1,0:T(8,128)(2,1)S(1)}, bf16[512,512]{1,0:T(8,128)(2,1)}, u32[]{:S(2)}, u32[]{:S(2)}) collective-permute-start(bf16[512,512]{1,0:T(8,128)(2,1)S(1)} %pad_maximum_fusion.9), channel_id=1, source_target_pairs={{0,1},{1,0},{2,3},{3,2},{4,5},{5,4},{6,7},{7,6},{8,9},{9,8},{10,11... | collective-permute-start | bytes 1572872 | tf_op jit(solution)/shard_map/ppermute | solution.py:632
  500.1 25.4 %collective-permute-start.64 = (bf16[512,512]{1,0:T(8,128)(2,1)S(1)}, bf16[512,512]{1,0:T(8,128)(2,1)}, u32[]{:S(2)}, u32[]{:S(2)}) collective-permute-start(bf16[512,512]{1,0:T(8,128)(2,1)S(1)} %pad_maximum_fusion.10), channel_id=1, source_target_pairs={{0,2},{2,0},{1,3},{3,1},{4,6},{6,4},{5,7},{7,5},{8,10},{10,8},{9,1... | collective-permute-start | bytes 1572872 | tf_op jit(solution)/shard_map/ppermute | solution.py:632
  500.2 43.3 %collective-permute-start.65 = (bf16[512,512]{1,0:T(8,128)(2,1)S(1)}, bf16[512,512]{1,0:T(8,128)(2,1)}, u32[]{:S(2)}, u32[]{:S(2)}) collective-permute-start(bf16[512,512]{1,0:T(8,128)(2,1)S(1)} %pad_maximum_fusion.11), channel_id=1, source_target_pairs={{0,3},{1,2},{2,1},{3,0},{4,7},{5,6},{6,5},{7,4},{8,11},{9,10},{10,... | collective-permute-start | bytes 1572872 | tf_op jit(solution)/shard_map/ppermute | solution.py:652
  551.4 25.4 %all-to-all-start.3 = ((bf16[8,64,384]{2,1,0:T(8,128)(2,1)}), bf16[8,64,384]{2,1,0:T(8,128)(2,1)S(1)}, u32[]{:S(2)}, u32[]{:S(2)}) async-start(bf16[8,64,384]{2,1,0:T(8,128)(2,1)} %bitcast.50), calls=%async_computation.5 | async-start | bytes 786432 | tf_op jit(solution)/shard_map/all_to_all | solution.py:927
  555.8 22.3 %collective-permute-start.67 = (bf16[192,2048]{1,0:T(8,128)(2,1)}, bf16[192,2048]{1,0:T(8,128)(2,1)}, u32[]{:S(2)}, u32[]{:S(2)}) collective-permute-start(bf16[192,2048]{1,0:T(8,128)(2,1)} %fusion.34), channel_id=1, source_target_pairs={{0,1},{1,0},{2,3},{3,2},{4,5},{5,4},{6,7},{7,6},{8,9},{9,8},{10,11... | collective-permute-start | bytes 2359304 | tf_op jit(solution)/shard_map/ppermute | solution.py:632
  578.1 25.4 %collective-permute-start.74 = (bf16[192,2048]{1,0:T(8,128)(2,1)}, bf16[192,2048]{1,0:T(8,128)(2,1)}, u32[]{:S(2)}, u32[]{:S(2)}) collective-permute-start(bf16[192,2048]{1,0:T(8,128)(2,1)} %fusion.33), channel_id=1, source_target_pairs={{0,2},{2,0},{1,3},{3,1},{4,6},{6,4},{5,7},{7,5},{8,10},{10,8},{9,1... | collective-permute-start | bytes 2359304 | tf_op jit(solution)/shard_map/ppermute | solution.py:632
  (105 other events, 1648.6 us)
Sparse Core Ops, SparseCore 0:
  10.5 30.7 all-gather.2
  42.9 61.4 all-gather.4
  341.5 71.7 reduce-scatter.3
  416.0 79.4 reduce-scatter.5
  497.7 54.3 reduce-scatter.7

commit v4 on v3

--- a/solution.py
+++ b/solution.py
@@ -369,16 +369,29 @@
     )(q, k, v, grad, out, unit, scale, head_gain, cosine, sine)
 
 
+def cut(arrays, sizes, half):
+    tiles = [[] for _ in range(sum(sizes) // half)]
+    row = 0
+    for array, size in zip(arrays, sizes):
+        start = 0
+        while start < size:
+            count = min(size - start, half - row % half)
+            tiles[row // half].append((array, start, count))
+            start += count
+            row += count
+    return tiles
+
+
 def feed_kernel(layouts, weight_count, index_ref, *refs):
-    tiles = sum(layouts[0][1])
+    tiles = len(layouts[0][0])
+    half = refs[-6].shape[1] // 2
     sides = []
     for pieces, layout in layouts:
         own = []
         for count in pieces:
             own.append(refs[:count])
             refs = refs[count:]
-        others = refs[:len(layout)]
-        sides.append((own, [(o, t) for o, count in zip(others, layout) for t in range(count)]))
+        sides.append((own, cut(refs[:len(layout)], layout, half)))
         refs = refs[len(layout):]
     gate_ref, up_ref, down_ref = refs[:3]
     da_ref, db_ref, ma_ref, mb_ref, hidden_ref, dgu_ref, x_scr, c_scr, gu_scr, down_scr, sem, w_sem = refs[3:]
@@ -389,19 +402,21 @@
         slot = t % 2
         found = []
         for (own, others), scratch, which in ((sides[0], x_scr, 0), (sides[1], c_scr, 1)):
-            other, place = others[t]
             size = half // len(own[t])
             for n, piece in enumerate(own[t]):
                 found.append(
-                    pltpu.make_async_copy(piece, scratch.at[slot, pl.ds(n * size, size)], sem.at[slot, which, n + 1])
+                    pltpu.make_async_copy(piece, scratch.at[slot, pl.ds(n * size, size)], sem.at[slot, which, n])
                 )
-            found.append(
-                pltpu.make_async_copy(
-                    other.at[pl.ds(place * half, half)],
-                    scratch.at[slot, pl.ds(half, half)],
-                    sem.at[slot, which, 0],
+            row = half
+            for n, (other, start, size) in enumerate(others[t]):
+                found.append(
+                    pltpu.make_async_copy(
+                        other.at[pl.ds(start, size)],
+                        scratch.at[slot, pl.ds(row, size)],
+                        sem.at[slot, which, n + 2],
+                    )
                 )
-            )
+                row += size
         return found
 
     mine = hidden_ref.shape[1]
@@ -453,7 +468,7 @@
     tiles = len(x_own)
     half = x_own[0][0].shape[0] * len(x_own[0])
     layouts = tuple(
-        (tuple(len(t) for t in own), tuple(o.shape[0] // half for o in others))
+        (tuple(len(t) for t in own), tuple(o.shape[0] for o in others))
         for own, others in ((x_own, x_others), (c_own, c_others))
     )
     arrays = [a for own, others in ((x_own, x_others), (c_own, c_others)) for a in sum(own, []) + list(others)]
@@ -479,7 +494,7 @@
                 pltpu.VMEM((2, rows, width), BF16),
                 pltpu.VMEM((width, 2 * mine), BF16),
                 pltpu.VMEM((mine, width), BF16),
-                pltpu.SemaphoreType.DMA((2, 2, 3)),
+                pltpu.SemaphoreType.DMA((2, 2, 4)),
                 pltpu.SemaphoreType.DMA((blocks, 3)),
             ],
         ),
@@ -499,27 +514,29 @@
     for own, others in stages:
         half = own[0][0].shape[0] * len(own[0])
         arrays += sum(own, []) + list(others)
-        layout.append((half, tuple(len(t) for t in own), tuple(o.shape[0] // half for o in others)))
+        layout.append((half, tuple(len(t) for t in own), tuple(o.shape[0] for o in others)))
     return arrays, tuple(layout)
 
 
 def stack_rows(refs, layout, scratch):
     at = row = 0
     for half, tiles, others in layout:
-        places = [(at + sum(tiles) + n, t) for n, count in enumerate(others) for t in range(count)]
-        for pieces, (other, place) in zip(tiles, places):
+        first = at + sum(tiles)
+        for pieces, across in zip(tiles, cut(refs[first:first + len(others)], others, half)):
             size = half // pieces
             for n in range(pieces):
-                scratch[row + n * size:row + (n + 1) * size, :] = refs[at + n][...]
+                scratch[row:row + size, :] = refs[at + n][...]
+                row += size
             at += pieces
-            scratch[row + half:row + 2 * half, :] = refs[other][place * half:(place + 1) * half, :]
-            row += 2 * half
+            for other, start, size in across:
+                scratch[row:row + size, :] = other[start:start + size, :]
+                row += size
         at += len(others)
 
 
 def gate_grad_kernel(array_count, layout, *refs):
     arrays, refs = refs[:array_count], refs[array_count:]
-    rights, (gate_ref, up_ref, scratch) = refs[:len(layout)], refs[len(layout):]
+    rights, (out_ref, scratch) = refs[:len(layout)], refs[len(layout):]
     stack_rows(arrays, layout, scratch)
     row = 0
     total = None
@@ -528,10 +545,7 @@
         term = dot(scratch[row:row + size, :], right[...], TN)
         total = term if total is None else total + term
         row += size
-    total = total.astype(BF16)
-    mine = total.shape[1] // 2
-    gate_ref[...] = total[:, :mine]
-    up_ref[...] = total[:, mine:]
+    out_ref[...] = total.astype(BF16)
 
 
 def gate_grad(stages, rights):
@@ -545,8 +559,8 @@
         grid=(width // step,),
         in_specs=[pl.BlockSpec((p.shape[0], step), lambda i: (0, i)) for p in arrays]
         + [pl.BlockSpec(r.shape, lambda i: (0, 0)) for r in rights],
-        out_specs=[pl.BlockSpec((step, units // 2), lambda i: (i, 0))] * 2,
-        out_shape=[jax.ShapeDtypeStruct((width, units // 2), BF16)] * 2,
+        out_specs=pl.BlockSpec((step, units), lambda i: (i, 0)),
+        out_shape=jax.ShapeDtypeStruct((width, units), BF16),
         scratch_shapes=[pltpu.VMEM((rows, step), BF16)],
         compiler_params=pltpu.CompilerParams(vmem_limit_bytes=VMEM),
         cost_estimate=COST,
@@ -592,36 +606,38 @@
 
 def place_kernel(index_ref, *refs):
     parts, outs = refs[:-2], refs[-2:]
-    for d, ref in enumerate(parts):
+    devices = len(parts) // 2
+    for d in range(devices):
         @pl.when(pl.program_id(1) == d)
-        def _(ref=ref):
-            rows = outs[0].shape[0]
-            for n, out_ref in enumerate(outs):
-                out_ref[...] = ref[n * rows:(n + 1) * rows, :].astype(F32)
+        def _(d=d):
+            outs[0][...] = parts[d][...].astype(F32)
+            outs[1][...] = parts[devices + d][...].astype(F32)
 
 
 def place(parts, own, part):
     devices = len(parts)
-    rows, mine = parts[0].shape[0] // 2, parts[0].shape[1]
+    rows, mine = parts[0].shape[0], parts[0].shape[1] // 2
     blocks = mine // part
     if part % LANES:
-        stack = jnp.stack(parts).reshape(devices, 2, rows, blocks, part)
+        stack = jnp.stack(parts).reshape(devices, rows, 2, blocks, part)
         stack = jnp.stack([take(stack, own ^ d) for d in range(devices)])
-        both = stack.transpose(1, 2, 3, 0, 4).reshape(2, rows, -1).astype(F32)
+        both = stack.transpose(2, 1, 3, 0, 4).reshape(2, rows, -1).astype(F32)
         return both[0], both[1]
+    first = pl.BlockSpec((rows, part), lambda b, d, n: (0, b))
+    second = pl.BlockSpec((rows, part), lambda b, d, n: (0, blocks + b))
     return pl.pallas_call(
         place_kernel,
         grid_spec=pltpu.PrefetchScalarGridSpec(
             num_scalar_prefetch=1,
             grid=(blocks, devices),
-            in_specs=[pl.BlockSpec((2 * rows, part), lambda b, d, n: (0, b))] * devices,
+            in_specs=[first] * devices + [second] * devices,
             out_specs=[pl.BlockSpec((rows, part), lambda b, d, n: (0, b * devices + (n[0] ^ d)))] * 2,
         ),
         out_shape=[jax.ShapeDtypeStruct((rows, devices * mine), F32)] * 2,
         compiler_params=pltpu.CompilerParams(vmem_limit_bytes=VMEM),
         cost_estimate=COST,
         name="place",
-    )(own.astype(jnp.int32).reshape(1), *parts)
+    )(own.astype(jnp.int32).reshape(1), *parts, *parts)
 
 
 X, Y, Z, C = "fo", "si", "zb", "fi"
@@ -782,9 +798,7 @@
     c_yz = swap(c_z, Y)
     c_one = [c_x, c_y, c_z]
     c_one_other = other_core(c_one)
-    c_xyz.append(swap(c_xz[1], Y))
     heads_out, c_xz, c_xy, c_yz, c_xyz, c_one_other = sync(heads_out, c_xz, c_xy, c_yz, c_xyz, c_one_other)
-    c_two = [c_xz, c_xy, [c_yz], c_xyz]
 
     inputs = tokens.astype(F32)
     square_one = jnp.mean(inputs * inputs, axis=1, keepdims=True)
@@ -793,7 +807,9 @@
     square_two = jnp.mean(residual * residual, axis=1, keepdims=True)
     scale_two = lax.rsqrt(square_two + EPSILON)
     inner = (residual * scale_two * ffn_gain).astype(BF16)
-    (inner,) = sync(inner)
+    c_xyz.append(swap(c_yz[mid:], X))
+    c_two_other = [swap(c, C) for c in c_xz + c_xy]
+    inner, c_xyz, c_two_other, c_yz = sync(inner, c_xyz, c_two_other, c_yz)
 
     units = gate_weight.shape[1]
     part = units // s_count
@@ -818,21 +834,23 @@
         width_of_part = mine
     run = lambda x_stage, c_stage: feed(x_stage, c_stage, unit_index, weights, width_of_part)
     x, y, z = swap(inner, X), swap(inner, Y), swap(inner, Z)
+    c_two_other.append(swap(c_yz, C))
     x_stages = [([[inner]], [other_core([inner])])]
     c_stages = [([[cot]], [c_own_other])]
     fed = [run(x_stages[0], c_stages[0])]
-    x, y, z, fed, inner, c_two = sync(x, y, z, fed, inner, c_two)
+    x, y, z, fed, inner, c_xyz, c_two_other = sync(x, y, z, fed, inner, c_xyz, c_two_other)
+    c_two = [c_xz, c_xy, [c_yz], c_xyz]
     xy, xz, yz = swap(x, Y), swap(z, X), swap(y, Z)
     xyz = swap_cube(inner, (X, Z, Y))
     x_stages.append(([[x], [y], [z]], [other_core([x, y, z])]))
     c_stages.append(([[c] for c in c_one], [c_one_other]))
-    c_two_other = other_core(sum(c_two, []))
+    c_two_other += [swap(c, C) for c in c_xyz]
     fed.append(run(x_stages[1], c_stages[1]))
     xy, xz, yz, xyz, fed, x_stages, w_parts, c_two, c_two_other = sync(
         xy, xz, yz, xyz, fed, x_stages, w_parts, c_two, c_two_other
     )
     x_stages.append(([[xz], [xy], [yz], [xyz]], [other_core([xz, xy, yz, xyz])]))
-    c_stages.append((c_two, [c_two_other]))
+    c_stages.append((c_two, c_two_other))
     d_home = send_home(0, fed[0][0], swap(fed[0][1], C)) + send_home(1, fed[1][0], swap(fed[1][1], C))
     w_x.append(swap(w_parts[1], X))
     fed.append(run(x_stages[2], c_stages[2]))
@@ -843,23 +861,19 @@
     far_xz, hops, d_home, down_part, fed = sync(far_xz, hops, d_home, down_part, fed)
     d_home += [swap_cube(add_low(far_xz, hops[0]), (X, Z)), swap(add_low(hops[1], hops[2]), Y)]
     m_other = [swap(f[3], C) for f in fed[:2]]
-    gate_part, up_part = gate_grad(x_stages, [f[5] for f in fed])
-    d_home, down_part, gate_part, up_part, fed, m_other, heads_out = sync(
-        d_home, down_part, gate_part, up_part, fed, m_other, heads_out
-    )
-    gate_far = lax.psum_scatter(gate_part, "za", scatter_dimension=0, tiled=True)
-    up_far = lax.psum_scatter(up_part, "za", scatter_dimension=0, tiled=True)
+    gu_part = gate_grad(x_stages, [f[5] for f in fed])
+    d_home, down_part, gu_part, fed, m_other, heads_out = sync(
+        d_home, down_part, gu_part, fed, m_other, heads_out
+    )
+    gu_far = lax.psum_scatter(gu_part, "za", scatter_dimension=0, tiled=True)
     down_far = lax.psum_scatter(down_part, "za", scatter_dimension=0, tiled=True)
     quarter = width // far // 4
 
-    def owner_block(values, offset):
-        return lax.dynamic_slice_in_dim(values, (own_block ^ offset) * quarter, quarter, 0)
-
-    def to_owners(gates, ups):
+    def to_owners(values):
         spread = []
         for offset, axes in enumerate(((), (Y,), (Z,), (Z, Y))):
-            both = jnp.concatenate([owner_block(gates, offset), owner_block(ups, offset)], axis=0)
-            spread.append(swap_cube(both, axes) if axes else both)
+            block = lax.dynamic_slice_in_dim(values, (own_block ^ offset) * quarter, quarter, 0)
+            spread.append(swap_cube(block, axes) if axes else block)
         return spread
 
     m_other.append(swap(fed[2][3], C))
@@ -905,11 +919,11 @@
     m_x, m_yz = swap(m[2][1], X), swap(m[2][2], Y)
     out_part = add_low(pick(out_part, si, 2), out_y)
     m_xz = add_low(m[2][0], m_far)
-    d_tok, proj_core, proj_x, w_xc, out_part, m, m_x, m_yz, m_xz, gain_parts, gate_far, up_far = sync(
-        d_tok, proj_core, proj_x, w_xc, out_part, m, m_x, m_yz, m_xz, gain_parts, gate_far, up_far
+    d_tok, proj_core, proj_x, w_xc, out_part, m, m_x, m_yz, m_xz, gain_parts, gu_far = sync(
+        d_tok, proj_core, proj_x, w_xc, out_part, m, m_x, m_yz, m_xz, gain_parts, gu_far
     )
     m_z = [swap(m_xz, X), m_yz]
-    spread = to_owners(gate_far, up_far)
+    spread = to_owners(gu_far)
     blocks = [w_rows, w_c, jnp.concatenate(w_x, axis=0), jnp.concatenate(w_xc, axis=0)]
     by_offset = jnp.stack([dot(d_tok, w, NT) for w in blocks])
     d_normed = jnp.concatenate([take(by_offset, f_index ^ n) for n in range(f_count)], axis=1)

time: 622 us -> 608 us (0.977)
  waiting for transfers between devices: 177 us -> 160 us
  starting transfers between devices: 91.5 us -> 98.8 us
    ppermute x73 -> x79, waiting for transfers between devices: 107 us -> 94.3 us  [swap(): return lax.ppermute(values, axis, [(i, i ^ offset) for i in range(size)])]
    all_to_all x1, waiting for transfers between devices: 22 us -> 13.3 us  [per_device(): d_tok = lax.all_to_all(d_qkv, seq, split_axis=0, concat_axis=1, tiled=True)]
    reduce_scatter x2 -> x1, waiting for transfers between devices: 7.65 us -> 0.01 us  [per_device(): gu_far = lax.psum_scatter(gu_part, 'za', scatter_dimension=0, tiled=True)]
    all_to_all x1, waiting for transfers between devices: 6.9 us -> 14.5 us  [per_device(): lax.all_to_all(attended_low, seq, split_axis=0, concat_axis=1, tiled=True)]
    ppermute x73 -> x79, starting transfers between devices: 68.6 us -> 74.6 us  [swap(): return lax.ppermute(values, axis, [(i, i ^ offset) for i in range(size)])]
    unnamed x151 -> x139, local copies, waits for them, and re-layouts: 25.7 us -> 22.9 us
  transfers between devices with their start and end apart: 85 -> 90, of which waited for: 34 -> 35; matrix products, arithmetic and copies ran while one was open for 23% -> 23% of each run, Pallas kernels for 26% -> 27%
where the time goes in v4:
time: 608 us; the launch traced here: 599 us
  Pallas kernels  161 us (26%)
  waiting for transfers between devices  160 us (26%)
  starting transfers between devices  98.8 us (16%)
  other arithmetic  70.9 us (12%)
  local copies, waits for them, and re-layouts  56.5 us (9%)
  matrix products  35.8 us (6%)
  between operations  15.1 us (2%)
    ppermute x79, waiting for transfers between devices, swap(): return lax.ppermute(values, axis, [(i, i ^ offset) for i in range(size)])  94.3 us
    ppermute x79, starting transfers between devices, swap(): return lax.ppermute(values, axis, [(i, i ^ offset) for i in range(size)])  74.6 us
    pallas_call x3, Pallas kernels, feed(): pl.pallas_call(functools.partial(feed_kernel, layouts, blocks), grid_spec...  61.8 us
    dot_general x8, matrix products, dot(): return lax.dot_general(left, right, dims, preferred_element_type=F32)  35.8 us
    convert_element_type x13, other arithmetic, add_low(): return (left.astype(F32) + right.astype(F32)).astype(BF16)  31.9 us
    ppermute x3, waiting for transfers between devices, swap_cube(): return lax.ppermute(values, offset, pairs)  28.7 us
    pallas_call x1, Pallas kernels, attend_back(): pl.pallas_call(functools.partial(attend_back_kernel, heads), in_specs=[vm...  26.8 us
    unnamed x139, local copies, waits for them, and re-layouts  22.9 us
  transfers between devices with their start and end apart: 90, of which 35 were waited for; matrix products, arithmetic and copies ran while one was open for 23% of the time, Pallas kernels for 27%

profile of v4, /device:TPU:0, one launch (start us, length us, event | category | flops | bytes accessed | tf_op | source)
XLA Modules:
  0.0 598.6 jit_solution(9374064341444233888)
XLA Ops:
  11.0 4.1 collective-permute-start
  42.8 6.9 %collective-permute-done.refs_0_ = bf16[192,2048]{1,0:T(8,128)(2,1)} collective-permute-done((bf16[192,2048]{1,0:T(8,128)(2,1)S(1)}, bf16[192,2048]{1,0:T(8,128)(2,1)}, u32[]{:S(2)}, u32[]{:S(2)}) %collective-permute-start) | collective-permute-done | bytes 786464 | tf_op jit(solution)/shard_map/ppermute | solution.py:648
  54.3 8.3 %project.3 = (bf16[1536,2048]{1,0:T(8,128)(2,1)}, bf16[4,1536,128]{2,1,0:T(8,128)(2,1)}, bf16[1536,128]{1,0:T(8,128)(2,1)}, bf16[1536,128]{1,0:T(8,128)(2,1)}, f32[1536,384]{1,0:T(8,128)}, /*index=5*/f32[1536,384]{1,0:T(8,128)}) custom-call(s32[3]{0:T(128)} %get-tuple-element.658.index_ref, s32[2]{0:T(128)} %bitcast.185, bf16[192,2048]{1,0:T(8,128)(2,1)} %refs_0_.1, ...), custom_call_target="tpu_custom_call" | custom-call | flops 1000 | bytes 1000 | tf_op jit(solution)/shard_map/project/pallas_call | solution.py:123
  62.6 8.8 %collective-permute-done.4.refs_1_ = bf16[192,2048]{1,0:T(8,128)(2,1)} collective-permute-done((bf16[192,2048]{1,0:T(8,128)(2,1)}, bf16[192,2048]{1,0:T(8,128)(2,1)}, u32[]{:S(2)}, u32[]{:S(2)}) %collective-permute-start.4) | collective-permute-done | bytes 786464 | tf_op jit(solution)/shard_map/ppermute | solution.py:648
  74.3 8.0 %project.4 = (bf16[1536,2048]{1,0:T(8,128)(2,1)}, bf16[4,1536,128]{2,1,0:T(8,128)(2,1)}, bf16[1536,128]{1,0:T(8,128)(2,1)}, bf16[1536,128]{1,0:T(8,128)(2,1)}, f32[1536,384]{1,0:T(8,128)}, /*index=5*/f32[1536,384]{1,0:T(8,128)}) custom-call(s32[3]{0:T(128)} %get-tuple-element.659.index_ref, ...), custom_call_target="tpu_custom_call", output_to_operand_aliasing={{0}: (10, {}), {1}: (11, {}), {2}: (12, {}), {3}: (13, {}),... | custom-call | flops 1000 | bytes 1000 | tf_op jit(solution)/shard_map/project/pallas_call | solution.py:123
  82.3 9.3 %collective-permute-done.6.refs_0_ = bf16[192,2048]{1,0:T(8,128)(2,1)S(1)} collective-permute-done((bf16[192,2048]{1,0:T(8,128)(2,1)}, bf16[192,2048]{1,0:T(8,128)(2,1)S(1)}, u32[]{:S(2)}, u32[]{:S(2)}) %collective-permute-start.6) | collective-permute-done | bytes 786464 | tf_op jit(solution)/shard_map/ppermute | solution.py:648
  99.6 6.3 %project.5 = (bf16[1536,2048]{1,0:T(8,128)(2,1)}, bf16[4,1536,128]{2,1,0:T(8,128)(2,1)}, bf16[1536,128]{1,0:T(8,128)(2,1)}, bf16[1536,128]{1,0:T(8,128)(2,1)}, f32[1536,384]{1,0:T(8,128)}, /*index=5*/f32[1536,384]{1,0:T(8,128)}) custom-call(s32[2]{0:T(128)} %pad_add_fusion.2.index_ref, ...), custom_call_target="tpu_custom_call", output_to_operand_aliasing={{0}: (9, {}), {1}: (10, {}), {2}: (11, {}), {3}: (12, {}), ... | custom-call | flops 1000 | bytes 1000 | tf_op jit(solution)/shard_map/project/pallas_call | solution.py:123
  105.9 10.0 %attend.1 = (bf16[1536,256]{1,0:T(8,128)(2,1)}, f32[1536,256]{1,0:T(8,128)}, bf16[4,1536,128]{2,1,0:T(8,128)(2,1)}) custom-call(bf16[4,1536,128]{2,1,0:T(8,128)(2,1)} %get-tuple-element.354.q_ref, bf16[1536,128]{1,0:T(8,128)(2,1)} %get-tuple-element.355.k_ref, bf16[1536,128]{1,0:T(8,128)(2,1)} %get-tuple-element.356.v_ref), custom_call_target="tpu_custom_call" | custom-call | flops 1000 | bytes 1000 | tf_op jit(solution)/shard_map/attend/pallas_call | solution.py:215
  115.9 3.1 collective-permute-done.12.refs_7_.refs_8_
  122.1 4.3 all-to-all-start
  132.8 14.5 %all-to-all-done = bf16[8,192,256]{2,1,0:T(8,128)(2,1)S(1)} async-done(((bf16[8,192,256]{2,1,0:T(8,128)(2,1)}), bf16[8,192,256]{2,1,0:T(8,128)(2,1)S(1)}, u32[]{:S(2)}, u32[]{:S(2)}) %all-to-all-start) | async-done | bytes 786464 | tf_op jit(solution)/shard_map/all_to_all | solution.py:794
  150.5 4.3 collective-permute-done.17.refs_9_.refs_10_
  159.1 5.6 multiply_reduce_fusion.2
  172.2 11.1 %feed.3 = (bf16[1,192,2048]{2,1,0:T(8,128)(2,1)}, bf16[1,192,2048]{2,1,0:T(8,128)(2,1)}, bf16[1,192,2048]{2,1,0:T(8,128)(2,1)}, bf16[1,192,2048]{2,1,0:T(8,128)(...) custom-call(s32[2]{0:T(128)} %multiply_add_fusion.3.index_ref, ...), custom_call_target="tpu_custom_call" | custom-call | flops 1000 | bytes 1000 | tf_op jit(solution)/shard_map/feed/pallas_call | solution.py:481
  183.3 4.9 collective-permute-done.25.refs_0_.refs_2_
  199.9 22.5 %feed.4 = (bf16[3,192,2048]{2,1,0:T(8,128)(2,1)}, bf16[3,192,2048]{2,1,0:T(8,128)(2,1)}, bf16[3,192,2048]{2,1,0:T(8,128)(2,1)}, bf16[3,192,2048]{2,1,0:T(8,128)(...) custom-call(s32[2]{0:T(128)} %multiply_add_fusion.3.index_ref, bf16[192,2048]{1,0:T(8,128)(2,1)} %copy-done.10, ...), custom_call_target="tpu_custom_call" | custom-call | flops 1000 | bytes 1000 | tf_op jit(solution)/shard_map/feed/pallas_call | solution.py:481
  222.4 8.7 %collective-permute-done.33.refs_3_.refs_9_ = bf16[192,2048]{1,0:T(8,128)(2,1)} collective-permute-done((bf16[192,2048]{1,0:T(8,128)(2,1)}, bf16[192,2048]{1,0:T(8,128)(2,1)}, u32[]{:S(2)}, u32[]{:S(2)}) %collective-permute-start.33) | collective-permute-done | bytes 786464 | tf_op jit(solution)/shard_map/ppermute | solution.py:668
  243.1 28.2 %feed.5 = (bf16[4,192,2048]{2,1,0:T(8,128)(2,1)}, bf16[4,192,2048]{2,1,0:T(8,128)(2,1)}, bf16[4,192,2048]{2,1,0:T(8,128)(2,1)}, bf16[4,192,2048]{2,1,0:T(8,128)(...) custom-call(s32[2]{0:T(128)} %multiply_add_fusion.3.index_ref, ...), custom_call_target="tpu_custom_call" | custom-call | flops 1000 | bytes 1000 | tf_op jit(solution)/shard_map/feed/pallas_call | solution.py:481
  271.5 5.9 collective-permute-done.44
  277.3 3.2 add_convert_fusion
  285.1 13.6 %down_grad.1 = bf16[512,2048]{1,0:T(8,128)(2,1)} custom-call(bf16[192,2048]{1,0:T(8,128)(2,1)} %refs_0_.2, bf16[192,2048]{1,0:T(8,128)(2,1)} %copy-done.18, bf16[192,2048]{1,0:T(8,128)(2,1)} %copy-done.5, bf16[192,2048]{1,0:T(8,128)(2,1)} %copy-done.6, bf16[192,2048]{1,0:T(8,128)(2,1)} %copy-done.7, ...), custom_call_target="tpu_custom_call" | custom-call | flops 1000 | bytes 1000 | tf_op jit(solution)/shard_map/down_grad/pallas_call | solution.py:593
  298.6 3.3 collective-permute-done.45
  310.8 20.6 %gate_grad.1 = bf16[2048,1024]{1,0:T(8,128)(2,1)} custom-call(bf16[192,2048]{1,0:T(8,128)(2,1)} %multiply_convert_fusion.refs_0_, bf16[192,2048]{1,0:T(8,128)(2,1)} %collective-permute-done.28.refs_1_, bf16[192,2048]{1,0:T(8,128)(2,1)} %copy-done.10, bf16[192,2048]{1,0:T(8,128)(2,1)} %copy-done.11, bf16[192,2048]{1,0:T(8,128)(2,1)} %copy-done.12, ...), custom_call_target="tpu_custom_call" | custom-call | flops 1000 | bytes 1000 | tf_op jit(solution)/shard_map/gate_grad/pallas_call | solution.py:557
  334.9 3.8 multiply_reduce_fusion
  340.0 7.4 %convolution_convert_fusion.1 = bf16[192,2048]{1,0:T(8,128)(2,1)} fusion(bf16[192,2048]{1,0:T(8,128)(2,1)} %fusion.64, bf16[2048,2048]{1,0:T(8,128)(2,1)} %all-gather.5.cloned.1.call-done), kind=kOutput, calls=%fused_computation.29 | convolution fusion | flops 1611005952 | bytes 9961472 | tf_op jit(solution)/shard_map/dot_general | solution.py:29
  352.4 5.2 all-to-all-start.1
  357.6 5.3 fusion.47
  364.9 4.4 collective-permute-done.57
  371.6 4.1 add_convert_fusion.1
  375.8 10.7 %collective-permute-done.59 = bf16[192,2048]{1,0:T(8,128)(2,1)} collective-permute-done((bf16[192,2048]{1,0:T(8,128)(2,1)S(1)}, bf16[192,2048]{1,0:T(8,128)(2,1)}, u32[]{:S(2)}, u32[]{:S(2)}) %collective-permute-start.59) | collective-permute-done | bytes 786464 | tf_op jit(solution)/shard_map/ppermute | solution.py:648
  386.4 8.8 %all-to-all-done.1 = bf16[192,8,256]{2,0,1:T(8,128)(2,1)} async-done(((bf16[192,8,256]{2,0,1:T(8,128)(2,1)}), bf16[192,8,256]{2,0,1:T(8,128)(2,1)}, u32[]{:S(2)}, u32[]{:S(2)}) %all-to-all-start.1) | async-done | bytes 786464 | tf_op jit(solution)/shard_map/all_to_all | solution.py:894
  399.5 3.7 fusion.18
  407.0 26.8 %attend_back.1 = (bf16[1536,384]{1,0:T(8,128)(2,1)}, f32[8,384]{1,0:T(8,128)}) custom-call(bf16[4,1536,128]{2,1,0:T(8,128)(2,1)} %get-tuple-element.367.q_ref, bf16[1536,128]{1,0:T(8,128)(2,1)} %get-tuple-element.355.k_ref, bf16[1536,128]{1,0:T(8,128)(2,1)} %get-tuple-element.356.v_ref, bf16[1536,256]{1,0:T(8,128)(2,1)} %bitcast.25.grad_ref, ...), custom_call_target="tpu_custom_call" | custom-call | flops 1000 | bytes 1000 | tf_op jit(solution)/shard_map/attend_back/pallas_call | solution.py:347
  433.8 4.3 all-to-all-start.2
  438.2 6.6 %convolution_convert_fusion = bf16[2048,384]{1,0:T(8,128)(2,1)S(1)} fusion(bf16[1536,2048]{1,0:T(8,128)(2,1)} %get-tuple-element.555, bf16[1536,384]{1,0:T(8,128)(2,1)} %get-tuple-element.554), kind=kOutput, calls=%fused_computation.24 | convolution fusion | flops 2416705536 | bytes 9043968 | tf_op jit(solution)/shard_map/dot_general | solution.py:29
  449.9 2.9 fusion.21
  459.6 13.3 %all-to-all-done.2 = bf16[8,192,384]{2,1,0:T(8,128)(2,1)} async-done(((bf16[8,192,384]{2,1,0:T(8,128)(2,1)}), bf16[8,192,384]{2,1,0:T(8,128)(2,1)}, u32[]{:S(2)}, u32[]{:S(2)}) %all-to-all-start.2) | async-done | bytes 1179680 | tf_op jit(solution)/shard_map/all_to_all | solution.py:913
  483.0 3.1 convolution_bitcast_fusion.1
  486.2 3.2 convolution_bitcast_fusion
  489.3 3.1 fusion.36
  492.5 3.1 fusion.39
  506.9 20.0 %collective-permute-done.71.refs_3_.refs_7_ = bf16[256,1024]{1,0:T(8,128)(2,1)} collective-permute-done((bf16[256,1024]{1,0:T(8,128)(2,1)S(1)}, bf16[256,1024]{1,0:T(8,128)(2,1)}, u32[]{:S(2)}, u32[]{:S(2)}) %collective-permute-start.71) | collective-permute-done | bytes 524320 | tf_op jit(solution)/shard_map/ppermute | solution.py:668
  534.9 5.2 all-to-all-start.3
  547.8 4.3 collective-permute-start.79
  552.1 2.9 fusion.33
  555.0 5.7 place.1
  577.0 9.7 %collective-permute-done.81 = bf16[64,2048]{1,0:T(8,128)(2,1)} collective-permute-done((bf16[64,2048]{1,0:T(8,128)(2,1)}, bf16[64,2048]{1,0:T(8,128)(2,1)}, u32[]{:S(2)}, u32[]{:S(2)}) %collective-permute-start.81) | collective-permute-done | bytes 262176 | tf_op jit(solution)/shard_map/ppermute | solution.py:648
  588.5 3.1 fusion.31
  (381 shorter events, 197.1 us)
Async XLA Ops:
  7.2 47.1 %all-gather.3.cloned.1.call-start = ((), (), s32[]{:S(2)}) async-start(), calls=%async_computation.6 | async-start | bytes 1966080 | tf_op jit(solution)/shard_map/all_gather | solution.py:743
  10.3 148.8 %all-gather.5.cloned.1.call-start = ((), (), s32[]{:S(2)}) async-start(), calls=%async_computation.7 | async-start | bytes 10485760 | tf_op jit(solution)/shard_map/all_gather | solution.py:744
  11.0 38.7 %collective-permute-start = (bf16[192,2048]{1,0:T(8,128)(2,1)S(1)}, bf16[192,2048]{1,0:T(8,128)(2,1)}, u32[]{:S(2)}, u32[]{:S(2)}) collective-permute-start(bf16[192,2048]{1,0:T(8,128)(2,1)S(1)} %copy-done.13), channel_id=1, source_target_pairs={{0,4},{4,0},{1,5},{5,1},{2,6},{6,2},{3,7},{7,3},{8,12},{12,8},{9,1... | collective-permute-start | bytes 2359304 | tf_op jit(solution)/shard_map/ppermute | solution.py:648
  15.1 34.6 %collective-permute-start.1 = (bf16[192,2048]{1,0:T(8,128)(2,1)S(1)}, bf16[192,2048]{1,0:T(8,128)(2,1)}, u32[]{:S(2)}, u32[]{:S(2)}) collective-permute-start(bf16[192,2048]{1,0:T(8,128)(2,1)S(1)} %copy-done.13), channel_id=1, source_target_pairs={{0,1},{1,0},{2,3},{3,2},{4,5},{5,4},{6,7},{7,6},{8,9},{9,8},{10,11... | collective-permute-start | bytes 2359304 | tf_op jit(solution)/shard_map/ppermute | solution.py:648
  16.7 34.5 %collective-permute-start.2 = (bf16[192,2048]{1,0:T(8,128)(2,1)S(1)}, bf16[192,2048]{1,0:T(8,128)(2,1)}, u32[]{:S(2)}, u32[]{:S(2)}) collective-permute-start(bf16[192,2048]{1,0:T(8,128)(2,1)S(1)} %copy-done.13), channel_id=1, source_target_pairs={{0,2},{2,0},{1,3},{3,1},{4,6},{6,4},{5,7},{7,5},{8,10},{10,8},{9,1... | collective-permute-start | bytes 2359304 | tf_op jit(solution)/shard_map/ppermute | solution.py:648
  18.2 32.9 %collective-permute-start.3 = (bf16[192,2048]{1,0:T(8,128)(2,1)S(1)}, bf16[192,2048]{1,0:T(8,128)(2,1)S(1)}, u32[]{:S(2)}, u32[]{:S(2)}) collective-permute-start(bf16[192,2048]{1,0:T(8,128)(2,1)S(1)} %copy-done.1), channel_id=1, source_target_pairs={{0,16},{16,0},{1,17},{17,1},{2,18},{18,2},{3,19},{19,3},{4,20},{20... | collective-permute-start | bytes 2359304 | tf_op jit(solution)/shard_map/ppermute | solution.py:648
  51.2 41.5 %collective-permute-start.8 = (bf16[512,3072]{1,0:T(8,128)(2,1)}, bf16[512,3072]{1,0:T(8,128)(2,1)}, u32[]{:S(2)}, u32[]{:S(2)}) collective-permute-start(bf16[512,3072]{1,0:T(8,128)(2,1)} %bitcast.84), channel_id=1, source_target_pairs={{0,8},{8,0},{1,9},{9,1},{2,10},{10,2},{3,11},{11,3},{4,12},{12,4},... | collective-permute-start | bytes 9437192 | tf_op jit(solution)/shard_map/ppermute | solution.py:648
  53.0 29.3 %collective-permute-start.9 = (bf16[192,2048]{1,0:T(8,128)(2,1)S(1)}, bf16[192,2048]{1,0:T(8,128)(2,1)S(1)}, u32[]{:S(2)}, u32[]{:S(2)}) collective-permute-start(bf16[192,2048]{1,0:T(8,128)(2,1)S(1)} %copy-done.1), channel_id=1, source_target_pairs={{0,8},{8,0},{1,9},{9,1},{2,10},{10,2},{3,11},{11,3},{4,12},{12,4},... | collective-permute-start | bytes 2359304 | tf_op jit(solution)/shard_map/ppermute | solution.py:648
  92.6 27.6 %collective-permute-start.10 = (bf16[192,2048]{1,0:T(8,128)(2,1)S(1)}, bf16[192,2048]{1,0:T(8,128)(2,1)S(1)}, u32[]{:S(2)}, u32[]{:S(2)}) collective-permute-start(bf16[192,2048]{1,0:T(8,128)(2,1)S(1)} %copy-done.1), channel_id=1, source_target_pairs={{0,1},{1,0},{2,3},{3,2},{4,5},{5,4},{6,7},{7,6},{8,9},{9,8},{10,11... | collective-permute-start | bytes 2359304 | tf_op jit(solution)/shard_map/ppermute | solution.py:648
  93.9 26.3 %collective-permute-start.11 = (bf16[192,2048]{1,0:T(8,128)(2,1)S(1)}, bf16[192,2048]{1,0:T(8,128)(2,1)S(1)}, u32[]{:S(2)}, u32[]{:S(2)}) collective-permute-start(bf16[192,2048]{1,0:T(8,128)(2,1)S(1)} %copy-done.1), channel_id=1, source_target_pairs={{0,2},{2,0},{1,3},{3,1},{4,6},{6,4},{5,7},{7,5},{8,10},{10,8},{9,1... | collective-permute-start | bytes 2359304 | tf_op jit(solution)/shard_map/ppermute | solution.py:648
  95.0 25.3 %collective-permute-start.14 = (bf16[128,3072]{1,0:T(8,128)(2,1)}, bf16[128,3072]{1,0:T(8,128)(2,1)}, u32[]{:S(2)}, u32[]{:S(2)}) collective-permute-start(bf16[128,3072]{1,0:T(8,128)(2,1)} %bitcast.177), channel_id=1, source_target_pairs={{0,16},{16,0},{1,17},{17,1},{2,18},{18,2},{3,19},{19,3},{4,20},{20... | collective-permute-start | bytes 2359304 | tf_op jit(solution)/shard_map/ppermute | solution.py:648
  97.3 21.7 %collective-permute-start.12 = (bf16[96,2048]{1,0:T(8,128)(2,1)}, bf16[96,2048]{1,0:T(8,128)(2,1)S(1)}, u32[]{:S(2)}, u32[]{:S(2)}) collective-permute-start(bf16[96,2048]{1,0:T(8,128)(2,1)} %slice.115), channel_id=1, source_target_pairs={{0,1},{1,0},{2,3},{3,2},{4,5},{5,4},{6,7},{7,6},{8,9},{9,8},{10,11... | collective-permute-start | bytes 1179656 | tf_op jit(solution)/shard_map/ppermute | solution.py:648
  98.0 22.3 %collective-permute-start.13 = (bf16[96,2048]{1,0:T(8,128)(2,1)}, bf16[96,2048]{1,0:T(8,128)(2,1)}, u32[]{:S(2)}, u32[]{:S(2)}) collective-permute-start(bf16[96,2048]{1,0:T(8,128)(2,1)} %slice.115), channel_id=1, source_target_pairs={{0,2},{2,0},{1,3},{3,1},{4,6},{6,4},{5,7},{7,5},{8,10},{10,8},{9,1... | collective-permute-start | bytes 1179656 | tf_op jit(solution)/shard_map/ppermute | solution.py:648
  122.1 32.8 %collective-permute-start.19 = (bf16[576,2048]{1,0:T(8,128)(2,1)}, bf16[576,2048]{1,0:T(8,128)(2,1)}, u32[]{:S(2)}, u32[]{:S(2)}) collective-permute-start(bf16[576,2048]{1,0:T(8,128)(2,1)} %pad_maximum_fusion.2), channel_id=1, source_target_pairs={{0,8},{8,0},{1,9},{9,1},{2,10},{10,2},{3,11},{11,3},{4,12},{12,4},... | collective-permute-start | bytes 7077896 | tf_op jit(solution)/shard_map/ppermute | solution.py:648
  122.1 25.3 %all-to-all-start = ((bf16[8,192,256]{2,1,0:T(8,128)(2,1)}), bf16[8,192,256]{2,1,0:T(8,128)(2,1)S(1)}, u32[]{:S(2)}, u32[]{:S(2)}) async-start(bf16[8,192,256]{2,1,0:T(8,128)(2,1)} %bitcast.178), calls=%async_computation | async-start | bytes 1572864 | tf_op jit(solution)/shard_map/all_to_all | solution.py:794
  126.4 349.4 %reduce-scatter.3.cloned.1.call-start = ((), (), s32[]{:S(2)}) async-start(), calls=%async_computation.8 | async-start | bytes 6291456 | tf_op jit(solution)/shard_map/reduce_scatter | solution.py:868
  126.4 28.4 %collective-permute-start.17 = (bf16[192,2048]{1,0:T(8,128)(2,1)S(1)}, bf16[192,2048]{1,0:T(8,128)(2,1)}, u32[]{:S(2)}, u32[]{:S(2)}) collective-permute-start(bf16[192,2048]{1,0:T(8,128)(2,1)S(1)} %collective-permute-done.11.refs_6_.refs_4_), channel_id=1, source_target_pairs={{0,1},{1,0},{2,3},{3,2},{4,5},{5,4},{6,7},{7,6},{8,9},{9,8},{10,11... | collective-permute-start | bytes 2359304 | tf_op jit(solution)/shard_map/ppermute | solution.py:648
  191.7 30.7 %collective-permute-start.30 = (bf16[192,2048]{1,0:T(8,128)(2,1)}, bf16[192,2048]{1,0:T(8,128)(2,1)}, u32[]{:S(2)}, u32[]{:S(2)}) collective-permute-start(bf16[192,2048]{1,0:T(8,128)(2,1)} %copy-done.10), channel_id=1, source_target_pairs={{0,1},{1,0},{2,3},{3,2},{4,5},{5,4},{6,7},{7,6},{8,9},{9,8},{10,11... | collective-permute-start | bytes 2359304 | tf_op jit(solution)/shard_map/ppermute | solution.py:648
  193.1 29.3 %collective-permute-start.31 = (bf16[192,2048]{1,0:T(8,128)(2,1)}, bf16[192,2048]{1,0:T(8,128)(2,1)}, u32[]{:S(2)}, u32[]{:S(2)}) collective-permute-start(bf16[192,2048]{1,0:T(8,128)(2,1)} %copy-done.12), channel_id=1, source_target_pairs={{0,16},{16,0},{1,17},{17,1},{2,18},{18,2},{3,19},{19,3},{4,20},{20... | collective-permute-start | bytes 2359304 | tf_op jit(solution)/shard_map/ppermute | solution.py:648
  193.7 28.8 %collective-permute-start.32 = (bf16[192,2048]{1,0:T(8,128)(2,1)}, bf16[192,2048]{1,0:T(8,128)(2,1)}, u32[]{:S(2)}, u32[]{:S(2)}) collective-permute-start(bf16[192,2048]{1,0:T(8,128)(2,1)} %copy-done.11), channel_id=1, source_target_pairs={{0,2},{2,0},{1,3},{3,1},{4,6},{6,4},{5,7},{7,5},{8,10},{10,8},{9,1... | collective-permute-start | bytes 2359304 | tf_op jit(solution)/shard_map/ppermute | solution.py:648
  196.2 35.0 %collective-permute-start.33 = (bf16[192,2048]{1,0:T(8,128)(2,1)}, bf16[192,2048]{1,0:T(8,128)(2,1)}, u32[]{:S(2)}, u32[]{:S(2)}) collective-permute-start(bf16[192,2048]{1,0:T(8,128)(2,1)} %multiply_convert_fusion.refs_0_), channel_id=1, source_target_pairs={{0,19},{1,18},{2,17},{3,16},{16,3},{17,2},{18,1},{19,0},{4,23},{5,... | collective-permute-start | bytes 2359304 | tf_op jit(solution)/shard_map/ppermute | solution.py:668
  198.5 23.9 %collective-permute-start.36 = (bf16[96,2048]{1,0:T(8,128)(2,1)}, bf16[96,2048]{1,0:T(8,128)(2,1)}, u32[]{:S(2)}, u32[]{:S(2)}) collective-permute-start(bf16[96,2048]{1,0:T(8,128)(2,1)} %collective-permute-done.20.refs_11_.refs_12_), channel_id=1, source_target_pairs={{0,8},{8,0},{1,9},{9,1},{2,10},{10,2},{3,11},{11,3},{4,12},{12,4},... | collective-permute-start | bytes 1179656 | tf_op jit(solution)/shard_map/ppermute | solution.py:648
  234.0 37.3 %collective-permute-start.43 = (bf16[128,3072]{1,0:T(8,128)(2,1)}, bf16[128,3072]{1,0:T(8,128)(2,1)}, u32[]{:S(2)}, u32[]{:S(2)}) collective-permute-start(bf16[128,3072]{1,0:T(8,128)(2,1)} %bitcast.88), channel_id=1, source_target_pairs={{0,16},{16,0},{1,17},{17,1},{2,18},{18,2},{3,19},{19,3},{4,20},{20... | collective-permute-start | bytes 2359304 | tf_op jit(solution)/shard_map/ppermute | solution.py:648
  238.5 32.8 %collective-permute-start.39 = (bf16[192,2048]{1,0:T(8,128)(2,1)}, bf16[192,2048]{1,0:T(8,128)(2,1)S(1)}, u32[]{:S(2)}, u32[]{:S(2)}) collective-permute-start(bf16[192,2048]{1,0:T(8,128)(2,1)} %get-tuple-element.629), channel_id=1, source_target_pairs={{0,16},{16,0},{1,17},{17,1},{2,18},{18,2},{3,19},{19,3},{4,20},{20... | collective-permute-start | bytes 2359304 | tf_op jit(solution)/shard_map/ppermute | solution.py:648
  239.1 32.3 %collective-permute-start.40 = (bf16[192,2048]{1,0:T(8,128)(2,1)}, bf16[192,2048]{1,0:T(8,128)(2,1)S(1)}, u32[]{:S(2)}, u32[]{:S(2)}) collective-permute-start(bf16[192,2048]{1,0:T(8,128)(2,1)} %get-tuple-element.628), channel_id=1, source_target_pairs={{0,1},{1,0},{2,3},{3,2},{4,5},{5,4},{6,7},{7,6},{8,9},{9,8},{10,11... | collective-permute-start | bytes 2359304 | tf_op jit(solution)/shard_map/ppermute | solution.py:648
  240.5 30.9 %collective-permute-start.41 = (bf16[192,2048]{1,0:T(8,128)(2,1)}, bf16[192,2048]{1,0:T(8,128)(2,1)S(1)}, u32[]{:S(2)}, u32[]{:S(2)}) collective-permute-start(bf16[192,2048]{1,0:T(8,128)(2,1)} %get-tuple-element.627), channel_id=1, source_target_pairs={{0,2},{2,0},{1,3},{3,1},{4,6},{6,4},{5,7},{7,5},{8,10},{10,8},{9,1... | collective-permute-start | bytes 2359304 | tf_op jit(solution)/shard_map/ppermute | solution.py:648
  303.4 28.0 %collective-permute-start.51 = (bf16[3,192,2048]{2,1,0:T(8,128)(2,1)}, bf16[3,192,2048]{2,1,0:T(8,128)(2,1)}, u32[]{:S(2)}, u32[]{:S(2)}) collective-permute-start(bf16[3,192,2048]{2,1,0:T(8,128)(2,1)} %get-tuple-element.503), channel_id=1, source_target_pairs={{0,8},{8,0},{1,9},{9,1},{2,10},{10,2},{3,11},{11,3},{4,12},{12,4},... | collective-permute-start | bytes 7077896 | tf_op jit(solution)/shard_map/ppermute | solution.py:648
  305.8 25.6 %collective-permute-start.48 = (bf16[192,2048]{1,0:T(8,128)(2,1)}, bf16[192,2048]{1,0:T(8,128)(2,1)S(1)}, u32[]{:S(2)}, u32[]{:S(2)}) collective-permute-start(bf16[192,2048]{1,0:T(8,128)(2,1)} %add_convert_fusion.10), channel_id=1, source_target_pairs={{0,18},{2,16},{16,2},{18,0},{1,19},{3,17},{17,3},{19,1},{4,22},{6,... | collective-permute-start | bytes 2359304 | tf_op jit(solution)/shard_map/ppermute | solution.py:668
  310.2 21.2 %collective-permute-start.49 = (bf16[192,2048]{1,0:T(8,128)(2,1)}, bf16[192,2048]{1,0:T(8,128)(2,1)}, u32[]{:S(2)}, u32[]{:S(2)}) collective-permute-start(bf16[192,2048]{1,0:T(8,128)(2,1)} %add_convert_fusion.9), channel_id=1, source_target_pairs={{0,1},{1,0},{2,3},{3,2},{4,5},{5,4},{6,7},{7,6},{8,9},{9,8},{10,11... | collective-permute-start | bytes 2359304 | tf_op jit(solution)/shard_map/ppermute | solution.py:648
  349.9 25.9 %collective-permute-start.56 = (bf16[192,2048]{1,0:T(8,128)(2,1)}, bf16[192,2048]{1,0:T(8,128)(2,1)}, u32[]{:S(2)}, u32[]{:S(2)}) collective-permute-start(bf16[192,2048]{1,0:T(8,128)(2,1)} %fusion.64), channel_id=1, source_target_pairs={{0,8},{8,0},{1,9},{9,1},{2,10},{10,2},{3,11},{11,3},{4,12},{12,4},... | collective-permute-start | bytes 2359304 | tf_op jit(solution)/shard_map/ppermute | solution.py:648
  352.4 42.9 %all-to-all-start.1 = ((bf16[192,8,256]{2,0,1:T(8,128)(2,1)}), bf16[192,8,256]{2,0,1:T(8,128)(2,1)}, u32[]{:S(2)}, u32[]{:S(2)}) async-start(bf16[192,8,256]{2,0,1:T(8,128)(2,1)} %bitcast.162), calls=%async_computation.1 | async-start | bytes 1572864 | tf_op jit(solution)/shard_map/all_to_all | solution.py:894
  362.9 23.6 %collective-permute-start.59 = (bf16[192,2048]{1,0:T(8,128)(2,1)S(1)}, bf16[192,2048]{1,0:T(8,128)(2,1)}, u32[]{:S(2)}, u32[]{:S(2)}) collective-permute-start(bf16[192,2048]{1,0:T(8,128)(2,1)S(1)} %get-tuple-element.617), channel_id=1, source_target_pairs={{0,1},{1,0},{2,3},{3,2},{4,5},{5,4},{6,7},{7,6},{8,9},{9,8},{10,11... | collective-permute-start | bytes 2359304 | tf_op jit(solution)/shard_map/ppermute | solution.py:648
  369.3 25.9 %collective-permute-start.58 = (bf16[192,2048]{1,0:T(8,128)(2,1)}, bf16[192,2048]{1,0:T(8,128)(2,1)}, u32[]{:S(2)}, u32[]{:S(2)}) collective-permute-start(bf16[192,2048]{1,0:T(8,128)(2,1)} %collective-permute-done.57), channel_id=1, source_target_pairs={{0,8},{8,0},{1,9},{9,1},{2,10},{10,2},{3,11},{11,3},{4,12},{12,4},... | collective-permute-start | bytes 2359304 | tf_op jit(solution)/shard_map/ppermute | solution.py:648
  395.3 38.6 %collective-permute-start.60 = (bf16[256,3072]{1,0:T(8,128)(2,1)}, bf16[256,3072]{1,0:T(8,128)(2,1)}, u32[]{:S(2)}, u32[]{:S(2)}) collective-permute-start(bf16[256,3072]{1,0:T(8,128)(2,1)} %bitcast.172), channel_id=1, source_target_pairs={{0,16},{16,0},{1,17},{17,1},{2,18},{18,2},{3,19},{19,3},{4,20},{20... | collective-permute-start | bytes 4718600 | tf_op jit(solution)/shard_map/ppermute | solution.py:648
  399.5 34.3 %collective-permute-start.61 = (bf16[256,3072]{1,0:T(8,128)(2,1)}, bf16[256,3072]{1,0:T(8,128)(2,1)}, u32[]{:S(2)}, u32[]{:S(2)}) collective-permute-start(bf16[256,3072]{1,0:T(8,128)(2,1)} %pad_maximum_fusion.4), channel_id=1, source_target_pairs={{0,8},{8,0},{1,9},{9,1},{2,10},{10,2},{3,11},{11,3},{4,12},{12,4},... | collective-permute-start | bytes 4718600 | tf_op jit(solution)/shard_map/ppermute | solution.py:648
  405.6 28.2 %collective-permute-start.62 = (bf16[2,2,64,2048]{3,2,0,1:T(8,128)(2,1)}, bf16[2,2,64,2048]{3,2,0,1:T(8,128)(2,1)}, u32[]{:S(2)}, u32[]{:S(2)}) collective-permute-start(bf16[2,2,64,2048]{3,2,0,1:T(8,128)(2,1)} %copy_bitcast_fusion), channel_id=1, source_target_pairs={{0,1},{1,0},{2,3},{3,2},{4,5},{5,4},{6,7},{7,6},{8,9},{9,8},{10,11... | collective-permute-start | bytes 3145736 | tf_op jit(solution)/shard_map/ppermute | solution.py:648
  433.8 39.1 %all-to-all-start.2 = ((bf16[8,192,384]{2,1,0:T(8,128)(2,1)}), bf16[8,192,384]{2,1,0:T(8,128)(2,1)}, u32[]{:S(2)}, u32[]{:S(2)}) async-start(bf16[8,192,384]{2,1,0:T(8,128)(2,1)} %bitcast.176), calls=%async_computation.2 | async-start | bytes 2359296 | tf_op jit(solution)/shard_map/all_to_all | solution.py:913
  438.1 122.8 %reduce-scatter.5.cloned.1.call-start = ((), (), s32[]{:S(2)}) async-start(), calls=%async_computation.9 | async-start | bytes 3145728 | tf_op jit(solution)/shard_map/reduce_scatter | solution.py:869
  447.1 28.7 %collective-permute-start.65 = (bf16[256,3072]{1,0:T(8,128)(2,1)}, bf16[256,3072]{1,0:T(8,128)(2,1)}, u32[]{:S(2)}, u32[]{:S(2)}) collective-permute-start(bf16[256,3072]{1,0:T(8,128)(2,1)} %collective-permute-done.60), channel_id=1, source_target_pairs={{0,8},{8,0},{1,9},{9,1},{2,10},{10,2},{3,11},{11,3},{4,12},{12,4},... | collective-permute-start | bytes 4718600 | tf_op jit(solution)/shard_map/ppermute | solution.py:648
  447.4 28.0 %collective-permute-start.66 = (bf16[192,2048]{1,0:T(8,128)(2,1)}, bf16[192,2048]{1,0:T(8,128)(2,1)}, u32[]{:S(2)}, u32[]{:S(2)}) collective-permute-start(bf16[192,2048]{1,0:T(8,128)(2,1)} %get-tuple-element.563), channel_id=1, source_target_pairs={{0,16},{16,0},{1,17},{17,1},{2,18},{18,2},{3,19},{19,3},{4,20},{20... | collective-permute-start | bytes 2359304 | tf_op jit(solution)/shard_map/ppermute | solution.py:648
  448.1 27.3 %collective-permute-start.67 = (bf16[192,2048]{1,0:T(8,128)(2,1)}, bf16[192,2048]{1,0:T(8,128)(2,1)}, u32[]{:S(2)}, u32[]{:S(2)}) collective-permute-start(bf16[192,2048]{1,0:T(8,128)(2,1)} %get-tuple-element.564), channel_id=1, source_target_pairs={{0,1},{1,0},{2,3},{3,2},{4,5},{5,4},{6,7},{7,6},{8,9},{9,8},{10,11... | collective-permute-start | bytes 2359304 | tf_op jit(solution)/shard_map/ppermute | solution.py:648
  475.8 51.0 %collective-permute-start.68 = (bf16[192,2048]{1,0:T(8,128)(2,1)}, bf16[192,2048]{1,0:T(8,128)(2,1)}, u32[]{:S(2)}, u32[]{:S(2)}) collective-permute-start(bf16[192,2048]{1,0:T(8,128)(2,1)} %add_convert_fusion.3), channel_id=1, source_target_pairs={{0,16},{16,0},{1,17},{17,1},{2,18},{18,2},{3,19},{19,3},{4,20},{20... | collective-permute-start | bytes 2359304 | tf_op jit(solution)/shard_map/ppermute | solution.py:648
  479.5 25.0 %collective-permute-start.69 = (bf16[256,1024]{1,0:T(8,128)(2,1)S(1)}, bf16[256,1024]{1,0:T(8,128)(2,1)}, u32[]{:S(2)}, u32[]{:S(2)}) collective-permute-start(bf16[256,1024]{1,0:T(8,128)(2,1)S(1)} %get-tuple-element.632), channel_id=1, source_target_pairs={{0,1},{1,0},{2,3},{3,2},{4,5},{5,4},{6,7},{7,6},{8,9},{9,8},{10,11... | collective-permute-start | bytes 1572872 | tf_op jit(solution)/shard_map/ppermute | solution.py:648
  481.1 25.8 %collective-permute-start.70 = (bf16[256,1024]{1,0:T(8,128)(2,1)S(1)}, bf16[256,1024]{1,0:T(8,128)(2,1)}, u32[]{:S(2)}, u32[]{:S(2)}) collective-permute-start(bf16[256,1024]{1,0:T(8,128)(2,1)S(1)} %get-tuple-element.631), channel_id=1, source_target_pairs={{0,2},{2,0},{1,3},{3,1},{4,6},{6,4},{5,7},{7,5},{8,10},{10,8},{9,1... | collective-permute-start | bytes 1572872 | tf_op jit(solution)/shard_map/ppermute | solution.py:648
  482.0 44.8 %collective-permute-start.71 = (bf16[256,1024]{1,0:T(8,128)(2,1)S(1)}, bf16[256,1024]{1,0:T(8,128)(2,1)}, u32[]{:S(2)}, u32[]{:S(2)}) collective-permute-start(bf16[256,1024]{1,0:T(8,128)(2,1)S(1)} %get-tuple-element.630), channel_id=1, source_target_pairs={{0,3},{1,2},{2,1},{3,0},{4,7},{5,6},{6,5},{7,4},{8,11},{9,10},{10,... | collective-permute-start | bytes 1572872 | tf_op jit(solution)/shard_map/ppermute | solution.py:668
  534.9 25.9 %all-to-all-start.3 = ((bf16[8,64,384]{2,1,0:T(8,128)(2,1)}), bf16[8,64,384]{2,1,0:T(8,128)(2,1)S(1)}, u32[]{:S(2)}, u32[]{:S(2)}) async-start(bf16[8,64,384]{2,1,0:T(8,128)(2,1)} %bitcast.50), calls=%async_computation.4 | async-start | bytes 786432 | tf_op jit(solution)/shard_map/all_to_all | solution.py:941
  541.4 21.6 %collective-permute-start.73 = (bf16[192,2048]{1,0:T(8,128)(2,1)}, bf16[192,2048]{1,0:T(8,128)(2,1)}, u32[]{:S(2)}, u32[]{:S(2)}) collective-permute-start(bf16[192,2048]{1,0:T(8,128)(2,1)} %fusion.34), channel_id=1, source_target_pairs={{0,1},{1,0},{2,3},{3,2},{4,5},{5,4},{6,7},{7,6},{8,9},{9,8},{10,11... | collective-permute-start | bytes 2359304 | tf_op jit(solution)/shard_map/ppermute | solution.py:648
  563.0 25.5 %collective-permute-start.80 = (bf16[192,2048]{1,0:T(8,128)(2,1)}, bf16[192,2048]{1,0:T(8,128)(2,1)}, u32[]{:S(2)}, u32[]{:S(2)}) collective-permute-start(bf16[192,2048]{1,0:T(8,128)(2,1)} %fusion.33), channel_id=1, source_target_pairs={{0,2},{2,0},{1,3},{3,1},{4,6},{6,4},{5,7},{7,5},{8,10},{10,8},{9,1... | collective-permute-start | bytes 2359304 | tf_op jit(solution)/shard_map/ppermute | solution.py:648
  (107 other events, 1625.6 us)
Sparse Core Ops, SparseCore 0:
  10.4 30.7 all-gather.2
  42.8 61.4 all-gather.4
  331.6 135.4 reduce-scatter.2
  469.2 55.2 reduce-scatter.4

commit v5 on v4

--- a/solution.py
+++ b/solution.py
@@ -897,9 +897,9 @@
     m = [add_low(f[2], other) for f, other in zip(fed[:2], m_other)]
     m.append([add_low(fed[2][2][n], m_other[2][n]) for n in range(4)])
     m_far = swap(m[2][3], Y)
-    d_attended, right, m, m_far, w_parts, w_x = sync(d_attended, right, m, m_far, w_parts, w_x)
+    w_xc = [swap(jnp.concatenate(w_x, axis=0), C)]
+    d_attended, right, m, m_far, w_parts, w_xc = sync(d_attended, right, m, m_far, w_parts, w_xc)
     w_x.append(swap(w_parts[2], X))
-    w_xc = [swap(jnp.concatenate(w_x[:2], axis=0), C)]
     out_part = dot(jnp.concatenate(left, axis=0), jnp.concatenate(right, axis=0), TN).astype(BF16)
     out_part = out_part.reshape(far, 2, 2, -1, width)
     pick = lambda values, index, axis: lax.dynamic_index_in_dim(values, index, axis, keepdims=False)
@@ -934,14 +934,6 @@
         * (weighted - inputs * scale_one * scale_one * jnp.mean(weighted * inputs, axis=1, keepdims=True))
     ).astype(BF16)
     proj_rows = add_low(take(proj_core, fo), proj_x)
-    m_one = [m[1][0], add_low(m[1][1], m_x)]
-    m_z, spread, input_grad, proj_rows, m, m_one, out_part, gain_parts = sync(
-        m_z, spread, input_grad, proj_rows, m, m_one, out_part, gain_parts
-    )
-    proj = lax.all_to_all(proj_rows, seq, split_axis=0, concat_axis=1, tiled=True)
-    m_last = [swap(m_one[0], X), swap(m_one[1], Y)]
-    m_one.append((m[1][2].astype(F32) + m_z[0].astype(F32) + m_z[1].astype(F32)).astype(BF16))
-    out_z = swap(pick(out_part, 1 - zb, 1), Z)
     gain_row = gain_parts[0]
     pack = jnp.concatenate(
         [
@@ -956,13 +948,20 @@
             pack = pack + swap(pack, axis, offset)
             offset *= 2
     pack = pack.reshape(-1)
+    m_one = [m[1][0], add_low(m[1][1], m_x)]
+    m_z, spread, input_grad, proj_rows, m, m_one, out_part, pack = sync(
+        m_z, spread, input_grad, proj_rows, m, m_one, out_part, pack
+    )
+    proj = lax.all_to_all(proj_rows, seq, split_axis=0, concat_axis=1, tiled=True)
+    m_last = [swap(m_one[0], X), swap(m_one[1], Y)]
+    m_last.append(swap((m[1][2].astype(F32) + m_z[0].astype(F32) + m_z[1].astype(F32)).astype(BF16), Z))
+    out_z = swap(pick(out_part, 1 - zb, 1), Z)
     gate_mine, up_mine = place(spread, own_block, part)
-    proj, gate_mine, up_mine, m, m_one, m_last, out_part, out_z, down_far, pack = sync(
-        proj, gate_mine, up_mine, m, m_one, m_last, out_part, out_z, down_far, pack
+    proj, gate_mine, up_mine, m, m_last, out_part, out_z, down_far = sync(
+        proj, gate_mine, up_mine, m, m_last, out_part, out_z, down_far
     )
     out_part = add_low(pick(out_part, zb, 1), out_z)
     out_got = send_far(out_part, za)
-    m_last.append(swap(m_one[2], Z))
     down_mine = down_far.astype(F32)
     mlp_out = m[0][0].astype(F32) + sum(a.astype(F32) for a in m_last)
     block_output = (residual + mlp_out).astype(BF16)

time: 608 us -> 603 us (level)
  starting transfers between devices: 98.8 us -> 92 us
    ppermute x3, waiting for transfers between devices: 28.7 us -> 8.86 us  [swap_cube(): return lax.ppermute(values, offset, pairs)]
    all_to_all x1, waiting for transfers between devices: 0.01 us -> 13.2 us  [per_device(): lax.all_to_all(proj_rows, seq, split_axis=0, concat_axis=1, tiled=True)]
    ppermute x79, starting transfers between devices: 74.6 us -> 66.6 us  [swap(): return lax.ppermute(values, axis, [(i, i ^ offset) for i in range(size)])]
    ppermute x79, waiting for transfers between devices: 94.3 us -> 101 us  [swap(): return lax.ppermute(values, axis, [(i, i ^ offset) for i in range(size)])]
    unnamed x139 -> x149, local copies, waits for them, and re-layouts: 22.9 us -> 21.2 us
  transfers between devices with their start and end apart: 90 -> 90, of which waited for: 35 -> 35; matrix products, arithmetic and copies ran while one was open for 23% -> 24% of each run, Pallas kernels for 27% -> 27%
where the time goes in v5:
time: 603 us; the launch traced here: 595 us
  waiting for transfers between devices  163 us (27%)
  Pallas kernels  161 us (27%)
  starting transfers between devices  92 us (15%)
  other arithmetic  70.5 us (12%)
  local copies, waits for them, and re-layouts  56.1 us (9%)
  matrix products  36.4 us (6%)
  between operations  15.2 us (3%)
    ppermute x79, waiting for transfers between devices, swap(): return lax.ppermute(values, axis, [(i, i ^ offset) for i in range(size)])  101 us
    ppermute x79, starting transfers between devices, swap(): return lax.ppermute(values, axis, [(i, i ^ offset) for i in range(size)])  66.6 us
    pallas_call x3, Pallas kernels, feed(): pl.pallas_call(functools.partial(feed_kernel, layouts, blocks), grid_spec...  61.7 us
    dot_general x8, matrix products, dot(): return lax.dot_general(left, right, dims, preferred_element_type=F32)  36.4 us
    convert_element_type x13, other arithmetic, add_low(): return (left.astype(F32) + right.astype(F32)).astype(BF16)  31.9 us
    pallas_call x1, Pallas kernels, attend_back(): pl.pallas_call(functools.partial(attend_back_kernel, heads), in_specs=[vm...  26.8 us
    pallas_call x3, Pallas kernels, project(): pl.pallas_call(functools.partial(project_kernel, heads, count, fresh), gr...  22.7 us
    unnamed x149, local copies, waits for them, and re-layouts  21.2 us
  transfers between devices with their start and end apart: 90, of which 35 were waited for; matrix products, arithmetic and copies ran while one was open for 24% of the time, Pallas kernels for 27%

profile of v5, /device:TPU:0, one launch (start us, length us, event | category | flops | bytes accessed | tf_op | source)
XLA Modules:
  0.0 594.6 jit_solution(2560298561033340674)
XLA Ops:
  11.0 4.1 collective-permute-start
  42.8 7.0 %collective-permute-done.refs_0_ = bf16[192,2048]{1,0:T(8,128)(2,1)} collective-permute-done((bf16[192,2048]{1,0:T(8,128)(2,1)S(1)}, bf16[192,2048]{1,0:T(8,128)(2,1)}, u32[]{:S(2)}, u32[]{:S(2)}) %collective-permute-start) | collective-permute-done | bytes 786464 | tf_op jit(solution)/shard_map/ppermute | solution.py:648
  54.3 8.3 %project.3 = (bf16[1536,2048]{1,0:T(8,128)(2,1)}, bf16[4,1536,128]{2,1,0:T(8,128)(2,1)}, bf16[1536,128]{1,0:T(8,128)(2,1)}, bf16[1536,128]{1,0:T(8,128)(2,1)}, f32[1536,384]{1,0:T(8,128)}, /*index=5*/f32[1536,384]{1,0:T(8,128)}) custom-call(s32[3]{0:T(128)} %get-tuple-element.654.index_ref, s32[2]{0:T(128)} %bitcast.185, bf16[192,2048]{1,0:T(8,128)(2,1)} %refs_0_.1, ...), custom_call_target="tpu_custom_call" | custom-call | flops 1000 | bytes 1000 | tf_op jit(solution)/shard_map/project/pallas_call | solution.py:123
  62.6 8.9 %collective-permute-done.4.refs_1_ = bf16[192,2048]{1,0:T(8,128)(2,1)} collective-permute-done((bf16[192,2048]{1,0:T(8,128)(2,1)}, bf16[192,2048]{1,0:T(8,128)(2,1)}, u32[]{:S(2)}, u32[]{:S(2)}) %collective-permute-start.4) | collective-permute-done | bytes 786464 | tf_op jit(solution)/shard_map/ppermute | solution.py:648
  74.3 8.0 %project.4 = (bf16[1536,2048]{1,0:T(8,128)(2,1)}, bf16[4,1536,128]{2,1,0:T(8,128)(2,1)}, bf16[1536,128]{1,0:T(8,128)(2,1)}, bf16[1536,128]{1,0:T(8,128)(2,1)}, f32[1536,384]{1,0:T(8,128)}, /*index=5*/f32[1536,384]{1,0:T(8,128)}) custom-call(s32[3]{0:T(128)} %get-tuple-element.655.index_ref, ...), custom_call_target="tpu_custom_call", output_to_operand_aliasing={{0}: (10, {}), {1}: (11, {}), {2}: (12, {}), {3}: (13, {}),... | custom-call | flops 1000 | bytes 1000 | tf_op jit(solution)/shard_map/project/pallas_call | solution.py:123
  82.3 9.3 %collective-permute-done.6.refs_0_ = bf16[192,2048]{1,0:T(8,128)(2,1)S(1)} collective-permute-done((bf16[192,2048]{1,0:T(8,128)(2,1)}, bf16[192,2048]{1,0:T(8,128)(2,1)S(1)}, u32[]{:S(2)}, u32[]{:S(2)}) %collective-permute-start.6) | collective-permute-done | bytes 786464 | tf_op jit(solution)/shard_map/ppermute | solution.py:648
  99.6 6.4 %project.5 = (bf16[1536,2048]{1,0:T(8,128)(2,1)}, bf16[4,1536,128]{2,1,0:T(8,128)(2,1)}, bf16[1536,128]{1,0:T(8,128)(2,1)}, bf16[1536,128]{1,0:T(8,128)(2,1)}, f32[1536,384]{1,0:T(8,128)}, /*index=5*/f32[1536,384]{1,0:T(8,128)}) custom-call(s32[2]{0:T(128)} %pad_add_fusion.2.index_ref, ...), custom_call_target="tpu_custom_call", output_to_operand_aliasing={{0}: (9, {}), {1}: (10, {}), {2}: (11, {}), {3}: (12, {}), ... | custom-call | flops 1000 | bytes 1000 | tf_op jit(solution)/shard_map/project/pallas_call | solution.py:123
  106.0 10.0 %attend.1 = (bf16[1536,256]{1,0:T(8,128)(2,1)}, f32[1536,256]{1,0:T(8,128)}, bf16[4,1536,128]{2,1,0:T(8,128)(2,1)}) custom-call(bf16[4,1536,128]{2,1,0:T(8,128)(2,1)} %get-tuple-element.352.q_ref, bf16[1536,128]{1,0:T(8,128)(2,1)} %get-tuple-element.353.k_ref, bf16[1536,128]{1,0:T(8,128)(2,1)} %get-tuple-element.354.v_ref), custom_call_target="tpu_custom_call" | custom-call | flops 1000 | bytes 1000 | tf_op jit(solution)/shard_map/attend/pallas_call | solution.py:215
  116.0 3.1 collective-permute-done.12.refs_7_.refs_8_
  122.1 4.3 all-to-all-start
  132.8 14.5 %all-to-all-done = bf16[8,192,256]{2,1,0:T(8,128)(2,1)S(1)} async-done(((bf16[8,192,256]{2,1,0:T(8,128)(2,1)}), bf16[8,192,256]{2,1,0:T(8,128)(2,1)S(1)}, u32[]{:S(2)}, u32[]{:S(2)}) %all-to-all-start) | async-done | bytes 786464 | tf_op jit(solution)/shard_map/all_to_all | solution.py:794
  150.6 4.3 collective-permute-done.17.refs_9_.refs_10_
  159.1 5.6 multiply_reduce_fusion.2
  172.3 11.1 %feed.3 = (bf16[1,192,2048]{2,1,0:T(8,128)(2,1)}, bf16[1,192,2048]{2,1,0:T(8,128)(2,1)}, bf16[1,192,2048]{2,1,0:T(8,128)(2,1)}, bf16[1,192,2048]{2,1,0:T(8,128)(...) custom-call(s32[2]{0:T(128)} %multiply_add_fusion.3.index_ref, ...), custom_call_target="tpu_custom_call" | custom-call | flops 1000 | bytes 1000 | tf_op jit(solution)/shard_map/feed/pallas_call | solution.py:481
  183.4 4.9 collective-permute-done.25.refs_0_.refs_2_
  199.9 22.4 %feed.4 = (bf16[3,192,2048]{2,1,0:T(8,128)(2,1)}, bf16[3,192,2048]{2,1,0:T(8,128)(2,1)}, bf16[3,192,2048]{2,1,0:T(8,128)(2,1)}, bf16[3,192,2048]{2,1,0:T(8,128)(...) custom-call(s32[2]{0:T(128)} %multiply_add_fusion.3.index_ref, bf16[192,2048]{1,0:T(8,128)(2,1)} %copy-done.11, ...), custom_call_target="tpu_custom_call" | custom-call | flops 1000 | bytes 1000 | tf_op jit(solution)/shard_map/feed/pallas_call | solution.py:481
  222.3 8.9 %collective-permute-done.33.refs_3_.refs_9_ = bf16[192,2048]{1,0:T(8,128)(2,1)} collective-permute-done((bf16[192,2048]{1,0:T(8,128)(2,1)}, bf16[192,2048]{1,0:T(8,128)(2,1)}, u32[]{:S(2)}, u32[]{:S(2)}) %collective-permute-start.33) | collective-permute-done | bytes 786464 | tf_op jit(solution)/shard_map/ppermute | solution.py:668
  243.1 28.2 %feed.5 = (bf16[4,192,2048]{2,1,0:T(8,128)(2,1)}, bf16[4,192,2048]{2,1,0:T(8,128)(2,1)}, bf16[4,192,2048]{2,1,0:T(8,128)(2,1)}, bf16[4,192,2048]{2,1,0:T(8,128)(...) custom-call(s32[2]{0:T(128)} %multiply_add_fusion.3.index_ref, ...), custom_call_target="tpu_custom_call" | custom-call | flops 1000 | bytes 1000 | tf_op jit(solution)/shard_map/feed/pallas_call | solution.py:481
  271.5 5.9 collective-permute-done.44
  277.4 3.2 add_convert_fusion
  285.1 13.6 %down_grad.1 = bf16[512,2048]{1,0:T(8,128)(2,1)} custom-call(bf16[192,2048]{1,0:T(8,128)(2,1)} %refs_0_.2, bf16[192,2048]{1,0:T(8,128)(2,1)} %copy-done.19, bf16[192,2048]{1,0:T(8,128)(2,1)} %copy-done.6, bf16[192,2048]{1,0:T(8,128)(2,1)} %copy-done.7, bf16[192,2048]{1,0:T(8,128)(2,1)} %copy-done.8, ...), custom_call_target="tpu_custom_call" | custom-call | flops 1000 | bytes 1000 | tf_op jit(solution)/shard_map/down_grad/pallas_call | solution.py:593
  298.7 3.3 collective-permute-done.45
  310.8 20.6 %gate_grad.1 = bf16[2048,1024]{1,0:T(8,128)(2,1)} custom-call(bf16[192,2048]{1,0:T(8,128)(2,1)} %multiply_convert_fusion.refs_0_, bf16[192,2048]{1,0:T(8,128)(2,1)} %collective-permute-done.28.refs_1_, bf16[192,2048]{1,0:T(8,128)(2,1)} %copy-done.11, bf16[192,2048]{1,0:T(8,128)(2,1)} %copy-done.12, bf16[192,2048]{1,0:T(8,128)(2,1)} %copy-done.13, ...), custom_call_target="tpu_custom_call" | custom-call | flops 1000 | bytes 1000 | tf_op jit(solution)/shard_map/gate_grad/pallas_call | solution.py:557
  334.9 3.2 multiply_reduce_fusion
  339.5 6.5 %convolution_convert_fusion.1 = bf16[192,2048]{1,0:T(8,128)(2,1)S(1)} fusion(bf16[192,2048]{1,0:T(8,128)(2,1)} %fusion.64, bf16[2048,2048]{1,0:T(8,128)(2,1)} %all-gather.5.cloned.1.call-done), kind=kOutput, calls=%fused_computation.29 | convolution fusion | flops 1611005952 | bytes 9961472 | tf_op jit(solution)/shard_map/dot_general | solution.py:29
  351.4 5.2 all-to-all-start.1
  356.6 5.3 fusion.47
  369.0 4.2 add_convert_fusion.1
  373.2 12.6 %collective-permute-done.59 = bf16[192,2048]{1,0:T(8,128)(2,1)} collective-permute-done((bf16[192,2048]{1,0:T(8,128)(2,1)S(1)}, bf16[192,2048]{1,0:T(8,128)(2,1)}, u32[]{:S(2)}, u32[]{:S(2)}) %collective-permute-start.59) | collective-permute-done | bytes 786464 | tf_op jit(solution)/shard_map/ppermute | solution.py:648
  385.8 9.4 %all-to-all-done.1 = bf16[192,8,256]{2,0,1:T(8,128)(2,1)} async-done(((bf16[192,8,256]{2,0,1:T(8,128)(2,1)}), bf16[192,8,256]{2,0,1:T(8,128)(2,1)}, u32[]{:S(2)}, u32[]{:S(2)}) %all-to-all-start.1) | async-done | bytes 786464 | tf_op jit(solution)/shard_map/all_to_all | solution.py:894
  396.7 3.9 fusion.18
  404.6 26.8 %attend_back.1 = (bf16[1536,384]{1,0:T(8,128)(2,1)}, f32[8,384]{1,0:T(8,128)}) custom-call(bf16[4,1536,128]{2,1,0:T(8,128)(2,1)} %get-tuple-element.365.q_ref, bf16[1536,128]{1,0:T(8,128)(2,1)} %get-tuple-element.353.k_ref, bf16[1536,128]{1,0:T(8,128)(2,1)} %get-tuple-element.354.v_ref, bf16[1536,256]{1,0:T(8,128)(2,1)} %bitcast.25.grad_ref, ...), custom_call_target="tpu_custom_call" | custom-call | flops 1000 | bytes 1000 | tf_op jit(solution)/shard_map/attend_back/pallas_call | solution.py:347
  432.0 4.3 all-to-all-start.2
  436.3 6.6 %convolution_convert_fusion = bf16[2048,384]{1,0:T(8,128)(2,1)S(1)} fusion(bf16[1536,2048]{1,0:T(8,128)(2,1)} %get-tuple-element.552, bf16[1536,384]{1,0:T(8,128)(2,1)} %get-tuple-element.551), kind=kOutput, calls=%fused_computation.24 | convolution fusion | flops 2416705536 | bytes 9043968 | tf_op jit(solution)/shard_map/dot_general | solution.py:29
  448.9 2.9 fusion.21
  457.8 15.0 %all-to-all-done.2 = bf16[8,192,384]{2,1,0:T(8,128)(2,1)} async-done(((bf16[8,192,384]{2,1,0:T(8,128)(2,1)}), bf16[8,192,384]{2,1,0:T(8,128)(2,1)}, u32[]{:S(2)}, u32[]{:S(2)}) %all-to-all-start.2) | async-done | bytes 1179680 | tf_op jit(solution)/shard_map/all_to_all | solution.py:913
  479.4 2.9 constant_dynamic-slice_fusion
  485.8 3.1 convolution_bitcast_fusion.1
  488.9 3.8 convolution_bitcast_fusion
  496.6 3.6 fusion.36
  500.2 3.1 fusion.39
  514.4 15.6 %collective-permute-done.75 = f32[17,128]{1,0:T(8,128)S(1)} collective-permute-done((f32[17,128]{1,0:T(8,128)S(1)}, f32[17,128]{1,0:T(8,128)S(1)}, u32[]{:S(2)}, u32[]{:S(2)}) %collective-permute-start.75) | collective-permute-done | bytes 8736 | tf_op jit(solution)/shard_map/ppermute | solution.py:648
  535.9 2.9 fusion.33
  539.2 5.3 all-to-all-start.3
  547.4 5.7 place.1
  553.7 13.2 %all-to-all-done.3 = bf16[8,64,384]{2,1,0:T(8,128)(2,1)S(1)} async-done(((bf16[8,64,384]{2,1,0:T(8,128)(2,1)}), bf16[8,64,384]{2,1,0:T(8,128)(2,1)S(1)}, u32[]{:S(2)}, u32[]{:S(2)}) %all-to-all-start.3) | async-done | bytes 393248 | tf_op jit(solution)/shard_map/all_to_all | solution.py:955
  567.0 6.4 %collective-permute-done.80 = bf16[2,64,2048]{2,1,0:T(8,128)(2,1)} collective-permute-done((bf16[2,64,2048]{2,1,0:T(8,128)(2,1)}, bf16[2,64,2048]{2,1,0:T(8,128)(2,1)}, u32[]{:S(2)}, u32[]{:S(2)}) %collective-permute-start.80) | collective-permute-done | bytes 524320 | tf_op jit(solution)/shard_map/ppermute | solution.py:648
  577.3 3.1 fusion.31
  (391 shorter events, 188.9 us)
Async XLA Ops:
  7.2 47.1 %all-gather.3.cloned.1.call-start = ((), (), s32[]{:S(2)}) async-start(), calls=%async_computation.6 | async-start | bytes 1966080 | tf_op jit(solution)/shard_map/all_gather | solution.py:743
  10.3 148.9 %all-gather.5.cloned.1.call-start = ((), (), s32[]{:S(2)}) async-start(), calls=%async_computation.7 | async-start | bytes 10485760 | tf_op jit(solution)/shard_map/all_gather | solution.py:744
  11.0 38.7 %collective-permute-start = (bf16[192,2048]{1,0:T(8,128)(2,1)S(1)}, bf16[192,2048]{1,0:T(8,128)(2,1)}, u32[]{:S(2)}, u32[]{:S(2)}) collective-permute-start(bf16[192,2048]{1,0:T(8,128)(2,1)S(1)} %copy-done.14), channel_id=1, source_target_pairs={{0,4},{4,0},{1,5},{5,1},{2,6},{6,2},{3,7},{7,3},{8,12},{12,8},{9,1... | collective-permute-start | bytes 2359304 | tf_op jit(solution)/shard_map/ppermute | solution.py:648
  15.1 34.6 %collective-permute-start.1 = (bf16[192,2048]{1,0:T(8,128)(2,1)S(1)}, bf16[192,2048]{1,0:T(8,128)(2,1)}, u32[]{:S(2)}, u32[]{:S(2)}) collective-permute-start(bf16[192,2048]{1,0:T(8,128)(2,1)S(1)} %copy-done.14), channel_id=1, source_target_pairs={{0,1},{1,0},{2,3},{3,2},{4,5},{5,4},{6,7},{7,6},{8,9},{9,8},{10,11... | collective-permute-start | bytes 2359304 | tf_op jit(solution)/shard_map/ppermute | solution.py:648
  16.7 34.5 %collective-permute-start.2 = (bf16[192,2048]{1,0:T(8,128)(2,1)S(1)}, bf16[192,2048]{1,0:T(8,128)(2,1)}, u32[]{:S(2)}, u32[]{:S(2)}) collective-permute-start(bf16[192,2048]{1,0:T(8,128)(2,1)S(1)} %copy-done.14), channel_id=1, source_target_pairs={{0,2},{2,0},{1,3},{3,1},{4,6},{6,4},{5,7},{7,5},{8,10},{10,8},{9,1... | collective-permute-start | bytes 2359304 | tf_op jit(solution)/shard_map/ppermute | solution.py:648
  18.2 32.9 %collective-permute-start.3 = (bf16[192,2048]{1,0:T(8,128)(2,1)S(1)}, bf16[192,2048]{1,0:T(8,128)(2,1)S(1)}, u32[]{:S(2)}, u32[]{:S(2)}) collective-permute-start(bf16[192,2048]{1,0:T(8,128)(2,1)S(1)} %copy-done.1), channel_id=1, source_target_pairs={{0,16},{16,0},{1,17},{17,1},{2,18},{18,2},{3,19},{19,3},{4,20},{20... | collective-permute-start | bytes 2359304 | tf_op jit(solution)/shard_map/ppermute | solution.py:648
  51.2 41.5 %collective-permute-start.8 = (bf16[512,3072]{1,0:T(8,128)(2,1)}, bf16[512,3072]{1,0:T(8,128)(2,1)}, u32[]{:S(2)}, u32[]{:S(2)}) collective-permute-start(bf16[512,3072]{1,0:T(8,128)(2,1)} %bitcast.84), channel_id=1, source_target_pairs={{0,8},{8,0},{1,9},{9,1},{2,10},{10,2},{3,11},{11,3},{4,12},{12,4},... | collective-permute-start | bytes 9437192 | tf_op jit(solution)/shard_map/ppermute | solution.py:648
  53.0 29.3 %collective-permute-start.9 = (bf16[192,2048]{1,0:T(8,128)(2,1)S(1)}, bf16[192,2048]{1,0:T(8,128)(2,1)S(1)}, u32[]{:S(2)}, u32[]{:S(2)}) collective-permute-start(bf16[192,2048]{1,0:T(8,128)(2,1)S(1)} %copy-done.1), channel_id=1, source_target_pairs={{0,8},{8,0},{1,9},{9,1},{2,10},{10,2},{3,11},{11,3},{4,12},{12,4},... | collective-permute-start | bytes 2359304 | tf_op jit(solution)/shard_map/ppermute | solution.py:648
  92.6 27.6 %collective-permute-start.10 = (bf16[192,2048]{1,0:T(8,128)(2,1)S(1)}, bf16[192,2048]{1,0:T(8,128)(2,1)S(1)}, u32[]{:S(2)}, u32[]{:S(2)}) collective-permute-start(bf16[192,2048]{1,0:T(8,128)(2,1)S(1)} %copy-done.1), channel_id=1, source_target_pairs={{0,1},{1,0},{2,3},{3,2},{4,5},{5,4},{6,7},{7,6},{8,9},{9,8},{10,11... | collective-permute-start | bytes 2359304 | tf_op jit(solution)/shard_map/ppermute | solution.py:648
  93.9 26.3 %collective-permute-start.11 = (bf16[192,2048]{1,0:T(8,128)(2,1)S(1)}, bf16[192,2048]{1,0:T(8,128)(2,1)S(1)}, u32[]{:S(2)}, u32[]{:S(2)}) collective-permute-start(bf16[192,2048]{1,0:T(8,128)(2,1)S(1)} %copy-done.1), channel_id=1, source_target_pairs={{0,2},{2,0},{1,3},{3,1},{4,6},{6,4},{5,7},{7,5},{8,10},{10,8},{9,1... | collective-permute-start | bytes 2359304 | tf_op jit(solution)/shard_map/ppermute | solution.py:648
  95.0 25.3 %collective-permute-start.14 = (bf16[128,3072]{1,0:T(8,128)(2,1)}, bf16[128,3072]{1,0:T(8,128)(2,1)}, u32[]{:S(2)}, u32[]{:S(2)}) collective-permute-start(bf16[128,3072]{1,0:T(8,128)(2,1)} %bitcast.177), channel_id=1, source_target_pairs={{0,16},{16,0},{1,17},{17,1},{2,18},{18,2},{3,19},{19,3},{4,20},{20... | collective-permute-start | bytes 2359304 | tf_op jit(solution)/shard_map/ppermute | solution.py:648
  98.0 22.3 %collective-permute-start.13 = (bf16[96,2048]{1,0:T(8,128)(2,1)}, bf16[96,2048]{1,0:T(8,128)(2,1)}, u32[]{:S(2)}, u32[]{:S(2)}) collective-permute-start(bf16[96,2048]{1,0:T(8,128)(2,1)} %slice.115), channel_id=1, source_target_pairs={{0,2},{2,0},{1,3},{3,1},{4,6},{6,4},{5,7},{7,5},{8,10},{10,8},{9,1... | collective-permute-start | bytes 1179656 | tf_op jit(solution)/shard_map/ppermute | solution.py:648
  122.1 32.8 %collective-permute-start.19 = (bf16[576,2048]{1,0:T(8,128)(2,1)}, bf16[576,2048]{1,0:T(8,128)(2,1)}, u32[]{:S(2)}, u32[]{:S(2)}) collective-permute-start(bf16[576,2048]{1,0:T(8,128)(2,1)} %pad_maximum_fusion.2), channel_id=1, source_target_pairs={{0,8},{8,0},{1,9},{9,1},{2,10},{10,2},{3,11},{11,3},{4,12},{12,4},... | collective-permute-start | bytes 7077896 | tf_op jit(solution)/shard_map/ppermute | solution.py:648
  122.1 25.3 %all-to-all-start = ((bf16[8,192,256]{2,1,0:T(8,128)(2,1)}), bf16[8,192,256]{2,1,0:T(8,128)(2,1)S(1)}, u32[]{:S(2)}, u32[]{:S(2)}) async-start(bf16[8,192,256]{2,1,0:T(8,128)(2,1)} %bitcast.178), calls=%async_computation | async-start | bytes 1572864 | tf_op jit(solution)/shard_map/all_to_all | solution.py:794
  126.4 349.0 %reduce-scatter.3.cloned.1.call-start = ((), (), s32[]{:S(2)}) async-start(), calls=%async_computation.8 | async-start | bytes 6291456 | tf_op jit(solution)/shard_map/reduce_scatter | solution.py:868
  126.5 28.4 %collective-permute-start.17 = (bf16[192,2048]{1,0:T(8,128)(2,1)S(1)}, bf16[192,2048]{1,0:T(8,128)(2,1)}, u32[]{:S(2)}, u32[]{:S(2)}) collective-permute-start(bf16[192,2048]{1,0:T(8,128)(2,1)S(1)} %collective-permute-done.11.refs_6_.refs_4_), channel_id=1, source_target_pairs={{0,1},{1,0},{2,3},{3,2},{4,5},{5,4},{6,7},{7,6},{8,9},{9,8},{10,11... | collective-permute-start | bytes 2359304 | tf_op jit(solution)/shard_map/ppermute | solution.py:648
  191.7 30.6 %collective-permute-start.30 = (bf16[192,2048]{1,0:T(8,128)(2,1)}, bf16[192,2048]{1,0:T(8,128)(2,1)}, u32[]{:S(2)}, u32[]{:S(2)}) collective-permute-start(bf16[192,2048]{1,0:T(8,128)(2,1)} %copy-done.11), channel_id=1, source_target_pairs={{0,1},{1,0},{2,3},{3,2},{4,5},{5,4},{6,7},{7,6},{8,9},{9,8},{10,11... | collective-permute-start | bytes 2359304 | tf_op jit(solution)/shard_map/ppermute | solution.py:648
  193.1 29.2 %collective-permute-start.31 = (bf16[192,2048]{1,0:T(8,128)(2,1)}, bf16[192,2048]{1,0:T(8,128)(2,1)}, u32[]{:S(2)}, u32[]{:S(2)}) collective-permute-start(bf16[192,2048]{1,0:T(8,128)(2,1)} %copy-done.13), channel_id=1, source_target_pairs={{0,16},{16,0},{1,17},{17,1},{2,18},{18,2},{3,19},{19,3},{4,20},{20... | collective-permute-start | bytes 2359304 | tf_op jit(solution)/shard_map/ppermute | solution.py:648
  193.7 28.7 %collective-permute-start.32 = (bf16[192,2048]{1,0:T(8,128)(2,1)}, bf16[192,2048]{1,0:T(8,128)(2,1)}, u32[]{:S(2)}, u32[]{:S(2)}) collective-permute-start(bf16[192,2048]{1,0:T(8,128)(2,1)} %copy-done.12), channel_id=1, source_target_pairs={{0,2},{2,0},{1,3},{3,1},{4,6},{6,4},{5,7},{7,5},{8,10},{10,8},{9,1... | collective-permute-start | bytes 2359304 | tf_op jit(solution)/shard_map/ppermute | solution.py:648
  196.2 35.0 %collective-permute-start.33 = (bf16[192,2048]{1,0:T(8,128)(2,1)}, bf16[192,2048]{1,0:T(8,128)(2,1)}, u32[]{:S(2)}, u32[]{:S(2)}) collective-permute-start(bf16[192,2048]{1,0:T(8,128)(2,1)} %multiply_convert_fusion.refs_0_), channel_id=1, source_target_pairs={{0,19},{1,18},{2,17},{3,16},{16,3},{17,2},{18,1},{19,0},{4,23},{5,... | collective-permute-start | bytes 2359304 | tf_op jit(solution)/shard_map/ppermute | solution.py:668
  198.5 23.8 %collective-permute-start.36 = (bf16[96,2048]{1,0:T(8,128)(2,1)}, bf16[96,2048]{1,0:T(8,128)(2,1)}, u32[]{:S(2)}, u32[]{:S(2)}) collective-permute-start(bf16[96,2048]{1,0:T(8,128)(2,1)} %collective-permute-done.20.refs_11_.refs_12_), channel_id=1, source_target_pairs={{0,8},{8,0},{1,9},{9,1},{2,10},{10,2},{3,11},{11,3},{4,12},{12,4},... | collective-permute-start | bytes 1179656 | tf_op jit(solution)/shard_map/ppermute | solution.py:648
  234.0 37.3 %collective-permute-start.43 = (bf16[128,3072]{1,0:T(8,128)(2,1)}, bf16[128,3072]{1,0:T(8,128)(2,1)}, u32[]{:S(2)}, u32[]{:S(2)}) collective-permute-start(bf16[128,3072]{1,0:T(8,128)(2,1)} %bitcast.88), channel_id=1, source_target_pairs={{0,16},{16,0},{1,17},{17,1},{2,18},{18,2},{3,19},{19,3},{4,20},{20... | collective-permute-start | bytes 2359304 | tf_op jit(solution)/shard_map/ppermute | solution.py:648
  238.6 32.8 %collective-permute-start.39 = (bf16[192,2048]{1,0:T(8,128)(2,1)}, bf16[192,2048]{1,0:T(8,128)(2,1)S(1)}, u32[]{:S(2)}, u32[]{:S(2)}) collective-permute-start(bf16[192,2048]{1,0:T(8,128)(2,1)} %get-tuple-element.625), channel_id=1, source_target_pairs={{0,16},{16,0},{1,17},{17,1},{2,18},{18,2},{3,19},{19,3},{4,20},{20... | collective-permute-start | bytes 2359304 | tf_op jit(solution)/shard_map/ppermute | solution.py:648
  239.1 32.3 %collective-permute-start.40 = (bf16[192,2048]{1,0:T(8,128)(2,1)}, bf16[192,2048]{1,0:T(8,128)(2,1)S(1)}, u32[]{:S(2)}, u32[]{:S(2)}) collective-permute-start(bf16[192,2048]{1,0:T(8,128)(2,1)} %get-tuple-element.624), channel_id=1, source_target_pairs={{0,1},{1,0},{2,3},{3,2},{4,5},{5,4},{6,7},{7,6},{8,9},{9,8},{10,11... | collective-permute-start | bytes 2359304 | tf_op jit(solution)/shard_map/ppermute | solution.py:648
  240.5 30.9 %collective-permute-start.41 = (bf16[192,2048]{1,0:T(8,128)(2,1)}, bf16[192,2048]{1,0:T(8,128)(2,1)S(1)}, u32[]{:S(2)}, u32[]{:S(2)}) collective-permute-start(bf16[192,2048]{1,0:T(8,128)(2,1)} %get-tuple-element.623), channel_id=1, source_target_pairs={{0,2},{2,0},{1,3},{3,1},{4,6},{6,4},{5,7},{7,5},{8,10},{10,8},{9,1... | collective-permute-start | bytes 2359304 | tf_op jit(solution)/shard_map/ppermute | solution.py:648
  303.5 28.0 %collective-permute-start.51 = (bf16[3,192,2048]{2,1,0:T(8,128)(2,1)}, bf16[3,192,2048]{2,1,0:T(8,128)(2,1)}, u32[]{:S(2)}, u32[]{:S(2)}) collective-permute-start(bf16[3,192,2048]{2,1,0:T(8,128)(2,1)} %get-tuple-element.501), channel_id=1, source_target_pairs={{0,8},{8,0},{1,9},{9,1},{2,10},{10,2},{3,11},{11,3},{4,12},{12,4},... | collective-permute-start | bytes 7077896 | tf_op jit(solution)/shard_map/ppermute | solution.py:648
  305.8 25.6 %collective-permute-start.48 = (bf16[192,2048]{1,0:T(8,128)(2,1)}, bf16[192,2048]{1,0:T(8,128)(2,1)S(1)}, u32[]{:S(2)}, u32[]{:S(2)}) collective-permute-start(bf16[192,2048]{1,0:T(8,128)(2,1)} %add_convert_fusion.10), channel_id=1, source_target_pairs={{0,18},{2,16},{16,2},{18,0},{1,19},{3,17},{17,3},{19,1},{4,22},{6,... | collective-permute-start | bytes 2359304 | tf_op jit(solution)/shard_map/ppermute | solution.py:668
  349.8 23.4 %collective-permute-start.60 = (bf16[256,3072]{1,0:T(8,128)(2,1)}, bf16[256,3072]{1,0:T(8,128)(2,1)}, u32[]{:S(2)}, u32[]{:S(2)}) collective-permute-start(bf16[256,3072]{1,0:T(8,128)(2,1)} %pad_maximum_fusion.4), channel_id=1, source_target_pairs={{0,8},{8,0},{1,9},{9,1},{2,10},{10,2},{3,11},{11,3},{4,12},{12,4},... | collective-permute-start | bytes 4718600 | tf_op jit(solution)/shard_map/ppermute | solution.py:648
  350.3 22.9 %collective-permute-start.56 = (bf16[192,2048]{1,0:T(8,128)(2,1)}, bf16[192,2048]{1,0:T(8,128)(2,1)}, u32[]{:S(2)}, u32[]{:S(2)}) collective-permute-start(bf16[192,2048]{1,0:T(8,128)(2,1)} %fusion.64), channel_id=1, source_target_pairs={{0,8},{8,0},{1,9},{9,1},{2,10},{10,2},{3,11},{11,3},{4,12},{12,4},... | collective-permute-start | bytes 2359304 | tf_op jit(solution)/shard_map/ppermute | solution.py:648
  351.4 43.9 %all-to-all-start.1 = ((bf16[192,8,256]{2,0,1:T(8,128)(2,1)}), bf16[192,8,256]{2,0,1:T(8,128)(2,1)}, u32[]{:S(2)}, u32[]{:S(2)}) async-start(bf16[192,8,256]{2,0,1:T(8,128)(2,1)} %bitcast.162), calls=%async_computation.1 | async-start | bytes 1572864 | tf_op jit(solution)/shard_map/all_to_all | solution.py:894
  361.9 23.9 %collective-permute-start.59 = (bf16[192,2048]{1,0:T(8,128)(2,1)S(1)}, bf16[192,2048]{1,0:T(8,128)(2,1)}, u32[]{:S(2)}, u32[]{:S(2)}) collective-permute-start(bf16[192,2048]{1,0:T(8,128)(2,1)S(1)} %get-tuple-element.613), channel_id=1, source_target_pairs={{0,1},{1,0},{2,3},{3,2},{4,5},{5,4},{6,7},{7,6},{8,9},{9,8},{10,11... | collective-permute-start | bytes 2359304 | tf_op jit(solution)/shard_map/ppermute | solution.py:648
  366.7 28.6 %collective-permute-start.58 = (bf16[192,2048]{1,0:T(8,128)(2,1)}, bf16[192,2048]{1,0:T(8,128)(2,1)}, u32[]{:S(2)}, u32[]{:S(2)}) collective-permute-start(bf16[192,2048]{1,0:T(8,128)(2,1)} %collective-permute-done.57), channel_id=1, source_target_pairs={{0,8},{8,0},{1,9},{9,1},{2,10},{10,2},{3,11},{11,3},{4,12},{12,4},... | collective-permute-start | bytes 2359304 | tf_op jit(solution)/shard_map/ppermute | solution.py:648
  395.2 36.7 %collective-permute-start.61 = (bf16[256,3072]{1,0:T(8,128)(2,1)}, bf16[256,3072]{1,0:T(8,128)(2,1)}, u32[]{:S(2)}, u32[]{:S(2)}) collective-permute-start(bf16[256,3072]{1,0:T(8,128)(2,1)} %bitcast.172), channel_id=1, source_target_pairs={{0,16},{16,0},{1,17},{17,1},{2,18},{18,2},{3,19},{19,3},{4,20},{20... | collective-permute-start | bytes 4718600 | tf_op jit(solution)/shard_map/ppermute | solution.py:648
  403.1 28.3 %collective-permute-start.62 = (bf16[2,2,64,2048]{3,2,0,1:T(8,128)(2,1)}, bf16[2,2,64,2048]{3,2,0,1:T(8,128)(2,1)}, u32[]{:S(2)}, u32[]{:S(2)}) collective-permute-start(bf16[2,2,64,2048]{3,2,0,1:T(8,128)(2,1)} %copy_bitcast_fusion), channel_id=1, source_target_pairs={{0,1},{1,0},{2,3},{3,2},{4,5},{5,4},{6,7},{7,6},{8,9},{9,8},{10,11... | collective-permute-start | bytes 3145736 | tf_op jit(solution)/shard_map/ppermute | solution.py:648
  432.0 40.9 %all-to-all-start.2 = ((bf16[8,192,384]{2,1,0:T(8,128)(2,1)}), bf16[8,192,384]{2,1,0:T(8,128)(2,1)}, u32[]{:S(2)}, u32[]{:S(2)}) async-start(bf16[8,192,384]{2,1,0:T(8,128)(2,1)} %bitcast.176), calls=%async_computation.2 | async-start | bytes 2359296 | tf_op jit(solution)/shard_map/all_to_all | solution.py:913
  436.2 130.8 %reduce-scatter.5.cloned.1.call-start = ((), (), s32[]{:S(2)}) async-start(), calls=%async_computation.9 | async-start | bytes 3145728 | tf_op jit(solution)/shard_map/reduce_scatter | solution.py:869
  445.0 30.4 %collective-permute-start.65 = (bf16[256,3072]{1,0:T(8,128)(2,1)}, bf16[256,3072]{1,0:T(8,128)(2,1)}, u32[]{:S(2)}, u32[]{:S(2)}) collective-permute-start(bf16[256,3072]{1,0:T(8,128)(2,1)} %collective-permute-done.61), channel_id=1, source_target_pairs={{0,8},{8,0},{1,9},{9,1},{2,10},{10,2},{3,11},{11,3},{4,12},{12,4},... | collective-permute-start | bytes 4718600 | tf_op jit(solution)/shard_map/ppermute | solution.py:648
  445.6 29.8 %collective-permute-start.66 = (bf16[192,2048]{1,0:T(8,128)(2,1)}, bf16[192,2048]{1,0:T(8,128)(2,1)}, u32[]{:S(2)}, u32[]{:S(2)}) collective-permute-start(bf16[192,2048]{1,0:T(8,128)(2,1)} %get-tuple-element.560), channel_id=1, source_target_pairs={{0,16},{16,0},{1,17},{17,1},{2,18},{18,2},{3,19},{19,3},{4,20},{20... | collective-permute-start | bytes 2359304 | tf_op jit(solution)/shard_map/ppermute | solution.py:648
  447.1 28.3 %collective-permute-start.67 = (bf16[192,2048]{1,0:T(8,128)(2,1)}, bf16[192,2048]{1,0:T(8,128)(2,1)}, u32[]{:S(2)}, u32[]{:S(2)}) collective-permute-start(bf16[192,2048]{1,0:T(8,128)(2,1)} %get-tuple-element.561), channel_id=1, source_target_pairs={{0,1},{1,0},{2,3},{3,2},{4,5},{5,4},{6,7},{7,6},{8,9},{9,8},{10,11... | collective-permute-start | bytes 2359304 | tf_op jit(solution)/shard_map/ppermute | solution.py:648
  478.0 56.7 %collective-permute-start.68 = (bf16[192,2048]{1,0:T(8,128)(2,1)}, bf16[192,2048]{1,0:T(8,128)(2,1)}, u32[]{:S(2)}, u32[]{:S(2)}) collective-permute-start(bf16[192,2048]{1,0:T(8,128)(2,1)} %add_convert_fusion.3), channel_id=1, source_target_pairs={{0,16},{16,0},{1,17},{17,1},{2,18},{18,2},{3,19},{19,3},{4,20},{20... | collective-permute-start | bytes 2359304 | tf_op jit(solution)/shard_map/ppermute | solution.py:648
  482.3 52.3 %collective-permute-start.69 = (bf16[256,1024]{1,0:T(8,128)(2,1)}, bf16[256,1024]{1,0:T(8,128)(2,1)}, u32[]{:S(2)}, u32[]{:S(2)}) collective-permute-start(bf16[256,1024]{1,0:T(8,128)(2,1)} %get-tuple-element.628), channel_id=1, source_target_pairs={{0,1},{1,0},{2,3},{3,2},{4,5},{5,4},{6,7},{7,6},{8,9},{9,8},{10,11... | collective-permute-start | bytes 1572872 | tf_op jit(solution)/shard_map/ppermute | solution.py:648
  483.8 50.8 %collective-permute-start.70 = (bf16[256,1024]{1,0:T(8,128)(2,1)}, bf16[256,1024]{1,0:T(8,128)(2,1)}, u32[]{:S(2)}, u32[]{:S(2)}) collective-permute-start(bf16[256,1024]{1,0:T(8,128)(2,1)} %get-tuple-element.627), channel_id=1, source_target_pairs={{0,2},{2,0},{1,3},{3,1},{4,6},{6,4},{5,7},{7,5},{8,10},{10,8},{9,1... | collective-permute-start | bytes 1572872 | tf_op jit(solution)/shard_map/ppermute | solution.py:648
  483.8 50.8 %collective-permute-start.71 = (bf16[256,1024]{1,0:T(8,128)(2,1)}, bf16[256,1024]{1,0:T(8,128)(2,1)}, u32[]{:S(2)}, u32[]{:S(2)}) collective-permute-start(bf16[256,1024]{1,0:T(8,128)(2,1)} %get-tuple-element.626), channel_id=1, source_target_pairs={{0,3},{1,2},{2,1},{3,0},{4,7},{5,6},{6,5},{7,4},{8,11},{9,10},{10,... | collective-permute-start | bytes 1572872 | tf_op jit(solution)/shard_map/ppermute | solution.py:668
  534.7 38.8 %collective-permute-start.77 = (bf16[192,2048]{1,0:T(8,128)(2,1)}, bf16[192,2048]{1,0:T(8,128)(2,1)}, u32[]{:S(2)}, u32[]{:S(2)}) collective-permute-start(bf16[192,2048]{1,0:T(8,128)(2,1)} %slice_bitcast_fusion.7), channel_id=1, source_target_pairs={{0,16},{16,0},{1,17},{17,1},{2,18},{18,2},{3,19},{19,3},{4,20},{20... | collective-permute-start | bytes 2359304 | tf_op jit(solution)/shard_map/ppermute | solution.py:648
  535.6 37.9 %collective-permute-start.78 = (bf16[192,2048]{1,0:T(8,128)(2,1)}, bf16[192,2048]{1,0:T(8,128)(2,1)}, u32[]{:S(2)}, u32[]{:S(2)}) collective-permute-start(bf16[192,2048]{1,0:T(8,128)(2,1)} %fusion.34), channel_id=1, source_target_pairs={{0,1},{1,0},{2,3},{3,2},{4,5},{5,4},{6,7},{7,6},{8,9},{9,8},{10,11... | collective-permute-start | bytes 2359304 | tf_op jit(solution)/shard_map/ppermute | solution.py:648
  538.8 34.6 %collective-permute-start.79 = (bf16[192,2048]{1,0:T(8,128)(2,1)}, bf16[192,2048]{1,0:T(8,128)(2,1)}, u32[]{:S(2)}, u32[]{:S(2)}) collective-permute-start(bf16[192,2048]{1,0:T(8,128)(2,1)} %fusion.33), channel_id=1, source_target_pairs={{0,2},{2,0},{1,3},{3,1},{4,6},{6,4},{5,7},{7,5},{8,10},{10,8},{9,1... | collective-permute-start | bytes 2359304 | tf_op jit(solution)/shard_map/ppermute | solution.py:648
  539.2 27.7 %all-to-all-start.3 = ((bf16[8,64,384]{2,1,0:T(8,128)(2,1)}), bf16[8,64,384]{2,1,0:T(8,128)(2,1)S(1)}, u32[]{:S(2)}, u32[]{:S(2)}) async-start(bf16[8,64,384]{2,1,0:T(8,128)(2,1)} %bitcast.53), calls=%async_computation.4 | async-start | bytes 786432 | tf_op jit(solution)/shard_map/all_to_all | solution.py:955
  545.4 28.0 %collective-permute-start.80 = (bf16[2,64,2048]{2,1,0:T(8,128)(2,1)}, bf16[2,64,2048]{2,1,0:T(8,128)(2,1)}, u32[]{:S(2)}, u32[]{:S(2)}) collective-permute-start(bf16[2,64,2048]{2,1,0:T(8,128)(2,1)} %dynamic-slice_bitcast_fusion.1), channel_id=1, source_target_pairs={{0,2},{2,0},{1,3},{3,1},{4,6},{6,4},{5,7},{7,5},{8,10},{10,8},{9,1... | collective-permute-start | bytes 1572872 | tf_op jit(solution)/shard_map/ppermute | solution.py:648
  (112 other events, 1477.2 us)
Sparse Core Ops, SparseCore 0:
  10.4 30.7 all-gather.2
  42.8 61.4 all-gather.4
  331.6 137.9 reduce-scatter.2
  471.8 54.4 reduce-scatter.4

commit v6 on v5

--- a/solution.py
+++ b/solution.py
@@ -779,9 +779,9 @@
     for n, k in enumerate(range(1, far)):
         held = some_project([((k, 0, 0), far_list[n]), ((k, 0, 1), far_y[n]), ((k, 1, 0), far_z[n])], held)
     w_c = swap(w_rows, C)
-    c_own_other = other_core([cotangent])
-    x_yz, far_yz, held, w_c, c_own_other, cot, c_x, w_parts = sync(
-        x_yz, far_yz, held, w_c, c_own_other, cotangent, c_x, w_parts
+    c_own_other, c_x_other = swap(cotangent, C), swap(c_x, C)
+    x_yz, far_yz, held, w_c, c_own_other, c_x_other, cot, c_x, w_parts = sync(
+        x_yz, far_yz, held, w_c, c_own_other, c_x_other, cotangent, c_x, w_parts
     )
     c_y, c_z = swap(cot, Y), swap(cot, Z)
     w_x = [swap(w_parts[0], X)]
@@ -797,7 +797,7 @@
     c_xz.append(swap(c_z[mid:], X))
     c_yz = swap(c_z, Y)
     c_one = [c_x, c_y, c_z]
-    c_one_other = other_core(c_one)
+    c_one_other = [c_x_other, swap(c_y, C), swap(c_z, C)]
     heads_out, c_xz, c_xy, c_yz, c_xyz, c_one_other = sync(heads_out, c_xz, c_xy, c_yz, c_xyz, c_one_other)
 
     inputs = tokens.astype(F32)
@@ -843,7 +843,7 @@
     xy, xz, yz = swap(x, Y), swap(z, X), swap(y, Z)
     xyz = swap_cube(inner, (X, Z, Y))
     x_stages.append(([[x], [y], [z]], [other_core([x, y, z])]))
-    c_stages.append(([[c] for c in c_one], [c_one_other]))
+    c_stages.append(([[c] for c in c_one], c_one_other))
     c_two_other += [swap(c, C) for c in c_xyz]
     fed.append(run(x_stages[1], c_stages[1]))
     xy, xz, yz, xyz, fed, x_stages, w_parts, c_two, c_two_other = sync(

time: 603 us -> 595 us (0.987)
  waiting for transfers between devices: 163 us -> 153 us
    all_to_all x1, waiting for transfers between devices: 14.5 us -> 6.47 us  [per_device(): lax.all_to_all(attended_low, seq, split_axis=0, concat_axis=1, tiled=True)]
    ppermute x79 -> x81, starting transfers between devices: 66.6 us -> 69.8 us  [swap(): return lax.ppermute(values, axis, [(i, i ^ offset) for i in range(size)])]
    unnamed x149 -> x147, local copies, waits for them, and re-layouts: 21.2 us -> 19.4 us
    ppermute x79 -> x81, waiting for transfers between devices: 101 us -> 101 us  [swap(): return lax.ppermute(values, axis, [(i, i ^ offset) for i in range(size)])]
  transfers between devices with their start and end apart: 90 -> 92, of which waited for: 35 -> 34; matrix products, arithmetic and copies ran while one was open for 24% -> 24% of each run, Pallas kernels for 27% -> 27%
where the time goes in v6:
time: 595 us; the launch traced here: 586 us
  Pallas kernels  161 us (27%)
  waiting for transfers between devices  153 us (26%)
  starting transfers between devices  95.8 us (16%)
  other arithmetic  68.8 us (12%)
  local copies, waits for them, and re-layouts  55.8 us (9%)
  matrix products  36.4 us (6%)
  between operations  15.3 us (3%)
    ppermute x81, waiting for transfers between devices, swap(): return lax.ppermute(values, axis, [(i, i ^ offset) for i in range(size)])  101 us
    ppermute x81, starting transfers between devices, swap(): return lax.ppermute(values, axis, [(i, i ^ offset) for i in range(size)])  69.8 us
    pallas_call x3, Pallas kernels, feed(): pl.pallas_call(functools.partial(feed_kernel, layouts, blocks), grid_spec...  61.8 us
    dot_general x8, matrix products, dot(): return lax.dot_general(left, right, dims, preferred_element_type=F32)  36.4 us
    convert_element_type x13, other arithmetic, add_low(): return (left.astype(F32) + right.astype(F32)).astype(BF16)  31.9 us
    pallas_call x1, Pallas kernels, attend_back(): pl.pallas_call(functools.partial(attend_back_kernel, heads), in_specs=[vm...  26.8 us
    pallas_call x3, Pallas kernels, project(): pl.pallas_call(functools.partial(project_kernel, heads, count, fresh), gr...  22.6 us
    pallas_call x1, Pallas kernels, gate_grad(): pl.pallas_call(functools.partial(gate_grad_kernel, len(arrays), layout),...  20.6 us
  transfers between devices with their start and end apart: 92, of which 34 were waited for; matrix products, arithmetic and copies ran while one was open for 24% of the time, Pallas kernels for 27%

profile of v6, /device:TPU:0, one launch (start us, length us, event | category | flops | bytes accessed | tf_op | source)
XLA Modules:
  0.0 585.9 jit_solution(11393252988296191039)
XLA Ops:
  11.0 4.1 collective-permute-start
  42.8 7.0 %collective-permute-done.refs_0_ = bf16[192,2048]{1,0:T(8,128)(2,1)} collective-permute-done((bf16[192,2048]{1,0:T(8,128)(2,1)S(1)}, bf16[192,2048]{1,0:T(8,128)(2,1)}, u32[]{:S(2)}, u32[]{:S(2)}) %collective-permute-start) | collective-permute-done | bytes 786464 | tf_op jit(solution)/shard_map/ppermute | solution.py:648
  54.8 8.2 %project.3 = (bf16[1536,2048]{1,0:T(8,128)(2,1)}, bf16[4,1536,128]{2,1,0:T(8,128)(2,1)}, bf16[1536,128]{1,0:T(8,128)(2,1)}, bf16[1536,128]{1,0:T(8,128)(2,1)}, f32[1536,384]{1,0:T(8,128)}, /*index=5*/f32[1536,384]{1,0:T(8,128)}) custom-call(s32[3]{0:T(128)} %get-tuple-element.660.index_ref, s32[2]{0:T(128)} %bitcast.184, bf16[192,2048]{1,0:T(8,128)(2,1)} %refs_0_.1, ...), custom_call_target="tpu_custom_call" | custom-call | flops 1000 | bytes 1000 | tf_op jit(solution)/shard_map/project/pallas_call | solution.py:123
  63.0 8.4 %collective-permute-done.4.refs_1_ = bf16[192,2048]{1,0:T(8,128)(2,1)} collective-permute-done((bf16[192,2048]{1,0:T(8,128)(2,1)}, bf16[192,2048]{1,0:T(8,128)(2,1)}, u32[]{:S(2)}, u32[]{:S(2)}) %collective-permute-start.4) | collective-permute-done | bytes 786464 | tf_op jit(solution)/shard_map/ppermute | solution.py:648
  73.5 8.0 %project.4 = (bf16[1536,2048]{1,0:T(8,128)(2,1)}, bf16[4,1536,128]{2,1,0:T(8,128)(2,1)}, bf16[1536,128]{1,0:T(8,128)(2,1)}, bf16[1536,128]{1,0:T(8,128)(2,1)}, f32[1536,384]{1,0:T(8,128)}, /*index=5*/f32[1536,384]{1,0:T(8,128)}) custom-call(s32[3]{0:T(128)} %get-tuple-element.661.index_ref, ...), custom_call_target="tpu_custom_call", output_to_operand_aliasing={{0}: (10, {}), {1}: (11, {}), {2}: (12, {}), {3}: (13, {}),... | custom-call | flops 1000 | bytes 1000 | tf_op jit(solution)/shard_map/project/pallas_call | solution.py:123
  81.6 9.3 %collective-permute-done.6.refs_0_ = bf16[192,2048]{1,0:T(8,128)(2,1)} collective-permute-done((bf16[192,2048]{1,0:T(8,128)(2,1)}, bf16[192,2048]{1,0:T(8,128)(2,1)}, u32[]{:S(2)}, u32[]{:S(2)}) %collective-permute-start.6) | collective-permute-done | bytes 786464 | tf_op jit(solution)/shard_map/ppermute | solution.py:648
  98.8 6.4 %project.5 = (bf16[1536,2048]{1,0:T(8,128)(2,1)}, bf16[4,1536,128]{2,1,0:T(8,128)(2,1)}, bf16[1536,128]{1,0:T(8,128)(2,1)}, bf16[1536,128]{1,0:T(8,128)(2,1)}, f32[1536,384]{1,0:T(8,128)}, /*index=5*/f32[1536,384]{1,0:T(8,128)}) custom-call(s32[2]{0:T(128)} %pad_add_fusion.2.index_ref, ...), custom_call_target="tpu_custom_call", output_to_operand_aliasing={{0}: (9, {}), {1}: (10, {}), {2}: (11, {}), {3}: (12, {}), ... | custom-call | flops 1000 | bytes 1000 | tf_op jit(solution)/shard_map/project/pallas_call | solution.py:123
  105.1 9.6 %attend.1 = (bf16[1536,256]{1,0:T(8,128)(2,1)}, f32[1536,256]{1,0:T(8,128)}, bf16[4,1536,128]{2,1,0:T(8,128)(2,1)}) custom-call(bf16[4,1536,128]{2,1,0:T(8,128)(2,1)} %get-tuple-element.355.q_ref, bf16[1536,128]{1,0:T(8,128)(2,1)} %get-tuple-element.356.k_ref, bf16[1536,128]{1,0:T(8,128)(2,1)} %get-tuple-element.357.v_ref), custom_call_target="tpu_custom_call" | custom-call | flops 1000 | bytes 1000 | tf_op jit(solution)/shard_map/attend/pallas_call | solution.py:215
  114.7 3.1 collective-permute-done.13.refs_7_.refs_10_
  118.5 5.2 all-to-all-start
  129.2 3.8 collective-permute-done.16.refs_6_.refs_9_
  135.0 6.5 %all-to-all-done = bf16[8,192,256]{2,1,0:T(8,128)(2,1)} async-done(((bf16[8,192,256]{2,1,0:T(8,128)(2,1)}), bf16[8,192,256]{2,1,0:T(8,128)(2,1)}, u32[]{:S(2)}, u32[]{:S(2)}) %all-to-all-start) | async-done | bytes 786464 | tf_op jit(solution)/shard_map/all_to_all | solution.py:794
  145.9 3.3 collective-permute-done.18.refs_9_.refs_12_
  153.4 5.6 multiply_reduce_fusion.2
  165.2 11.1 %feed.3 = (bf16[1,192,2048]{2,1,0:T(8,128)(2,1)}, bf16[1,192,2048]{2,1,0:T(8,128)(2,1)}, bf16[1,192,2048]{2,1,0:T(8,128)(2,1)}, bf16[1,192,2048]{2,1,0:T(8,128)(...) custom-call(s32[2]{0:T(128)} %multiply_add_fusion.3.index_ref, ...), custom_call_target="tpu_custom_call" | custom-call | flops 1000 | bytes 1000 | tf_op jit(solution)/shard_map/feed/pallas_call | solution.py:481
  176.4 4.9 collective-permute-done.27.refs_0_.refs_2_
  192.8 22.6 %feed.4 = (bf16[3,192,2048]{2,1,0:T(8,128)(2,1)}, bf16[3,192,2048]{2,1,0:T(8,128)(2,1)}, bf16[3,192,2048]{2,1,0:T(8,128)(2,1)}, bf16[3,192,2048]{2,1,0:T(8,128)(...) custom-call(s32[2]{0:T(128)} %multiply_add_fusion.3.index_ref, bf16[192,2048]{1,0:T(8,128)(2,1)} %copy-done.8, ...), custom_call_target="tpu_custom_call" | custom-call | flops 1000 | bytes 1000 | tf_op jit(solution)/shard_map/feed/pallas_call | solution.py:481
  215.4 7.7 %collective-permute-done.35.refs_3_.refs_9_ = bf16[192,2048]{1,0:T(8,128)(2,1)} collective-permute-done((bf16[192,2048]{1,0:T(8,128)(2,1)}, bf16[192,2048]{1,0:T(8,128)(2,1)}, u32[]{:S(2)}, u32[]{:S(2)}) %collective-permute-start.35) | collective-permute-done | bytes 786464 | tf_op jit(solution)/shard_map/ppermute | solution.py:668
  235.6 28.2 %feed.5 = (bf16[4,192,2048]{2,1,0:T(8,128)(2,1)}, bf16[4,192,2048]{2,1,0:T(8,128)(2,1)}, bf16[4,192,2048]{2,1,0:T(8,128)(2,1)}, bf16[4,192,2048]{2,1,0:T(8,128)(...) custom-call(s32[2]{0:T(128)} %multiply_add_fusion.3.index_ref, ...), custom_call_target="tpu_custom_call" | custom-call | flops 1000 | bytes 1000 | tf_op jit(solution)/shard_map/feed/pallas_call | solution.py:481
  263.9 5.9 collective-permute-done.46
  269.8 3.2 add_convert_fusion
  277.6 13.7 %down_grad.1 = bf16[512,2048]{1,0:T(8,128)(2,1)} custom-call(bf16[192,2048]{1,0:T(8,128)(2,1)} %refs_0_.2, bf16[192,2048]{1,0:T(8,128)(2,1)} %copy-done.19, bf16[192,2048]{1,0:T(8,128)(2,1)} %copy-done.14, bf16[192,2048]{1,0:T(8,128)(2,1)} %copy-done.15, bf16[192,2048]{1,0:T(8,128)(2,1)} %copy-done.16, bf16[192,2048]{1,0:T(8,128)(2,1)} %copy-done.20, ...), custom_call_target="tpu_custom_call" | custom-call | flops 1000 | bytes 1000 | tf_op jit(solution)/shard_map/down_grad/pallas_call | solution.py:593
  291.3 3.1 collective-permute-done.47
  302.9 20.6 %gate_grad.1 = bf16[2048,1024]{1,0:T(8,128)(2,1)} custom-call(bf16[192,2048]{1,0:T(8,128)(2,1)} %multiply_convert_fusion.refs_0_, bf16[192,2048]{1,0:T(8,128)(2,1)} %collective-permute-done.30.refs_1_, bf16[192,2048]{1,0:T(8,128)(2,1)} %copy-done.8, bf16[192,2048]{1,0:T(8,128)(2,1)} %copy-done.9, bf16[192,2048]{1,0:T(8,128)(2,1)} %copy-done.10, ...), custom_call_target="tpu_custom_call" | custom-call | flops 1000 | bytes 1000 | tf_op jit(solution)/shard_map/gate_grad/pallas_call | solution.py:557
  327.0 3.2 multiply_reduce_fusion
  331.6 6.5 %convolution_convert_fusion.1 = bf16[192,2048]{1,0:T(8,128)(2,1)S(1)} fusion(bf16[192,2048]{1,0:T(8,128)(2,1)} %fusion.64, bf16[2048,2048]{1,0:T(8,128)(2,1)} %all-gather.5.cloned.1.call-done), kind=kOutput, calls=%fused_computation.29 | convolution fusion | flops 1611005952 | bytes 9961472 | tf_op jit(solution)/shard_map/dot_general | solution.py:29
  343.5 4.4 all-to-all-start.1
  347.9 5.3 fusion.47
  355.3 3.7 collective-permute-done.59
  361.5 4.2 add_convert_fusion.1
  365.7 11.6 %collective-permute-done.61 = bf16[192,2048]{1,0:T(8,128)(2,1)} collective-permute-done((bf16[192,2048]{1,0:T(8,128)(2,1)S(1)}, bf16[192,2048]{1,0:T(8,128)(2,1)}, u32[]{:S(2)}, u32[]{:S(2)}) %collective-permute-start.61) | collective-permute-done | bytes 786464 | tf_op jit(solution)/shard_map/ppermute | solution.py:648
  377.3 9.3 %all-to-all-done.1 = bf16[192,8,256]{2,0,1:T(8,128)(2,1)} async-done(((bf16[192,8,256]{2,0,1:T(8,128)(2,1)}), bf16[192,8,256]{2,0,1:T(8,128)(2,1)}, u32[]{:S(2)}, u32[]{:S(2)}) %all-to-all-start.1) | async-done | bytes 786464 | tf_op jit(solution)/shard_map/all_to_all | solution.py:894
  388.0 3.9 fusion.18
  395.9 26.8 %attend_back.1 = (bf16[1536,384]{1,0:T(8,128)(2,1)}, f32[8,384]{1,0:T(8,128)}) custom-call(bf16[4,1536,128]{2,1,0:T(8,128)(2,1)} %get-tuple-element.368.q_ref, bf16[1536,128]{1,0:T(8,128)(2,1)} %get-tuple-element.356.k_ref, bf16[1536,128]{1,0:T(8,128)(2,1)} %get-tuple-element.357.v_ref, bf16[1536,256]{1,0:T(8,128)(2,1)} %bitcast.25.grad_ref, ...), custom_call_target="tpu_custom_call" | custom-call | flops 1000 | bytes 1000 | tf_op jit(solution)/shard_map/attend_back/pallas_call | solution.py:347
  423.3 4.2 all-to-all-start.2
  427.6 6.6 %convolution_convert_fusion = bf16[2048,384]{1,0:T(8,128)(2,1)S(1)} fusion(bf16[1536,2048]{1,0:T(8,128)(2,1)} %get-tuple-element.558, bf16[1536,384]{1,0:T(8,128)(2,1)} %get-tuple-element.557), kind=kOutput, calls=%fused_computation.24 | convolution fusion | flops 2416705536 | bytes 9043968 | tf_op jit(solution)/shard_map/dot_general | solution.py:29
  440.3 2.9 fusion.21
  449.2 15.0 %all-to-all-done.2 = bf16[8,192,384]{2,1,0:T(8,128)(2,1)} async-done(((bf16[8,192,384]{2,1,0:T(8,128)(2,1)}), bf16[8,192,384]{2,1,0:T(8,128)(2,1)}, u32[]{:S(2)}, u32[]{:S(2)}) %all-to-all-start.2) | async-done | bytes 1179680 | tf_op jit(solution)/shard_map/all_to_all | solution.py:913
  477.1 3.1 convolution_bitcast_fusion.1
  480.2 3.8 convolution_bitcast_fusion
  487.9 3.6 fusion.36
  491.5 3.1 fusion.39
  505.7 15.6 %collective-permute-done.77 = f32[17,128]{1,0:T(8,128)S(1)} collective-permute-done((f32[17,128]{1,0:T(8,128)S(1)}, f32[17,128]{1,0:T(8,128)S(1)}, u32[]{:S(2)}, u32[]{:S(2)}) %collective-permute-start.77) | collective-permute-done | bytes 8736 | tf_op jit(solution)/shard_map/ppermute | solution.py:648
  530.6 5.3 all-to-all-start.3
  538.7 5.7 place.1
  545.1 13.2 %all-to-all-done.3 = bf16[8,64,384]{2,1,0:T(8,128)(2,1)S(1)} async-done(((bf16[8,64,384]{2,1,0:T(8,128)(2,1)}), bf16[8,64,384]{2,1,0:T(8,128)(2,1)S(1)}, u32[]{:S(2)}, u32[]{:S(2)}) %all-to-all-start.3) | async-done | bytes 393248 | tf_op jit(solution)/shard_map/all_to_all | solution.py:955
  558.3 6.4 %collective-permute-done.82 = bf16[2,64,2048]{2,1,0:T(8,128)(2,1)} collective-permute-done((bf16[2,64,2048]{2,1,0:T(8,128)(2,1)}, bf16[2,64,2048]{2,1,0:T(8,128)(2,1)}, u32[]{:S(2)}, u32[]{:S(2)}) %collective-permute-start.82) | collective-permute-done | bytes 524320 | tf_op jit(solution)/shard_map/ppermute | solution.py:648
  568.6 3.1 fusion.31
  (392 shorter events, 190.4 us)
Async XLA Ops:
  7.2 47.6 %all-gather.3.cloned.1.call-start = ((), (), s32[]{:S(2)}) async-start(), calls=%async_computation.6 | async-start | bytes 1966080 | tf_op jit(solution)/shard_map/all_gather | solution.py:743
  10.3 143.2 %all-gather.5.cloned.1.call-start = ((), (), s32[]{:S(2)}) async-start(), calls=%async_computation.7 | async-start | bytes 10485760 | tf_op jit(solution)/shard_map/all_gather | solution.py:744
  11.0 38.7 %collective-permute-start = (bf16[192,2048]{1,0:T(8,128)(2,1)S(1)}, bf16[192,2048]{1,0:T(8,128)(2,1)}, u32[]{:S(2)}, u32[]{:S(2)}) collective-permute-start(bf16[192,2048]{1,0:T(8,128)(2,1)S(1)} %copy-done.11), channel_id=1, source_target_pairs={{0,4},{4,0},{1,5},{5,1},{2,6},{6,2},{3,7},{7,3},{8,12},{12,8},{9,1... | collective-permute-start | bytes 2359304 | tf_op jit(solution)/shard_map/ppermute | solution.py:648
  15.1 34.6 %collective-permute-start.1 = (bf16[192,2048]{1,0:T(8,128)(2,1)S(1)}, bf16[192,2048]{1,0:T(8,128)(2,1)}, u32[]{:S(2)}, u32[]{:S(2)}) collective-permute-start(bf16[192,2048]{1,0:T(8,128)(2,1)S(1)} %copy-done.11), channel_id=1, source_target_pairs={{0,1},{1,0},{2,3},{3,2},{4,5},{5,4},{6,7},{7,6},{8,9},{9,8},{10,11... | collective-permute-start | bytes 2359304 | tf_op jit(solution)/shard_map/ppermute | solution.py:648
  16.7 34.5 %collective-permute-start.2 = (bf16[192,2048]{1,0:T(8,128)(2,1)S(1)}, bf16[192,2048]{1,0:T(8,128)(2,1)}, u32[]{:S(2)}, u32[]{:S(2)}) collective-permute-start(bf16[192,2048]{1,0:T(8,128)(2,1)S(1)} %copy-done.11), channel_id=1, source_target_pairs={{0,2},{2,0},{1,3},{3,1},{4,6},{6,4},{5,7},{7,5},{8,10},{10,8},{9,1... | collective-permute-start | bytes 2359304 | tf_op jit(solution)/shard_map/ppermute | solution.py:648
  18.2 32.9 %collective-permute-start.3 = (bf16[192,2048]{1,0:T(8,128)(2,1)S(1)}, bf16[192,2048]{1,0:T(8,128)(2,1)S(1)}, u32[]{:S(2)}, u32[]{:S(2)}) collective-permute-start(bf16[192,2048]{1,0:T(8,128)(2,1)S(1)} %copy-done.1), channel_id=1, source_target_pairs={{0,16},{16,0},{1,17},{17,1},{2,18},{18,2},{3,19},{19,3},{4,20},{20... | collective-permute-start | bytes 2359304 | tf_op jit(solution)/shard_map/ppermute | solution.py:648
  51.2 40.6 %collective-permute-start.8 = (bf16[512,3072]{1,0:T(8,128)(2,1)}, bf16[512,3072]{1,0:T(8,128)(2,1)}, u32[]{:S(2)}, u32[]{:S(2)}) collective-permute-start(bf16[512,3072]{1,0:T(8,128)(2,1)} %bitcast.84), channel_id=1, source_target_pairs={{0,8},{8,0},{1,9},{9,1},{2,10},{10,2},{3,11},{11,3},{4,12},{12,4},... | collective-permute-start | bytes 9437192 | tf_op jit(solution)/shard_map/ppermute | solution.py:648
  53.0 28.5 %collective-permute-start.9 = (bf16[192,2048]{1,0:T(8,128)(2,1)S(1)}, bf16[192,2048]{1,0:T(8,128)(2,1)S(1)}, u32[]{:S(2)}, u32[]{:S(2)}) collective-permute-start(bf16[192,2048]{1,0:T(8,128)(2,1)S(1)} %copy-done.1), channel_id=1, source_target_pairs={{0,8},{8,0},{1,9},{9,1},{2,10},{10,2},{3,11},{11,3},{4,12},{12,4},... | collective-permute-start | bytes 2359304 | tf_op jit(solution)/shard_map/ppermute | solution.py:648
  54.3 27.3 %collective-permute-start.10 = (bf16[192,2048]{1,0:T(8,128)(2,1)S(1)}, bf16[192,2048]{1,0:T(8,128)(2,1)S(1)}, u32[]{:S(2)}, u32[]{:S(2)}) collective-permute-start(bf16[192,2048]{1,0:T(8,128)(2,1)S(1)} %collective-permute-done.3.refs_4_.refs_2_), channel_id=1, source_target_pairs={{0,8},{8,0},{1,9},{9,1},{2,10},{10,2},{3,11},{11,3},{4,12},{12,4},... | collective-permute-start | bytes 2359304 | tf_op jit(solution)/shard_map/ppermute | solution.py:648
  91.8 26.7 %collective-permute-start.11 = (bf16[192,2048]{1,0:T(8,128)(2,1)S(1)}, bf16[192,2048]{1,0:T(8,128)(2,1)S(1)}, u32[]{:S(2)}, u32[]{:S(2)}) collective-permute-start(bf16[192,2048]{1,0:T(8,128)(2,1)S(1)} %copy-done.1), channel_id=1, source_target_pairs={{0,1},{1,0},{2,3},{3,2},{4,5},{5,4},{6,7},{7,6},{8,9},{9,8},{10,11... | collective-permute-start | bytes 2359304 | tf_op jit(solution)/shard_map/ppermute | solution.py:648
  92.5 26.0 %collective-permute-start.12 = (bf16[192,2048]{1,0:T(8,128)(2,1)S(1)}, bf16[192,2048]{1,0:T(8,128)(2,1)S(1)}, u32[]{:S(2)}, u32[]{:S(2)}) collective-permute-start(bf16[192,2048]{1,0:T(8,128)(2,1)S(1)} %copy-done.1), channel_id=1, source_target_pairs={{0,2},{2,0},{1,3},{3,1},{4,6},{6,4},{5,7},{7,5},{8,10},{10,8},{9,1... | collective-permute-start | bytes 2359304 | tf_op jit(solution)/shard_map/ppermute | solution.py:648
  94.1 24.4 %collective-permute-start.15 = (bf16[128,3072]{1,0:T(8,128)(2,1)}, bf16[128,3072]{1,0:T(8,128)(2,1)}, u32[]{:S(2)}, u32[]{:S(2)}) collective-permute-start(bf16[128,3072]{1,0:T(8,128)(2,1)} %bitcast.176), channel_id=1, source_target_pairs={{0,16},{16,0},{1,17},{17,1},{2,18},{18,2},{3,19},{19,3},{4,20},{20... | collective-permute-start | bytes 2359304 | tf_op jit(solution)/shard_map/ppermute | solution.py:648
  118.5 23.0 %all-to-all-start = ((bf16[8,192,256]{2,1,0:T(8,128)(2,1)}), bf16[8,192,256]{2,1,0:T(8,128)(2,1)}, u32[]{:S(2)}, u32[]{:S(2)}) async-start(bf16[8,192,256]{2,1,0:T(8,128)(2,1)} %bitcast.177), calls=%async_computation | async-start | bytes 1572864 | tf_op jit(solution)/shard_map/all_to_all | solution.py:794
  123.7 343.0 %reduce-scatter.3.cloned.1.call-start = ((), (), s32[]{:S(2)}) async-start(), calls=%async_computation.8 | async-start | bytes 6291456 | tf_op jit(solution)/shard_map/reduce_scatter | solution.py:868
  125.4 23.8 %collective-permute-start.18 = (bf16[192,2048]{1,0:T(8,128)(2,1)}, bf16[192,2048]{1,0:T(8,128)(2,1)}, u32[]{:S(2)}, u32[]{:S(2)}) collective-permute-start(bf16[192,2048]{1,0:T(8,128)(2,1)} %copy-done.16), channel_id=1, source_target_pairs={{0,1},{1,0},{2,3},{3,2},{4,5},{5,4},{6,7},{7,6},{8,9},{9,8},{10,11... | collective-permute-start | bytes 2359304 | tf_op jit(solution)/shard_map/ppermute | solution.py:648
  127.4 21.8 %collective-permute-start.21 = (bf16[192,2048]{1,0:T(8,128)(2,1)}, bf16[192,2048]{1,0:T(8,128)(2,1)S(1)}, u32[]{:S(2)}, u32[]{:S(2)}) collective-permute-start(bf16[192,2048]{1,0:T(8,128)(2,1)} %copy-done.16), channel_id=1, source_target_pairs={{0,8},{8,0},{1,9},{9,1},{2,10},{10,2},{3,11},{11,3},{4,12},{12,4},... | collective-permute-start | bytes 2359304 | tf_op jit(solution)/shard_map/ppermute | solution.py:648
  184.1 31.3 %collective-permute-start.32 = (bf16[192,2048]{1,0:T(8,128)(2,1)}, bf16[192,2048]{1,0:T(8,128)(2,1)}, u32[]{:S(2)}, u32[]{:S(2)}) collective-permute-start(bf16[192,2048]{1,0:T(8,128)(2,1)} %copy-done.8), channel_id=1, source_target_pairs={{0,1},{1,0},{2,3},{3,2},{4,5},{5,4},{6,7},{7,6},{8,9},{9,8},{10,11... | collective-permute-start | bytes 2359304 | tf_op jit(solution)/shard_map/ppermute | solution.py:648
  185.5 29.9 %collective-permute-start.33 = (bf16[192,2048]{1,0:T(8,128)(2,1)}, bf16[192,2048]{1,0:T(8,128)(2,1)}, u32[]{:S(2)}, u32[]{:S(2)}) collective-permute-start(bf16[192,2048]{1,0:T(8,128)(2,1)} %copy-done.10), channel_id=1, source_target_pairs={{0,16},{16,0},{1,17},{17,1},{2,18},{18,2},{3,19},{19,3},{4,20},{20... | collective-permute-start | bytes 2359304 | tf_op jit(solution)/shard_map/ppermute | solution.py:648
  186.5 28.9 %collective-permute-start.34 = (bf16[192,2048]{1,0:T(8,128)(2,1)}, bf16[192,2048]{1,0:T(8,128)(2,1)}, u32[]{:S(2)}, u32[]{:S(2)}) collective-permute-start(bf16[192,2048]{1,0:T(8,128)(2,1)} %copy-done.9), channel_id=1, source_target_pairs={{0,2},{2,0},{1,3},{3,1},{4,6},{6,4},{5,7},{7,5},{8,10},{10,8},{9,1... | collective-permute-start | bytes 2359304 | tf_op jit(solution)/shard_map/ppermute | solution.py:648
  188.5 34.6 %collective-permute-start.35 = (bf16[192,2048]{1,0:T(8,128)(2,1)}, bf16[192,2048]{1,0:T(8,128)(2,1)}, u32[]{:S(2)}, u32[]{:S(2)}) collective-permute-start(bf16[192,2048]{1,0:T(8,128)(2,1)} %multiply_convert_fusion.refs_0_), channel_id=1, source_target_pairs={{0,19},{1,18},{2,17},{3,16},{16,3},{17,2},{18,1},{19,0},{4,23},{5,... | collective-permute-start | bytes 2359304 | tf_op jit(solution)/shard_map/ppermute | solution.py:668
  191.4 24.0 %collective-permute-start.38 = (bf16[96,2048]{1,0:T(8,128)(2,1)}, bf16[96,2048]{1,0:T(8,128)(2,1)}, u32[]{:S(2)}, u32[]{:S(2)}) collective-permute-start(bf16[96,2048]{1,0:T(8,128)(2,1)} %collective-permute-done.22.refs_11_.refs_14_), channel_id=1, source_target_pairs={{0,8},{8,0},{1,9},{9,1},{2,10},{10,2},{3,11},{11,3},{4,12},{12,4},... | collective-permute-start | bytes 1179656 | tf_op jit(solution)/shard_map/ppermute | solution.py:648
  226.0 37.8 %collective-permute-start.45 = (bf16[128,3072]{1,0:T(8,128)(2,1)}, bf16[128,3072]{1,0:T(8,128)(2,1)}, u32[]{:S(2)}, u32[]{:S(2)}) collective-permute-start(bf16[128,3072]{1,0:T(8,128)(2,1)} %bitcast.88), channel_id=1, source_target_pairs={{0,16},{16,0},{1,17},{17,1},{2,18},{18,2},{3,19},{19,3},{4,20},{20... | collective-permute-start | bytes 2359304 | tf_op jit(solution)/shard_map/ppermute | solution.py:648
  230.4 33.3 %collective-permute-start.41 = (bf16[192,2048]{1,0:T(8,128)(2,1)}, bf16[192,2048]{1,0:T(8,128)(2,1)S(1)}, u32[]{:S(2)}, u32[]{:S(2)}) collective-permute-start(bf16[192,2048]{1,0:T(8,128)(2,1)} %get-tuple-element.631), channel_id=1, source_target_pairs={{0,16},{16,0},{1,17},{17,1},{2,18},{18,2},{3,19},{19,3},{4,20},{20... | collective-permute-start | bytes 2359304 | tf_op jit(solution)/shard_map/ppermute | solution.py:648
  231.4 32.4 %collective-permute-start.42 = (bf16[192,2048]{1,0:T(8,128)(2,1)}, bf16[192,2048]{1,0:T(8,128)(2,1)S(1)}, u32[]{:S(2)}, u32[]{:S(2)}) collective-permute-start(bf16[192,2048]{1,0:T(8,128)(2,1)} %get-tuple-element.630), channel_id=1, source_target_pairs={{0,1},{1,0},{2,3},{3,2},{4,5},{5,4},{6,7},{7,6},{8,9},{9,8},{10,11... | collective-permute-start | bytes 2359304 | tf_op jit(solution)/shard_map/ppermute | solution.py:648
  232.9 31.0 %collective-permute-start.43 = (bf16[192,2048]{1,0:T(8,128)(2,1)}, bf16[192,2048]{1,0:T(8,128)(2,1)S(1)}, u32[]{:S(2)}, u32[]{:S(2)}) collective-permute-start(bf16[192,2048]{1,0:T(8,128)(2,1)} %get-tuple-element.629), channel_id=1, source_target_pairs={{0,2},{2,0},{1,3},{3,1},{4,6},{6,4},{5,7},{7,5},{8,10},{10,8},{9,1... | collective-permute-start | bytes 2359304 | tf_op jit(solution)/shard_map/ppermute | solution.py:648
  295.6 27.9 %collective-permute-start.53 = (bf16[3,192,2048]{2,1,0:T(8,128)(2,1)}, bf16[3,192,2048]{2,1,0:T(8,128)(2,1)}, u32[]{:S(2)}, u32[]{:S(2)}) collective-permute-start(bf16[3,192,2048]{2,1,0:T(8,128)(2,1)} %get-tuple-element.507), channel_id=1, source_target_pairs={{0,8},{8,0},{1,9},{9,1},{2,10},{10,2},{3,11},{11,3},{4,12},{12,4},... | collective-permute-start | bytes 7077896 | tf_op jit(solution)/shard_map/ppermute | solution.py:648
  297.9 25.6 %collective-permute-start.50 = (bf16[192,2048]{1,0:T(8,128)(2,1)}, bf16[192,2048]{1,0:T(8,128)(2,1)S(1)}, u32[]{:S(2)}, u32[]{:S(2)}) collective-permute-start(bf16[192,2048]{1,0:T(8,128)(2,1)} %add_convert_fusion.10), channel_id=1, source_target_pairs={{0,18},{2,16},{16,2},{18,0},{1,19},{3,17},{17,3},{19,1},{4,22},{6,... | collective-permute-start | bytes 2359304 | tf_op jit(solution)/shard_map/ppermute | solution.py:668
  341.9 23.8 %collective-permute-start.62 = (bf16[256,3072]{1,0:T(8,128)(2,1)}, bf16[256,3072]{1,0:T(8,128)(2,1)}, u32[]{:S(2)}, u32[]{:S(2)}) collective-permute-start(bf16[256,3072]{1,0:T(8,128)(2,1)} %pad_maximum_fusion.3), channel_id=1, source_target_pairs={{0,8},{8,0},{1,9},{9,1},{2,10},{10,2},{3,11},{11,3},{4,12},{12,4},... | collective-permute-start | bytes 4718600 | tf_op jit(solution)/shard_map/ppermute | solution.py:648
  342.4 23.3 %collective-permute-start.58 = (bf16[192,2048]{1,0:T(8,128)(2,1)}, bf16[192,2048]{1,0:T(8,128)(2,1)}, u32[]{:S(2)}, u32[]{:S(2)}) collective-permute-start(bf16[192,2048]{1,0:T(8,128)(2,1)} %fusion.64), channel_id=1, source_target_pairs={{0,8},{8,0},{1,9},{9,1},{2,10},{10,2},{3,11},{11,3},{4,12},{12,4},... | collective-permute-start | bytes 2359304 | tf_op jit(solution)/shard_map/ppermute | solution.py:648
  343.5 43.0 %all-to-all-start.1 = ((bf16[192,8,256]{2,0,1:T(8,128)(2,1)}), bf16[192,8,256]{2,0,1:T(8,128)(2,1)}, u32[]{:S(2)}, u32[]{:S(2)}) async-start(bf16[192,8,256]{2,0,1:T(8,128)(2,1)} %bitcast.162), calls=%async_computation.1 | async-start | bytes 1572864 | tf_op jit(solution)/shard_map/all_to_all | solution.py:894
  353.2 24.0 %collective-permute-start.61 = (bf16[192,2048]{1,0:T(8,128)(2,1)S(1)}, bf16[192,2048]{1,0:T(8,128)(2,1)}, u32[]{:S(2)}, u32[]{:S(2)}) collective-permute-start(bf16[192,2048]{1,0:T(8,128)(2,1)S(1)} %get-tuple-element.619), channel_id=1, source_target_pairs={{0,1},{1,0},{2,3},{3,2},{4,5},{5,4},{6,7},{7,6},{8,9},{9,8},{10,11... | collective-permute-start | bytes 2359304 | tf_op jit(solution)/shard_map/ppermute | solution.py:648
  359.0 27.6 %collective-permute-start.60 = (bf16[192,2048]{1,0:T(8,128)(2,1)}, bf16[192,2048]{1,0:T(8,128)(2,1)}, u32[]{:S(2)}, u32[]{:S(2)}) collective-permute-start(bf16[192,2048]{1,0:T(8,128)(2,1)} %collective-permute-done.59), channel_id=1, source_target_pairs={{0,8},{8,0},{1,9},{9,1},{2,10},{10,2},{3,11},{11,3},{4,12},{12,4},... | collective-permute-start | bytes 2359304 | tf_op jit(solution)/shard_map/ppermute | solution.py:648
  386.5 36.7 %collective-permute-start.63 = (bf16[256,3072]{1,0:T(8,128)(2,1)}, bf16[256,3072]{1,0:T(8,128)(2,1)}, u32[]{:S(2)}, u32[]{:S(2)}) collective-permute-start(bf16[256,3072]{1,0:T(8,128)(2,1)} %bitcast.171), channel_id=1, source_target_pairs={{0,16},{16,0},{1,17},{17,1},{2,18},{18,2},{3,19},{19,3},{4,20},{20... | collective-permute-start | bytes 4718600 | tf_op jit(solution)/shard_map/ppermute | solution.py:648
  394.4 28.3 %collective-permute-start.64 = (bf16[2,2,64,2048]{3,2,0,1:T(8,128)(2,1)}, bf16[2,2,64,2048]{3,2,0,1:T(8,128)(2,1)}, u32[]{:S(2)}, u32[]{:S(2)}) collective-permute-start(bf16[2,2,64,2048]{3,2,0,1:T(8,128)(2,1)} %copy_bitcast_fusion), channel_id=1, source_target_pairs={{0,1},{1,0},{2,3},{3,2},{4,5},{5,4},{6,7},{7,6},{8,9},{9,8},{10,11... | collective-permute-start | bytes 3145736 | tf_op jit(solution)/shard_map/ppermute | solution.py:648
  423.3 40.9 %all-to-all-start.2 = ((bf16[8,192,384]{2,1,0:T(8,128)(2,1)}), bf16[8,192,384]{2,1,0:T(8,128)(2,1)}, u32[]{:S(2)}, u32[]{:S(2)}) async-start(bf16[8,192,384]{2,1,0:T(8,128)(2,1)} %bitcast.175), calls=%async_computation.2 | async-start | bytes 2359296 | tf_op jit(solution)/shard_map/all_to_all | solution.py:913
  427.5 130.8 %reduce-scatter.5.cloned.1.call-start = ((), (), s32[]{:S(2)}) async-start(), calls=%async_computation.9 | async-start | bytes 3145728 | tf_op jit(solution)/shard_map/reduce_scatter | solution.py:869
  436.3 30.4 %collective-permute-start.67 = (bf16[256,3072]{1,0:T(8,128)(2,1)}, bf16[256,3072]{1,0:T(8,128)(2,1)}, u32[]{:S(2)}, u32[]{:S(2)}) collective-permute-start(bf16[256,3072]{1,0:T(8,128)(2,1)} %collective-permute-done.63), channel_id=1, source_target_pairs={{0,8},{8,0},{1,9},{9,1},{2,10},{10,2},{3,11},{11,3},{4,12},{12,4},... | collective-permute-start | bytes 4718600 | tf_op jit(solution)/shard_map/ppermute | solution.py:648
  436.9 29.8 %collective-permute-start.68 = (bf16[192,2048]{1,0:T(8,128)(2,1)}, bf16[192,2048]{1,0:T(8,128)(2,1)}, u32[]{:S(2)}, u32[]{:S(2)}) collective-permute-start(bf16[192,2048]{1,0:T(8,128)(2,1)} %get-tuple-element.566), channel_id=1, source_target_pairs={{0,16},{16,0},{1,17},{17,1},{2,18},{18,2},{3,19},{19,3},{4,20},{20... | collective-permute-start | bytes 2359304 | tf_op jit(solution)/shard_map/ppermute | solution.py:648
  438.4 28.3 %collective-permute-start.69 = (bf16[192,2048]{1,0:T(8,128)(2,1)}, bf16[192,2048]{1,0:T(8,128)(2,1)}, u32[]{:S(2)}, u32[]{:S(2)}) collective-permute-start(bf16[192,2048]{1,0:T(8,128)(2,1)} %get-tuple-element.567), channel_id=1, source_target_pairs={{0,1},{1,0},{2,3},{3,2},{4,5},{5,4},{6,7},{7,6},{8,9},{9,8},{10,11... | collective-permute-start | bytes 2359304 | tf_op jit(solution)/shard_map/ppermute | solution.py:648
  469.3 56.7 %collective-permute-start.70 = (bf16[192,2048]{1,0:T(8,128)(2,1)}, bf16[192,2048]{1,0:T(8,128)(2,1)}, u32[]{:S(2)}, u32[]{:S(2)}) collective-permute-start(bf16[192,2048]{1,0:T(8,128)(2,1)} %add_convert_fusion.3), channel_id=1, source_target_pairs={{0,16},{16,0},{1,17},{17,1},{2,18},{18,2},{3,19},{19,3},{4,20},{20... | collective-permute-start | bytes 2359304 | tf_op jit(solution)/shard_map/ppermute | solution.py:648
  473.6 52.3 %collective-permute-start.71 = (bf16[256,1024]{1,0:T(8,128)(2,1)}, bf16[256,1024]{1,0:T(8,128)(2,1)}, u32[]{:S(2)}, u32[]{:S(2)}) collective-permute-start(bf16[256,1024]{1,0:T(8,128)(2,1)} %get-tuple-element.634), channel_id=1, source_target_pairs={{0,1},{1,0},{2,3},{3,2},{4,5},{5,4},{6,7},{7,6},{8,9},{9,8},{10,11... | collective-permute-start | bytes 1572872 | tf_op jit(solution)/shard_map/ppermute | solution.py:648
  475.1 50.8 %collective-permute-start.72 = (bf16[256,1024]{1,0:T(8,128)(2,1)}, bf16[256,1024]{1,0:T(8,128)(2,1)}, u32[]{:S(2)}, u32[]{:S(2)}) collective-permute-start(bf16[256,1024]{1,0:T(8,128)(2,1)} %get-tuple-element.633), channel_id=1, source_target_pairs={{0,2},{2,0},{1,3},{3,1},{4,6},{6,4},{5,7},{7,5},{8,10},{10,8},{9,1... | collective-permute-start | bytes 1572872 | tf_op jit(solution)/shard_map/ppermute | solution.py:648
  475.2 50.8 %collective-permute-start.73 = (bf16[256,1024]{1,0:T(8,128)(2,1)}, bf16[256,1024]{1,0:T(8,128)(2,1)}, u32[]{:S(2)}, u32[]{:S(2)}) collective-permute-start(bf16[256,1024]{1,0:T(8,128)(2,1)} %get-tuple-element.632), channel_id=1, source_target_pairs={{0,3},{1,2},{2,1},{3,0},{4,7},{5,6},{6,5},{7,4},{8,11},{9,10},{10,... | collective-permute-start | bytes 1572872 | tf_op jit(solution)/shard_map/ppermute | solution.py:668
  526.0 38.8 %collective-permute-start.79 = (bf16[192,2048]{1,0:T(8,128)(2,1)}, bf16[192,2048]{1,0:T(8,128)(2,1)}, u32[]{:S(2)}, u32[]{:S(2)}) collective-permute-start(bf16[192,2048]{1,0:T(8,128)(2,1)} %slice_bitcast_fusion.7), channel_id=1, source_target_pairs={{0,16},{16,0},{1,17},{17,1},{2,18},{18,2},{3,19},{19,3},{4,20},{20... | collective-permute-start | bytes 2359304 | tf_op jit(solution)/shard_map/ppermute | solution.py:648
  526.9 37.9 %collective-permute-start.80 = (bf16[192,2048]{1,0:T(8,128)(2,1)}, bf16[192,2048]{1,0:T(8,128)(2,1)}, u32[]{:S(2)}, u32[]{:S(2)}) collective-permute-start(bf16[192,2048]{1,0:T(8,128)(2,1)} %fusion.34), channel_id=1, source_target_pairs={{0,1},{1,0},{2,3},{3,2},{4,5},{5,4},{6,7},{7,6},{8,9},{9,8},{10,11... | collective-permute-start | bytes 2359304 | tf_op jit(solution)/shard_map/ppermute | solution.py:648
  530.1 34.6 %collective-permute-start.81 = (bf16[192,2048]{1,0:T(8,128)(2,1)}, bf16[192,2048]{1,0:T(8,128)(2,1)}, u32[]{:S(2)}, u32[]{:S(2)}) collective-permute-start(bf16[192,2048]{1,0:T(8,128)(2,1)} %fusion.33), channel_id=1, source_target_pairs={{0,2},{2,0},{1,3},{3,1},{4,6},{6,4},{5,7},{7,5},{8,10},{10,8},{9,1... | collective-permute-start | bytes 2359304 | tf_op jit(solution)/shard_map/ppermute | solution.py:648
  530.6 27.7 %all-to-all-start.3 = ((bf16[8,64,384]{2,1,0:T(8,128)(2,1)}), bf16[8,64,384]{2,1,0:T(8,128)(2,1)S(1)}, u32[]{:S(2)}, u32[]{:S(2)}) async-start(bf16[8,64,384]{2,1,0:T(8,128)(2,1)} %bitcast.53), calls=%async_computation.4 | async-start | bytes 786432 | tf_op jit(solution)/shard_map/all_to_all | solution.py:955
  536.7 28.0 %collective-permute-start.82 = (bf16[2,64,2048]{2,1,0:T(8,128)(2,1)}, bf16[2,64,2048]{2,1,0:T(8,128)(2,1)}, u32[]{:S(2)}, u32[]{:S(2)}) collective-permute-start(bf16[2,64,2048]{2,1,0:T(8,128)(2,1)} %dynamic-slice_bitcast_fusion.1), channel_id=1, source_target_pairs={{0,2},{2,0},{1,3},{3,1},{4,6},{6,4},{5,7},{7,5},{8,10},{10,8},{9,1... | collective-permute-start | bytes 1572872 | tf_op jit(solution)/shard_map/ppermute | solution.py:648
  (113 other events, 1477.1 us)
Sparse Core Ops, SparseCore 0:
  10.4 30.7 all-gather.2
  42.8 62.4 all-gather.4
  323.7 137.2 reduce-scatter.2
  463.1 54.5 reduce-scatter.4
